TPU v7x, 512 devices: a whole 4x4x16 slice. The times are simulated.
512 devices in a mesh: dp: 8 (over x, core), expert: 64 (over z, y).
Axes of the slice: x: 4, y: 4, z: 16, core: 2. Of those that a mesh axis runs over, the one named last changes fastest.
Arguments:
- tokens: bfloat16 [2048, 4096], P('expert', 'dp'), may hold values from -6 to 6
- grad_out: bfloat16 [2048, 4096], P('expert', 'dp'), may hold values from -6 to 6
- route_prob: float32 [2048, 8], P('expert'), may hold values from 0.05 to 0.5
- expert_ids: int32 [2048, 8], P('expert'), may hold values from 0 to 63, all different within a row; in each aligned block of 32 rows (0 to 31, 32 to 63, ...) at most 5 rows name the same one
- w_gate: bfloat16 [64, 1536, 4096], P('expert', 'dp'), may hold values from -0.09375 to 0.09375
- w_up: bfloat16 [64, 1536, 4096], P('expert', 'dp'), may hold values from -0.09375 to 0.09375
- w_down: bfloat16 [64, 1536, 4096], P('expert', 'dp'), may hold values from -0.15625 to 0.15625
- adapter_a: bfloat16 [64, 64, 1536], P('expert', None, 'dp'), may hold values from -0.15625 to 0.15625
- adapter_b: bfloat16 [64, 64, 4096], P('expert', None, 'dp'), may hold values from -0.09375 to 0.09375
Outputs:
- grad_tokens: bfloat16 [2048, 4096], P('expert', 'dp')
- grad_adapter_a: float32 [64, 64, 1536], P('expert', None, 'dp')
- grad_adapter_b: float32 [64, 64, 4096], P('expert', None, 'dp')
Inputs may be any that keep to these rules, and one draw needn't show every extreme that they name: `expert_ids`: each row names 8 different experts. In each aligned block of 32 tokens (those of one index of the expert axis) no expert is named by more than 5 rows, a bound that some block reaches.
All inputs are finite; a program needn't handle non-finite values.
Results may differ from a plain program's by a relative error of at most 0.019.
Values may be sent and summed in bfloat16 or wider, within the bound.
No kernel may reach another device: no remote copies, remote signals or barrier semaphores. Data moves between devices by JAX's collectives and lax.ppermute only.
A program may use at most 64 MiB of HBM per device.

v0:
```python
import jax
import jax.numpy as jnp
from jax import lax
from jax.sharding import PartitionSpec as P


def contract(left, right, left_dim, right_dim):
    return lax.dot_general(
        left, right, (((left_dim,), (right_dim,)), ((), ())), preferred_element_type=jnp.float32
    )


def per_device(
    tokens, grad_out, route_prob, expert_ids, w_gate, w_up, w_down, adapter_a, adapter_b
):
    expert_count = lax.axis_size("expert")
    unit_count = lax.axis_size("dp")
    local_tokens, top_count = expert_ids.shape
    capacity = 5 * local_tokens * top_count // (4 * expert_count)
    slot_count = expert_count * capacity
    d_block = tokens.shape[1]
    full_width = d_block * unit_count
    hits = (
        expert_ids[:, :, None] == jnp.arange(expert_count, dtype=jnp.int32)[None, None, :]
    ).astype(jnp.int32)
    flat_hits = hits.reshape(local_tokens * top_count, expert_count)
    earlier = jnp.cumsum(flat_hits, axis=0) - flat_hits
    slot_of = jnp.sum(earlier * flat_hits, axis=1)
    target = expert_ids.reshape(local_tokens * top_count) * capacity + slot_of
    placed = (target[None, :] == jnp.arange(slot_count, dtype=jnp.int32)[:, None]).astype(
        jnp.float32
    )
    placed_low = placed.astype(jnp.bfloat16)
    token_map = jnp.sum(placed.reshape(slot_count, local_tokens, top_count), axis=2)
    map_low = token_map.astype(jnp.bfloat16)
    x_whole, dy_whole, b_whole = (
        lax.all_gather(tokens, "dp", axis=1, tiled=True),
        lax.all_gather(grad_out, "dp", axis=1, tiled=True),
        lax.all_gather(adapter_b, "dp", axis=2, tiled=True),
    )
    packed = jnp.dot(map_low, x_whole, preferred_element_type=jnp.float32).astype(jnp.bfloat16)
    x_sent = lax.all_to_all(
        packed.reshape(expert_count, capacity, x_whole.shape[1]),
        "expert",
        split_axis=0,
        concat_axis=0,
        tiled=True,
    )
    weighted = (route_prob[:, :, None] * dy_whole[:, None, :].astype(jnp.float32)).astype(
        jnp.bfloat16
    )
    weighted = weighted.reshape(local_tokens * top_count, dy_whole.shape[1])
    packed = jnp.dot(placed_low, weighted, preferred_element_type=jnp.float32).astype(jnp.bfloat16)
    dy_sent = lax.all_to_all(
        packed.reshape(expert_count, capacity, dy_whole.shape[1]),
        "expert",
        split_axis=0,
        concat_axis=0,
        tiled=True,
    )
    x_rows = x_sent.reshape(slot_count, full_width)
    scaled = dy_sent.reshape(slot_count, full_width)
    gate_mat = w_gate[0]
    up_mat = w_up[0]
    down_mat = w_down[0]
    low_a = adapter_a[0]
    low_b = b_whole[0]
    gate_pre = contract(x_rows, gate_mat, 1, 1)
    up_pre = contract(x_rows, up_mat, 1, 1)
    sigma = jax.nn.sigmoid(gate_pre)
    active = gate_pre * sigma
    hidden = (active * up_pre).astype(jnp.bfloat16)
    low_u = contract(scaled, low_b, 1, 1).astype(jnp.bfloat16)
    grad_hidden = contract(scaled, down_mat, 1, 1) + jnp.dot(
        low_u, low_a, preferred_element_type=jnp.float32
    )
    partial_v = contract(hidden, low_a, 1, 1)
    low_v = lax.psum(partial_v.astype(jnp.bfloat16), "dp")
    grad_gate = (grad_hidden * up_pre * sigma * (1.0 + gate_pre * (1.0 - sigma))).astype(
        jnp.bfloat16
    )
    grad_up = (grad_hidden * active).astype(jnp.bfloat16)
    unit_term = jnp.dot(grad_gate, gate_mat, preferred_element_type=jnp.float32) + jnp.dot(
        grad_up, up_mat, preferred_element_type=jnp.float32
    )
    grad_a = contract(low_u, hidden, 0, 0)[None]
    offset = lax.axis_index("dp") * d_block
    own_scaled = lax.dynamic_slice_in_dim(scaled, offset, d_block, 1)
    grad_b = contract(low_v, own_scaled, 0, 0)[None]
    unit_sums = lax.psum_scatter(
        unit_term.reshape(expert_count, capacity, full_width).astype(jnp.bfloat16),
        "dp",
        scatter_dimension=2,
        tiled=True,
    ).astype(jnp.float32)
    returned = lax.all_to_all(
        unit_sums.astype(jnp.bfloat16), "expert", split_axis=0, concat_axis=0, tiled=True
    ).astype(unit_sums.dtype)
    grad_tokens = jnp.dot(
        token_map.T,
        returned.reshape(slot_count, d_block),
        precision=lax.Precision.HIGHEST,
        preferred_element_type=jnp.float32,
    )
    return (grad_tokens.astype(jnp.bfloat16), grad_a, grad_b)


def solution(mesh):
    placed = (
        P("expert", "dp"),
        P("expert", "dp"),
        P("expert", None),
        P("expert", None),
        P("expert", "dp", None),
        P("expert", "dp", None),
        P("expert", "dp", None),
        P("expert", None, "dp"),
        P("expert", None, "dp"),
    )
    return jax.shard_map(
        per_device,
        mesh=mesh,
        in_specs=placed,
        out_specs=(P("expert", "dp"), P("expert", None, "dp"), P("expert", None, "dp")),
        check_vma=False,
    )
```

profile of v0, /device:TPU:7, one launch (start us, length us, event | category | flops | bytes accessed | tf_op | source)
XLA Modules:
  0.0 545.3 jit_solution(10109363348016319839)
XLA Ops:
  7.2 0.0 copy-start
  7.2 0.9 copy.18
  8.1 0.1 eq.46
  8.1 0.1 eq.50
  8.3 0.6 reduce-window.6
  8.9 0.2 slice_reduce_fusion
  9.1 0.1 fusion.24
  9.2 0.1 reduce_sum.21
  9.3 0.2 convert_reduce_fusion
  9.5 16.3 %all_gather.11 = bf16[32,4096]{1,0:T(8,128)(2,1)S(1)} all-gather(bf16[32,512]{1,0:T(8,128)(2,1)} %param.9), channel_id=1, replica_groups=mesh['dp'=8,'expert'=64] {'dp'}, dimensions={1}, use_global_device_ids=true | all-gather | bytes 294912 | tf_op jit(solution)/shard_map/all_gather | solution.py:37
  25.8 2.4 convolution_convert_fusion
  28.1 4.7 reshape.70
  32.8 0.0 copy-start.7
  32.8 0.0 copy-start.8
  32.8 16.1 %all-to-all-start.1 = ((bf16[64,5,4096]{2,1,0:T(8,128)(2,1)}), bf16[64,5,4096]{2,1,0:T(8,128)(2,1)}, u32[]{:S(2)}, u32[]{:S(2)}) async-start(bf16[64,5,4096]{2,1,0:T(8,128)(2,1)} %reshape.70), calls=%async_computation.1 | async-start | bytes 8388608 | tf_op jit(solution)/shard_map/all_to_all | solution.py:42
  49.0 0.0 copy-done.7
  49.0 13.1 %all_gather.9 = bf16[32,4096]{1,0:T(8,128)(2,1)S(1)} all-gather(bf16[32,512]{1,0:T(8,128)(2,1)S(1)} %copy-done.7), channel_id=1, replica_groups=mesh['dp'=8,'expert'=64] {'dp'}, dimensions={1}, use_global_device_ids=true | all-gather | bytes 294912 | tf_op jit(solution)/shard_map/all_gather | solution.py:38
  62.2 0.0 copy-done.8
  62.2 0.1 copy.22
  62.2 0.1 mul.65
  62.4 2.4 convolution_convert_fusion.1
  64.8 4.8 reshape.68
  69.6 0.0 copy-start.6
  69.6 162.9 %all-to-all-done.1 = bf16[64,5,4096]{2,1,0:T(8,128)(2,1)} async-done(((bf16[64,5,4096]{2,1,0:T(8,128)(2,1)}), bf16[64,5,4096]{2,1,0:T(8,128)(2,1)}, u32[]{:S(2)}, u32[]{:S(2)}) %all-to-all-start.1) | async-done | bytes 2621472 | tf_op jit(solution)/shard_map/all_to_all | solution.py:42
  232.5 12.1 %all-to-all-start = ((bf16[64,5,4096]{2,1,0:T(8,128)(2,1)}), bf16[64,5,4096]{2,1,0:T(8,128)(2,1)}, u32[]{:S(2)}, u32[]{:S(2)}) async-start(bf16[64,5,4096]{2,1,0:T(8,128)(2,1)} %reshape.68), calls=%async_computation | async-start | bytes 8388608 | tf_op jit(solution)/shard_map/all_to_all | solution.py:54
  244.6 0.0 reduce-scatter.2.cloned.1.call-start
  244.6 0.0 copy-done.6
  244.6 14.6 %all_gather.10 = bf16[1,64,4096]{2,1,0:T(8,128)(2,1)S(1)} all-gather(bf16[1,64,512]{2,1,0:T(8,128)(2,1)S(1)} %copy-done.6), channel_id=1, replica_groups=mesh['dp'=8,'expert'=64] {'dp'}, dimensions={2}, use_global_device_ids=true | all-gather | bytes 589824 | tf_op jit(solution)/shard_map/all_gather | solution.py:39
  259.2 4.8 reshape.71
  264.0 3.4 fusion.7
  267.4 160.9 %all-to-all-done = bf16[64,5,4096]{2,1,0:T(8,128)(2,1)} async-done(((bf16[64,5,4096]{2,1,0:T(8,128)(2,1)}), bf16[64,5,4096]{2,1,0:T(8,128)(2,1)}, u32[]{:S(2)}, u32[]{:S(2)}) %all-to-all-start) | async-done | bytes 2621472 | tf_op jit(solution)/shard_map/all_to_all | solution.py:54
  428.3 4.9 reshape.69
  433.1 0.0 copy-start.5
  433.1 0.0 copy-start.1
  433.1 0.0 copy-start.3
  433.1 2.8 convolution_convert_fusion.3
  435.9 0.0 copy-done.5
  435.9 0.2 fusion.28
  436.2 0.0 copy-done.1
  436.2 0.0 copy-done.3
  436.2 0.0 copy-start.2
  436.2 1.2 fusion.14
  437.4 0.0 copy-done
  437.4 0.5 copy-done.2
  437.9 0.0 copy-start.4
  437.9 1.2 multiply_convert_fusion
  439.1 0.2 copy-done.4
  439.3 0.9 fusion.5
  440.3 2.5 fusion
  442.8 4.7 convert_element_type.75
  447.5 0.0 reduce-scatter.2.cloned.1.call-update
  447.5 42.7 %reduce-scatter.2.cloned.1.call-done = bf16[64,5,512]{2,1,0:T(8,128)(2,1)} async-done(((bf16[64,5,4096]{2,1,0:T(8,128)(2,1)}), bf16[64,5,512]{2,1,0:T(8,128)(2,1)}) %reduce-scatter.2.cloned.1.call-update) | async-done | bytes 327696 | tf_op jit(solution)/shard_map/reduce_scatter | solution.py:90
  490.2 14.7 %all-to-all-start.2 = ((bf16[64,5,512]{2,1,0:T(8,128)(2,1)}), bf16[64,5,512]{2,1,0:T(8,128)(2,1)S(1)}, u32[]{:S(2)}, u32[]{:S(2)}) async-start(bf16[64,5,512]{2,1,0:T(8,128)(2,1)} %reduce-scatter.2.cloned.1.call-done), calls=%async_computation.3 | async-start | bytes 1048576 | tf_op jit(solution)/shard_map/all_to_all | solution.py:96
  504.9 0.2 convolution_convert_fusion.2
  505.1 25.1 %psum.7 = bf16[320,64]{0,1:T(8,128)(2,1)S(1)} all-reduce(bf16[320,64]{0,1:T(8,128)(2,1)S(1)} %convolution_convert_fusion.2), channel_id=1, replica_groups=mesh['dp'=8,'expert'=64] {'dp'}, use_global_device_ids=true, to_apply=%region_5.6 | all-reduce | flops 20480 | bytes 81920 | tf_op jit(solution)/shard_map/psum | solution.py:78
  530.1 1.8 convolution_bitcast_fusion
  532.0 0.8 convolution_bitcast_fusion.1
  532.8 4.6 all-to-all-done.2
  537.4 0.1 reshape.72
  537.5 0.9 convolution_convert_fusion.4
  (6 shorter events, 0.1 us)
Async XLA Ops:
  7.2 430.2 %copy-start = (bf16[1,192,4096]{2,1,0:T(8,128)(2,1)S(1)}, bf16[1,192,4096]{2,1,0:T(8,128)(2,1)}, u32[]{:S(2)}) copy-start(bf16[1,192,4096]{2,1,0:T(8,128)(2,1)} %param.14) | copy-start | bytes 4718596
  32.8 16.2 %copy-start.7 = (bf16[32,512]{1,0:T(8,128)(2,1)S(1)}, bf16[32,512]{1,0:T(8,128)(2,1)}, u32[]{:S(2)}) copy-start(bf16[32,512]{1,0:T(8,128)(2,1)} %param.10) | copy-start | bytes 98308
  32.8 29.3 %copy-start.8 = (f32[32,8]{0,1:T(8,128)S(1)}, f32[32,8]{0,1:T(8,128)}, u32[]{:S(2)}) copy-start(f32[32,8]{0,1:T(8,128)} %param.11) | copy-start | bytes 3076
  32.8 199.6 %all-to-all-start.1 = ((bf16[64,5,4096]{2,1,0:T(8,128)(2,1)}), bf16[64,5,4096]{2,1,0:T(8,128)(2,1)}, u32[]{:S(2)}, u32[]{:S(2)}) async-start(bf16[64,5,4096]{2,1,0:T(8,128)(2,1)} %reshape.70), calls=%async_computation.1 | async-start | bytes 8388608 | tf_op jit(solution)/shard_map/all_to_all | solution.py:42
  69.6 175.1 %copy-start.6 = (bf16[1,64,512]{2,1,0:T(8,128)(2,1)S(1)}, bf16[1,64,512]{2,1,0:T(8,128)(2,1)}, u32[]{:S(2)}) copy-start(bf16[1,64,512]{2,1,0:T(8,128)(2,1)} %param.17) | copy-start | bytes 196612
  232.5 195.8 %all-to-all-start = ((bf16[64,5,4096]{2,1,0:T(8,128)(2,1)}), bf16[64,5,4096]{2,1,0:T(8,128)(2,1)}, u32[]{:S(2)}, u32[]{:S(2)}) async-start(bf16[64,5,4096]{2,1,0:T(8,128)(2,1)} %reshape.68), calls=%async_computation | async-start | bytes 8388608 | tf_op jit(solution)/shard_map/all_to_all | solution.py:54
  244.6 245.6 %reduce-scatter.2.cloned.1.call-start = ((), (), s32[]{:S(2)}) async-start(), calls=%async_computation.4 | async-start | bytes 4718592 | tf_op jit(solution)/shard_map/reduce_scatter | solution.py:90
  433.1 2.8 copy-start.5
  433.1 3.0 copy-start.1
  433.1 3.0 copy-start.3
  436.2 1.7 copy-start.2
  437.9 1.4 copy-start.4
  490.2 47.2 %all-to-all-start.2 = ((bf16[64,5,512]{2,1,0:T(8,128)(2,1)}), bf16[64,5,512]{2,1,0:T(8,128)(2,1)S(1)}, u32[]{:S(2)}, u32[]{:S(2)}) async-start(bf16[64,5,512]{2,1,0:T(8,128)(2,1)} %reduce-scatter.2.cloned.1.call-done), calls=%async_computation.3 | async-start | bytes 1048576 | tf_op jit(solution)/shard_map/all_to_all | solution.py:96
Sparse Core Ops, SparseCore 0:
  447.6 42.4 reduce-scatter.1
where the time goes:
time: 546 us; the launch traced here: 545 us
  waiting for transfers between devices  371 us (68%)
  blocking collectives  69 us (13%)
  starting transfers between devices  43 us (8%)
  local copies, waits for them, and re-layouts  26.3 us (5%)
  matrix products  20.7 us (4%)
  between operations  14.2 us (3%)
    all_to_all x1, waiting for transfers between devices, per_device(): lax.all_to_all(packed.reshape(expert_count, capacity, x_whole.shape[1]),...  163 us
    all_to_all x1, waiting for transfers between devices, per_device(): lax.all_to_all(packed.reshape(expert_count, capacity, dy_whole.shape[1]),...  161 us
    reduce_scatter x1, waiting for transfers between devices, per_device(): lax.psum_scatter(unit_term.reshape(expert_count, capacity, full_width).as...  42.7 us
    psum x1, blocking collectives, per_device(): low_v = lax.psum(partial_v.astype(jnp.bfloat16), 'dp')  25.1 us
    all_gather x1, blocking collectives, per_device(): lax.all_gather(tokens, 'dp', axis=1, tiled=True)  16.3 us
    all_to_all x1, starting transfers between devices, per_device(): lax.all_to_all(packed.reshape(expert_count, capacity, x_whole.shape[1]),...  16.1 us
    all_to_all x1, starting transfers between devices, per_device(): lax.all_to_all(unit_sums.astype(jnp.bfloat16), 'expert', split_axis=0, co...  14.7 us
    all_gather x1, blocking collectives, per_device(): lax.all_gather(adapter_b, 'dp', axis=2, tiled=True)  14.6 us
  transfers between devices with their start and end apart: 4, of which 4 were waited for; matrix products, arithmetic and copies ran while one was open for 3% of the time, Pallas kernels for 0%

commit v1 on v0

v1 whole, which is shorter than its diff:
```python
import functools

import jax
import jax.numpy as jnp
from jax import lax
from jax.experimental import pallas as pl
from jax.experimental.pallas import tpu as pltpu
from jax.sharding import Mesh, PartitionSpec as P

CAP = 5
BF = jnp.bfloat16
F32 = jnp.float32
PARAMS = pltpu.CompilerParams(vmem_limit_bytes=48 * 1024 * 1024)


def nt(left, right):
    return lax.dot_general(left, right, (((1,), (1,)), ((), ())), preferred_element_type=F32)


def tn(left, right):
    return lax.dot_general(left, right, (((0,), (0,)), ((), ())), preferred_element_type=F32)


def nn(left, right):
    return jnp.dot(left, right, preferred_element_type=F32)


def pack_kernel(ids_ref, prob_ref, tok_ref, dy_ref, x_ref, s_ref, code_ref):
    experts, width = code_ref.shape[0], tok_ref.shape[1]
    count = ids_ref.shape[1]
    own = lax.broadcasted_iota(jnp.int32, (experts, count), 0)
    hit = jnp.zeros((experts, count), F32)
    weight = jnp.zeros((experts, count), F32)
    for k in range(ids_ref.shape[0]):
        same = ids_ref[k : k + 1, :] == own
        hit = jnp.where(same, 1.0, hit)
        weight = jnp.where(same, prob_ref[k : k + 1, :], weight)
    first = lax.broadcasted_iota(jnp.int32, (count, count), 0)
    second = lax.broadcasted_iota(jnp.int32, (count, count), 1)
    before = jnp.where(first < second, 1.0, 0.0).astype(BF)
    slot = nn(hit.astype(BF), before)
    code = jnp.where(hit > 0.5, slot, -1.0)
    code_ref[...] = code
    for s in range(CAP):
        mine = code == float(s)
        pick = jnp.where(mine, 1.0, 0.0).astype(BF)
        scale = jnp.sum(jnp.where(mine, weight, 0.0), axis=1, keepdims=True)
        cols = slice(s * width, (s + 1) * width)
        x_ref[:, cols] = nn(pick, tok_ref[...]).astype(BF)
        s_ref[:, cols] = (nn(pick, dy_ref[...]) * scale).astype(BF)


def rows_of(block, width):
    return jnp.concatenate([block[:, s * width : (s + 1) * width] for s in range(CAP)], axis=0)


def gate_kernel(core_ref, own_ref, other_ref, wg_ref, wu_ref, a_ref, gate_ref, up_ref, hid_ref, v_ref):
    chips, experts, wide = own_ref.shape
    width = wide // CAP
    core = core_ref[0]
    gate = jnp.zeros(gate_ref.shape, F32)
    up = jnp.zeros(up_ref.shape, F32)
    for ref, which in ((own_ref, core), (other_ref, 1 - core)):
        for x in range(chips):
            rows = rows_of(ref[x], width)
            cols = pl.ds(pl.multiple_of((2 * x + which) * width, width), width)
            gate += nt(rows, wg_ref[:, cols])
            up += nt(rows, wu_ref[:, cols])
    gate_ref[...] = gate
    up_ref[...] = up
    hidden = (gate * jax.nn.sigmoid(gate) * up).astype(BF)
    hid_ref[...] = hidden
    v_ref[...] = nt(hidden, a_ref[...]).astype(BF)


def grad_kernel(
    core_ref, own_ref, other_ref, gate_ref, up_ref, hid_ref, v_ref, wg_ref, wu_ref, wd_ref, a_ref,
    keep_ref, send_ref, ga_ref,
):
    chips, experts = own_ref.shape[:2]
    width = wd_ref.shape[1] // (2 * chips)
    rank = a_ref.shape[0]
    core = core_ref[0]
    grad = jnp.zeros(gate_ref.shape, F32)
    low = jnp.zeros((experts * CAP, rank), F32)
    for ref, which in ((own_ref, core), (other_ref, 1 - core)):
        for x in range(chips):
            block = ref[x]
            rows = rows_of(block, width)
            cols = pl.ds(pl.multiple_of((2 * x + which) * width, width), width)
            grad += nt(rows, wd_ref[:, cols])
            low += nt(rows, block[:, CAP * width :])
    low_u = low.astype(BF)
    grad += nn(low_u, a_ref[...])
    ga_ref[...] = tn(low_u, hid_ref[...])
    gate = gate_ref[...]
    sigma = jax.nn.sigmoid(gate)
    grad_gate = (grad * up_ref[...] * sigma * (1.0 + gate * (1.0 - sigma))).astype(BF)
    grad_up = (grad * (gate * sigma)).astype(BF)
    for ref, which in ((keep_ref, core), (send_ref, 1 - core)):
        for x in range(chips):
            cols = pl.ds(pl.multiple_of((2 * x + which) * width, width), width)
            term = (nn(grad_gate, wg_ref[:, cols]) + nn(grad_up, wu_ref[:, cols])).astype(BF)
            for s in range(CAP):
                ref[x, :, s * width : (s + 1) * width] = term[s * experts : (s + 1) * experts]
            for s in range(CAP):
                ref[x, :, CAP * width + s * rank : CAP * width + (s + 1) * rank] = v_ref[
                    s * experts : (s + 1) * experts
                ]


def pair_kernel(a_ref, b_ref, o_ref):
    o_ref[...] = (a_ref[...].astype(F32) + b_ref[...].astype(F32)).astype(BF)


def total_kernel(in_ref, out_ref, v_ref):
    total = in_ref[0].astype(F32)
    for x in range(1, in_ref.shape[0]):
        total += in_ref[x].astype(F32)
    low = total.astype(BF)
    wide = out_ref.shape[1]
    experts, rank = out_ref.shape[0], v_ref.shape[1]
    out_ref[...] = low[:, :wide]
    for s in range(CAP):
        v_ref[s * experts : (s + 1) * experts] = low[:, wide + s * rank : wide + (s + 1) * rank]


def adapter_kernel(v_ref, s_ref, o_ref):
    o_ref[...] = tn(v_ref[...], rows_of(s_ref[...], o_ref.shape[1]))


def combine_kernel(code_ref, r_ref, o_ref):
    width = o_ref.shape[1]
    total = jnp.zeros(o_ref.shape, F32)
    for s in range(CAP):
        pick = jnp.where(code_ref[...] == float(s), 1.0, 0.0).astype(BF)
        total += tn(pick, r_ref[:, s * width : (s + 1) * width])
    o_ref[...] = total.astype(BF)


def call(body, outs, *args, scalars=0):
    vmem = pl.BlockSpec(memory_space=pltpu.VMEM)
    smem = pl.BlockSpec(memory_space=pltpu.SMEM)
    return pl.pallas_call(
        body,
        out_shape=outs,
        in_specs=[smem] * scalars + [vmem] * (len(args) - scalars),
        out_specs=jax.tree.map(lambda _: vmem, outs),
        compiler_params=PARAMS,
    )(*args)


def per_device(tokens, grad_out, prob, ids, w_gate, w_up, w_down, adapter_a, adapter_b):
    experts = lax.axis_size(("z", "y"))
    chips = lax.axis_size("x")
    width = tokens.shape[1]
    wide = CAP * width
    rank = adapter_b.shape[1]
    sds = jax.ShapeDtypeStruct
    core = lax.axis_index("c").reshape(1).astype(jnp.int32)
    swap = [(0, 1), (1, 0)]

    def route(block):
        return lax.all_to_all(block, ("z", "y"), 0, 0, tiled=True)

    def spread(block):
        own = lax.all_to_all(jnp.broadcast_to(block[None], (chips,) + block.shape), "x", 0, 0, tiled=True)
        return own, lax.ppermute(own, "c", swap)

    x_pack, s_pack, code = call(
        pack_kernel,
        (sds((experts, wide), BF), sds((experts, wide), BF), sds((experts, tokens.shape[0]), F32)),
        ids.T, prob.T, tokens, grad_out,
    )
    x_in = route(x_pack)
    s_in = route(s_pack)
    x_own, x_other = spread(x_in)
    s_own, s_other = spread(jnp.concatenate([s_in, adapter_b[0]], axis=1))
    hidden_units = w_gate.shape[1]
    routes = experts * CAP
    gate, up, hidden, part_v = call(
        gate_kernel,
        (
            sds((routes, hidden_units), F32), sds((routes, hidden_units), F32),
            sds((routes, hidden_units), BF), sds((routes, rank), BF),
        ),
        core, x_own, x_other, w_gate[0], w_up[0], adapter_a[0], scalars=1,
    )
    full = wide + CAP * rank
    keep, send, grad_a = call(
        grad_kernel,
        (sds((chips, experts, full), BF), sds((chips, experts, full), BF), sds((rank, hidden_units), F32)),
        core, s_own, s_other, gate, up, hidden, part_v, w_gate[0], w_up[0], w_down[0], adapter_a[0],
        scalars=1,
    )
    got = lax.ppermute(send, "c", swap)
    pair = call(pair_kernel, sds((chips, experts, full), BF), keep, got)
    quad = lax.all_to_all(pair, "x", 0, 0, tiled=True)
    total, low_v = call(total_kernel, (sds((experts, wide), BF), sds((routes, rank), BF)), quad)
    back = route(total)
    grad_b = call(adapter_kernel, sds((rank, width), F32), low_v, s_in)
    out = call(combine_kernel, sds(tokens.shape, BF), code, back)
    return out, grad_a[None], grad_b[None]


def solution(mesh):
    fine = Mesh(mesh.devices.reshape(4, 2, 16, 4), ("x", "c", "z", "y"))
    dp, ex = ("x", "c"), ("z", "y")
    specs = (
        P(ex, dp), P(ex, dp), P(ex, None), P(ex, None),
        P(ex, dp, None), P(ex, dp, None), P(ex, dp, None), P(ex, None, dp), P(ex, None, dp),
    )
    return jax.shard_map(
        per_device,
        mesh=fine,
        in_specs=specs,
        out_specs=(P(ex, dp), P(ex, None, dp), P(ex, None, dp)),
        check_vma=False,
    )
```

time: 546 us -> 203 us (0.37)
  the two profiles are of different devices: /device:TPU:7 before, /device:TPU:32 now
where the time goes in v1:
time: 203 us; the launch traced here: 202 us
  waiting for transfers between devices  102 us (50%)
  starting transfers between devices  51.8 us (26%)
  blocking collectives  23 us (11%)
  Pallas kernels  12.7 us (6%)
  local copies, waits for them, and re-layouts  9.27 us (5%)
  other arithmetic  2.54 us (1%)
    all_to_all x3, waiting for transfers between devices, route(): return lax.all_to_all(block, ('z', 'y'), 0, 0, tiled=True)  69.2 us
    all_to_all x3, starting transfers between devices, route(): return lax.all_to_all(block, ('z', 'y'), 0, 0, tiled=True)  37.2 us
    all_to_all x2, waiting for transfers between devices, spread(): lax.all_to_all(jnp.broadcast_to(block[None], (chips,) + block.shape), 'x'...  26.3 us
    all_to_all x1, blocking collectives, per_device(): quad = lax.all_to_all(pair, 'x', 0, 0, tiled=True)  23 us
    pallas_call x7, Pallas kernels, call(): pl.pallas_call(body, out_shape=outs, in_specs=[smem] * scalars + [vmem] *...  12.7 us
    all_to_all x2, starting transfers between devices, spread(): lax.all_to_all(jnp.broadcast_to(block[None], (chips,) + block.shape), 'x'...  8.72 us
    unnamed x23, local copies, waits for them, and re-layouts  6.24 us
  transfers between devices with their start and end apart: 8, of which 7 were waited for; matrix products, arithmetic and copies ran while one was open for 1% of the time, Pallas kernels for 2%

profile of v1, /device:TPU:32, one launch (start us, length us, event | category | flops | bytes accessed | tf_op | source)
XLA Modules:
  0.0 202.3 jit_solution(16308882434143410467)
XLA Ops:
  0.6 0.0 copy-start.2
  0.6 0.7 copy-done.2
  1.4 0.0 copy-start.3
  1.4 0.8 copy-done.3
  2.1 0.0 copy-start.4
  2.2 0.7 copy-done.4
  2.8 0.0 copy-start.5
  2.8 0.7 copy-done.5
  3.5 0.4 shard_map.112
  4.0 0.5 broadcast.1
  4.5 0.8 reduce
  5.3 0.8 reshape.19
  6.1 18.4 %all-to-all-start = ((bf16[64,2,1280]{2,1,0:T(2,128)(2,1)}), bf16[64,2,1280]{2,1,0:T(2,128)(2,1)S(1)}, u32[]{:S(2)}, u32[]{:S(2)}) async-start(bf16[64,2,1280]{2,1,0:T(2,128)(2,1)} %reshape.19), calls=%async_computation | async-start | bytes 655360 | tf_op jit(solution)/shard_map/all_to_all | solution.py:164
  24.5 0.8 reduce.1
  25.4 0.0 copy-start.6
  25.4 0.8 reshape.21
  26.2 22.7 %all-to-all-done = bf16[64,2,1280]{2,1,0:T(2,128)(2,1)S(1)} async-done(((bf16[64,2,1280]{2,1,0:T(2,128)(2,1)}), bf16[64,2,1280]{2,1,0:T(2,128)(2,1)S(1)}, u32[]{:S(2)}, u32[]{:S(2)}) %all-to-all-start) | async-done | bytes 327712 | tf_op jit(solution)/shard_map/all_to_all | solution.py:164
  48.9 5.9 %all-to-all-start.2 = ((bf16[64,2,1280]{2,1,0:T(2,128)(2,1)}), bf16[64,2,1280]{2,1,0:T(2,128)(2,1)S(1)}, u32[]{:S(2)}, u32[]{:S(2)}) async-start(bf16[64,2,1280]{2,1,0:T(2,128)(2,1)} %reshape.21), calls=%async_computation.2 | async-start | bytes 655360 | tf_op jit(solution)/shard_map/all_to_all | solution.py:164
  54.8 0.3 reshape.20
  55.1 0.0 copy-done.6
  55.1 23.5 %all-to-all-done.2 = bf16[64,2,1280]{2,1,0:T(2,128)(2,1)S(1)} async-done(((bf16[64,2,1280]{2,1,0:T(2,128)(2,1)}), bf16[64,2,1280]{2,1,0:T(2,128)(2,1)S(1)}, u32[]{:S(2)}, u32[]{:S(2)}) %all-to-all-start.2) | async-done | bytes 327712 | tf_op jit(solution)/shard_map/all_to_all | solution.py:164
  78.6 1.3 broadcast_in_dim.20
  80.0 4.3 %all-to-all-start.1 = ((bf16[4,64,3072]{2,1,0:T(8,128)(2,1)}), bf16[4,64,3072]{2,1,0:T(8,128)(2,1)S(1)}, u32[]{:S(2)}, u32[]{:S(2)}) async-start(bf16[4,64,3072]{2,1,0:T(8,128)(2,1)} %broadcast_in_dim.20), calls=%async_computation.1 | async-start | bytes 3145728 | tf_op jit(solution)/shard_map/all_to_all | solution.py:167
  84.3 0.3 reshape.22
  84.6 15.9 %all-to-all-done.1.own_ref = bf16[4,64,3072]{2,1,0:T(8,128)(2,1)S(1)} async-done(((bf16[4,64,3072]{2,1,0:T(8,128)(2,1)}), bf16[4,64,3072]{2,1,0:T(8,128)(2,1)S(1)}, u32[]{:S(2)}, u32[]{:S(2)}) %all-to-all-start.1) | async-done | bytes 1572896 | tf_op jit(solution)/shard_map/all_to_all | solution.py:167
  100.5 1.2 broadcast_in_dim.22
  101.7 0.0 copy-start
  101.7 0.0 copy-start.1
  101.7 4.4 %all-to-all-start.3 = ((bf16[4,64,2560]{2,1,0:T(8,128)(2,1)}), bf16[4,64,2560]{2,1,0:T(8,128)(2,1)}, u32[]{:S(2)}, u32[]{:S(2)}) async-start(bf16[4,64,2560]{2,1,0:T(8,128)(2,1)} %broadcast_in_dim.22), calls=%async_computation.3 | async-start | bytes 2621440 | tf_op jit(solution)/shard_map/all_to_all | solution.py:167
  106.1 1.9 collective-permute-start
  108.0 10.4 %all-to-all-done.3.own_ref = bf16[4,64,2560]{2,1,0:T(8,128)(2,1)} async-done(((bf16[4,64,2560]{2,1,0:T(8,128)(2,1)}), bf16[4,64,2560]{2,1,0:T(8,128)(2,1)}, u32[]{:S(2)}, u32[]{:S(2)}) %all-to-all-start.3) | async-done | bytes 1310752 | tf_op jit(solution)/shard_map/all_to_all | solution.py:167
  118.5 1.9 collective-permute-start.1
  120.4 3.3 %collective-permute-done.1.other_ref = bf16[4,64,2560]{2,1,0:T(8,128)(2,1)} collective-permute-done((bf16[4,64,2560]{2,1,0:T(8,128)(2,1)}, bf16[4,64,2560]{2,1,0:T(8,128)(2,1)}, u32[]{:S(2)}, u32[]{:S(2)}) %collective-permute-start.1) | collective-permute-done | bytes 1310752 | tf_op jit(solution)/shard_map/ppermute | solution.py:168
  123.7 0.0 copy-done
  123.7 0.0 copy-done.1
  123.7 3.9 %shard_map.113 = (f32[320,192]{1,0:T(8,128)S(1)}, f32[320,192]{1,0:T(8,128)S(1)}, bf16[320,192]{1,0:T(8,128)(2,1)S(1)}, bf16[320,64]{1,0:T(8,128)(2,1)S(1)}) custom-call(s32[1]{0:T(128)} %bitcast.2.core_ref, bf16[4,64,2560]{2,1,0:T(8,128)(2,1)} %all-to-all-done.3.own_ref, bf16[4,64,2560]{2,1,0:T(8,128)(2,1)} %collective-permute-done.1.other_ref, ...), custom_call_target="tpu_custom_call" | custom-call | tf_op jit(solution)/shard_map/pallas_call | solution.py:144
  127.6 0.0 collective-permute-done.other_ref
  127.6 6.1 %shard_map.114 = (bf16[4,64,2880]{2,1,0:T(8,128)(2,1)S(1)}, bf16[4,64,2880]{2,1,0:T(8,128)(2,1)S(1)}, f32[64,192]{1,0:T(8,128)}) custom-call(s32[1]{0:T(128)} %bitcast.2.core_ref, bf16[4,64,3072]{2,1,0:T(8,128)(2,1)S(1)} %all-to-all-done.1.own_ref, bf16[4,64,3072]{2,1,0:T(8,128)(2,1)} %collective-permute-done.other_ref, ...), custom_call_target="tpu_custom_call" | custom-call | tf_op jit(solution)/shard_map/pallas_call | solution.py:144
  133.7 2.1 %collective-permute-start.2 = (bf16[4,64,2880]{2,1,0:T(8,128)(2,1)S(1)}, bf16[4,64,2880]{2,1,0:T(8,128)(2,1)S(1)}, u32[]{:S(2)}, u32[]{:S(2)}) collective-permute-start(bf16[4,64,2880]{2,1,0:T(8,128)(2,1)S(1)} %get-tuple-element.23), channel_id=1, source_target_pairs={{0,64},{64,0},{1,65},{65,1},{2,66},{66,2},{3,67},{67,3},{4,68},{68... | collective-permute-start | bytes 4423688 | tf_op jit(solution)/shard_map/ppermute | solution.py:196
  135.7 3.1 %collective-permute-done.2.b_ref = bf16[4,64,2880]{2,1,0:T(8,128)(2,1)S(1)} collective-permute-done((bf16[4,64,2880]{2,1,0:T(8,128)(2,1)S(1)}, bf16[4,64,2880]{2,1,0:T(8,128)(2,1)S(1)}, u32[]{:S(2)}, u32[]{:S(2)}) %collective-permute-start.2) | collective-permute-done | bytes 1474592 | tf_op jit(solution)/shard_map/ppermute | solution.py:196
  138.9 0.3 shard_map.115
  139.2 23.0 %all_to_all.46.in_ref = bf16[4,64,2880]{2,1,0:T(8,128)(2,1)S(1)} all-to-all(bf16[4,64,2880]{2,1,0:T(8,128)(2,1)S(1)} %shard_map.115), channel_id=1, replica_groups=mesh['x'=4,'c'=2,'z'=16,'y'=4] {'x'}, dimensions={0} | all-to-all | bytes 2949120 | tf_op jit(solution)/shard_map/all_to_all | solution.py:198
  162.3 0.3 shard_map.116
  162.6 0.8 reduce.2
  163.4 0.8 reshape.23
  164.2 13.0 %all-to-all-start.5 = ((bf16[64,2,1280]{2,1,0:T(2,128)(2,1)}), bf16[64,2,1280]{2,1,0:T(2,128)(2,1)S(1)}, u32[]{:S(2)}, u32[]{:S(2)}) async-start(bf16[64,2,1280]{2,1,0:T(2,128)(2,1)} %reshape.23), calls=%async_computation.5 | async-start | bytes 655360 | tf_op jit(solution)/shard_map/all_to_all | solution.py:164
  177.2 0.9 shard_map.118
  178.0 23.1 %all-to-all-done.5 = bf16[64,2,1280]{2,1,0:T(2,128)(2,1)S(1)} async-done(((bf16[64,2,1280]{2,1,0:T(2,128)(2,1)}), bf16[64,2,1280]{2,1,0:T(2,128)(2,1)S(1)}, u32[]{:S(2)}, u32[]{:S(2)}) %all-to-all-start.5) | async-done | bytes 327712 | tf_op jit(solution)/shard_map/all_to_all | solution.py:164
  201.1 0.3 reshape.24
  201.4 0.8 shard_map.117
  (4 shorter events, 0.1 us)
Async XLA Ops:
  0.6 0.8 copy-start.2
  1.4 0.8 copy-start.3
  2.1 0.7 copy-start.4
  2.8 0.7 copy-start.5
  6.1 42.7 %all-to-all-start = ((bf16[64,2,1280]{2,1,0:T(2,128)(2,1)}), bf16[64,2,1280]{2,1,0:T(2,128)(2,1)S(1)}, u32[]{:S(2)}, u32[]{:S(2)}) async-start(bf16[64,2,1280]{2,1,0:T(2,128)(2,1)} %reshape.19), calls=%async_computation | async-start | bytes 655360 | tf_op jit(solution)/shard_map/all_to_all | solution.py:164
  25.4 29.7 %copy-start.6 = (bf16[1,64,512]{2,1,0:T(8,128)(2,1)S(1)}, bf16[1,64,512]{2,1,0:T(8,128)(2,1)}, u32[]{:S(2)}) copy-start(bf16[1,64,512]{2,1,0:T(8,128)(2,1)} %param.17) | copy-start | bytes 196612
  48.9 29.8 %all-to-all-start.2 = ((bf16[64,2,1280]{2,1,0:T(2,128)(2,1)}), bf16[64,2,1280]{2,1,0:T(2,128)(2,1)S(1)}, u32[]{:S(2)}, u32[]{:S(2)}) async-start(bf16[64,2,1280]{2,1,0:T(2,128)(2,1)} %reshape.21), calls=%async_computation.2 | async-start | bytes 655360 | tf_op jit(solution)/shard_map/all_to_all | solution.py:164
  80.0 20.5 %all-to-all-start.1 = ((bf16[4,64,3072]{2,1,0:T(8,128)(2,1)}), bf16[4,64,3072]{2,1,0:T(8,128)(2,1)S(1)}, u32[]{:S(2)}, u32[]{:S(2)}) async-start(bf16[4,64,3072]{2,1,0:T(8,128)(2,1)} %broadcast_in_dim.20), calls=%async_computation.1 | async-start | bytes 3145728 | tf_op jit(solution)/shard_map/all_to_all | solution.py:167
  101.7 22.1 %copy-start = (bf16[1,192,4096]{2,1,0:T(8,128)(2,1)S(1)}, bf16[1,192,4096]{2,1,0:T(8,128)(2,1)}, u32[]{:S(2)}) copy-start(bf16[1,192,4096]{2,1,0:T(8,128)(2,1)} %param.13) | copy-start | bytes 4718596
  101.7 22.1 %copy-start.1 = (bf16[1,64,192]{2,1,0:T(8,128)(2,1)S(1)}, bf16[1,64,192]{2,1,0:T(8,128)(2,1)}, u32[]{:S(2)}) copy-start(bf16[1,64,192]{2,1,0:T(8,128)(2,1)} %param.16) | copy-start | bytes 73732
  101.7 16.8 %all-to-all-start.3 = ((bf16[4,64,2560]{2,1,0:T(8,128)(2,1)}), bf16[4,64,2560]{2,1,0:T(8,128)(2,1)}, u32[]{:S(2)}, u32[]{:S(2)}) async-start(bf16[4,64,2560]{2,1,0:T(8,128)(2,1)} %broadcast_in_dim.22), calls=%async_computation.3 | async-start | bytes 2621440 | tf_op jit(solution)/shard_map/all_to_all | solution.py:167
  106.1 21.5 %collective-permute-start = (bf16[4,64,3072]{2,1,0:T(8,128)(2,1)S(1)}, bf16[4,64,3072]{2,1,0:T(8,128)(2,1)}, u32[]{:S(2)}, u32[]{:S(2)}) collective-permute-start(bf16[4,64,3072]{2,1,0:T(8,128)(2,1)S(1)} %all-to-all-done.1.own_ref), channel_id=1, source_target_pairs={{0,64},{64,0},{1,65},{65,1},{2,66},{66,2},{3,67},{67,3},{4,68},{68... | collective-permute-start | bytes 4718600 | tf_op jit(solution)/shard_map/ppermute | solution.py:168
  118.5 5.3 %collective-permute-start.1 = (bf16[4,64,2560]{2,1,0:T(8,128)(2,1)}, bf16[4,64,2560]{2,1,0:T(8,128)(2,1)}, u32[]{:S(2)}, u32[]{:S(2)}) collective-permute-start(bf16[4,64,2560]{2,1,0:T(8,128)(2,1)} %all-to-all-done.3.own_ref), channel_id=1, source_target_pairs={{0,64},{64,0},{1,65},{65,1},{2,66},{66,2},{3,67},{67,3},{4,68},{68... | collective-permute-start | bytes 3932168 | tf_op jit(solution)/shard_map/ppermute | solution.py:168
  133.7 5.2 %collective-permute-start.2 = (bf16[4,64,2880]{2,1,0:T(8,128)(2,1)S(1)}, bf16[4,64,2880]{2,1,0:T(8,128)(2,1)S(1)}, u32[]{:S(2)}, u32[]{:S(2)}) collective-permute-start(bf16[4,64,2880]{2,1,0:T(8,128)(2,1)S(1)} %get-tuple-element.23), channel_id=1, source_target_pairs={{0,64},{64,0},{1,65},{65,1},{2,66},{66,2},{3,67},{67,3},{4,68},{68... | collective-permute-start | bytes 4423688 | tf_op jit(solution)/shard_map/ppermute | solution.py:196
  164.2 36.9 %all-to-all-start.5 = ((bf16[64,2,1280]{2,1,0:T(2,128)(2,1)}), bf16[64,2,1280]{2,1,0:T(2,128)(2,1)S(1)}, u32[]{:S(2)}, u32[]{:S(2)}) async-start(bf16[64,2,1280]{2,1,0:T(2,128)(2,1)} %reshape.23), calls=%async_computation.5 | async-start | bytes 655360 | tf_op jit(solution)/shard_map/all_to_all | solution.py:164

commit v2 on v1

v2 whole, which is shorter than its diff:
```python
import jax
import jax.numpy as jnp
from jax import lax
from jax.experimental import pallas as pl
from jax.experimental.pallas import tpu as pltpu
from jax.sharding import Mesh, PartitionSpec as P

CAP = 5
BF = jnp.bfloat16
F32 = jnp.float32
PARAMS = pltpu.CompilerParams(vmem_limit_bytes=16 * 1024 * 1024)


def nt(left, right):
    return lax.dot_general(left, right, (((1,), (1,)), ((), ())), preferred_element_type=F32)


def tn(left, right):
    return lax.dot_general(left, right, (((0,), (0,)), ((), ())), preferred_element_type=F32)


def nn(left, right):
    return jnp.dot(left, right, preferred_element_type=F32)


def lanes(index, width):
    return pl.ds(pl.multiple_of(index * width, width), width)


def pack_kernel(ids_ref, prob_ref, tok_ref, dy_ref, out_ref, code_ref):
    experts, width = code_ref.shape[0], tok_ref.shape[1]
    count = ids_ref.shape[1]
    own = lax.broadcasted_iota(jnp.int32, (experts, count), 0)
    hit = jnp.zeros((experts, count), F32)
    weight = jnp.zeros((experts, count), F32)
    for k in range(ids_ref.shape[0]):
        same = ids_ref[k : k + 1, :] == own
        hit = jnp.where(same, 1.0, hit)
        weight = jnp.where(same, prob_ref[k : k + 1, :], weight)
    first = lax.broadcasted_iota(jnp.int32, (count, count), 0)
    second = lax.broadcasted_iota(jnp.int32, (count, count), 1)
    before = jnp.where(first < second, 1.0, 0.0).astype(BF)
    slot = nn(hit.astype(BF), before)
    code = jnp.where(hit > 0.5, slot, -1.0)
    code_ref[...] = code
    for s in range(CAP):
        mine = code == float(s)
        pick = jnp.where(mine, 1.0, 0.0).astype(BF)
        scale = jnp.sum(jnp.where(mine, weight, 0.0), axis=1, keepdims=True)
        base = 2 * s * width
        out_ref[:, base : base + width] = nn(pick, tok_ref[...]).astype(BF)
        out_ref[:, base + width : base + 2 * width] = (nn(pick, dy_ref[...]) * scale).astype(BF)


def split_kernel(in_ref, x_ref, s_ref):
    experts = in_ref.shape[0]
    width = s_ref.shape[1]
    for s in range(CAP):
        rows = slice(s * experts, (s + 1) * experts)
        base = 2 * s * width
        block = in_ref[:, base : base + width]
        for x in range(x_ref.shape[0]):
            x_ref[x, rows] = block
        s_ref[rows] = in_ref[:, base + width : base + 2 * width]


def prep_kernel(me_ref, wg_ref, wu_ref, wd_ref, swap_ref, d1_ref, d2_ref, d3_ref):
    chip, core = me_ref[0], me_ref[1]
    chips, units, width = swap_ref.shape[1:]
    for x in range(chips):
        cols = lanes(2 * x + 1 - core, width)
        swap_ref[0, x] = wg_ref[:, cols]
        swap_ref[1, x] = wu_ref[:, cols]
    for d, ref in ((1, d1_ref), (2, d2_ref), (3, d3_ref)):
        ref[...] = wd_ref[:, lanes(lax.rem(chip + d, chips), 2 * width)]


def part_kernel(me_ref, s_ref, t_ref, wd_ref, d1_ref, d2_ref, d3_ref, b_ref, o_ref, out_ref):
    chip, core = me_ref[0], me_ref[1]
    chips = out_ref.shape[0]
    units = wd_ref.shape[0]
    width = s_ref.shape[1]
    mine, other = s_ref[...], t_ref[...]
    low = (nt(mine, b_ref[...]) + nt(other, o_ref[...])).astype(BF)
    for d, ref in ((0, None), (1, d1_ref), (2, d2_ref), (3, d3_ref)):
        if ref is None:
            w_mine = wd_ref[:, lanes(2 * chip + core, width)]
            w_other = wd_ref[:, lanes(2 * chip + 1 - core, width)]
        else:
            w_mine = ref[:, lanes(core, width)]
            w_other = ref[:, lanes(1 - core, width)]
        to = lax.rem(chip + chips - d, chips)
        out_ref[to, :, :units] = (nt(mine, w_mine) + nt(other, w_other)).astype(BF)
        out_ref[to, :, units:] = low


def gate_kernel(me_ref, x_ref, wg_ref, wu_ref, swap_ref, keep_ref, send_ref):
    core = me_ref[1]
    chips, routes, width = x_ref.shape
    units = wg_ref.shape[0]
    keep = [jnp.zeros((routes, units), F32)] * 2
    send = [jnp.zeros((routes, units), F32)] * 2
    for x in range(chips):
        rows = x_ref[x]
        cols = lanes(2 * x + core, width)
        for i, ref in enumerate((wg_ref, wu_ref)):
            keep[i] = keep[i] + nt(rows, ref[:, cols])
            send[i] = send[i] + nt(rows, swap_ref[i, x])
    for i in range(2):
        keep_ref[i] = keep[i]
        send_ref[i] = send[i].astype(BF)


def act_kernel(keep_ref, got_ref, a_ref, gate_ref, up_ref, hid_ref, v_ref):
    gate = keep_ref[0] + got_ref[0].astype(F32)
    up = keep_ref[1] + got_ref[1].astype(F32)
    gate_ref[...] = gate
    up_ref[...] = up
    hidden = (gate * jax.nn.sigmoid(gate) * up).astype(BF)
    hid_ref[...] = hidden
    v_ref[...] = nt(hidden, a_ref[...]).astype(BF)


def grad_kernel(in_ref, gate_ref, up_ref, hid_ref, a_ref, out_ref, ga_ref):
    units = gate_ref.shape[1]
    total = in_ref[0].astype(F32)
    for x in range(1, in_ref.shape[0]):
        total += in_ref[x].astype(F32)
    low_u = total[:, units:].astype(BF)
    grad = total[:, :units] + nn(low_u, a_ref[...])
    ga_ref[...] = tn(low_u, hid_ref[...])
    gate = gate_ref[...]
    sigma = jax.nn.sigmoid(gate)
    out_ref[0] = (grad * up_ref[...] * sigma * (1.0 + gate * (1.0 - sigma))).astype(BF)
    out_ref[1] = (grad * (gate * sigma)).astype(BF)


def back_kernel(me_ref, g_ref, h_ref, wg_ref, wu_ref, swap_ref, out_ref):
    core = me_ref[1]
    chips, _, width = out_ref.shape
    for x in range(chips):
        cols = lanes(2 * x + core, width)
        term = nn(g_ref[0], wg_ref[:, cols]) + nn(g_ref[1], wu_ref[:, cols])
        term += nn(h_ref[0], swap_ref[0, x]) + nn(h_ref[1], swap_ref[1, x])
        out_ref[x] = term.astype(BF)


def total_kernel(in_ref, out_ref):
    experts = out_ref.shape[0]
    width = in_ref.shape[2]
    for s in range(CAP):
        rows = slice(s * experts, (s + 1) * experts)
        total = in_ref[0, rows].astype(F32)
        for x in range(1, in_ref.shape[0]):
            total += in_ref[x, rows].astype(F32)
        out_ref[:, s * width : (s + 1) * width] = total.astype(BF)


def pair_kernel(a_ref, b_ref, o_ref):
    o_ref[...] = (a_ref[...].astype(F32) + b_ref[...].astype(F32)).astype(BF)


def adapter_kernel(v0_ref, v1_ref, v2_ref, v3_ref, s_ref, o_ref):
    low = v0_ref[...].astype(F32) + v1_ref[...].astype(F32)
    low += v2_ref[...].astype(F32) + v3_ref[...].astype(F32)
    o_ref[...] = tn(low.astype(BF), s_ref[...])


def combine_kernel(code_ref, r_ref, o_ref):
    width = o_ref.shape[1]
    total = jnp.zeros(o_ref.shape, F32)
    for s in range(CAP):
        pick = jnp.where(code_ref[...] == float(s), 1.0, 0.0).astype(BF)
        total += tn(pick, r_ref[:, s * width : (s + 1) * width])
    o_ref[...] = total.astype(BF)


def call(body, outs, *args, scalars=0):
    vmem = pl.BlockSpec(memory_space=pltpu.VMEM)
    smem = pl.BlockSpec(memory_space=pltpu.SMEM)
    return pl.pallas_call(
        body,
        out_shape=outs,
        in_specs=[smem] * scalars + [vmem] * (len(args) - scalars),
        out_specs=jax.tree.map(lambda _: vmem, outs),
        compiler_params=PARAMS,
    )(*args)


def per_device(tokens, grad_out, prob, ids, w_gate, w_up, w_down, adapter_a, adapter_b):
    experts = lax.axis_size(("z", "y"))
    chips = lax.axis_size("x")
    count, width = tokens.shape
    rank = adapter_b.shape[1]
    units = w_gate.shape[1]
    routes = experts * CAP
    w_gate, w_up, w_down, adapter_a, adapter_b = (
        w_gate[0], w_up[0], w_down[0], adapter_a[0], adapter_b[0],
    )
    sds = jax.ShapeDtypeStruct
    me = jnp.stack([lax.axis_index("x"), lax.axis_index("c")]).astype(jnp.int32)

    def swap(block):
        return lax.ppermute(block, "c", [(0, 1), (1, 0)])

    def shift(block, by):
        return lax.ppermute(block, "x", [(i, (i + by) % chips) for i in range(chips)])

    def over_x(block):
        return lax.all_to_all(block, "x", 0, 0, tiled=True)

    def route(block):
        return lax.all_to_all(block, ("z", "y"), 0, 0, tiled=True)

    packed, code = call(
        pack_kernel,
        (sds((experts, 2 * CAP * width), BF), sds((experts, count), F32)),
        ids.T, prob.T, tokens, grad_out,
    )
    arrived = route(packed)

    half, *down = call(
        prep_kernel,
        (sds((2, chips, units, width), BF),) + (sds((units, 2 * width), BF),) * 3,
        me, w_gate, w_up, w_down, scalars=1,
    )
    half = swap(half)
    down = [shift(block, d + 1) for d, block in enumerate(down)]
    b_other = swap(adapter_b)
    arrived, half, b_other, *down = lax.optimization_barrier((arrived, half, b_other, *down))

    x_four, s_own = call(split_kernel, (sds((chips, routes, width), BF), sds((routes, width), BF)), arrived)
    x_all = over_x(x_four)
    s_other = swap(s_own)
    part = call(
        part_kernel, sds((chips, routes, units + rank), BF),
        me, s_own, s_other, w_down, *down, adapter_b, b_other, scalars=1,
    )
    parts = over_x(part)
    keep, send = call(
        gate_kernel,
        (sds((2, routes, units), F32), sds((2, routes, units), BF)),
        me, x_all, w_gate, w_up, half, scalars=1,
    )
    got = swap(send)
    gate, up, hidden, v_own = call(
        act_kernel,
        (sds((routes, units), F32),) * 2 + (sds((routes, units), BF), sds((routes, rank), BF)),
        keep, got, adapter_a,
    )
    grads, grad_a = call(
        grad_kernel,
        (sds((2, routes, units), BF), sds((rank, units), F32)),
        parts, gate, up, hidden, adapter_a,
    )
    grads_other = swap(grads)
    back = call(
        back_kernel, sds((chips, routes, width), BF),
        me, grads, grads_other, w_gate, w_up, half, scalars=1,
    )
    backs = over_x(back)
    total = call(total_kernel, sds((experts, CAP * width), BF), backs)
    home = route(total)

    v_pair = call(pair_kernel, sds((routes, rank), BF), v_own, swap(v_own))
    v_all = [v_pair] + [shift(v_pair, d) for d in (1, 2, 3)]
    grad_b = call(adapter_kernel, sds((rank, width), F32), *v_all, s_own)
    out = call(combine_kernel, sds(tokens.shape, BF), code, home)
    return out, grad_a[None], grad_b[None]


def solution(mesh):
    fine = Mesh(mesh.devices.reshape(4, 2, 16, 4), ("x", "c", "z", "y"))
    dp, ex = ("x", "c"), ("z", "y")
    specs = (
        P(ex, dp), P(ex, dp), P(ex, None), P(ex, None),
        P(ex, dp, None), P(ex, dp, None), P(ex, dp, None), P(ex, None, dp), P(ex, None, dp),
    )
    return jax.shard_map(
        per_device,
        mesh=fine,
        in_specs=specs,
        out_specs=(P(ex, dp), P(ex, None, dp), P(ex, None, dp)),
        check_vma=False,
    )
```

time: 203 us -> 180 us (0.89)
  the two profiles are of different devices: /device:TPU:32 before, /device:TPU:8 now
where the time goes in v2:
time: 180 us; the launch traced here: 178 us
  starting transfers between devices  67.5 us (38%)
  waiting for transfers between devices  42 us (23%)
  local copies, waits for them, and re-layouts  26.9 us (15%)
  blocking collectives  22.8 us (13%)
  Pallas kernels  15.4 us (9%)
  other arithmetic  2.74 us (2%)
    all_to_all x2, starting transfers between devices, route(): return lax.all_to_all(block, ('z', 'y'), 0, 0, tiled=True)  26.8 us
    unnamed x52, local copies, waits for them, and re-layouts  26.3 us
    all_to_all x2, waiting for transfers between devices, route(): return lax.all_to_all(block, ('z', 'y'), 0, 0, tiled=True)  25.6 us
    all_to_all x1, blocking collectives, over_x(): return lax.all_to_all(block, 'x', 0, 0, tiled=True)  22.8 us
    ppermute x6, starting transfers between devices, shift(): lax.ppermute(block, 'x', [(i, (i + by) % chips) for i in range(chips)])  20.6 us
    pallas_call x12, Pallas kernels, call(): pl.pallas_call(body, out_shape=outs, in_specs=[smem] * scalars + [vmem] *...  15.4 us
    ppermute x6, starting transfers between devices, swap(): return lax.ppermute(block, 'c', [(0, 1), (1, 0)])  11.6 us
    all_to_all x2, starting transfers between devices, over_x(): return lax.all_to_all(block, 'x', 0, 0, tiled=True)  8.45 us
  transfers between devices with their start and end apart: 16, of which 9 were waited for; matrix products, arithmetic and copies ran while one was open for 4% of the time, Pallas kernels for 5%

profile of v2, /device:TPU:8, one launch (start us, length us, event | category | flops | bytes accessed | tf_op | source)
XLA Modules:
  0.0 178.1 jit_solution(13678861592058967503)
XLA Ops:
  0.6 0.7 copy-done.19
  1.4 0.8 copy-done.20
  2.2 0.7 copy-done.21
  2.8 0.7 copy-done.22
  3.5 0.4 shard_map.112
  4.0 0.6 copy-done.17
  4.6 0.6 broadcast
  5.2 1.9 %reduce = bf16[64,5120]{1,0:T(8,128)(2,1)} reduce(bf16[64,1,5120]{2,0,1:T(8,128)(2,1)S(1)} %bitcast.30, bf16[]{:T(256)} %broadcast), dimensions={1}, to_apply=%copy.14.reduce_sub_computation | reduce | bytes 1310722 | tf_op jit(solution)/shard_map/all_to_all | solution.py:213
  7.0 3.1 %reshape.10 = bf16[64,2,2560]{2,1,0:T(2,128)(2,1)} reshape(bf16[64,5120]{1,0:T(8,128)(2,1)} %reduce) | data formatting | bytes 1310720
  10.1 18.9 %all-to-all-start = ((bf16[64,2,2560]{2,1,0:T(2,128)(2,1)}), bf16[64,2,2560]{2,1,0:T(2,128)(2,1)}, u32[]{:S(2)}, u32[]{:S(2)}) async-start(bf16[64,2,2560]{2,1,0:T(2,128)(2,1)} %reshape.10), calls=%async_computation | async-start | bytes 1310720 | tf_op jit(solution)/shard_map/all_to_all | solution.py:213
  29.0 0.1 pad_add_fusion.me_ref
  29.1 1.4 copy-done.2
  30.5 2.3 %shard_map.113 = (bf16[2,4,192,512]{3,2,1,0:T(8,128)(2,1)}, bf16[192,1024]{1,0:T(8,128)(2,1)}, bf16[192,1024]{1,0:T(8,128)(2,1)}, bf16[192,1024]{1,0:T(8,128)(2,1)}) custom-call(s32[2]{0:T(128)S(1)} %pad_add_fusion.me_ref, bf16[192,4096]{1,0:T(8,128)(2,1)S(1)} %bitcast.19, bf16[192,4096]{1,0:T(8,128)(2,1)S(1)} %bitcast.22, bf16[192,4096]{1,0:T(8,128)(2,1)S(1)} %bitcast.25), custom_call_target="tpu_custom_call" | custom-call | tf_op jit(solution)/shard_map/pallas_call | solution.py:181
  32.8 1.9 %collective-permute-start = (bf16[2,4,192,512]{3,2,1,0:T(8,128)(2,1)}, bf16[2,4,192,512]{3,2,1,0:T(8,128)(2,1)}, u32[]{:S(2)}, u32[]{:S(2)}) collective-permute-start(bf16[2,4,192,512]{3,2,1,0:T(8,128)(2,1)} %get-tuple-element.27), channel_id=1, source_target_pairs={{0,64},{64,0},{1,65},{65,1},{2,66},{66,2},{3,67},{67,3},{4,68},{68... | collective-permute-start | bytes 4718600 | tf_op jit(solution)/shard_map/ppermute | solution.py:204
  34.7 3.4 %collective-permute-start.2 = (bf16[192,1024]{1,0:T(8,128)(2,1)}, bf16[192,1024]{1,0:T(8,128)(2,1)S(1)}, u32[]{:S(2)}, u32[]{:S(2)}) collective-permute-start(bf16[192,1024]{1,0:T(8,128)(2,1)} %get-tuple-element.28), channel_id=1, source_target_pairs={{0,128},{128,256},{256,384},{384,0},{1,129},{129,257},{257,385},{3... | collective-permute-start | bytes 1179656 | tf_op jit(solution)/shard_map/ppermute | solution.py:207
  38.1 4.6 %collective-permute-start.3 = (bf16[192,1024]{1,0:T(8,128)(2,1)}, bf16[192,1024]{1,0:T(8,128)(2,1)}, u32[]{:S(2)}, u32[]{:S(2)}) collective-permute-start(bf16[192,1024]{1,0:T(8,128)(2,1)} %get-tuple-element.29), channel_id=1, source_target_pairs={{0,256},{128,384},{256,0},{384,128},{1,257},{129,385},{257,1},{385... | collective-permute-start | bytes 1179656 | tf_op jit(solution)/shard_map/ppermute | solution.py:207
  42.7 3.3 %collective-permute-start.4 = (bf16[192,1024]{1,0:T(8,128)(2,1)}, bf16[192,1024]{1,0:T(8,128)(2,1)}, u32[]{:S(2)}, u32[]{:S(2)}) collective-permute-start(bf16[192,1024]{1,0:T(8,128)(2,1)} %get-tuple-element.30), channel_id=1, source_target_pairs={{0,384},{128,0},{256,128},{384,256},{1,385},{129,1},{257,129},{385... | collective-permute-start | bytes 1179656 | tf_op jit(solution)/shard_map/ppermute | solution.py:207
  46.1 1.9 %collective-permute-start.1 = (bf16[64,512]{1,0:T(8,128)(2,1)}, bf16[64,512]{1,0:T(8,128)(2,1)}, u32[]{:S(2)}, u32[]{:S(2)}) collective-permute-start(bf16[64,512]{1,0:T(8,128)(2,1)} %bitcast.8.b_ref), channel_id=1, source_target_pairs={{0,64},{64,0},{1,65},{65,1},{2,66},{66,2},{3,67},{67,3},{4,68},{68... | collective-permute-start | bytes 196616 | tf_op jit(solution)/shard_map/ppermute | solution.py:204
  48.0 19.2 %all-to-all-done = bf16[64,2,2560]{2,1,0:T(2,128)(2,1)} async-done(((bf16[64,2,2560]{2,1,0:T(2,128)(2,1)}), bf16[64,2,2560]{2,1,0:T(2,128)(2,1)}, u32[]{:S(2)}, u32[]{:S(2)}) %all-to-all-start) | async-done | bytes 655392 | tf_op jit(solution)/shard_map/all_to_all | solution.py:213
  67.3 5.0 %reshape.11 = bf16[64,1,5120]{2,1,0:T(2,128)(2,1)} reshape(bf16[64,2,2560]{2,1,0:T(2,128)(2,1)} %all-to-all-done) | data formatting | bytes 1310720
  72.2 1.5 copy.20
  73.8 0.7 copy-done.6
  74.6 0.1 shard_map.114
  74.7 1.1 copy-done.5
  75.8 4.3 %all-to-all-start.2 = ((bf16[4,320,512]{2,1,0:T(8,128)(2,1)}), bf16[4,320,512]{2,1,0:T(8,128)(2,1)}, u32[]{:S(2)}, u32[]{:S(2)}) async-start(bf16[4,320,512]{2,1,0:T(8,128)(2,1)} %copy-done.5), calls=%async_computation.2 | async-start | bytes 2621440 | tf_op jit(solution)/shard_map/all_to_all | solution.py:210
  80.1 1.9 %collective-permute-start.5 = (bf16[320,512]{1,0:T(8,128)(2,1)S(1)}, bf16[320,512]{1,0:T(8,128)(2,1)S(1)}, u32[]{:S(2)}, u32[]{:S(2)}) collective-permute-start(bf16[320,512]{1,0:T(8,128)(2,1)S(1)} %get-tuple-element.32.s_ref), channel_id=1, source_target_pairs={{0,64},{64,0},{1,65},{65,1},{2,66},{66,2},{3,67},{67,3},{4,68},{68... | collective-permute-start | bytes 983048 | tf_op jit(solution)/shard_map/ppermute | solution.py:204
  82.0 1.6 collective-permute-done.5.t_ref
  83.6 1.4 copy-done.3
  85.0 1.0 copy-done.7
  86.0 2.1 %shard_map.115 = bf16[4,320,256]{2,1,0:T(8,128)(2,1)S(1)} custom-call(s32[2]{0:T(128)S(1)} %pad_add_fusion.me_ref, bf16[320,512]{1,0:T(8,128)(2,1)S(1)} %get-tuple-element.32.s_ref, bf16[320,512]{1,0:T(8,128)(2,1)S(1)} %collective-permute-done.5.t_ref, bf16[192,4096]{1,0:T(8,128)(2,1)S(1)} %bitcast.26, bf16[192,1024]{1,0:T(8,128)(2,1)S(1)} %copy-done.7, ...), custom_call_target="tpu_custom_call" | custom-call | tf_op jit(solution)/shard_map/pallas_call | solution.py:181
  88.1 0.8 copy-done.4
  89.0 6.9 %all-to-all-done.2.x_ref = bf16[4,320,512]{2,1,0:T(8,128)(2,1)} async-done(((bf16[4,320,512]{2,1,0:T(8,128)(2,1)}), bf16[4,320,512]{2,1,0:T(8,128)(2,1)}, u32[]{:S(2)}, u32[]{:S(2)}) %all-to-all-start.2) | async-done | bytes 1310752 | tf_op jit(solution)/shard_map/all_to_all | solution.py:210
  95.8 4.2 %all-to-all-start.1 = ((bf16[4,320,256]{2,1,0:T(8,128)(2,1)}), bf16[4,320,256]{2,1,0:T(8,128)(2,1)}, u32[]{:S(2)}, u32[]{:S(2)}) async-start(bf16[4,320,256]{2,1,0:T(8,128)(2,1)} %copy-done.4), calls=%async_computation.1 | async-start | bytes 1310720 | tf_op jit(solution)/shard_map/all_to_all | solution.py:210
  100.0 3.4 %shard_map.116 = (f32[2,320,192]{2,1,0:T(8,128)S(1)}, bf16[2,320,192]{2,1,0:T(8,128)(2,1)S(1)}) custom-call(s32[2]{0:T(128)S(1)} %pad_add_fusion.me_ref, bf16[4,320,512]{2,1,0:T(8,128)(2,1)} %all-to-all-done.2.x_ref, bf16[192,4096]{1,0:T(8,128)(2,1)S(1)} %bitcast.20, bf16[192,4096]{1,0:T(8,128)(2,1)S(1)} %bitcast.23, ...), custom_call_target="tpu_custom_call" | custom-call | tf_op jit(solution)/shard_map/pallas_call | solution.py:181
  103.3 1.9 %collective-permute-start.6 = (bf16[2,320,192]{2,1,0:T(8,128)(2,1)S(1)}, bf16[2,320,192]{2,1,0:T(8,128)(2,1)S(1)}, u32[]{:S(2)}, u32[]{:S(2)}) collective-permute-start(bf16[2,320,192]{2,1,0:T(8,128)(2,1)S(1)} %get-tuple-element.40), channel_id=1, source_target_pairs={{0,64},{64,0},{1,65},{65,1},{2,66},{66,2},{3,67},{67,3},{4,68},{68... | collective-permute-start | bytes 737288 | tf_op jit(solution)/shard_map/ppermute | solution.py:204
  105.3 1.6 collective-permute-done.6.got_ref
  106.9 0.2 shard_map.117
  107.1 0.7 copy-done.8
  107.8 0.7 copy-done.10
  108.6 0.7 copy-done.12
  109.2 0.6 copy-done.15
  109.8 1.0 copy-done.9
  110.8 1.0 copy-done.11
  111.8 0.9 copy-done.13
  112.7 2.0 %shard_map.118 = (bf16[2,320,192]{2,1,0:T(8,128)(2,1)S(1)}, f32[64,192]{1,0:T(8,128)}) custom-call(bf16[4,320,256]{2,1,0:T(8,128)(2,1)} %all-to-all-done.1.in_ref, f32[320,192]{1,0:T(8,128)S(1)} %copy-done.9, f32[320,192]{1,0:T(8,128)S(1)} %copy-done.11, bf16[320,192]{1,0:T(8,128)(2,1)S(1)} %copy-done.13, bf16[64,192]{1,0:T(8,128)(2,1)S(1)} %bitcast.32), custom_call_target="tpu_custom_call" | custom-call | tf_op jit(solution)/shard_map/pallas_call | solution.py:181
  114.7 2.0 %collective-permute-start.7 = (bf16[2,320,192]{2,1,0:T(8,128)(2,1)S(1)}, bf16[2,320,192]{2,1,0:T(8,128)(2,1)S(1)}, u32[]{:S(2)}, u32[]{:S(2)}) collective-permute-start(bf16[2,320,192]{2,1,0:T(8,128)(2,1)S(1)} %get-tuple-element.44.g_ref), channel_id=1, source_target_pairs={{0,64},{64,0},{1,65},{65,1},{2,66},{66,2},{3,67},{67,3},{4,68},{68... | collective-permute-start | bytes 737288 | tf_op jit(solution)/shard_map/ppermute | solution.py:204
  116.8 1.5 collective-permute-done.7.h_ref
  118.2 2.9 %shard_map.119 = bf16[4,320,512]{2,1,0:T(8,128)(2,1)S(1)} custom-call(s32[2]{0:T(128)S(1)} %pad_add_fusion.me_ref, bf16[2,320,192]{2,1,0:T(8,128)(2,1)S(1)} %get-tuple-element.44.g_ref, bf16[2,320,192]{2,1,0:T(8,128)(2,1)S(1)} %collective-permute-done.7.h_ref, bf16[192,4096]{1,0:T(8,128)(2,1)S(1)} %bitcast.21, bf16[192,4096]{1,0:T(8,128)(2,1)S(1)} %bitcast.24, ...), custom_call_target="tpu_custom_call" | custom-call | tf_op jit(solution)/shard_map/pallas_call | solution.py:181
  121.2 22.8 %all_to_all.38.in_ref = bf16[4,320,512]{2,1,0:T(8,128)(2,1)S(1)} all-to-all(bf16[4,320,512]{2,1,0:T(8,128)(2,1)S(1)} %shard_map.119), channel_id=1, replica_groups=mesh['x'=4,'c'=2,'z'=16,'y'=4] {'x'}, dimensions={0} | all-to-all | bytes 2621440 | tf_op jit(solution)/shard_map/all_to_all | solution.py:210
  143.9 0.2 shard_map.120
  144.1 0.8 reduce.1
  144.9 0.8 reshape.12
  145.7 7.9 %all-to-all-start.4 = ((bf16[64,2,1280]{2,1,0:T(2,128)(2,1)}), bf16[64,2,1280]{2,1,0:T(2,128)(2,1)S(1)}, u32[]{:S(2)}, u32[]{:S(2)}) async-start(bf16[64,2,1280]{2,1,0:T(2,128)(2,1)} %reshape.12), calls=%async_computation.4 | async-start | bytes 655360 | tf_op jit(solution)/shard_map/all_to_all | solution.py:213
  153.7 1.9 %collective-permute-start.8 = (bf16[320,64]{1,0:T(8,128)(2,1)S(1)}, bf16[320,64]{1,0:T(8,128)(2,1)S(1)}, u32[]{:S(2)}, u32[]{:S(2)}) collective-permute-start(bf16[320,64]{1,0:T(8,128)(2,1)S(1)} %copy-done.16), channel_id=1, source_target_pairs={{0,64},{64,0},{1,65},{65,1},{2,66},{66,2},{3,67},{67,3},{4,68},{68... | collective-permute-start | bytes 122888 | tf_op jit(solution)/shard_map/ppermute | solution.py:204
  155.6 1.2 collective-permute-done.8.b_ref
  156.9 2.5 %collective-permute-start.9 = (bf16[320,64]{1,0:T(8,128)(2,1)S(1)}, bf16[320,64]{1,0:T(8,128)(2,1)S(1)}, u32[]{:S(2)}, u32[]{:S(2)}) collective-permute-start(bf16[320,64]{1,0:T(8,128)(2,1)S(1)} %shard_map.122.v0_ref), channel_id=1, source_target_pairs={{0,128},{128,256},{256,384},{384,0},{1,129},{129,257},{257,385},{3... | collective-permute-start | bytes 122888 | tf_op jit(solution)/shard_map/ppermute | solution.py:207
  159.4 4.0 %collective-permute-start.10 = (bf16[320,64]{1,0:T(8,128)(2,1)S(1)}, bf16[320,64]{1,0:T(8,128)(2,1)S(1)}, u32[]{:S(2)}, u32[]{:S(2)}) collective-permute-start(bf16[320,64]{1,0:T(8,128)(2,1)S(1)} %shard_map.122.v0_ref), channel_id=1, source_target_pairs={{0,256},{128,384},{256,0},{384,128},{1,257},{129,385},{257,1},{385... | collective-permute-start | bytes 122888 | tf_op jit(solution)/shard_map/ppermute | solution.py:207
  163.4 2.7 %collective-permute-start.11 = (bf16[320,64]{1,0:T(8,128)(2,1)S(1)}, bf16[320,64]{1,0:T(8,128)(2,1)S(1)}, u32[]{:S(2)}, u32[]{:S(2)}) collective-permute-start(bf16[320,64]{1,0:T(8,128)(2,1)S(1)} %shard_map.122.v0_ref), channel_id=1, source_target_pairs={{0,384},{128,0},{256,128},{384,256},{1,385},{129,1},{257,129},{385... | collective-permute-start | bytes 122888 | tf_op jit(solution)/shard_map/ppermute | solution.py:207
  166.1 1.1 collective-permute-done.10.v2_ref
  167.2 2.5 %collective-permute-done.11.v3_ref = bf16[320,64]{1,0:T(8,128)(2,1)S(1)} collective-permute-done((bf16[320,64]{1,0:T(8,128)(2,1)S(1)}, bf16[320,64]{1,0:T(8,128)(2,1)S(1)}, u32[]{:S(2)}, u32[]{:S(2)}) %collective-permute-start.11) | collective-permute-done | bytes 40992 | tf_op jit(solution)/shard_map/ppermute | solution.py:207
  169.7 0.9 shard_map.123
  170.6 6.4 %all-to-all-done.4 = bf16[64,2,1280]{2,1,0:T(2,128)(2,1)S(1)} async-done(((bf16[64,2,1280]{2,1,0:T(2,128)(2,1)}), bf16[64,2,1280]{2,1,0:T(2,128)(2,1)S(1)}, u32[]{:S(2)}, u32[]{:S(2)}) %all-to-all-start.4) | async-done | bytes 327712 | tf_op jit(solution)/shard_map/all_to_all | solution.py:213
  176.9 0.3 reshape.13
  177.3 0.8 shard_map.121
  (37 shorter events, 0.1 us)
Async XLA Ops:
  0.6 0.8 copy-start.19
  1.4 0.8 copy-start.20
  2.1 0.7 copy-start.21
  2.8 0.7 copy-start.22
  4.0 0.6 copy-start.17
  5.2 23.9 %copy-start.1 = (bf16[1,192,4096]{2,1,0:T(8,128)(2,1)S(1)}, bf16[1,192,4096]{2,1,0:T(8,128)(2,1)}, u32[]{:S(2)}) copy-start(bf16[1,192,4096]{2,1,0:T(8,128)(2,1)} %param.14) | copy-start | bytes 4718596
  7.0 22.1 %copy-start = (bf16[1,192,4096]{2,1,0:T(8,128)(2,1)S(1)}, bf16[1,192,4096]{2,1,0:T(8,128)(2,1)}, u32[]{:S(2)}) copy-start(bf16[1,192,4096]{2,1,0:T(8,128)(2,1)} %param.13) | copy-start | bytes 4718596
  10.1 57.2 %all-to-all-start = ((bf16[64,2,2560]{2,1,0:T(2,128)(2,1)}), bf16[64,2,2560]{2,1,0:T(2,128)(2,1)}, u32[]{:S(2)}, u32[]{:S(2)}) async-start(bf16[64,2,2560]{2,1,0:T(2,128)(2,1)} %reshape.10), calls=%async_computation | async-start | bytes 1310720 | tf_op jit(solution)/shard_map/all_to_all | solution.py:213
  29.1 1.4 copy-start.2
  32.8 41.8 %collective-permute-start = (bf16[2,4,192,512]{3,2,1,0:T(8,128)(2,1)}, bf16[2,4,192,512]{3,2,1,0:T(8,128)(2,1)}, u32[]{:S(2)}, u32[]{:S(2)}) collective-permute-start(bf16[2,4,192,512]{3,2,1,0:T(8,128)(2,1)} %get-tuple-element.27), channel_id=1, source_target_pairs={{0,64},{64,0},{1,65},{65,1},{2,66},{66,2},{3,67},{67,3},{4,68},{68... | collective-permute-start | bytes 4718600 | tf_op jit(solution)/shard_map/ppermute | solution.py:204
  34.7 39.1 %collective-permute-start.2 = (bf16[192,1024]{1,0:T(8,128)(2,1)}, bf16[192,1024]{1,0:T(8,128)(2,1)S(1)}, u32[]{:S(2)}, u32[]{:S(2)}) collective-permute-start(bf16[192,1024]{1,0:T(8,128)(2,1)} %get-tuple-element.28), channel_id=1, source_target_pairs={{0,128},{128,256},{256,384},{384,0},{1,129},{129,257},{257,385},{3... | collective-permute-start | bytes 1179656 | tf_op jit(solution)/shard_map/ppermute | solution.py:207
  38.1 36.5 %collective-permute-start.3 = (bf16[192,1024]{1,0:T(8,128)(2,1)}, bf16[192,1024]{1,0:T(8,128)(2,1)}, u32[]{:S(2)}, u32[]{:S(2)}) collective-permute-start(bf16[192,1024]{1,0:T(8,128)(2,1)} %get-tuple-element.29), channel_id=1, source_target_pairs={{0,256},{128,384},{256,0},{384,128},{1,257},{129,385},{257,1},{385... | collective-permute-start | bytes 1179656 | tf_op jit(solution)/shard_map/ppermute | solution.py:207
  42.7 31.8 %collective-permute-start.4 = (bf16[192,1024]{1,0:T(8,128)(2,1)}, bf16[192,1024]{1,0:T(8,128)(2,1)}, u32[]{:S(2)}, u32[]{:S(2)}) collective-permute-start(bf16[192,1024]{1,0:T(8,128)(2,1)} %get-tuple-element.30), channel_id=1, source_target_pairs={{0,384},{128,0},{256,128},{384,256},{1,385},{129,1},{257,129},{385... | collective-permute-start | bytes 1179656 | tf_op jit(solution)/shard_map/ppermute | solution.py:207
  46.1 27.7 %collective-permute-start.1 = (bf16[64,512]{1,0:T(8,128)(2,1)}, bf16[64,512]{1,0:T(8,128)(2,1)}, u32[]{:S(2)}, u32[]{:S(2)}) collective-permute-start(bf16[64,512]{1,0:T(8,128)(2,1)} %bitcast.8.b_ref), channel_id=1, source_target_pairs={{0,64},{64,0},{1,65},{65,1},{2,66},{66,2},{3,67},{67,3},{4,68},{68... | collective-permute-start | bytes 196616 | tf_op jit(solution)/shard_map/ppermute | solution.py:204
  73.8 0.8 copy-start.6
  74.7 1.1 copy-start.5
  75.8 20.1 %all-to-all-start.2 = ((bf16[4,320,512]{2,1,0:T(8,128)(2,1)}), bf16[4,320,512]{2,1,0:T(8,128)(2,1)}, u32[]{:S(2)}, u32[]{:S(2)}) async-start(bf16[4,320,512]{2,1,0:T(8,128)(2,1)} %copy-done.5), calls=%async_computation.2 | async-start | bytes 2621440 | tf_op jit(solution)/shard_map/all_to_all | solution.py:210
  80.1 3.5 %collective-permute-start.5 = (bf16[320,512]{1,0:T(8,128)(2,1)S(1)}, bf16[320,512]{1,0:T(8,128)(2,1)S(1)}, u32[]{:S(2)}, u32[]{:S(2)}) collective-permute-start(bf16[320,512]{1,0:T(8,128)(2,1)S(1)} %get-tuple-element.32.s_ref), channel_id=1, source_target_pairs={{0,64},{64,0},{1,65},{65,1},{2,66},{66,2},{3,67},{67,3},{4,68},{68... | collective-permute-start | bytes 983048 | tf_op jit(solution)/shard_map/ppermute | solution.py:204
  83.6 1.4 copy-start.3
  85.0 1.0 copy-start.7
  88.1 0.8 copy-start.4
  95.8 14.0 %all-to-all-start.1 = ((bf16[4,320,256]{2,1,0:T(8,128)(2,1)}), bf16[4,320,256]{2,1,0:T(8,128)(2,1)}, u32[]{:S(2)}, u32[]{:S(2)}) async-start(bf16[4,320,256]{2,1,0:T(8,128)(2,1)} %copy-done.4), calls=%async_computation.1 | async-start | bytes 1310720 | tf_op jit(solution)/shard_map/all_to_all | solution.py:210
  100.0 6.9 %copy-start.14 = (bf16[1,64,192]{2,1,0:T(8,128)(2,1)S(1)}, bf16[1,64,192]{2,1,0:T(8,128)(2,1)}, u32[]{:S(2)}) copy-start(bf16[1,64,192]{2,1,0:T(8,128)(2,1)} %param.16) | copy-start | bytes 73732
  103.3 3.5 %collective-permute-start.6 = (bf16[2,320,192]{2,1,0:T(8,128)(2,1)S(1)}, bf16[2,320,192]{2,1,0:T(8,128)(2,1)S(1)}, u32[]{:S(2)}, u32[]{:S(2)}) collective-permute-start(bf16[2,320,192]{2,1,0:T(8,128)(2,1)S(1)} %get-tuple-element.40), channel_id=1, source_target_pairs={{0,64},{64,0},{1,65},{65,1},{2,66},{66,2},{3,67},{67,3},{4,68},{68... | collective-permute-start | bytes 737288 | tf_op jit(solution)/shard_map/ppermute | solution.py:204
  107.1 0.7 copy-start.8
  107.8 0.7 copy-start.10
  108.6 0.7 copy-start.12
  109.2 0.6 copy-start.15
  109.8 1.0 copy-start.9
  110.8 1.0 copy-start.11
  111.8 0.9 copy-start.13
  114.7 3.5 %collective-permute-start.7 = (bf16[2,320,192]{2,1,0:T(8,128)(2,1)S(1)}, bf16[2,320,192]{2,1,0:T(8,128)(2,1)S(1)}, u32[]{:S(2)}, u32[]{:S(2)}) collective-permute-start(bf16[2,320,192]{2,1,0:T(8,128)(2,1)S(1)} %get-tuple-element.44.g_ref), channel_id=1, source_target_pairs={{0,64},{64,0},{1,65},{65,1},{2,66},{66,2},{3,67},{67,3},{4,68},{68... | collective-permute-start | bytes 737288 | tf_op jit(solution)/shard_map/ppermute | solution.py:204
  143.9 9.8 %copy-start.16 = (bf16[320,64]{1,0:T(8,128)(2,1)S(1)}, bf16[320,64]{1,0:T(8,128)(2,1)}, u32[]{:S(2)}) copy-start(bf16[320,64]{1,0:T(8,128)(2,1)} %copy-done.15) | copy-start | bytes 122884
  145.7 31.2 %all-to-all-start.4 = ((bf16[64,2,1280]{2,1,0:T(2,128)(2,1)}), bf16[64,2,1280]{2,1,0:T(2,128)(2,1)S(1)}, u32[]{:S(2)}, u32[]{:S(2)}) async-start(bf16[64,2,1280]{2,1,0:T(2,128)(2,1)} %reshape.12), calls=%async_computation.4 | async-start | bytes 655360 | tf_op jit(solution)/shard_map/all_to_all | solution.py:213
  153.7 23.6 %copy-start.18 = (f32[64,32]{1,0:T(8,128)S(1)}, f32[64,32]{1,0:T(8,128)}, u32[]{:S(2)}) copy-start(f32[64,32]{1,0:T(8,128)} %copy-done.17) | copy-start | bytes 24580
  153.7 3.2 %collective-permute-start.8 = (bf16[320,64]{1,0:T(8,128)(2,1)S(1)}, bf16[320,64]{1,0:T(8,128)(2,1)S(1)}, u32[]{:S(2)}, u32[]{:S(2)}) collective-permute-start(bf16[320,64]{1,0:T(8,128)(2,1)S(1)} %copy-done.16), channel_id=1, source_target_pairs={{0,64},{64,0},{1,65},{65,1},{2,66},{66,2},{3,67},{67,3},{4,68},{68... | collective-permute-start | bytes 122888 | tf_op jit(solution)/shard_map/ppermute | solution.py:204
  156.9 9.2 %collective-permute-start.9 = (bf16[320,64]{1,0:T(8,128)(2,1)S(1)}, bf16[320,64]{1,0:T(8,128)(2,1)S(1)}, u32[]{:S(2)}, u32[]{:S(2)}) collective-permute-start(bf16[320,64]{1,0:T(8,128)(2,1)S(1)} %shard_map.122.v0_ref), channel_id=1, source_target_pairs={{0,128},{128,256},{256,384},{384,0},{1,129},{129,257},{257,385},{3... | collective-permute-start | bytes 122888 | tf_op jit(solution)/shard_map/ppermute | solution.py:207
  159.4 7.8 %collective-permute-start.10 = (bf16[320,64]{1,0:T(8,128)(2,1)S(1)}, bf16[320,64]{1,0:T(8,128)(2,1)S(1)}, u32[]{:S(2)}, u32[]{:S(2)}) collective-permute-start(bf16[320,64]{1,0:T(8,128)(2,1)S(1)} %shard_map.122.v0_ref), channel_id=1, source_target_pairs={{0,256},{128,384},{256,0},{384,128},{1,257},{129,385},{257,1},{385... | collective-permute-start | bytes 122888 | tf_op jit(solution)/shard_map/ppermute | solution.py:207
  163.4 6.3 %collective-permute-start.11 = (bf16[320,64]{1,0:T(8,128)(2,1)S(1)}, bf16[320,64]{1,0:T(8,128)(2,1)S(1)}, u32[]{:S(2)}, u32[]{:S(2)}) collective-permute-start(bf16[320,64]{1,0:T(8,128)(2,1)S(1)} %shard_map.122.v0_ref), channel_id=1, source_target_pairs={{0,384},{128,0},{256,128},{384,256},{1,385},{129,1},{257,129},{385... | collective-permute-start | bytes 122888 | tf_op jit(solution)/shard_map/ppermute | solution.py:207

commit v3 on v2

v3 whole, which is shorter than its diff:
```python
import jax
import jax.numpy as jnp
from jax import lax
from jax.experimental import pallas as pl
from jax.experimental.pallas import tpu as pltpu
from jax.sharding import Mesh, PartitionSpec as P

CAP = 5
BF = jnp.bfloat16
F32 = jnp.float32
LANE = 128
PARAMS = pltpu.CompilerParams(vmem_limit_bytes=16 * 1024 * 1024)


def nt(left, right):
    return lax.dot_general(left, right, (((1,), (1,)), ((), ())), preferred_element_type=F32)


def tn(left, right):
    return lax.dot_general(left, right, (((0,), (0,)), ((), ())), preferred_element_type=F32)


def nn(left, right):
    return jnp.dot(left, right, preferred_element_type=F32)


def lanes(index, width):
    return pl.ds(pl.multiple_of(index * width, width), width)


def fetch(pairs, sems):
    copies = [pltpu.make_async_copy(src, dst, sems.at[i]) for i, (src, dst) in enumerate(pairs)]
    for copy in copies:
        copy.start()
    for copy in copies:
        copy.wait()


def pack_kernel(ids_hbm, prob_hbm, tok_hbm, dy_hbm, out_ref, ids_ref, prob_ref, tok_ref, dy_ref, sems):
    fetch(
        [(ids_hbm, ids_ref), (prob_hbm, prob_ref), (tok_hbm, tok_ref), (dy_hbm, dy_ref)], sems
    )
    rows = out_ref.shape[0]
    count, width = tok_ref.shape
    parts = 2 * width // LANE
    span = parts * count
    row = lax.broadcasted_iota(jnp.int32, (rows, span), 0)
    lane = lax.broadcasted_iota(jnp.int32, (rows, span), 1)
    own = jnp.where(lax.rem(row, parts) == lax.div(lane, count), lax.div(row, parts), -1)
    ids = jnp.concatenate([ids_ref[...]] * parts, axis=1)
    prob = jnp.concatenate([prob_ref[...]] * parts, axis=1)
    hit = jnp.zeros((rows, span), F32)
    weight = jnp.zeros((rows, span), F32)
    for k in range(ids.shape[0]):
        same = ids[k : k + 1, :] == own
        hit = jnp.where(same, 1.0, hit)
        weight = jnp.where(same, prob[k : k + 1, :], weight)
    weight = jnp.where(lax.rem(row, parts) < parts // 2, hit, weight)
    first = lax.broadcasted_iota(jnp.int32, (span, span), 0)
    second = lax.broadcasted_iota(jnp.int32, (span, span), 1)
    near = lax.div(first, count) == lax.div(second, count)
    before = jnp.where(near & (first < second), 1.0, 0.0).astype(BF)
    slot = nn(hit.astype(BF), before)
    code = jnp.where(hit > 0.5, slot, -1.0)
    table = jnp.concatenate(
        [ref[:, c : c + LANE] for ref in (tok_ref, dy_ref) for c in range(0, width, LANE)], axis=0
    )
    for s in range(CAP):
        mine = code == float(s)
        pick = jnp.where(mine, 1.0, 0.0).astype(BF)
        scale = jnp.sum(jnp.where(mine, weight, 0.0), axis=1, keepdims=True)
        out_ref[:, s * LANE : (s + 1) * LANE] = (nn(pick, table) * scale).astype(BF)


def code_of(ids, experts):
    count = ids.shape[1]
    own = lax.broadcasted_iota(jnp.int32, (experts, count), 0)
    hit = jnp.zeros((experts, count), F32)
    for k in range(ids.shape[0]):
        hit = jnp.where(ids[k : k + 1, :] == own, 1.0, hit)
    first = lax.broadcasted_iota(jnp.int32, (count, count), 0)
    second = lax.broadcasted_iota(jnp.int32, (count, count), 1)
    before = jnp.where(first < second, 1.0, 0.0).astype(BF)
    return jnp.where(hit > 0.5, nn(hit.astype(BF), before), -1.0)


def split_kernel(in_ref, x_hbm, s_hbm, x_ref, s_ref, sems):
    total = in_ref.shape[0]
    width = s_ref.shape[1]
    parts = 2 * width // LANE
    experts = total // parts
    first = lax.broadcasted_iota(jnp.int32, (total, total), 0)
    second = lax.broadcasted_iota(jnp.int32, (total, total), 1)
    there = lax.rem(first, experts) * parts + lax.div(first, experts)
    perm = jnp.where(second == there, 1.0, 0.0).astype(BF)
    rows = nn(perm, in_ref[...]).astype(BF)
    for r in range(parts):
        ref = x_ref if r < parts // 2 else s_ref
        at = (r % (parts // 2)) * LANE
        for s in range(CAP):
            ref[s * experts : (s + 1) * experts, at : at + LANE] = rows[
                r * experts : (r + 1) * experts, s * LANE : (s + 1) * LANE
            ]
    chips = x_hbm.shape[0]
    fetch([(x_ref, x_hbm.at[x]) for x in range(chips)] + [(s_ref, s_hbm)], sems)


def prep_kernel(me_ref, wg_ref, wu_ref, wd_ref, swap_ref, d0_ref, d1_ref, d2_ref, d3_ref):
    chip, core = me_ref[0], me_ref[1]
    chips, units, width = swap_ref.shape[1:]
    for x in range(chips):
        cols = lanes(2 * x + 1 - core, width)
        swap_ref[0, x] = wg_ref[:, cols]
        swap_ref[1, x] = wu_ref[:, cols]
    for d, ref in enumerate((d0_ref, d1_ref, d2_ref, d3_ref)):
        ref[...] = wd_ref[:, lanes(lax.rem(chip + d, chips), 2 * width)]


def part_kernel(me_ref, *refs):
    core = me_ref[1]
    sources, outs, held, sems = refs[:8], refs[8:12], refs[12:20], refs[20]
    fetch(list(zip(sources, held)), sems)
    s_ref, t_ref, b_ref, o_ref = held[:4]
    units, width = held[4].shape[0], s_ref.shape[1]
    mine, other = s_ref[...], t_ref[...]
    low = (nt(mine, b_ref[...]) + nt(other, o_ref[...])).astype(BF)
    for ref, out in zip(held[4:], outs):
        w_mine, w_other = ref[:, lanes(core, width)], ref[:, lanes(1 - core, width)]
        out[:, :units] = (nt(mine, w_mine) + nt(other, w_other)).astype(BF)
        out[:, units:] = low


def gate_kernel(me_ref, x_ref, wg_ref, wu_ref, swap_ref, *refs):
    keep_ref, send_ref = refs[-2:]
    core = me_ref[1]
    chips, routes, width = x_ref.shape
    units = wg_ref.shape[0]
    keep = [jnp.zeros((routes, units), F32)] * 2
    send = [jnp.zeros((routes, units), F32)] * 2
    for x in range(chips):
        rows = x_ref[x]
        cols = lanes(2 * x + core, width)
        for i, ref in enumerate((wg_ref, wu_ref)):
            keep[i] = keep[i] + nt(rows, ref[:, cols])
            send[i] = send[i] + nt(rows, swap_ref[i, x])
    for i in range(2):
        keep_ref[i] = keep[i]
        send_ref[i] = send[i].astype(BF)


def grad_kernel(keep_ref, got_ref, p0_ref, p1_ref, p2_ref, p3_ref, a_ref, out_ref, ga_ref, v_ref):
    units = keep_ref.shape[2]
    gate = keep_ref[0] + got_ref[0].astype(F32)
    up = keep_ref[1] + got_ref[1].astype(F32)
    sigma = jax.nn.sigmoid(gate)
    active = gate * sigma
    hidden = (active * up).astype(BF)
    v_ref[...] = nt(hidden, a_ref[...]).astype(BF)
    total = p0_ref[...].astype(F32) + p1_ref[...].astype(F32)
    total += p2_ref[...].astype(F32) + p3_ref[...].astype(F32)
    low_u = total[:, units:].astype(BF)
    grad = total[:, :units] + nn(low_u, a_ref[...])
    ga_ref[...] = tn(low_u, hidden)
    out_ref[0] = (grad * up * sigma * (1.0 + gate * (1.0 - sigma))).astype(BF)
    out_ref[1] = (grad * active).astype(BF)


def back_kernel(me_ref, g_ref, h_ref, wg_ref, wu_ref, swap_ref, out_ref):
    core = me_ref[1]
    chips, _, width = out_ref.shape
    for x in range(chips):
        cols = lanes(2 * x + core, width)
        term = nn(g_ref[0], wg_ref[:, cols]) + nn(g_ref[1], wu_ref[:, cols])
        term += nn(h_ref[0], swap_ref[0, x]) + nn(h_ref[1], swap_ref[1, x])
        out_ref[x] = term.astype(BF)


def total_kernel(in_ref, out_ref):
    experts = out_ref.shape[0]
    width = in_ref.shape[2]
    for s in range(CAP):
        rows = slice(s * experts, (s + 1) * experts)
        total = in_ref[0, rows].astype(F32)
        for x in range(1, in_ref.shape[0]):
            total += in_ref[x, rows].astype(F32)
        out_ref[:, s * width : (s + 1) * width] = total.astype(BF)


def pair_kernel(a_ref, b_ref, o_ref):
    o_ref[...] = (a_ref[...].astype(F32) + b_ref[...].astype(F32)).astype(BF)


def adapter_kernel(ids_ref, v0_ref, v1_ref, v2_ref, v3_ref, s_ref, o_ref, code_ref):
    code_ref[...] = code_of(ids_ref[...], code_ref.shape[0])
    low = v0_ref[...].astype(F32) + v1_ref[...].astype(F32)
    low += v2_ref[...].astype(F32) + v3_ref[...].astype(F32)
    o_ref[...] = tn(low.astype(BF), s_ref[...])


def combine_kernel(code_ref, r_ref, o_ref):
    width = o_ref.shape[1]
    total = jnp.zeros(o_ref.shape, F32)
    for s in range(CAP):
        pick = jnp.where(code_ref[...] == float(s), 1.0, 0.0).astype(BF)
        total += tn(pick, r_ref[:, s * width : (s + 1) * width])
    o_ref[...] = total.astype(BF)


def call(body, outs, *args, scalars=0, places=(), ends=(), scratch=()):
    vmem = pl.BlockSpec(memory_space=pltpu.VMEM)
    smem = pl.BlockSpec(memory_space=pltpu.SMEM)
    places = places or [vmem] * (len(args) - scalars)
    return pl.pallas_call(
        body,
        out_shape=outs,
        in_specs=[smem] * scalars + list(places),
        out_specs=ends or jax.tree.map(lambda _: vmem, outs),
        scratch_shapes=list(scratch),
        compiler_params=PARAMS,
    )(*args)


def per_device(tokens, grad_out, prob, ids, w_gate, w_up, w_down, adapter_a, adapter_b):
    experts = lax.axis_size(("z", "y"))
    chips = lax.axis_size("x")
    count, width = tokens.shape
    rank = adapter_b.shape[1]
    units = w_gate.shape[1]
    routes = experts * CAP
    w_gate, w_up, w_down, adapter_a, adapter_b = (
        w_gate[0], w_up[0], w_down[0], adapter_a[0], adapter_b[0],
    )
    sds = jax.ShapeDtypeStruct
    me = jnp.stack([lax.axis_index("x"), lax.axis_index("c")]).astype(jnp.int32)

    def swap(block):
        return lax.ppermute(block, "c", [(0, 1), (1, 0)])

    def shift(block, by):
        return lax.ppermute(block, "x", [(i, (i + by) % chips) for i in range(chips)])

    def over_x(block):
        return lax.all_to_all(block, "x", 0, 0, tiled=True)

    def route(block):
        return lax.all_to_all(block, ("z", "y"), 0, 0, tiled=True)

    parts = 2 * width // LANE
    slow = pl.BlockSpec(memory_space=pltpu.HBM)

    def pin(*arrays):
        return [pltpu.with_memory_space_constraint(x, pltpu.HBM) for x in arrays]

    near = pl.BlockSpec(memory_space=pltpu.VMEM)
    far = pl.BlockSpec(memory_space=pltpu.HBM)
    dma = pltpu.SemaphoreType.DMA

    packed = call(
        pack_kernel, sds((experts * parts, CAP * LANE), BF),
        *pin(ids.T, prob.T, tokens, grad_out),
        places=[slow] * 4,
        scratch=[
            pltpu.VMEM(ids.T.shape, ids.dtype), pltpu.VMEM(prob.T.shape, F32),
            pltpu.VMEM(tokens.shape, BF), pltpu.VMEM(tokens.shape, BF), dma((4,)),
        ],
    )
    arrived = route(packed.reshape(experts, parts, CAP * LANE))

    half, *down = call(
        prep_kernel,
        (sds((2, chips, units, width), BF),) + (sds((units, 2 * width), BF),) * 4,
        me, w_gate, w_up, w_down, scalars=1,
    )
    half = swap(half)
    down = down[:1] + [shift(block, d + 1) for d, block in enumerate(down[1:])]
    b_other = swap(adapter_b)
    arrived, half, b_other, *down = lax.optimization_barrier((arrived, half, b_other, *down))

    x_four, s_own = call(
        split_kernel, (pltpu.HBM((chips, routes, width), BF), pltpu.HBM((routes, width), BF)),
        arrived.reshape(experts * parts, CAP * LANE),
        ends=(far, far),
        scratch=[pltpu.VMEM((routes, width), BF)] * 2 + [dma((chips + 1,))],
    )
    x_all = over_x(x_four)
    s_other = swap(s_own)
    share = sds((routes, units + rank), BF)
    sources = (s_own, s_other, adapter_b, b_other, *down)
    part, *sent = call(
        part_kernel, (share,) * chips, me, *pin(*sources), scalars=1, places=[slow] * len(sources),
        scratch=[pltpu.VMEM(x.shape, BF) for x in sources] + [dma((len(sources),))],
    )
    sent = [shift(block, chips - 1 - d) for d, block in enumerate(sent)]
    keep, send = call(
        gate_kernel,
        (sds((2, routes, units), F32), sds((2, routes, units), BF)),
        me, x_all, w_gate, w_up, half, *sent, scalars=1,
        places=[near] * 4 + [pl.BlockSpec(memory_space=pl.ANY)] * len(sent),
    )
    got = swap(send)
    grads, grad_a, v_own = call(
        grad_kernel,
        (sds((2, routes, units), BF), sds((rank, units), F32), sds((routes, rank), BF)),
        keep, got, part, *sent, adapter_a,
    )
    grads_other = swap(grads)
    back = call(
        back_kernel, sds((chips, routes, width), BF),
        me, grads, grads_other, w_gate, w_up, half, scalars=1,
    )
    backs = over_x(back)
    total = call(total_kernel, sds((experts, CAP * width), BF), backs)
    home = route(total.reshape(experts, 2, CAP * width // 2)).reshape(experts, CAP * width)

    v_pair = call(pair_kernel, sds((routes, rank), BF), v_own, swap(v_own))
    v_all = [v_pair] + [shift(v_pair, d) for d in (1, 2, 3)]
    grad_b, code = call(
        adapter_kernel, (sds((rank, width), F32), sds((experts, count), F32)), ids.T, *v_all, s_own
    )
    out = call(combine_kernel, sds(tokens.shape, BF), code, home)
    return out, grad_a[None], grad_b[None]


def solution(mesh):
    fine = Mesh(mesh.devices.reshape(4, 2, 16, 4), ("x", "c", "z", "y"))
    dp, ex = ("x", "c"), ("z", "y")
    specs = (
        P(ex, dp), P(ex, dp), P(ex, None), P(ex, None),
        P(ex, dp, None), P(ex, dp, None), P(ex, dp, None), P(ex, None, dp), P(ex, None, dp),
    )
    return jax.shard_map(
        per_device,
        mesh=fine,
        in_specs=specs,
        out_specs=(P(ex, dp), P(ex, None, dp), P(ex, None, dp)),
        check_vma=False,
    )
```

time: 180 us -> 168 us (0.933)
  local copies, waits for them, and re-layouts: 26.9 us -> 10.8 us
  starting transfers between devices: 67.5 us -> 77 us
  other arithmetic: 2.74 us -> 0.08 us
  blocking collectives: 22.8 us -> 20.9 us
    ppermute x6 -> x9, waiting for transfers between devices: 3.6 us -> 21.9 us  [shift(): lax.ppermute(block, 'x', [(i, (i + by) % chips) for i in range(chips)])]
    unnamed x52 -> x49, local copies, waits for them, and re-layouts: 26.3 us -> 9.99 us
    all_to_all x2, waiting for transfers between devices: 25.6 us -> 11.3 us  [route(): return lax.all_to_all(block, ('z', 'y'), 0, 0, tiled=True)]
    ppermute x6 -> x9, starting transfers between devices: 20.6 us -> 31.2 us  [shift(): lax.ppermute(block, 'x', [(i, (i + by) % chips) for i in range(chips)])]
    all_to_all x2 -> x1, waiting for transfers between devices: 6.87 us -> 0.01 us  [over_x(): return lax.all_to_all(block, 'x', 0, 0, tiled=True)]
    all_to_all x2 -> x1, starting transfers between devices: 8.45 us -> 4.44 us  [over_x(): return lax.all_to_all(block, 'x', 0, 0, tiled=True)]
    all_to_all x2, starting transfers between devices: 26.8 us -> 29.5 us  [route(): return lax.all_to_all(block, ('z', 'y'), 0, 0, tiled=True)]
    all_to_all x2 -> x0, other arithmetic: 2.67 us -> none  [route(): return lax.all_to_all(block, ('z', 'y'), 0, 0, tiled=True)]
  transfers between devices with their start and end apart: 16 -> 18, of which waited for: 9 -> 15; matrix products, arithmetic and copies ran while one was open for 4% -> 0% of each run, Pallas kernels for 5% -> 3%
where the time goes in v3:
time: 168 us; the launch traced here: 167 us
  starting transfers between devices  77 us (46%)
  waiting for transfers between devices  40.4 us (24%)
  blocking collectives  20.9 us (12%)
  Pallas kernels  16.5 us (10%)
  local copies, waits for them, and re-layouts  10.8 us (6%)
    ppermute x9, starting transfers between devices, shift(): lax.ppermute(block, 'x', [(i, (i + by) % chips) for i in range(chips)])  31.2 us
    all_to_all x2, starting transfers between devices, route(): return lax.all_to_all(block, ('z', 'y'), 0, 0, tiled=True)  29.5 us
    ppermute x9, waiting for transfers between devices, shift(): lax.ppermute(block, 'x', [(i, (i + by) % chips) for i in range(chips)])  21.9 us
    all_to_all x1, blocking collectives, over_x(): return lax.all_to_all(block, 'x', 0, 0, tiled=True)  20.9 us
    pallas_call x11, Pallas kernels, call(): pl.pallas_call(body, out_shape=outs, in_specs=[smem] * scalars + list(pla...  16.5 us
    ppermute x6, starting transfers between devices, swap(): return lax.ppermute(block, 'c', [(0, 1), (1, 0)])  11.9 us
    all_to_all x2, waiting for transfers between devices, route(): return lax.all_to_all(block, ('z', 'y'), 0, 0, tiled=True)  11.3 us
    unnamed x49, local copies, waits for them, and re-layouts  9.99 us
  transfers between devices with their start and end apart: 18, of which 15 were waited for; matrix products, arithmetic and copies ran while one was open for 0% of the time, Pallas kernels for 3%

profile of v3, /device:TPU:8, one launch (start us, length us, event | category | flops | bytes accessed | tf_op | source)
XLA Modules:
  0.0 166.7 jit_solution(14075369301047610798)
XLA Ops:
  0.6 3.0 %shard_map.112 = bf16[512,640]{1,0:T(8,128)(2,1)} custom-call(s32[8,32]{1,0:T(8,128)} %bitcast.25, f32[8,32]{1,0:T(8,128)} %bitcast.30, bf16[32,512]{1,0:T(8,128)(2,1)} %tok_hbm.1, bf16[32,512]{1,0:T(8,128)(2,1)} %dy_hbm.1), custom_call_target="tpu_custom_call" | custom-call | tf_op jit(solution)/shard_map/pallas_call | solution.py:213
  3.6 18.7 %all-to-all-start = ((bf16[64,8,640]{2,1,0:T(8,128)(2,1)}), bf16[64,8,640]{2,1,0:T(8,128)(2,1)S(1)}, u32[]{:S(2)}, u32[]{:S(2)}) async-start(bf16[64,8,640]{2,1,0:T(8,128)(2,1)} %bitcast.4), calls=%async_computation | async-start | bytes 1310720 | tf_op jit(solution)/shard_map/all_to_all | solution.py:246
  22.4 0.1 pad_add_fusion.me_ref
  22.5 1.4 copy-done.1
  23.9 1.4 copy-done.6
  25.3 0.8 shard_map.113
  26.1 0.7 copy-done.11
  26.8 1.9 %collective-permute-start = (bf16[2,4,192,512]{3,2,1,0:T(8,128)(2,1)S(1)}, bf16[2,4,192,512]{3,2,1,0:T(8,128)(2,1)S(1)}, u32[]{:S(2)}, u32[]{:S(2)}) collective-permute-start(bf16[2,4,192,512]{3,2,1,0:T(8,128)(2,1)S(1)} %get-tuple-element.28), channel_id=1, source_target_pairs={{0,64},{64,0},{1,65},{65,1},{2,66},{66,2},{3,67},{67,3},{4,68},{68... | collective-permute-start | bytes 4718600 | tf_op jit(solution)/shard_map/ppermute | solution.py:237
  28.7 3.4 %collective-permute-start.2 = (bf16[192,1024]{1,0:T(8,128)(2,1)S(1)}, bf16[192,1024]{1,0:T(8,128)(2,1)S(1)}, u32[]{:S(2)}, u32[]{:S(2)}) collective-permute-start(bf16[192,1024]{1,0:T(8,128)(2,1)S(1)} %get-tuple-element.30), channel_id=1, source_target_pairs={{0,128},{128,256},{256,384},{384,0},{1,129},{129,257},{257,385},{3... | collective-permute-start | bytes 1179656 | tf_op jit(solution)/shard_map/ppermute | solution.py:240
  32.1 4.6 %collective-permute-start.3 = (bf16[192,1024]{1,0:T(8,128)(2,1)S(1)}, bf16[192,1024]{1,0:T(8,128)(2,1)S(1)}, u32[]{:S(2)}, u32[]{:S(2)}) collective-permute-start(bf16[192,1024]{1,0:T(8,128)(2,1)S(1)} %get-tuple-element.31), channel_id=1, source_target_pairs={{0,256},{128,384},{256,0},{384,128},{1,257},{129,385},{257,1},{385... | collective-permute-start | bytes 1179656 | tf_op jit(solution)/shard_map/ppermute | solution.py:240
  36.8 3.3 %collective-permute-start.4 = (bf16[192,1024]{1,0:T(8,128)(2,1)S(1)}, bf16[192,1024]{1,0:T(8,128)(2,1)S(1)}, u32[]{:S(2)}, u32[]{:S(2)}) collective-permute-start(bf16[192,1024]{1,0:T(8,128)(2,1)S(1)} %get-tuple-element.32), channel_id=1, source_target_pairs={{0,384},{128,0},{256,128},{384,256},{1,385},{129,1},{257,129},{385... | collective-permute-start | bytes 1179656 | tf_op jit(solution)/shard_map/ppermute | solution.py:240
  40.1 1.9 %collective-permute-start.1 = (bf16[64,512]{1,0:T(8,128)(2,1)S(1)}, bf16[64,512]{1,0:T(8,128)(2,1)S(1)}, u32[]{:S(2)}, u32[]{:S(2)}) collective-permute-start(bf16[64,512]{1,0:T(8,128)(2,1)S(1)} %bitcast.29), channel_id=1, source_target_pairs={{0,64},{64,0},{1,65},{65,1},{2,66},{66,2},{3,67},{67,3},{4,68},{68... | collective-permute-start | bytes 196616 | tf_op jit(solution)/shard_map/ppermute | solution.py:237
  42.1 1.2 collective-permute-done.1.refs_3_
  43.3 0.1 collective-permute-done.2.refs_5_
  43.3 9.4 %collective-permute-done.3.refs_6_ = bf16[192,1024]{1,0:T(8,128)(2,1)S(1)} collective-permute-done((bf16[192,1024]{1,0:T(8,128)(2,1)S(1)}, bf16[192,1024]{1,0:T(8,128)(2,1)S(1)}, u32[]{:S(2)}, u32[]{:S(2)}) %collective-permute-start.3) | collective-permute-done | bytes 393248 | tf_op jit(solution)/shard_map/ppermute | solution.py:240
  52.8 1.5 collective-permute-done.4.refs_7_
  54.3 0.0 copy-done.18
  54.3 0.8 copy-done.20
  55.1 0.0 collective-permute-done.swap_ref
  55.1 1.2 copy-done.3
  56.3 4.4 %all-to-all-done = bf16[64,8,640]{2,1,0:T(8,128)(2,1)S(1)} async-done(((bf16[64,8,640]{2,1,0:T(8,128)(2,1)}), bf16[64,8,640]{2,1,0:T(8,128)(2,1)S(1)}, u32[]{:S(2)}, u32[]{:S(2)}) %all-to-all-start) | async-done | bytes 655392 | tf_op jit(solution)/shard_map/all_to_all | solution.py:246
  60.7 0.0 copy-done.23
  60.7 1.7 %shard_map.114 = (bf16[4,320,512]{2,1,0:T(8,128)(2,1)}, bf16[320,512]{1,0:T(8,128)(2,1)}) custom-call(bf16[512,640]{1,0:T(8,128)(2,1)S(1)} %bitcast.21), custom_call_target="tpu_custom_call" | custom-call | tf_op jit(solution)/shard_map/pallas_call | solution.py:213
  62.4 4.4 %all-to-all-start.1 = ((bf16[4,320,512]{2,1,0:T(8,128)(2,1)}), bf16[4,320,512]{2,1,0:T(8,128)(2,1)}, u32[]{:S(2)}, u32[]{:S(2)}) async-start(bf16[4,320,512]{2,1,0:T(8,128)(2,1)} %get-tuple-element.34), calls=%async_computation.1 | async-start | bytes 2621440 | tf_op jit(solution)/shard_map/all_to_all | solution.py:243
  66.9 0.0 copy-start.2
  66.9 2.1 %collective-permute-start.5 = (bf16[320,512]{1,0:T(8,128)(2,1)S(1)}, bf16[320,512]{1,0:T(8,128)(2,1)S(1)}, u32[]{:S(2)}, u32[]{:S(2)}) collective-permute-start(bf16[320,512]{1,0:T(8,128)(2,1)S(1)} %copy-done.7), channel_id=1, source_target_pairs={{0,64},{64,0},{1,65},{65,1},{2,66},{66,2},{3,67},{67,3},{4,68},{68... | collective-permute-start | bytes 983048 | tf_op jit(solution)/shard_map/ppermute | solution.py:237
  69.0 1.6 collective-permute-done.5.refs_1_
  70.6 0.7 copy-done.21
  71.3 3.2 %shard_map.115 = (bf16[320,256]{1,0:T(8,128)(2,1)S(1)}, bf16[320,256]{1,0:T(8,128)(2,1)S(1)}, bf16[320,256]{1,0:T(8,128)(2,1)S(1)}, bf16[320,256]{1,0:T(8,128)(2,1)S(1)}) custom-call(s32[2]{0:T(128)S(1)} %pad_add_fusion.me_ref, bf16[320,512]{1,0:T(8,128)(2,1)} %get-tuple-element.36.refs_0_.s_ref, bf16[320,512]{1,0:T(8,128)(2,1)} %copy-done.21, ...), custom_call_target="tpu_custom_call" | custom-call | tf_op jit(solution)/shard_map/pallas_call | solution.py:213
  74.5 0.7 copy-done.12
  75.2 5.1 %collective-permute-start.6 = (bf16[320,256]{1,0:T(8,128)(2,1)S(1)}, bf16[320,256]{1,0:T(8,128)(2,1)S(1)}, u32[]{:S(2)}, u32[]{:S(2)}) collective-permute-start(bf16[320,256]{1,0:T(8,128)(2,1)S(1)} %get-tuple-element.42), channel_id=1, source_target_pairs={{0,384},{128,0},{256,128},{384,256},{1,385},{129,1},{257,129},{385... | collective-permute-start | bytes 491528 | tf_op jit(solution)/shard_map/ppermute | solution.py:240
  80.3 2.8 %collective-permute-start.7 = (bf16[320,256]{1,0:T(8,128)(2,1)S(1)}, bf16[320,256]{1,0:T(8,128)(2,1)S(1)}, u32[]{:S(2)}, u32[]{:S(2)}) collective-permute-start(bf16[320,256]{1,0:T(8,128)(2,1)S(1)} %get-tuple-element.43), channel_id=1, source_target_pairs={{0,256},{128,384},{256,0},{384,128},{1,257},{129,385},{257,1},{385... | collective-permute-start | bytes 491528 | tf_op jit(solution)/shard_map/ppermute | solution.py:240
  83.0 2.8 %collective-permute-start.8 = (bf16[320,256]{1,0:T(8,128)(2,1)S(1)}, bf16[320,256]{1,0:T(8,128)(2,1)S(1)}, u32[]{:S(2)}, u32[]{:S(2)}) collective-permute-start(bf16[320,256]{1,0:T(8,128)(2,1)S(1)} %get-tuple-element.44), channel_id=1, source_target_pairs={{0,128},{128,256},{256,384},{384,0},{1,129},{129,257},{257,385},{3... | collective-permute-start | bytes 491528 | tf_op jit(solution)/shard_map/ppermute | solution.py:240
  85.8 2.0 %collective-permute-done.6.refs_0_.p1_ref = bf16[320,256]{1,0:T(8,128)(2,1)S(1)} collective-permute-done((bf16[320,256]{1,0:T(8,128)(2,1)S(1)}, bf16[320,256]{1,0:T(8,128)(2,1)S(1)}, u32[]{:S(2)}, u32[]{:S(2)}) %collective-permute-start.6) | collective-permute-done | bytes 163872 | tf_op jit(solution)/shard_map/ppermute | solution.py:240
  87.8 3.0 %collective-permute-done.7.refs_1_.p2_ref = bf16[320,256]{1,0:T(8,128)(2,1)S(1)} collective-permute-done((bf16[320,256]{1,0:T(8,128)(2,1)S(1)}, bf16[320,256]{1,0:T(8,128)(2,1)S(1)}, u32[]{:S(2)}, u32[]{:S(2)}) %collective-permute-start.7) | collective-permute-done | bytes 163872 | tf_op jit(solution)/shard_map/ppermute | solution.py:240
  90.8 2.4 %collective-permute-done.8.refs_2_.p3_ref = bf16[320,256]{1,0:T(8,128)(2,1)S(1)} collective-permute-done((bf16[320,256]{1,0:T(8,128)(2,1)S(1)}, bf16[320,256]{1,0:T(8,128)(2,1)S(1)}, u32[]{:S(2)}, u32[]{:S(2)}) %collective-permute-start.8) | collective-permute-done | bytes 163872 | tf_op jit(solution)/shard_map/ppermute | solution.py:240
  93.1 0.7 copy-done.9
  93.8 0.0 all-to-all-done.1.x_ref
  93.8 0.0 copy-done.16
  93.8 1.4 copy-done.4
  95.2 0.9 copy-done.10
  96.2 2.9 %shard_map.116 = (f32[2,320,192]{2,1,0:T(8,128)S(1)}, bf16[2,320,192]{2,1,0:T(8,128)(2,1)S(1)}) custom-call(s32[2]{0:T(128)S(1)} %pad_add_fusion.me_ref, bf16[4,320,512]{2,1,0:T(8,128)(2,1)} %all-to-all-done.1.x_ref, bf16[192,4096]{1,0:T(8,128)(2,1)S(1)} %bitcast.16, bf16[192,4096]{1,0:T(8,128)(2,1)S(1)} %bitcast.19, bf16[2,4,192,512]{3,2,1,0:T(8,128)(2,1)S(1)} %copy-done.4, ...), custom_call_target="tpu_custom_call" | custom-call | tf_op jit(solution)/shard_map/pallas_call | solution.py:213
  99.1 0.0 copy-start.17
  99.1 2.1 %collective-permute-start.9 = (bf16[2,320,192]{2,1,0:T(8,128)(2,1)S(1)}, bf16[2,320,192]{2,1,0:T(8,128)(2,1)S(1)}, u32[]{:S(2)}, u32[]{:S(2)}) collective-permute-start(bf16[2,320,192]{2,1,0:T(8,128)(2,1)S(1)} %get-tuple-element.46), channel_id=1, source_target_pairs={{0,64},{64,0},{1,65},{65,1},{2,66},{66,2},{3,67},{67,3},{4,68},{68... | collective-permute-start | bytes 737288 | tf_op jit(solution)/shard_map/ppermute | solution.py:237
  101.1 1.6 collective-permute-done.9.got_ref
  102.7 1.0 shard_map.117
  103.7 2.0 %collective-permute-start.14 = (bf16[2,320,192]{2,1,0:T(8,128)(2,1)S(1)}, bf16[2,320,192]{2,1,0:T(8,128)(2,1)S(1)}, u32[]{:S(2)}, u32[]{:S(2)}) collective-permute-start(bf16[2,320,192]{2,1,0:T(8,128)(2,1)S(1)} %get-tuple-element.50.g_ref), channel_id=1, source_target_pairs={{0,64},{64,0},{1,65},{65,1},{2,66},{66,2},{3,67},{67,3},{4,68},{68... | collective-permute-start | bytes 737288 | tf_op jit(solution)/shard_map/ppermute | solution.py:237
  105.8 1.5 collective-permute-done.14.h_ref
  107.3 2.0 %shard_map.120 = bf16[4,320,512]{2,1,0:T(8,128)(2,1)S(1)} custom-call(s32[2]{0:T(128)S(1)} %copy-done.17, bf16[2,320,192]{2,1,0:T(8,128)(2,1)S(1)} %get-tuple-element.50.g_ref, bf16[2,320,192]{2,1,0:T(8,128)(2,1)S(1)} %collective-permute-done.14.h_ref, bf16[192,4096]{1,0:T(8,128)(2,1)S(1)} %bitcast.17, bf16[192,4096]{1,0:T(8,128)(2,1)S(1)} %bitcast.20, ...), custom_call_target="tpu_custom_call" | custom-call | tf_op jit(solution)/shard_map/pallas_call | solution.py:213
  109.3 20.9 %all_to_all.20.in_ref = bf16[4,320,512]{2,1,0:T(8,128)(2,1)S(1)} all-to-all(bf16[4,320,512]{2,1,0:T(8,128)(2,1)S(1)} %shard_map.120), channel_id=1, replica_groups=mesh['x'=4,'c'=2,'z'=16,'y'=4] {'x'}, dimensions={0} | all-to-all | bytes 2621440 | tf_op jit(solution)/shard_map/all_to_all | solution.py:243
  130.3 0.2 shard_map.121
  130.4 0.8 reshape.20
  131.2 10.8 %all-to-all-start.3 = ((bf16[64,2,1280]{2,1,0:T(2,128)(2,1)}), bf16[64,2,1280]{2,1,0:T(2,128)(2,1)S(1)}, u32[]{:S(2)}, u32[]{:S(2)}) async-start(bf16[64,2,1280]{2,1,0:T(2,128)(2,1)} %reshape.20), calls=%async_computation.3 | async-start | bytes 655360 | tf_op jit(solution)/shard_map/all_to_all | solution.py:246
  142.0 1.9 %collective-permute-start.10 = (bf16[320,64]{1,0:T(8,128)(2,1)S(1)}, bf16[320,64]{1,0:T(8,128)(2,1)S(1)}, u32[]{:S(2)}, u32[]{:S(2)}) collective-permute-start(bf16[320,64]{1,0:T(8,128)(2,1)S(1)} %get-tuple-element.48.a_ref), channel_id=1, source_target_pairs={{0,64},{64,0},{1,65},{65,1},{2,66},{66,2},{3,67},{67,3},{4,68},{68... | collective-permute-start | bytes 122888 | tf_op jit(solution)/shard_map/ppermute | solution.py:237
  143.9 1.2 collective-permute-done.10.b_ref
  145.2 2.5 %collective-permute-start.11 = (bf16[320,64]{1,0:T(8,128)(2,1)S(1)}, bf16[320,64]{1,0:T(8,128)(2,1)S(1)}, u32[]{:S(2)}, u32[]{:S(2)}) collective-permute-start(bf16[320,64]{1,0:T(8,128)(2,1)S(1)} %shard_map.118.v0_ref), channel_id=1, source_target_pairs={{0,128},{128,256},{256,384},{384,0},{1,129},{129,257},{257,385},{3... | collective-permute-start | bytes 122888 | tf_op jit(solution)/shard_map/ppermute | solution.py:240
  147.7 4.0 %collective-permute-start.12 = (bf16[320,64]{1,0:T(8,128)(2,1)S(1)}, bf16[320,64]{1,0:T(8,128)(2,1)S(1)}, u32[]{:S(2)}, u32[]{:S(2)}) collective-permute-start(bf16[320,64]{1,0:T(8,128)(2,1)S(1)} %shard_map.118.v0_ref), channel_id=1, source_target_pairs={{0,256},{128,384},{256,0},{384,128},{1,257},{129,385},{257,1},{385... | collective-permute-start | bytes 122888 | tf_op jit(solution)/shard_map/ppermute | solution.py:240
  151.7 2.7 %collective-permute-start.13 = (bf16[320,64]{1,0:T(8,128)(2,1)S(1)}, bf16[320,64]{1,0:T(8,128)(2,1)S(1)}, u32[]{:S(2)}, u32[]{:S(2)}) collective-permute-start(bf16[320,64]{1,0:T(8,128)(2,1)S(1)} %shard_map.118.v0_ref), channel_id=1, source_target_pairs={{0,384},{128,0},{256,128},{384,256},{1,385},{129,1},{257,129},{385... | collective-permute-start | bytes 122888 | tf_op jit(solution)/shard_map/ppermute | solution.py:240
  154.4 0.0 collective-permute-done.11.v1_ref
  154.4 1.1 collective-permute-done.12.v2_ref
  155.5 2.5 %collective-permute-done.13.v3_ref = bf16[320,64]{1,0:T(8,128)(2,1)S(1)} collective-permute-done((bf16[320,64]{1,0:T(8,128)(2,1)S(1)}, bf16[320,64]{1,0:T(8,128)(2,1)S(1)}, u32[]{:S(2)}, u32[]{:S(2)}) %collective-permute-start.13) | collective-permute-done | bytes 40992 | tf_op jit(solution)/shard_map/ppermute | solution.py:240
  158.0 0.9 shard_map.119
  158.9 6.9 %all-to-all-done.3 = bf16[64,2,1280]{2,1,0:T(2,128)(2,1)S(1)} async-done(((bf16[64,2,1280]{2,1,0:T(2,128)(2,1)}), bf16[64,2,1280]{2,1,0:T(2,128)(2,1)S(1)}, u32[]{:S(2)}, u32[]{:S(2)}) %all-to-all-start.3) | async-done | bytes 327712 | tf_op jit(solution)/shard_map/all_to_all | solution.py:246
  165.9 0.8 shard_map.122
  (35 shorter events, 0.1 us)
Async XLA Ops:
  0.6 21.8 %copy-start = (bf16[1,192,4096]{2,1,0:T(8,128)(2,1)S(1)}, bf16[1,192,4096]{2,1,0:T(8,128)(2,1)}, u32[]{:S(2)}) copy-start(bf16[1,192,4096]{2,1,0:T(8,128)(2,1)} %param.13) | copy-start | bytes 4718596
  3.6 57.1 %all-to-all-start = ((bf16[64,8,640]{2,1,0:T(8,128)(2,1)}), bf16[64,8,640]{2,1,0:T(8,128)(2,1)S(1)}, u32[]{:S(2)}, u32[]{:S(2)}) async-start(bf16[64,8,640]{2,1,0:T(8,128)(2,1)} %bitcast.4), calls=%async_computation | async-start | bytes 1310720 | tf_op jit(solution)/shard_map/all_to_all | solution.py:246
  22.5 71.4 %copy-start.16 = (s32[2]{0:T(128)}, s32[2]{0:T(128)S(1)}, u32[]{:S(2)}) copy-start(s32[2]{0:T(128)S(1)} %pad_add_fusion.me_ref) | copy-start | bytes 28
  22.5 1.4 copy-start.1
  23.9 1.4 copy-start.6
  25.3 14.8 %copy-start.22 = (bf16[1,64,512]{2,1,0:T(8,128)(2,1)S(1)}, bf16[1,64,512]{2,1,0:T(8,128)(2,1)}, u32[]{:S(2)}) copy-start(bf16[1,64,512]{2,1,0:T(8,128)(2,1)} %param.17) | copy-start | bytes 196612
  26.1 0.8 copy-start.11
  26.8 28.3 %collective-permute-start = (bf16[2,4,192,512]{3,2,1,0:T(8,128)(2,1)S(1)}, bf16[2,4,192,512]{3,2,1,0:T(8,128)(2,1)S(1)}, u32[]{:S(2)}, u32[]{:S(2)}) collective-permute-start(bf16[2,4,192,512]{3,2,1,0:T(8,128)(2,1)S(1)} %get-tuple-element.28), channel_id=1, source_target_pairs={{0,64},{64,0},{1,65},{65,1},{2,66},{66,2},{3,67},{67,3},{4,68},{68... | collective-permute-start | bytes 4718600 | tf_op jit(solution)/shard_map/ppermute | solution.py:237
  28.7 14.6 %collective-permute-start.2 = (bf16[192,1024]{1,0:T(8,128)(2,1)S(1)}, bf16[192,1024]{1,0:T(8,128)(2,1)S(1)}, u32[]{:S(2)}, u32[]{:S(2)}) collective-permute-start(bf16[192,1024]{1,0:T(8,128)(2,1)S(1)} %get-tuple-element.30), channel_id=1, source_target_pairs={{0,128},{128,256},{256,384},{384,0},{1,129},{129,257},{257,385},{3... | collective-permute-start | bytes 1179656 | tf_op jit(solution)/shard_map/ppermute | solution.py:240
  32.1 20.6 %collective-permute-start.3 = (bf16[192,1024]{1,0:T(8,128)(2,1)S(1)}, bf16[192,1024]{1,0:T(8,128)(2,1)S(1)}, u32[]{:S(2)}, u32[]{:S(2)}) collective-permute-start(bf16[192,1024]{1,0:T(8,128)(2,1)S(1)} %get-tuple-element.31), channel_id=1, source_target_pairs={{0,256},{128,384},{256,0},{384,128},{1,257},{129,385},{257,1},{385... | collective-permute-start | bytes 1179656 | tf_op jit(solution)/shard_map/ppermute | solution.py:240
  36.8 17.5 %collective-permute-start.4 = (bf16[192,1024]{1,0:T(8,128)(2,1)S(1)}, bf16[192,1024]{1,0:T(8,128)(2,1)S(1)}, u32[]{:S(2)}, u32[]{:S(2)}) collective-permute-start(bf16[192,1024]{1,0:T(8,128)(2,1)S(1)} %get-tuple-element.32), channel_id=1, source_target_pairs={{0,384},{128,0},{256,128},{384,256},{1,385},{129,1},{257,129},{385... | collective-permute-start | bytes 1179656 | tf_op jit(solution)/shard_map/ppermute | solution.py:240
  40.1 3.1 %collective-permute-start.1 = (bf16[64,512]{1,0:T(8,128)(2,1)S(1)}, bf16[64,512]{1,0:T(8,128)(2,1)S(1)}, u32[]{:S(2)}, u32[]{:S(2)}) collective-permute-start(bf16[64,512]{1,0:T(8,128)(2,1)S(1)} %bitcast.29), channel_id=1, source_target_pairs={{0,64},{64,0},{1,65},{65,1},{2,66},{66,2},{3,67},{67,3},{4,68},{68... | collective-permute-start | bytes 196616 | tf_op jit(solution)/shard_map/ppermute | solution.py:237
  43.3 17.4 %copy-start.23 = (bf16[64,512]{1,0:T(8,128)(2,1)}, bf16[64,512]{1,0:T(8,128)(2,1)S(1)}, u32[]{:S(2)}) copy-start(bf16[64,512]{1,0:T(8,128)(2,1)S(1)} %collective-permute-done.1.refs_3_) | copy-start | bytes 196612
  43.3 11.0 %copy-start.18 = (bf16[192,1024]{1,0:T(8,128)(2,1)}, bf16[192,1024]{1,0:T(8,128)(2,1)S(1)}, u32[]{:S(2)}) copy-start(bf16[192,1024]{1,0:T(8,128)(2,1)S(1)} %collective-permute-done.2.refs_5_) | copy-start | bytes 1179652
  52.8 1.6 copy-start.19
  54.3 0.8 copy-start.20
  55.1 1.2 copy-start.3
  62.4 4.5 %copy-start.7 = (bf16[320,512]{1,0:T(8,128)(2,1)S(1)}, bf16[320,512]{1,0:T(8,128)(2,1)}, u32[]{:S(2)}) copy-start(bf16[320,512]{1,0:T(8,128)(2,1)} %get-tuple-element.36.refs_0_.s_ref) | copy-start | bytes 983044
  62.4 31.4 %all-to-all-start.1 = ((bf16[4,320,512]{2,1,0:T(8,128)(2,1)}), bf16[4,320,512]{2,1,0:T(8,128)(2,1)}, u32[]{:S(2)}, u32[]{:S(2)}) async-start(bf16[4,320,512]{2,1,0:T(8,128)(2,1)} %get-tuple-element.34), calls=%async_computation.1 | async-start | bytes 2621440 | tf_op jit(solution)/shard_map/all_to_all | solution.py:243
  66.9 26.9 %copy-start.2 = (bf16[1,192,4096]{2,1,0:T(8,128)(2,1)S(1)}, bf16[1,192,4096]{2,1,0:T(8,128)(2,1)}, u32[]{:S(2)}) copy-start(bf16[1,192,4096]{2,1,0:T(8,128)(2,1)} %param.14) | copy-start | bytes 4718596
  66.9 3.7 %collective-permute-start.5 = (bf16[320,512]{1,0:T(8,128)(2,1)S(1)}, bf16[320,512]{1,0:T(8,128)(2,1)S(1)}, u32[]{:S(2)}, u32[]{:S(2)}) collective-permute-start(bf16[320,512]{1,0:T(8,128)(2,1)S(1)} %copy-done.7), channel_id=1, source_target_pairs={{0,64},{64,0},{1,65},{65,1},{2,66},{66,2},{3,67},{67,3},{4,68},{68... | collective-permute-start | bytes 983048 | tf_op jit(solution)/shard_map/ppermute | solution.py:237
  70.6 0.7 copy-start.21
  74.5 0.7 copy-start.12
  75.2 12.6 %collective-permute-start.6 = (bf16[320,256]{1,0:T(8,128)(2,1)S(1)}, bf16[320,256]{1,0:T(8,128)(2,1)S(1)}, u32[]{:S(2)}, u32[]{:S(2)}) collective-permute-start(bf16[320,256]{1,0:T(8,128)(2,1)S(1)} %get-tuple-element.42), channel_id=1, source_target_pairs={{0,384},{128,0},{256,128},{384,256},{1,385},{129,1},{257,129},{385... | collective-permute-start | bytes 491528 | tf_op jit(solution)/shard_map/ppermute | solution.py:240
  80.3 10.5 %collective-permute-start.7 = (bf16[320,256]{1,0:T(8,128)(2,1)S(1)}, bf16[320,256]{1,0:T(8,128)(2,1)S(1)}, u32[]{:S(2)}, u32[]{:S(2)}) collective-permute-start(bf16[320,256]{1,0:T(8,128)(2,1)S(1)} %get-tuple-element.43), channel_id=1, source_target_pairs={{0,256},{128,384},{256,0},{384,128},{1,257},{129,385},{257,1},{385... | collective-permute-start | bytes 491528 | tf_op jit(solution)/shard_map/ppermute | solution.py:240
  83.0 10.1 %collective-permute-start.8 = (bf16[320,256]{1,0:T(8,128)(2,1)S(1)}, bf16[320,256]{1,0:T(8,128)(2,1)S(1)}, u32[]{:S(2)}, u32[]{:S(2)}) collective-permute-start(bf16[320,256]{1,0:T(8,128)(2,1)S(1)} %get-tuple-element.44), channel_id=1, source_target_pairs={{0,128},{128,256},{256,384},{384,0},{1,129},{129,257},{257,385},{3... | collective-permute-start | bytes 491528 | tf_op jit(solution)/shard_map/ppermute | solution.py:240
  93.1 0.7 copy-start.9
  93.8 1.4 copy-start.4
  95.2 0.9 copy-start.10
  96.2 6.6 %copy-start.13 = (bf16[320,256]{1,0:T(8,128)(2,1)S(1)}, bf16[320,256]{1,0:T(8,128)(2,1)}, u32[]{:S(2)}) copy-start(bf16[320,256]{1,0:T(8,128)(2,1)} %copy-done.12) | copy-start | bytes 491524
  96.2 6.6 %copy-start.14 = (bf16[1,64,192]{2,1,0:T(8,128)(2,1)S(1)}, bf16[1,64,192]{2,1,0:T(8,128)(2,1)}, u32[]{:S(2)}) copy-start(bf16[1,64,192]{2,1,0:T(8,128)(2,1)} %param.16) | copy-start | bytes 73732
  99.1 8.2 %copy-start.5 = (bf16[2,4,192,512]{3,2,1,0:T(8,128)(2,1)S(1)}, bf16[2,4,192,512]{3,2,1,0:T(8,128)(2,1)}, u32[]{:S(2)}) copy-start(bf16[2,4,192,512]{3,2,1,0:T(8,128)(2,1)} %copy-done.3) | copy-start | bytes 4718596
  99.1 8.2 %copy-start.17 = (s32[2]{0:T(128)S(1)}, s32[2]{0:T(128)}, u32[]{:S(2)}) copy-start(s32[2]{0:T(128)} %copy-done.16) | copy-start | bytes 28
  99.1 3.7 %collective-permute-start.9 = (bf16[2,320,192]{2,1,0:T(8,128)(2,1)S(1)}, bf16[2,320,192]{2,1,0:T(8,128)(2,1)S(1)}, u32[]{:S(2)}, u32[]{:S(2)}) collective-permute-start(bf16[2,320,192]{2,1,0:T(8,128)(2,1)S(1)} %get-tuple-element.46), channel_id=1, source_target_pairs={{0,64},{64,0},{1,65},{65,1},{2,66},{66,2},{3,67},{67,3},{4,68},{68... | collective-permute-start | bytes 737288 | tf_op jit(solution)/shard_map/ppermute | solution.py:237
  103.7 3.5 %collective-permute-start.14 = (bf16[2,320,192]{2,1,0:T(8,128)(2,1)S(1)}, bf16[2,320,192]{2,1,0:T(8,128)(2,1)S(1)}, u32[]{:S(2)}, u32[]{:S(2)}) collective-permute-start(bf16[2,320,192]{2,1,0:T(8,128)(2,1)S(1)} %get-tuple-element.50.g_ref), channel_id=1, source_target_pairs={{0,64},{64,0},{1,65},{65,1},{2,66},{66,2},{3,67},{67,3},{4,68},{68... | collective-permute-start | bytes 737288 | tf_op jit(solution)/shard_map/ppermute | solution.py:237
  130.2 27.8 %copy-start.8 = (bf16[320,512]{1,0:T(8,128)(2,1)S(1)}, bf16[320,512]{1,0:T(8,128)(2,1)}, u32[]{:S(2)}) copy-start(bf16[320,512]{1,0:T(8,128)(2,1)} %get-tuple-element.36.refs_0_.s_ref) | copy-start | bytes 983044
  130.2 27.8 %copy-start.15 = (s32[32,8]{0,1:T(8,128)S(1)}, s32[32,8]{0,1:T(8,128)}, u32[]{:S(2)}) copy-start(s32[32,8]{0,1:T(8,128)} %param.12) | copy-start | bytes 3076
  131.2 34.6 %all-to-all-start.3 = ((bf16[64,2,1280]{2,1,0:T(2,128)(2,1)}), bf16[64,2,1280]{2,1,0:T(2,128)(2,1)S(1)}, u32[]{:S(2)}, u32[]{:S(2)}) async-start(bf16[64,2,1280]{2,1,0:T(2,128)(2,1)} %reshape.20), calls=%async_computation.3 | async-start | bytes 655360 | tf_op jit(solution)/shard_map/all_to_all | solution.py:246
  142.0 3.2 %collective-permute-start.10 = (bf16[320,64]{1,0:T(8,128)(2,1)S(1)}, bf16[320,64]{1,0:T(8,128)(2,1)S(1)}, u32[]{:S(2)}, u32[]{:S(2)}) collective-permute-start(bf16[320,64]{1,0:T(8,128)(2,1)S(1)} %get-tuple-element.48.a_ref), channel_id=1, source_target_pairs={{0,64},{64,0},{1,65},{65,1},{2,66},{66,2},{3,67},{67,3},{4,68},{68... | collective-permute-start | bytes 122888 | tf_op jit(solution)/shard_map/ppermute | solution.py:237
  145.2 9.2 %collective-permute-start.11 = (bf16[320,64]{1,0:T(8,128)(2,1)S(1)}, bf16[320,64]{1,0:T(8,128)(2,1)S(1)}, u32[]{:S(2)}, u32[]{:S(2)}) collective-permute-start(bf16[320,64]{1,0:T(8,128)(2,1)S(1)} %shard_map.118.v0_ref), channel_id=1, source_target_pairs={{0,128},{128,256},{256,384},{384,0},{1,129},{129,257},{257,385},{3... | collective-permute-start | bytes 122888 | tf_op jit(solution)/shard_map/ppermute | solution.py:240
  147.7 7.8 %collective-permute-start.12 = (bf16[320,64]{1,0:T(8,128)(2,1)S(1)}, bf16[320,64]{1,0:T(8,128)(2,1)S(1)}, u32[]{:S(2)}, u32[]{:S(2)}) collective-permute-start(bf16[320,64]{1,0:T(8,128)(2,1)S(1)} %shard_map.118.v0_ref), channel_id=1, source_target_pairs={{0,256},{128,384},{256,0},{384,128},{1,257},{129,385},{257,1},{385... | collective-permute-start | bytes 122888 | tf_op jit(solution)/shard_map/ppermute | solution.py:240
  151.7 6.3 %collective-permute-start.13 = (bf16[320,64]{1,0:T(8,128)(2,1)S(1)}, bf16[320,64]{1,0:T(8,128)(2,1)S(1)}, u32[]{:S(2)}, u32[]{:S(2)}) collective-permute-start(bf16[320,64]{1,0:T(8,128)(2,1)S(1)} %shard_map.118.v0_ref), channel_id=1, source_target_pairs={{0,384},{128,0},{256,128},{384,256},{1,385},{129,1},{257,129},{385... | collective-permute-start | bytes 122888 | tf_op jit(solution)/shard_map/ppermute | solution.py:240

commit v4 on v3

--- a/solution.py
+++ b/solution.py
@@ -117,38 +117,59 @@
 
 
 def part_kernel(me_ref, *refs):
-    core = me_ref[1]
-    sources, outs, held, sems = refs[:8], refs[8:12], refs[12:20], refs[20]
+    chip, core = me_ref[0], me_ref[1]
+    sources, out_hbm, held, out_ref, sems = refs[:8], refs[8], refs[9:17], refs[17], refs[18]
     fetch(list(zip(sources, held)), sems)
     s_ref, t_ref, b_ref, o_ref = held[:4]
     units, width = held[4].shape[0], s_ref.shape[1]
+    chips = out_ref.shape[0]
     mine, other = s_ref[...], t_ref[...]
     low = (nt(mine, b_ref[...]) + nt(other, o_ref[...])).astype(BF)
-    for ref, out in zip(held[4:], outs):
+    for d, ref in enumerate(held[4:]):
         w_mine, w_other = ref[:, lanes(core, width)], ref[:, lanes(1 - core, width)]
-        out[:, :units] = (nt(mine, w_mine) + nt(other, w_other)).astype(BF)
-        out[:, units:] = low
-
-
-def gate_kernel(me_ref, x_ref, wg_ref, wu_ref, swap_ref, *refs):
-    keep_ref, send_ref = refs[-2:]
+        to = lax.rem(chip + chips - d, chips)
+        out_ref[to, :, :units] = (nt(mine, w_mine) + nt(other, w_other)).astype(BF)
+        out_ref[to, :, units:] = low
+    fetch([(out_ref, out_hbm)], sems)
+
+
+def gate_kernel(
+    me_ref, x_hbm, wg_hbm, wu_hbm, half_hbm, keep_hbm, send_ref,
+    x_ref, w_ref, half_ref, keep_ref, sems, sem,
+):
     core = me_ref[1]
     chips, routes, width = x_ref.shape
-    units = wg_ref.shape[0]
+    units = w_ref.shape[2]
+    copies = []
+    for x in range(chips):
+        cols = lanes(2 * x + core, width)
+        pairs = [
+            (x_hbm.at[x], x_ref.at[x]), (wg_hbm.at[:, cols], w_ref.at[0, x]),
+            (wu_hbm.at[:, cols], w_ref.at[1, x]), (half_hbm.at[:, x], half_ref.at[:, x]),
+        ]
+        copies.append([pltpu.make_async_copy(p, q, sems.at[x, i]) for i, (p, q) in enumerate(pairs)])
+        for copy in copies[x]:
+            copy.start()
     keep = [jnp.zeros((routes, units), F32)] * 2
     send = [jnp.zeros((routes, units), F32)] * 2
     for x in range(chips):
+        for copy in copies[x]:
+            copy.wait()
         rows = x_ref[x]
-        cols = lanes(2 * x + core, width)
-        for i, ref in enumerate((wg_ref, wu_ref)):
-            keep[i] = keep[i] + nt(rows, ref[:, cols])
-            send[i] = send[i] + nt(rows, swap_ref[i, x])
+        for i in range(2):
+            keep[i] = keep[i] + nt(rows, w_ref[i, x])
+            send[i] = send[i] + nt(rows, half_ref[i, x])
     for i in range(2):
         keep_ref[i] = keep[i]
+    fetch_out = pltpu.make_async_copy(keep_ref, keep_hbm, sem.at[0])
+    fetch_out.start()
+    for i in range(2):
         send_ref[i] = send[i].astype(BF)
-
-
-def grad_kernel(keep_ref, got_ref, p0_ref, p1_ref, p2_ref, p3_ref, a_ref, out_ref, ga_ref, v_ref):
+    fetch_out.wait()
+
+
+def grad_kernel(keep_hbm, got_hbm, in_hbm, a_hbm, out_ref, ga_ref, v_ref, keep_ref, got_ref, in_ref, a_ref, sems):
+    fetch([(keep_hbm, keep_ref), (got_hbm, got_ref), (in_hbm, in_ref), (a_hbm, a_ref)], sems)
     units = keep_ref.shape[2]
     gate = keep_ref[0] + got_ref[0].astype(F32)
     up = keep_ref[1] + got_ref[1].astype(F32)
@@ -156,8 +177,9 @@
     active = gate * sigma
     hidden = (active * up).astype(BF)
     v_ref[...] = nt(hidden, a_ref[...]).astype(BF)
-    total = p0_ref[...].astype(F32) + p1_ref[...].astype(F32)
-    total += p2_ref[...].astype(F32) + p3_ref[...].astype(F32)
+    total = in_ref[0].astype(F32)
+    for x in range(1, in_ref.shape[0]):
+        total += in_ref[x].astype(F32)
     low_u = total[:, units:].astype(BF)
     grad = total[:, :units] + nn(low_u, a_ref[...])
     ga_ref[...] = tn(low_u, hidden)
@@ -284,24 +306,30 @@
     )
     x_all = over_x(x_four)
     s_other = swap(s_own)
-    share = sds((routes, units + rank), BF)
+    shares = (chips, routes, units + rank)
     sources = (s_own, s_other, adapter_b, b_other, *down)
-    part, *sent = call(
-        part_kernel, (share,) * chips, me, *pin(*sources), scalars=1, places=[slow] * len(sources),
-        scratch=[pltpu.VMEM(x.shape, BF) for x in sources] + [dma((len(sources),))],
-    )
-    sent = [shift(block, chips - 1 - d) for d, block in enumerate(sent)]
+    part = call(
+        part_kernel, pltpu.HBM(shares, BF), me, *pin(*sources), scalars=1,
+        places=[slow] * len(sources), ends=far,
+        scratch=[pltpu.VMEM(x.shape, BF) for x in (*sources, sds(shares, BF))] + [dma((len(sources),))],
+    )
+    sums = over_x(part)
     keep, send = call(
         gate_kernel,
-        (sds((2, routes, units), F32), sds((2, routes, units), BF)),
-        me, x_all, w_gate, w_up, half, *sent, scalars=1,
-        places=[near] * 4 + [pl.BlockSpec(memory_space=pl.ANY)] * len(sent),
+        (pltpu.HBM((2, routes, units), F32), sds((2, routes, units), BF)),
+        me, *pin(x_all, w_gate, w_up, half), scalars=1, places=[slow] * 4, ends=(far, near),
+        scratch=[
+            pltpu.VMEM(x_all.shape, BF), pltpu.VMEM((2, chips, units, width), BF),
+            pltpu.VMEM(half.shape, BF), pltpu.VMEM((2, routes, units), F32), dma((chips, 4)), dma((1,)),
+        ],
     )
     got = swap(send)
+    sources = (keep, got, sums, adapter_a)
     grads, grad_a, v_own = call(
         grad_kernel,
         (sds((2, routes, units), BF), sds((rank, units), F32), sds((routes, rank), BF)),
-        keep, got, part, *sent, adapter_a,
+        *pin(*sources), places=[slow] * 4,
+        scratch=[pltpu.VMEM(x.shape, x.dtype) for x in sources] + [dma((4,))],
     )
     grads_other = swap(grads)
     back = call(

time: 168 us -> 166 us (0.988)
  starting transfers between devices: 77 us -> 70.7 us
  Pallas kernels: 16.5 us -> 20.7 us
  local copies, waits for them, and re-layouts: 10.8 us -> 8.42 us
    ppermute x9 -> x6, starting transfers between devices: 31.2 us -> 19.9 us  [shift(): lax.ppermute(block, 'x', [(i, (i + by) % chips) for i in range(chips)])]
    all_to_all x1 -> x2, waiting for transfers between devices: 0.01 us -> 9.12 us  [over_x(): return lax.all_to_all(block, 'x', 0, 0, tiled=True)]
    ppermute x9 -> x6, waiting for transfers between devices: 21.9 us -> 16.1 us  [shift(): lax.ppermute(block, 'x', [(i, (i + by) % chips) for i in range(chips)])]
    pallas_call x11, Pallas kernels: 16.5 us -> 20.7 us  [call(): pl.pallas_call(body, out_shape=outs, in_specs=[smem] * scalars + list(pla...]
    all_to_all x1 -> x2, starting transfers between devices: 4.44 us -> 8.59 us  [over_x(): return lax.all_to_all(block, 'x', 0, 0, tiled=True)]
    unnamed x49 -> x37, local copies, waits for them, and re-layouts: 9.99 us -> 7.6 us
  transfers between devices with their start and end apart: 18 -> 16, of which waited for: 15 -> 13; matrix products, arithmetic and copies ran while one was open for 0% -> 0% of each run, Pallas kernels for 3% -> 6%
where the time goes in v4:
time: 166 us; the launch traced here: 165 us
  starting transfers between devices  70.7 us (43%)
  waiting for transfers between devices  41.9 us (25%)
  blocking collectives  22.5 us (14%)
  Pallas kernels  20.7 us (12%)
  local copies, waits for them, and re-layouts  8.42 us (5%)
    all_to_all x2, starting transfers between devices, route(): return lax.all_to_all(block, ('z', 'y'), 0, 0, tiled=True)  30.5 us
    all_to_all x1, blocking collectives, over_x(): return lax.all_to_all(block, 'x', 0, 0, tiled=True)  22.5 us
    pallas_call x11, Pallas kernels, call(): pl.pallas_call(body, out_shape=outs, in_specs=[smem] * scalars + list(pla...  20.7 us
    ppermute x6, starting transfers between devices, shift(): lax.ppermute(block, 'x', [(i, (i + by) % chips) for i in range(chips)])  19.9 us
    ppermute x6, waiting for transfers between devices, shift(): lax.ppermute(block, 'x', [(i, (i + by) % chips) for i in range(chips)])  16.1 us
    ppermute x6, starting transfers between devices, swap(): return lax.ppermute(block, 'c', [(0, 1), (1, 0)])  11.6 us
    all_to_all x2, waiting for transfers between devices, route(): return lax.all_to_all(block, ('z', 'y'), 0, 0, tiled=True)  11.1 us
    all_to_all x2, waiting for transfers between devices, over_x(): return lax.all_to_all(block, 'x', 0, 0, tiled=True)  9.12 us
  transfers between devices with their start and end apart: 16, of which 13 were waited for; matrix products, arithmetic and copies ran while one was open for 0% of the time, Pallas kernels for 6%

profile of v4, /device:TPU:8, one launch (start us, length us, event | category | flops | bytes accessed | tf_op | source)
XLA Modules:
  0.0 165.2 jit_solution(17536130042801236239)
XLA Ops:
  0.6 0.0 copy-start
  0.6 3.0 %shard_map.112 = bf16[512,640]{1,0:T(8,128)(2,1)} custom-call(s32[8,32]{1,0:T(8,128)} %bitcast.24, f32[8,32]{1,0:T(8,128)} %bitcast.30, bf16[32,512]{1,0:T(8,128)(2,1)} %tok_hbm.1, bf16[32,512]{1,0:T(8,128)(2,1)} %dy_hbm.1), custom_call_target="tpu_custom_call" | custom-call | tf_op jit(solution)/shard_map/pallas_call | solution.py:235
  3.6 18.7 %all-to-all-start = ((bf16[64,8,640]{2,1,0:T(8,128)(2,1)}), bf16[64,8,640]{2,1,0:T(8,128)(2,1)S(1)}, u32[]{:S(2)}, u32[]{:S(2)}) async-start(bf16[64,8,640]{2,1,0:T(8,128)(2,1)} %bitcast.4), calls=%async_computation | async-start | bytes 1310720 | tf_op jit(solution)/shard_map/all_to_all | solution.py:268
  22.4 0.1 pad_add_fusion.me_ref
  22.5 0.0 copy-done
  22.5 1.4 copy-done.2
  23.9 1.4 copy-done.6
  25.3 0.8 shard_map.113
  26.1 0.0 copy-start.9
  26.1 0.7 copy-done.9
  26.8 1.9 %collective-permute-start = (bf16[2,4,192,512]{3,2,1,0:T(8,128)(2,1)S(1)}, bf16[2,4,192,512]{3,2,1,0:T(8,128)(2,1)S(1)}, u32[]{:S(2)}, u32[]{:S(2)}) collective-permute-start(bf16[2,4,192,512]{3,2,1,0:T(8,128)(2,1)S(1)} %get-tuple-element.24), channel_id=1, source_target_pairs={{0,64},{64,0},{1,65},{65,1},{2,66},{66,2},{3,67},{67,3},{4,68},{68... | collective-permute-start | bytes 4718600 | tf_op jit(solution)/shard_map/ppermute | solution.py:259
  28.7 3.4 %collective-permute-start.2 = (bf16[192,1024]{1,0:T(8,128)(2,1)S(1)}, bf16[192,1024]{1,0:T(8,128)(2,1)S(1)}, u32[]{:S(2)}, u32[]{:S(2)}) collective-permute-start(bf16[192,1024]{1,0:T(8,128)(2,1)S(1)} %get-tuple-element.26), channel_id=1, source_target_pairs={{0,128},{128,256},{256,384},{384,0},{1,129},{129,257},{257,385},{3... | collective-permute-start | bytes 1179656 | tf_op jit(solution)/shard_map/ppermute | solution.py:262
  32.1 4.6 %collective-permute-start.3 = (bf16[192,1024]{1,0:T(8,128)(2,1)S(1)}, bf16[192,1024]{1,0:T(8,128)(2,1)S(1)}, u32[]{:S(2)}, u32[]{:S(2)}) collective-permute-start(bf16[192,1024]{1,0:T(8,128)(2,1)S(1)} %get-tuple-element.27), channel_id=1, source_target_pairs={{0,256},{128,384},{256,0},{384,128},{1,257},{129,385},{257,1},{385... | collective-permute-start | bytes 1179656 | tf_op jit(solution)/shard_map/ppermute | solution.py:262
  36.8 3.3 %collective-permute-start.4 = (bf16[192,1024]{1,0:T(8,128)(2,1)S(1)}, bf16[192,1024]{1,0:T(8,128)(2,1)S(1)}, u32[]{:S(2)}, u32[]{:S(2)}) collective-permute-start(bf16[192,1024]{1,0:T(8,128)(2,1)S(1)} %get-tuple-element.28), channel_id=1, source_target_pairs={{0,384},{128,0},{256,128},{384,256},{1,385},{129,1},{257,129},{385... | collective-permute-start | bytes 1179656 | tf_op jit(solution)/shard_map/ppermute | solution.py:262
  40.1 0.0 copy-done.16
  40.1 1.9 %collective-permute-start.1 = (bf16[64,512]{1,0:T(8,128)(2,1)S(1)}, bf16[64,512]{1,0:T(8,128)(2,1)S(1)}, u32[]{:S(2)}, u32[]{:S(2)}) collective-permute-start(bf16[64,512]{1,0:T(8,128)(2,1)S(1)} %bitcast.28), channel_id=1, source_target_pairs={{0,64},{64,0},{1,65},{65,1},{2,66},{66,2},{3,67},{67,3},{4,68},{68... | collective-permute-start | bytes 196616 | tf_op jit(solution)/shard_map/ppermute | solution.py:259
  42.1 1.2 collective-permute-done.1.refs_3_
  43.3 0.1 collective-permute-done.2.refs_5_
  43.3 9.4 %collective-permute-done.3.refs_6_ = bf16[192,1024]{1,0:T(8,128)(2,1)S(1)} collective-permute-done((bf16[192,1024]{1,0:T(8,128)(2,1)S(1)}, bf16[192,1024]{1,0:T(8,128)(2,1)S(1)}, u32[]{:S(2)}, u32[]{:S(2)}) %collective-permute-start.3) | collective-permute-done | bytes 393248 | tf_op jit(solution)/shard_map/ppermute | solution.py:262
  52.7 1.5 collective-permute-done.4.refs_7_
  54.3 0.0 copy-done.12
  54.3 0.0 copy-done.13
  54.3 0.8 copy-done.14
  55.1 0.0 collective-permute-done.half_hbm.swap_ref
  55.1 5.6 %all-to-all-done = bf16[64,8,640]{2,1,0:T(8,128)(2,1)S(1)} async-done(((bf16[64,8,640]{2,1,0:T(8,128)(2,1)}), bf16[64,8,640]{2,1,0:T(8,128)(2,1)S(1)}, u32[]{:S(2)}, u32[]{:S(2)}) %all-to-all-start) | async-done | bytes 655392 | tf_op jit(solution)/shard_map/all_to_all | solution.py:268
  60.7 0.0 copy-done.17
  60.7 1.7 %shard_map.114 = (bf16[4,320,512]{2,1,0:T(8,128)(2,1)}, bf16[320,512]{1,0:T(8,128)(2,1)}) custom-call(bf16[512,640]{1,0:T(8,128)(2,1)S(1)} %bitcast.21), custom_call_target="tpu_custom_call" | custom-call | tf_op jit(solution)/shard_map/pallas_call | solution.py:235
  62.5 0.0 copy-start.7
  62.5 4.4 %all-to-all-start.1 = ((bf16[4,320,512]{2,1,0:T(8,128)(2,1)}), bf16[4,320,512]{2,1,0:T(8,128)(2,1)S(1)}, u32[]{:S(2)}, u32[]{:S(2)}) async-start(bf16[4,320,512]{2,1,0:T(8,128)(2,1)} %get-tuple-element.30), calls=%async_computation.1 | async-start | bytes 2621440 | tf_op jit(solution)/shard_map/all_to_all | solution.py:265
  66.9 1.9 %collective-permute-start.6 = (bf16[320,512]{1,0:T(8,128)(2,1)S(1)}, bf16[320,512]{1,0:T(8,128)(2,1)S(1)}, u32[]{:S(2)}, u32[]{:S(2)}) collective-permute-start(bf16[320,512]{1,0:T(8,128)(2,1)S(1)} %copy-done.7), channel_id=1, source_target_pairs={{0,64},{64,0},{1,65},{65,1},{2,66},{66,2},{3,67},{67,3},{4,68},{68... | collective-permute-start | bytes 983048 | tf_op jit(solution)/shard_map/ppermute | solution.py:259
  68.8 1.6 collective-permute-done.6.refs_1_
  70.4 0.7 copy-done.15
  71.1 4.0 %shard_map.116 = bf16[4,320,256]{2,1,0:T(8,128)(2,1)} custom-call(s32[2]{0:T(128)S(1)} %pad_add_fusion.me_ref, bf16[320,512]{1,0:T(8,128)(2,1)} %get-tuple-element.34.refs_0_.s_ref, bf16[320,512]{1,0:T(8,128)(2,1)} %copy-done.15, bf16[64,512]{1,0:T(8,128)(2,1)} %bitcast.27, bf16[64,512]{1,0:T(8,128)(2,1)} %copy-done.17, bf16[192,1024]{1,0:T(8,128)(2,1)} %copy-done.9, ...), custom_call_target="tpu_custom_call" | custom-call | tf_op jit(solution)/shard_map/pallas_call | solution.py:235
  75.2 7.2 %all-to-all-done.1.x_hbm = bf16[4,320,512]{2,1,0:T(8,128)(2,1)S(1)} async-done(((bf16[4,320,512]{2,1,0:T(8,128)(2,1)}), bf16[4,320,512]{2,1,0:T(8,128)(2,1)S(1)}, u32[]{:S(2)}, u32[]{:S(2)}) %all-to-all-start.1) | async-done | bytes 1310752 | tf_op jit(solution)/shard_map/all_to_all | solution.py:265
  82.3 1.1 copy-done.11
  83.4 4.2 %all-to-all-start.2 = ((bf16[4,320,256]{2,1,0:T(8,128)(2,1)}), bf16[4,320,256]{2,1,0:T(8,128)(2,1)}, u32[]{:S(2)}, u32[]{:S(2)}) async-start(bf16[4,320,256]{2,1,0:T(8,128)(2,1)} %shard_map.116), calls=%async_computation.2 | async-start | bytes 1310720 | tf_op jit(solution)/shard_map/all_to_all | solution.py:265
  87.6 0.0 copy-start.3
  87.6 4.8 %shard_map.115 = (f32[2,320,192]{2,1,0:T(8,128)}, bf16[2,320,192]{2,1,0:T(8,128)(2,1)S(1)}) custom-call(s32[2]{0:T(128)S(1)} %pad_add_fusion.me_ref, bf16[4,320,512]{2,1,0:T(8,128)(2,1)} %copy-done.11, bf16[192,4096]{1,0:T(8,128)(2,1)} %bitcast.15, bf16[192,4096]{1,0:T(8,128)(2,1)} %bitcast.18, bf16[2,4,192,512]{3,2,1,0:T(8,128)(2,1)} %copy-done.4), custom_call_target="tpu_custom_call" | custom-call | tf_op jit(solution)/shard_map/pallas_call | solution.py:235
  92.4 0.0 copy-start.1
  92.4 2.1 %collective-permute-start.5 = (bf16[2,320,192]{2,1,0:T(8,128)(2,1)S(1)}, bf16[2,320,192]{2,1,0:T(8,128)(2,1)}, u32[]{:S(2)}, u32[]{:S(2)}) collective-permute-start(bf16[2,320,192]{2,1,0:T(8,128)(2,1)S(1)} %get-tuple-element.33), channel_id=1, source_target_pairs={{0,64},{64,0},{1,65},{65,1},{2,66},{66,2},{3,67},{67,3},{4,68},{68... | collective-permute-start | bytes 737288 | tf_op jit(solution)/shard_map/ppermute | solution.py:259
  94.5 2.0 %all-to-all-done.2.in_hbm = bf16[4,320,256]{2,1,0:T(8,128)(2,1)} async-done(((bf16[4,320,256]{2,1,0:T(8,128)(2,1)}), bf16[4,320,256]{2,1,0:T(8,128)(2,1)}, u32[]{:S(2)}, u32[]{:S(2)}) %all-to-all-start.2) | async-done | bytes 655392 | tf_op jit(solution)/shard_map/all_to_all | solution.py:265
  96.4 0.0 collective-permute-done.5.got_hbm
  96.4 2.4 %shard_map.117 = (bf16[2,320,192]{2,1,0:T(8,128)(2,1)S(1)}, f32[64,192]{1,0:T(8,128)}, bf16[320,64]{1,0:T(8,128)(2,1)S(1)}) custom-call(f32[2,320,192]{2,1,0:T(8,128)} %get-tuple-element.32.keep_hbm, bf16[2,320,192]{2,1,0:T(8,128)(2,1)} %collective-permute-done.5.got_hbm, bf16[4,320,256]{2,1,0:T(8,128)(2,1)} %all-to-all-done.2.in_hbm, bf16[64,192]{1,0:T(8,128)(2,1)} %bitcast.29), custom_call_target="tpu_custom_call" | custom-call | tf_op jit(solution)/shard_map/pallas_call | solution.py:235
  98.8 1.9 %collective-permute-start.11 = (bf16[2,320,192]{2,1,0:T(8,128)(2,1)S(1)}, bf16[2,320,192]{2,1,0:T(8,128)(2,1)S(1)}, u32[]{:S(2)}, u32[]{:S(2)}) collective-permute-start(bf16[2,320,192]{2,1,0:T(8,128)(2,1)S(1)} %get-tuple-element.42.g_ref), channel_id=1, source_target_pairs={{0,64},{64,0},{1,65},{65,1},{2,66},{66,2},{3,67},{67,3},{4,68},{68... | collective-permute-start | bytes 737288 | tf_op jit(solution)/shard_map/ppermute | solution.py:259
  100.7 1.6 collective-permute-done.11.h_ref
  102.3 0.0 copy-done.1
  102.3 1.4 copy-done.5
  103.7 2.1 %shard_map.120 = bf16[4,320,512]{2,1,0:T(8,128)(2,1)S(1)} custom-call(s32[2]{0:T(128)S(1)} %pad_add_fusion.me_ref, bf16[2,320,192]{2,1,0:T(8,128)(2,1)S(1)} %get-tuple-element.42.g_ref, bf16[2,320,192]{2,1,0:T(8,128)(2,1)S(1)} %collective-permute-done.11.h_ref, bf16[192,4096]{1,0:T(8,128)(2,1)S(1)} %bitcast.17, bf16[192,4096]{1,0:T(8,128)(2,1)S(1)} %bitcast.20, ...), custom_call_target="tpu_custom_call" | custom-call | tf_op jit(solution)/shard_map/pallas_call | solution.py:235
  105.8 22.5 %all_to_all.25.in_ref = bf16[4,320,512]{2,1,0:T(8,128)(2,1)S(1)} all-to-all(bf16[4,320,512]{2,1,0:T(8,128)(2,1)S(1)} %shard_map.120), channel_id=1, replica_groups=mesh['x'=4,'c'=2,'z'=16,'y'=4] {'x'}, dimensions={0} | all-to-all | bytes 2621440 | tf_op jit(solution)/shard_map/all_to_all | solution.py:265
  128.3 0.2 shard_map.121
  128.5 0.8 reshape.20
  129.3 11.8 %all-to-all-start.4 = ((bf16[64,2,1280]{2,1,0:T(2,128)(2,1)}), bf16[64,2,1280]{2,1,0:T(2,128)(2,1)S(1)}, u32[]{:S(2)}, u32[]{:S(2)}) async-start(bf16[64,2,1280]{2,1,0:T(2,128)(2,1)} %reshape.20), calls=%async_computation.4 | async-start | bytes 655360 | tf_op jit(solution)/shard_map/all_to_all | solution.py:268
  141.1 1.9 %collective-permute-start.7 = (bf16[320,64]{1,0:T(8,128)(2,1)S(1)}, bf16[320,64]{1,0:T(8,128)(2,1)S(1)}, u32[]{:S(2)}, u32[]{:S(2)}) collective-permute-start(bf16[320,64]{1,0:T(8,128)(2,1)S(1)} %get-tuple-element.40.a_ref), channel_id=1, source_target_pairs={{0,64},{64,0},{1,65},{65,1},{2,66},{66,2},{3,67},{67,3},{4,68},{68... | collective-permute-start | bytes 122888 | tf_op jit(solution)/shard_map/ppermute | solution.py:259
  143.0 1.2 collective-permute-done.7.b_ref
  144.3 3.1 %collective-permute-start.10 = (bf16[320,64]{1,0:T(8,128)(2,1)S(1)}, bf16[320,64]{1,0:T(8,128)(2,1)S(1)}, u32[]{:S(2)}, u32[]{:S(2)}) collective-permute-start(bf16[320,64]{1,0:T(8,128)(2,1)S(1)} %shard_map.118.v0_ref), channel_id=1, source_target_pairs={{0,384},{128,0},{256,128},{384,256},{1,385},{129,1},{257,129},{385... | collective-permute-start | bytes 122888 | tf_op jit(solution)/shard_map/ppermute | solution.py:262
  147.4 2.8 %collective-permute-start.8 = (bf16[320,64]{1,0:T(8,128)(2,1)S(1)}, bf16[320,64]{1,0:T(8,128)(2,1)S(1)}, u32[]{:S(2)}, u32[]{:S(2)}) collective-permute-start(bf16[320,64]{1,0:T(8,128)(2,1)S(1)} %shard_map.118.v0_ref), channel_id=1, source_target_pairs={{0,128},{128,256},{256,384},{384,0},{1,129},{129,257},{257,385},{3... | collective-permute-start | bytes 122888 | tf_op jit(solution)/shard_map/ppermute | solution.py:262
  150.1 2.7 %collective-permute-start.9 = (bf16[320,64]{1,0:T(8,128)(2,1)S(1)}, bf16[320,64]{1,0:T(8,128)(2,1)S(1)}, u32[]{:S(2)}, u32[]{:S(2)}) collective-permute-start(bf16[320,64]{1,0:T(8,128)(2,1)S(1)} %shard_map.118.v0_ref), channel_id=1, source_target_pairs={{0,256},{128,384},{256,0},{384,128},{1,257},{129,385},{257,1},{385... | collective-permute-start | bytes 122888 | tf_op jit(solution)/shard_map/ppermute | solution.py:262
  152.9 0.0 collective-permute-done.10.v3_ref
  152.9 2.0 %collective-permute-done.8.v1_ref = bf16[320,64]{1,0:T(8,128)(2,1)S(1)} collective-permute-done((bf16[320,64]{1,0:T(8,128)(2,1)S(1)}, bf16[320,64]{1,0:T(8,128)(2,1)S(1)}, u32[]{:S(2)}, u32[]{:S(2)}) %collective-permute-start.8) | collective-permute-done | bytes 40992 | tf_op jit(solution)/shard_map/ppermute | solution.py:262
  154.9 3.1 %collective-permute-done.9.v2_ref = bf16[320,64]{1,0:T(8,128)(2,1)S(1)} collective-permute-done((bf16[320,64]{1,0:T(8,128)(2,1)S(1)}, bf16[320,64]{1,0:T(8,128)(2,1)S(1)}, u32[]{:S(2)}, u32[]{:S(2)}) %collective-permute-start.9) | collective-permute-done | bytes 40992 | tf_op jit(solution)/shard_map/ppermute | solution.py:262
  158.0 0.0 copy-done.10
  158.0 0.9 shard_map.119
  158.9 5.5 %all-to-all-done.4 = bf16[64,2,1280]{2,1,0:T(2,128)(2,1)S(1)} async-done(((bf16[64,2,1280]{2,1,0:T(2,128)(2,1)}), bf16[64,2,1280]{2,1,0:T(2,128)(2,1)S(1)}, u32[]{:S(2)}, u32[]{:S(2)}) %all-to-all-start.4) | async-done | bytes 327712 | tf_op jit(solution)/shard_map/all_to_all | solution.py:268
  164.4 0.8 shard_map.122
  (19 shorter events, 0.1 us)
Async XLA Ops:
  0.6 21.8 %copy-start = (bf16[1,192,4096]{2,1,0:T(8,128)(2,1)S(1)}, bf16[1,192,4096]{2,1,0:T(8,128)(2,1)}, u32[]{:S(2)}) copy-start(bf16[1,192,4096]{2,1,0:T(8,128)(2,1)} %param.13) | copy-start | bytes 4718596
  3.6 57.1 %all-to-all-start = ((bf16[64,8,640]{2,1,0:T(8,128)(2,1)}), bf16[64,8,640]{2,1,0:T(8,128)(2,1)S(1)}, u32[]{:S(2)}, u32[]{:S(2)}) async-start(bf16[64,8,640]{2,1,0:T(8,128)(2,1)} %bitcast.4), calls=%async_computation | async-start | bytes 1310720 | tf_op jit(solution)/shard_map/all_to_all | solution.py:268
  22.5 1.4 copy-start.2
  23.9 1.4 copy-start.6
  25.3 14.8 %copy-start.16 = (bf16[1,64,512]{2,1,0:T(8,128)(2,1)S(1)}, bf16[1,64,512]{2,1,0:T(8,128)(2,1)}, u32[]{:S(2)}) copy-start(bf16[1,64,512]{2,1,0:T(8,128)(2,1)} %param.17) | copy-start | bytes 196612
  26.1 0.7 copy-start.9
  26.8 28.3 %collective-permute-start = (bf16[2,4,192,512]{3,2,1,0:T(8,128)(2,1)S(1)}, bf16[2,4,192,512]{3,2,1,0:T(8,128)(2,1)S(1)}, u32[]{:S(2)}, u32[]{:S(2)}) collective-permute-start(bf16[2,4,192,512]{3,2,1,0:T(8,128)(2,1)S(1)} %get-tuple-element.24), channel_id=1, source_target_pairs={{0,64},{64,0},{1,65},{65,1},{2,66},{66,2},{3,67},{67,3},{4,68},{68... | collective-permute-start | bytes 4718600 | tf_op jit(solution)/shard_map/ppermute | solution.py:259
  28.7 14.6 %collective-permute-start.2 = (bf16[192,1024]{1,0:T(8,128)(2,1)S(1)}, bf16[192,1024]{1,0:T(8,128)(2,1)S(1)}, u32[]{:S(2)}, u32[]{:S(2)}) collective-permute-start(bf16[192,1024]{1,0:T(8,128)(2,1)S(1)} %get-tuple-element.26), channel_id=1, source_target_pairs={{0,128},{128,256},{256,384},{384,0},{1,129},{129,257},{257,385},{3... | collective-permute-start | bytes 1179656 | tf_op jit(solution)/shard_map/ppermute | solution.py:262
  32.1 20.6 %collective-permute-start.3 = (bf16[192,1024]{1,0:T(8,128)(2,1)S(1)}, bf16[192,1024]{1,0:T(8,128)(2,1)S(1)}, u32[]{:S(2)}, u32[]{:S(2)}) collective-permute-start(bf16[192,1024]{1,0:T(8,128)(2,1)S(1)} %get-tuple-element.27), channel_id=1, source_target_pairs={{0,256},{128,384},{256,0},{384,128},{1,257},{129,385},{257,1},{385... | collective-permute-start | bytes 1179656 | tf_op jit(solution)/shard_map/ppermute | solution.py:262
  36.8 17.5 %collective-permute-start.4 = (bf16[192,1024]{1,0:T(8,128)(2,1)S(1)}, bf16[192,1024]{1,0:T(8,128)(2,1)S(1)}, u32[]{:S(2)}, u32[]{:S(2)}) collective-permute-start(bf16[192,1024]{1,0:T(8,128)(2,1)S(1)} %get-tuple-element.28), channel_id=1, source_target_pairs={{0,384},{128,0},{256,128},{384,256},{1,385},{129,1},{257,129},{385... | collective-permute-start | bytes 1179656 | tf_op jit(solution)/shard_map/ppermute | solution.py:262
  40.1 3.1 %collective-permute-start.1 = (bf16[64,512]{1,0:T(8,128)(2,1)S(1)}, bf16[64,512]{1,0:T(8,128)(2,1)S(1)}, u32[]{:S(2)}, u32[]{:S(2)}) collective-permute-start(bf16[64,512]{1,0:T(8,128)(2,1)S(1)} %bitcast.28), channel_id=1, source_target_pairs={{0,64},{64,0},{1,65},{65,1},{2,66},{66,2},{3,67},{67,3},{4,68},{68... | collective-permute-start | bytes 196616 | tf_op jit(solution)/shard_map/ppermute | solution.py:259
  43.3 17.4 %copy-start.17 = (bf16[64,512]{1,0:T(8,128)(2,1)}, bf16[64,512]{1,0:T(8,128)(2,1)S(1)}, u32[]{:S(2)}) copy-start(bf16[64,512]{1,0:T(8,128)(2,1)S(1)} %collective-permute-done.1.refs_3_) | copy-start | bytes 196612
  43.3 11.0 %copy-start.12 = (bf16[192,1024]{1,0:T(8,128)(2,1)}, bf16[192,1024]{1,0:T(8,128)(2,1)S(1)}, u32[]{:S(2)}) copy-start(bf16[192,1024]{1,0:T(8,128)(2,1)S(1)} %collective-permute-done.2.refs_5_) | copy-start | bytes 1179652
  52.7 1.6 copy-start.13
  54.3 0.8 copy-start.14
  55.1 7.4 %copy-start.4 = (bf16[2,4,192,512]{3,2,1,0:T(8,128)(2,1)}, bf16[2,4,192,512]{3,2,1,0:T(8,128)(2,1)S(1)}, u32[]{:S(2)}) copy-start(bf16[2,4,192,512]{3,2,1,0:T(8,128)(2,1)S(1)} %collective-permute-done.half_hbm.swap_ref) | copy-start | bytes 4718596
  62.5 4.5 %copy-start.7 = (bf16[320,512]{1,0:T(8,128)(2,1)S(1)}, bf16[320,512]{1,0:T(8,128)(2,1)}, u32[]{:S(2)}) copy-start(bf16[320,512]{1,0:T(8,128)(2,1)} %get-tuple-element.34.refs_0_.s_ref) | copy-start | bytes 983044
  62.5 19.9 %all-to-all-start.1 = ((bf16[4,320,512]{2,1,0:T(8,128)(2,1)}), bf16[4,320,512]{2,1,0:T(8,128)(2,1)S(1)}, u32[]{:S(2)}, u32[]{:S(2)}) async-start(bf16[4,320,512]{2,1,0:T(8,128)(2,1)} %get-tuple-element.30), calls=%async_computation.1 | async-start | bytes 2621440 | tf_op jit(solution)/shard_map/all_to_all | solution.py:265
  66.9 3.5 %collective-permute-start.6 = (bf16[320,512]{1,0:T(8,128)(2,1)S(1)}, bf16[320,512]{1,0:T(8,128)(2,1)S(1)}, u32[]{:S(2)}, u32[]{:S(2)}) collective-permute-start(bf16[320,512]{1,0:T(8,128)(2,1)S(1)} %copy-done.7), channel_id=1, source_target_pairs={{0,64},{64,0},{1,65},{65,1},{2,66},{66,2},{3,67},{67,3},{4,68},{68... | collective-permute-start | bytes 983048 | tf_op jit(solution)/shard_map/ppermute | solution.py:259
  70.4 0.7 copy-start.15
  82.3 1.1 copy-start.11
  83.4 13.0 %all-to-all-start.2 = ((bf16[4,320,256]{2,1,0:T(8,128)(2,1)}), bf16[4,320,256]{2,1,0:T(8,128)(2,1)}, u32[]{:S(2)}, u32[]{:S(2)}) async-start(bf16[4,320,256]{2,1,0:T(8,128)(2,1)} %shard_map.116), calls=%async_computation.2 | async-start | bytes 1310720 | tf_op jit(solution)/shard_map/all_to_all | solution.py:265
  87.6 14.8 %copy-start.3 = (bf16[1,192,4096]{2,1,0:T(8,128)(2,1)S(1)}, bf16[1,192,4096]{2,1,0:T(8,128)(2,1)}, u32[]{:S(2)}) copy-start(bf16[1,192,4096]{2,1,0:T(8,128)(2,1)} %param.14) | copy-start | bytes 4718596
  92.4 10.0 %copy-start.1 = (bf16[1,192,4096]{2,1,0:T(8,128)(2,1)S(1)}, bf16[1,192,4096]{2,1,0:T(8,128)(2,1)}, u32[]{:S(2)}) copy-start(bf16[1,192,4096]{2,1,0:T(8,128)(2,1)} %param.13) | copy-start | bytes 4718596
  92.4 4.0 %collective-permute-start.5 = (bf16[2,320,192]{2,1,0:T(8,128)(2,1)S(1)}, bf16[2,320,192]{2,1,0:T(8,128)(2,1)}, u32[]{:S(2)}, u32[]{:S(2)}) collective-permute-start(bf16[2,320,192]{2,1,0:T(8,128)(2,1)S(1)} %get-tuple-element.33), channel_id=1, source_target_pairs={{0,64},{64,0},{1,65},{65,1},{2,66},{66,2},{3,67},{67,3},{4,68},{68... | collective-permute-start | bytes 737288 | tf_op jit(solution)/shard_map/ppermute | solution.py:259
  98.8 3.5 %collective-permute-start.11 = (bf16[2,320,192]{2,1,0:T(8,128)(2,1)S(1)}, bf16[2,320,192]{2,1,0:T(8,128)(2,1)S(1)}, u32[]{:S(2)}, u32[]{:S(2)}) collective-permute-start(bf16[2,320,192]{2,1,0:T(8,128)(2,1)S(1)} %get-tuple-element.42.g_ref), channel_id=1, source_target_pairs={{0,64},{64,0},{1,65},{65,1},{2,66},{66,2},{3,67},{67,3},{4,68},{68... | collective-permute-start | bytes 737288 | tf_op jit(solution)/shard_map/ppermute | solution.py:259
  102.3 1.4 copy-start.5
  128.3 29.7 %copy-start.8 = (bf16[320,512]{1,0:T(8,128)(2,1)S(1)}, bf16[320,512]{1,0:T(8,128)(2,1)}, u32[]{:S(2)}) copy-start(bf16[320,512]{1,0:T(8,128)(2,1)} %get-tuple-element.34.refs_0_.s_ref) | copy-start | bytes 983044
  128.3 29.7 %copy-start.10 = (s32[32,8]{0,1:T(8,128)S(1)}, s32[32,8]{0,1:T(8,128)}, u32[]{:S(2)}) copy-start(s32[32,8]{0,1:T(8,128)} %param.12) | copy-start | bytes 3076
  129.3 35.0 %all-to-all-start.4 = ((bf16[64,2,1280]{2,1,0:T(2,128)(2,1)}), bf16[64,2,1280]{2,1,0:T(2,128)(2,1)S(1)}, u32[]{:S(2)}, u32[]{:S(2)}) async-start(bf16[64,2,1280]{2,1,0:T(2,128)(2,1)} %reshape.20), calls=%async_computation.4 | async-start | bytes 655360 | tf_op jit(solution)/shard_map/all_to_all | solution.py:268
  141.1 3.2 %collective-permute-start.7 = (bf16[320,64]{1,0:T(8,128)(2,1)S(1)}, bf16[320,64]{1,0:T(8,128)(2,1)S(1)}, u32[]{:S(2)}, u32[]{:S(2)}) collective-permute-start(bf16[320,64]{1,0:T(8,128)(2,1)S(1)} %get-tuple-element.40.a_ref), channel_id=1, source_target_pairs={{0,64},{64,0},{1,65},{65,1},{2,66},{66,2},{3,67},{67,3},{4,68},{68... | collective-permute-start | bytes 122888 | tf_op jit(solution)/shard_map/ppermute | solution.py:259
  144.3 8.6 %collective-permute-start.10 = (bf16[320,64]{1,0:T(8,128)(2,1)S(1)}, bf16[320,64]{1,0:T(8,128)(2,1)S(1)}, u32[]{:S(2)}, u32[]{:S(2)}) collective-permute-start(bf16[320,64]{1,0:T(8,128)(2,1)S(1)} %shard_map.118.v0_ref), channel_id=1, source_target_pairs={{0,384},{128,0},{256,128},{384,256},{1,385},{129,1},{257,129},{385... | collective-permute-start | bytes 122888 | tf_op jit(solution)/shard_map/ppermute | solution.py:262
  147.4 7.5 %collective-permute-start.8 = (bf16[320,64]{1,0:T(8,128)(2,1)S(1)}, bf16[320,64]{1,0:T(8,128)(2,1)S(1)}, u32[]{:S(2)}, u32[]{:S(2)}) collective-permute-start(bf16[320,64]{1,0:T(8,128)(2,1)S(1)} %shard_map.118.v0_ref), channel_id=1, source_target_pairs={{0,128},{128,256},{256,384},{384,0},{1,129},{129,257},{257,385},{3... | collective-permute-start | bytes 122888 | tf_op jit(solution)/shard_map/ppermute | solution.py:262
  150.1 7.8 %collective-permute-start.9 = (bf16[320,64]{1,0:T(8,128)(2,1)S(1)}, bf16[320,64]{1,0:T(8,128)(2,1)S(1)}, u32[]{:S(2)}, u32[]{:S(2)}) collective-permute-start(bf16[320,64]{1,0:T(8,128)(2,1)S(1)} %shard_map.118.v0_ref), channel_id=1, source_target_pairs={{0,256},{128,384},{256,0},{384,128},{1,257},{129,385},{257,1},{385... | collective-permute-start | bytes 122888 | tf_op jit(solution)/shard_map/ppermute | solution.py:262

commit v5 on v4

--- a/solution.py
+++ b/solution.py
@@ -44,31 +44,29 @@
     count, width = tok_ref.shape
     parts = 2 * width // LANE
     span = parts * count
-    row = lax.broadcasted_iota(jnp.int32, (rows, span), 0)
+    row = lax.broadcasted_iota(jnp.int32, (rows, count), 0)
+    own = lax.div(row, parts)
+    hit = jnp.zeros((rows, count), F32)
+    weight = jnp.zeros((rows, count), F32)
+    for k in range(ids_ref.shape[0]):
+        same = ids_ref[k : k + 1, :] == own
+        hit = jnp.where(same, 1.0, hit)
+        weight = jnp.where(same, prob_ref[k : k + 1, :], weight)
+    weight = jnp.where(lax.rem(row, parts) < parts // 2, hit, weight)
+    first = lax.broadcasted_iota(jnp.int32, (count, count), 0)
+    second = lax.broadcasted_iota(jnp.int32, (count, count), 1)
+    before = jnp.where(first < second, 1.0, 0.0).astype(BF)
+    code = jnp.where(hit > 0.5, nn(hit.astype(BF), before), -1.0)
+    wide_row = lax.broadcasted_iota(jnp.int32, (rows, span), 0)
     lane = lax.broadcasted_iota(jnp.int32, (rows, span), 1)
-    own = jnp.where(lax.rem(row, parts) == lax.div(lane, count), lax.div(row, parts), -1)
-    ids = jnp.concatenate([ids_ref[...]] * parts, axis=1)
-    prob = jnp.concatenate([prob_ref[...]] * parts, axis=1)
-    hit = jnp.zeros((rows, span), F32)
-    weight = jnp.zeros((rows, span), F32)
-    for k in range(ids.shape[0]):
-        same = ids[k : k + 1, :] == own
-        hit = jnp.where(same, 1.0, hit)
-        weight = jnp.where(same, prob[k : k + 1, :], weight)
-    weight = jnp.where(lax.rem(row, parts) < parts // 2, hit, weight)
-    first = lax.broadcasted_iota(jnp.int32, (span, span), 0)
-    second = lax.broadcasted_iota(jnp.int32, (span, span), 1)
-    near = lax.div(first, count) == lax.div(second, count)
-    before = jnp.where(near & (first < second), 1.0, 0.0).astype(BF)
-    slot = nn(hit.astype(BF), before)
-    code = jnp.where(hit > 0.5, slot, -1.0)
+    here = lax.rem(wide_row, parts) == lax.div(lane, count)
+    spread = jnp.where(here, jnp.concatenate([code] * parts, axis=1), -1.0)
     table = jnp.concatenate(
         [ref[:, c : c + LANE] for ref in (tok_ref, dy_ref) for c in range(0, width, LANE)], axis=0
     )
     for s in range(CAP):
-        mine = code == float(s)
-        pick = jnp.where(mine, 1.0, 0.0).astype(BF)
-        scale = jnp.sum(jnp.where(mine, weight, 0.0), axis=1, keepdims=True)
+        pick = jnp.where(spread == float(s), 1.0, 0.0).astype(BF)
+        scale = jnp.sum(jnp.where(code == float(s), weight, 0.0), axis=1, keepdims=True)
         out_ref[:, s * LANE : (s + 1) * LANE] = (nn(pick, table) * scale).astype(BF)
 
 
@@ -133,68 +131,89 @@
     fetch([(out_ref, out_hbm)], sems)
 
 
+def stream(half_hbm, half_ref, sems):
+    copies = [
+        pltpu.make_async_copy(half_hbm.at[:, x], half_ref.at[:, x], sems.at[x])
+        for x in range(half_ref.shape[1])
+    ]
+    for copy in copies:
+        copy.start()
+    return copies
+
+
 def gate_kernel(
-    me_ref, x_hbm, wg_hbm, wu_hbm, half_hbm, keep_hbm, send_ref,
-    x_ref, w_ref, half_ref, keep_ref, sems, sem,
+    me_ref, x_ref, wg_ref, wu_ref, half_hbm, keep_hbm, send_ref, half_ref, keep_ref, sems, sem
 ):
     core = me_ref[1]
     chips, routes, width = x_ref.shape
-    units = w_ref.shape[2]
-    copies = []
-    for x in range(chips):
-        cols = lanes(2 * x + core, width)
-        pairs = [
-            (x_hbm.at[x], x_ref.at[x]), (wg_hbm.at[:, cols], w_ref.at[0, x]),
-            (wu_hbm.at[:, cols], w_ref.at[1, x]), (half_hbm.at[:, x], half_ref.at[:, x]),
-        ]
-        copies.append([pltpu.make_async_copy(p, q, sems.at[x, i]) for i, (p, q) in enumerate(pairs)])
-        for copy in copies[x]:
-            copy.start()
+    units = wg_ref.shape[0]
+    copies = stream(half_hbm, half_ref, sems)
     keep = [jnp.zeros((routes, units), F32)] * 2
     send = [jnp.zeros((routes, units), F32)] * 2
     for x in range(chips):
-        for copy in copies[x]:
-            copy.wait()
-        rows = x_ref[x]
-        for i in range(2):
-            keep[i] = keep[i] + nt(rows, w_ref[i, x])
-            send[i] = send[i] + nt(rows, half_ref[i, x])
+        cols = lanes(2 * x + core, width)
+        keep[0] = keep[0] + nt(x_ref[x], wg_ref[:, cols])
+        keep[1] = keep[1] + nt(x_ref[x], wu_ref[:, cols])
     for i in range(2):
         keep_ref[i] = keep[i]
-    fetch_out = pltpu.make_async_copy(keep_ref, keep_hbm, sem.at[0])
-    fetch_out.start()
+    store = pltpu.make_async_copy(keep_ref, keep_hbm, sem.at[0])
+    store.start()
+    for x in range(chips):
+        copies[x].wait()
+        for i in range(2):
+            send[i] = send[i] + nt(x_ref[x], half_ref[i, x])
     for i in range(2):
         send_ref[i] = send[i].astype(BF)
-    fetch_out.wait()
-
-
-def grad_kernel(keep_hbm, got_hbm, in_hbm, a_hbm, out_ref, ga_ref, v_ref, keep_ref, got_ref, in_ref, a_ref, sems):
-    fetch([(keep_hbm, keep_ref), (got_hbm, got_ref), (in_hbm, in_ref), (a_hbm, a_ref)], sems)
+    store.wait()
+
+
+def grad_kernel(keep_hbm, got_ref, in_ref, a_ref, out_ref, ga_ref, keep_ref, sem):
+    fetch_keep = pltpu.make_async_copy(keep_hbm, keep_ref, sem.at[0])
+    fetch_keep.start()
     units = keep_ref.shape[2]
+    total = in_ref[0].astype(F32)
+    for x in range(1, in_ref.shape[0]):
+        total += in_ref[x].astype(F32)
+    low_u = total[:, units:].astype(BF)
+    grad = total[:, :units] + nn(low_u, a_ref[...])
+    fetch_keep.wait()
     gate = keep_ref[0] + got_ref[0].astype(F32)
     up = keep_ref[1] + got_ref[1].astype(F32)
     sigma = jax.nn.sigmoid(gate)
     active = gate * sigma
     hidden = (active * up).astype(BF)
-    v_ref[...] = nt(hidden, a_ref[...]).astype(BF)
-    total = in_ref[0].astype(F32)
-    for x in range(1, in_ref.shape[0]):
-        total += in_ref[x].astype(F32)
-    low_u = total[:, units:].astype(BF)
-    grad = total[:, :units] + nn(low_u, a_ref[...])
     ga_ref[...] = tn(low_u, hidden)
-    out_ref[0] = (grad * up * sigma * (1.0 + gate * (1.0 - sigma))).astype(BF)
-    out_ref[1] = (grad * active).astype(BF)
-
-
-def back_kernel(me_ref, g_ref, h_ref, wg_ref, wu_ref, swap_ref, out_ref):
+    grad_gate = (grad * up * sigma * (1.0 + gate * (1.0 - sigma))).astype(BF)
+    grad_up = (grad * active).astype(BF)
+    low_v = nt(hidden, a_ref[...]).astype(BF)
+    out_ref[...] = jnp.concatenate([grad_gate, grad_up, low_v], axis=1)
+
+
+def back_kernel(
+    me_ref, g_ref, h_ref, wg_ref, wu_ref, half_hbm, out_hbm, v_ref, half_ref, out_ref, sems, out_sems
+):
     core = me_ref[1]
     chips, _, width = out_ref.shape
+    units = wg_ref.shape[0]
+    copies = stream(half_hbm, half_ref, sems)
+    mine = [g_ref[:, i * units : (i + 1) * units] for i in range(2)]
+    other = [h_ref[:, i * units : (i + 1) * units] for i in range(2)]
+    stores = []
+    v_ref[...] = (g_ref[:, 2 * units :].astype(F32) + h_ref[:, 2 * units :].astype(F32)).astype(BF)
     for x in range(chips):
         cols = lanes(2 * x + core, width)
-        term = nn(g_ref[0], wg_ref[:, cols]) + nn(g_ref[1], wu_ref[:, cols])
-        term += nn(h_ref[0], swap_ref[0, x]) + nn(h_ref[1], swap_ref[1, x])
+        term = nn(mine[0], wg_ref[:, cols]) + nn(mine[1], wu_ref[:, cols])
+        copies[x].wait()
+        term += nn(other[0], half_ref[0, x]) + nn(other[1], half_ref[1, x])
         out_ref[x] = term.astype(BF)
+        stores.append(pltpu.make_async_copy(out_ref.at[x], out_hbm.at[x], out_sems.at[x]))
+        stores[x].start()
+    for store in stores:
+        store.wait()
+
+
+def code_kernel(ids_ref, code_ref):
+    code_ref[...] = code_of(ids_ref[...], code_ref.shape[0])
 
 
 def total_kernel(in_ref, out_ref):
@@ -208,12 +227,7 @@
         out_ref[:, s * width : (s + 1) * width] = total.astype(BF)
 
 
-def pair_kernel(a_ref, b_ref, o_ref):
-    o_ref[...] = (a_ref[...].astype(F32) + b_ref[...].astype(F32)).astype(BF)
-
-
-def adapter_kernel(ids_ref, v0_ref, v1_ref, v2_ref, v3_ref, s_ref, o_ref, code_ref):
-    code_ref[...] = code_of(ids_ref[...], code_ref.shape[0])
+def adapter_kernel(v0_ref, v1_ref, v2_ref, v3_ref, s_ref, o_ref):
     low = v0_ref[...].astype(F32) + v1_ref[...].astype(F32)
     low += v2_ref[...].astype(F32) + v3_ref[...].astype(F32)
     o_ref[...] = tn(low.astype(BF), s_ref[...])
@@ -317,34 +331,33 @@
     keep, send = call(
         gate_kernel,
         (pltpu.HBM((2, routes, units), F32), sds((2, routes, units), BF)),
-        me, *pin(x_all, w_gate, w_up, half), scalars=1, places=[slow] * 4, ends=(far, near),
+        me, x_all, w_gate, w_up, *pin(half), scalars=1, places=[near] * 3 + [slow], ends=(far, near),
         scratch=[
-            pltpu.VMEM(x_all.shape, BF), pltpu.VMEM((2, chips, units, width), BF),
-            pltpu.VMEM(half.shape, BF), pltpu.VMEM((2, routes, units), F32), dma((chips, 4)), dma((1,)),
+            pltpu.VMEM(half.shape, BF), pltpu.VMEM((2, routes, units), F32), dma((chips,)), dma((1,)),
         ],
     )
     got = swap(send)
-    sources = (keep, got, sums, adapter_a)
-    grads, grad_a, v_own = call(
+    grads, grad_a = call(
         grad_kernel,
-        (sds((2, routes, units), BF), sds((rank, units), F32), sds((routes, rank), BF)),
-        *pin(*sources), places=[slow] * 4,
-        scratch=[pltpu.VMEM(x.shape, x.dtype) for x in sources] + [dma((4,))],
+        (sds((routes, 2 * units + rank), BF), sds((rank, units), F32)),
+        *pin(keep), got, sums, adapter_a, places=[slow] + [near] * 3,
+        scratch=[pltpu.VMEM(keep.shape, F32), dma((1,))],
     )
     grads_other = swap(grads)
-    back = call(
-        back_kernel, sds((chips, routes, width), BF),
-        me, grads, grads_other, w_gate, w_up, half, scalars=1,
-    )
-    backs = over_x(back)
+    back_shape = (chips, routes, width)
+    back, v_pair = call(
+        back_kernel, (pltpu.HBM((chips, routes, width), BF), sds((routes, rank), BF)),
+        me, grads, grads_other, w_gate, w_up, *pin(half), scalars=1, places=[near] * 4 + [slow],
+        ends=(far, near),
+        scratch=[pltpu.VMEM(half.shape, BF), pltpu.VMEM(back_shape, BF), dma((chips,)), dma((chips,))],
+    )
+    code = call(code_kernel, sds((experts, count), F32), ids.T)
+    backs, code = lax.optimization_barrier((over_x(back), code))
     total = call(total_kernel, sds((experts, CAP * width), BF), backs)
     home = route(total.reshape(experts, 2, CAP * width // 2)).reshape(experts, CAP * width)
 
-    v_pair = call(pair_kernel, sds((routes, rank), BF), v_own, swap(v_own))
     v_all = [v_pair] + [shift(v_pair, d) for d in (1, 2, 3)]
-    grad_b, code = call(
-        adapter_kernel, (sds((rank, width), F32), sds((experts, count), F32)), ids.T, *v_all, s_own
-    )
+    grad_b = call(adapter_kernel, sds((rank, width), F32), *v_all, s_own)
     out = call(combine_kernel, sds(tokens.shape, BF), code, home)
     return out, grad_a[None], grad_b[None]
 

time: 166 us -> 168 us (1.012)
  blocking collectives: 22.5 us -> 0 us
  waiting for transfers between devices: 41.9 us -> 63.3 us
  starting transfers between devices: 70.7 us -> 73.5 us
  local copies, waits for them, and re-layouts: 8.42 us -> 5.96 us
  Pallas kernels: 20.7 us -> 22.8 us
    all_to_all x1 -> x0, blocking collectives: 22.5 us -> none  [over_x(): return lax.all_to_all(block, 'x', 0, 0, tiled=True)]
    all_to_all x2 -> x3, waiting for transfers between devices: 9.12 us -> 27.8 us  [over_x(): return lax.all_to_all(block, 'x', 0, 0, tiled=True)]
    all_to_all x2 -> x3, starting transfers between devices: 8.59 us -> 12.8 us  [over_x(): return lax.all_to_all(block, 'x', 0, 0, tiled=True)]
    all_to_all x2, waiting for transfers between devices: 11.1 us -> 14.8 us  [route(): return lax.all_to_all(block, ('z', 'y'), 0, 0, tiled=True)]
    unnamed x37 -> x31, local copies, waits for them, and re-layouts: 7.6 us -> 5.16 us
    pallas_call x11, Pallas kernels: 20.7 us -> 22.8 us  [call(): pl.pallas_call(body, out_shape=outs, in_specs=[smem] * scalars + list(pla...]
    ppermute x6 -> x5, starting transfers between devices: 11.6 us -> 9.72 us  [swap(): return lax.ppermute(block, 'c', [(0, 1), (1, 0)])]
    ppermute x6 -> x5, waiting for transfers between devices: 5.66 us -> 4.41 us  [swap(): return lax.ppermute(block, 'c', [(0, 1), (1, 0)])]
where the time goes in v5:
time: 168 us; the launch traced here: 167 us
  starting transfers between devices  73.5 us (44%)
  waiting for transfers between devices  63.3 us (38%)
  Pallas kernels  22.8 us (14%)
  local copies, waits for them, and re-layouts  5.96 us (4%)
    all_to_all x2, starting transfers between devices, route(): return lax.all_to_all(block, ('z', 'y'), 0, 0, tiled=True)  31.3 us
    all_to_all x3, waiting for transfers between devices, over_x(): return lax.all_to_all(block, 'x', 0, 0, tiled=True)  27.8 us
    pallas_call x11, Pallas kernels, call(): pl.pallas_call(body, out_shape=outs, in_specs=[smem] * scalars + list(pla...  22.8 us
    ppermute x6, starting transfers between devices, shift(): lax.ppermute(block, 'x', [(i, (i + by) % chips) for i in range(chips)])  19.8 us
    ppermute x6, waiting for transfers between devices, shift(): lax.ppermute(block, 'x', [(i, (i + by) % chips) for i in range(chips)])  16.3 us
    all_to_all x2, waiting for transfers between devices, route(): return lax.all_to_all(block, ('z', 'y'), 0, 0, tiled=True)  14.8 us
    all_to_all x3, starting transfers between devices, over_x(): return lax.all_to_all(block, 'x', 0, 0, tiled=True)  12.8 us
    ppermute x5, starting transfers between devices, swap(): return lax.ppermute(block, 'c', [(0, 1), (1, 0)])  9.72 us
  transfers between devices with their start and end apart: 16, of which 13 were waited for; matrix products, arithmetic and copies ran while one was open for 0% of the time, Pallas kernels for 6%

profile of v5, /device:TPU:8, one launch (start us, length us, event | category | flops | bytes accessed | tf_op | source)
XLA Modules:
  0.0 166.6 jit_solution(6229520366350111775)
XLA Ops:
  0.6 0.0 copy-start
  0.6 2.8 %shard_map.112 = bf16[512,640]{1,0:T(8,128)(2,1)} custom-call(s32[8,32]{1,0:T(8,128)} %bitcast.25, f32[8,32]{1,0:T(8,128)} %bitcast.31, bf16[32,512]{1,0:T(8,128)(2,1)} %tok_hbm.1, bf16[32,512]{1,0:T(8,128)(2,1)} %dy_hbm.1), custom_call_target="tpu_custom_call" | custom-call | tf_op jit(solution)/shard_map/pallas_call | solution.py:249
  3.4 18.7 %all-to-all-start = ((bf16[64,8,640]{2,1,0:T(8,128)(2,1)}), bf16[64,8,640]{2,1,0:T(8,128)(2,1)S(1)}, u32[]{:S(2)}, u32[]{:S(2)}) async-start(bf16[64,8,640]{2,1,0:T(8,128)(2,1)} %bitcast.4), calls=%async_computation | async-start | bytes 1310720 | tf_op jit(solution)/shard_map/all_to_all | solution.py:282
  22.2 0.1 pad_add_fusion.me_ref
  22.2 0.0 copy-done
  22.2 1.4 copy-done.1
  23.6 1.4 copy-done.3
  25.1 0.8 shard_map.113
  25.8 0.0 copy-start.6
  25.8 0.8 copy-done.6
  26.6 1.9 %collective-permute-start = (bf16[2,4,192,512]{3,2,1,0:T(8,128)(2,1)S(1)}, bf16[2,4,192,512]{3,2,1,0:T(8,128)(2,1)}, u32[]{:S(2)}, u32[]{:S(2)}) collective-permute-start(bf16[2,4,192,512]{3,2,1,0:T(8,128)(2,1)S(1)} %get-tuple-element.25), channel_id=1, source_target_pairs={{0,64},{64,0},{1,65},{65,1},{2,66},{66,2},{3,67},{67,3},{4,68},{68... | collective-permute-start | bytes 4718600 | tf_op jit(solution)/shard_map/ppermute | solution.py:273
  28.5 3.4 %collective-permute-start.2 = (bf16[192,1024]{1,0:T(8,128)(2,1)S(1)}, bf16[192,1024]{1,0:T(8,128)(2,1)S(1)}, u32[]{:S(2)}, u32[]{:S(2)}) collective-permute-start(bf16[192,1024]{1,0:T(8,128)(2,1)S(1)} %get-tuple-element.27), channel_id=1, source_target_pairs={{0,128},{128,256},{256,384},{384,0},{1,129},{129,257},{257,385},{3... | collective-permute-start | bytes 1179656 | tf_op jit(solution)/shard_map/ppermute | solution.py:276
  31.9 4.6 %collective-permute-start.3 = (bf16[192,1024]{1,0:T(8,128)(2,1)S(1)}, bf16[192,1024]{1,0:T(8,128)(2,1)S(1)}, u32[]{:S(2)}, u32[]{:S(2)}) collective-permute-start(bf16[192,1024]{1,0:T(8,128)(2,1)S(1)} %get-tuple-element.28), channel_id=1, source_target_pairs={{0,256},{128,384},{256,0},{384,128},{1,257},{129,385},{257,1},{385... | collective-permute-start | bytes 1179656 | tf_op jit(solution)/shard_map/ppermute | solution.py:276
  36.6 3.3 %collective-permute-start.4 = (bf16[192,1024]{1,0:T(8,128)(2,1)S(1)}, bf16[192,1024]{1,0:T(8,128)(2,1)S(1)}, u32[]{:S(2)}, u32[]{:S(2)}) collective-permute-start(bf16[192,1024]{1,0:T(8,128)(2,1)S(1)} %get-tuple-element.29), channel_id=1, source_target_pairs={{0,384},{128,0},{256,128},{384,256},{1,385},{129,1},{257,129},{385... | collective-permute-start | bytes 1179656 | tf_op jit(solution)/shard_map/ppermute | solution.py:276
  39.9 0.0 copy-done.13
  40.0 1.9 %collective-permute-start.1 = (bf16[64,512]{1,0:T(8,128)(2,1)S(1)}, bf16[64,512]{1,0:T(8,128)(2,1)S(1)}, u32[]{:S(2)}, u32[]{:S(2)}) collective-permute-start(bf16[64,512]{1,0:T(8,128)(2,1)S(1)} %bitcast.30), channel_id=1, source_target_pairs={{0,64},{64,0},{1,65},{65,1},{2,66},{66,2},{3,67},{67,3},{4,68},{68... | collective-permute-start | bytes 196616 | tf_op jit(solution)/shard_map/ppermute | solution.py:273
  41.9 1.2 collective-permute-done.1.refs_3_
  43.1 0.1 collective-permute-done.2.refs_5_
  43.2 9.4 %collective-permute-done.3.refs_6_ = bf16[192,1024]{1,0:T(8,128)(2,1)S(1)} collective-permute-done((bf16[192,1024]{1,0:T(8,128)(2,1)S(1)}, bf16[192,1024]{1,0:T(8,128)(2,1)S(1)}, u32[]{:S(2)}, u32[]{:S(2)}) %collective-permute-start.3) | collective-permute-done | bytes 393248 | tf_op jit(solution)/shard_map/ppermute | solution.py:276
  52.6 1.5 collective-permute-done.4.refs_7_
  54.1 0.0 copy-done.14
  54.1 0.0 copy-done.9
  54.1 0.0 copy-done.10
  54.1 0.0 copy-start.11
  54.1 0.8 copy-done.11
  54.9 0.0 collective-permute-done.half_hbm
  54.9 5.6 %all-to-all-done = bf16[64,8,640]{2,1,0:T(8,128)(2,1)S(1)} async-done(((bf16[64,8,640]{2,1,0:T(8,128)(2,1)}), bf16[64,8,640]{2,1,0:T(8,128)(2,1)S(1)}, u32[]{:S(2)}, u32[]{:S(2)}) %all-to-all-start) | async-done | bytes 655392 | tf_op jit(solution)/shard_map/all_to_all | solution.py:282
  60.5 1.8 %shard_map.114 = (bf16[4,320,512]{2,1,0:T(8,128)(2,1)}, bf16[320,512]{1,0:T(8,128)(2,1)}) custom-call(bf16[512,640]{1,0:T(8,128)(2,1)S(1)} %bitcast.21), custom_call_target="tpu_custom_call" | custom-call | tf_op jit(solution)/shard_map/pallas_call | solution.py:249
  62.2 0.0 copy-start.4
  62.3 4.4 %all-to-all-start.1 = ((bf16[4,320,512]{2,1,0:T(8,128)(2,1)}), bf16[4,320,512]{2,1,0:T(8,128)(2,1)}, u32[]{:S(2)}, u32[]{:S(2)}) async-start(bf16[4,320,512]{2,1,0:T(8,128)(2,1)} %get-tuple-element.31), calls=%async_computation.1 | async-start | bytes 2621440 | tf_op jit(solution)/shard_map/all_to_all | solution.py:279
  66.7 0.0 copy-start.2
  66.7 2.1 %collective-permute-start.6 = (bf16[320,512]{1,0:T(8,128)(2,1)S(1)}, bf16[320,512]{1,0:T(8,128)(2,1)S(1)}, u32[]{:S(2)}, u32[]{:S(2)}) collective-permute-start(bf16[320,512]{1,0:T(8,128)(2,1)S(1)} %copy-done.4), channel_id=1, source_target_pairs={{0,64},{64,0},{1,65},{65,1},{2,66},{66,2},{3,67},{67,3},{4,68},{68... | collective-permute-start | bytes 983048 | tf_op jit(solution)/shard_map/ppermute | solution.py:273
  68.8 1.6 collective-permute-done.6.refs_1_
  70.4 0.7 copy-done.12
  71.1 4.0 %shard_map.116 = bf16[4,320,256]{2,1,0:T(8,128)(2,1)} custom-call(s32[2]{0:T(128)S(1)} %pad_add_fusion.me_ref, bf16[320,512]{1,0:T(8,128)(2,1)} %get-tuple-element.35.refs_0_.s_ref, bf16[320,512]{1,0:T(8,128)(2,1)} %copy-done.12, bf16[64,512]{1,0:T(8,128)(2,1)} %bitcast.29, bf16[64,512]{1,0:T(8,128)(2,1)} %copy-done.14, bf16[192,1024]{1,0:T(8,128)(2,1)} %copy-done.6, ...), custom_call_target="tpu_custom_call" | custom-call | tf_op jit(solution)/shard_map/pallas_call | solution.py:249
  75.1 7.3 %all-to-all-done.1.x_ref = bf16[4,320,512]{2,1,0:T(8,128)(2,1)} async-done(((bf16[4,320,512]{2,1,0:T(8,128)(2,1)}), bf16[4,320,512]{2,1,0:T(8,128)(2,1)}, u32[]{:S(2)}, u32[]{:S(2)}) %all-to-all-start.1) | async-done | bytes 1310752 | tf_op jit(solution)/shard_map/all_to_all | solution.py:279
  82.5 4.2 %all-to-all-start.2 = ((bf16[4,320,256]{2,1,0:T(8,128)(2,1)}), bf16[4,320,256]{2,1,0:T(8,128)(2,1)}, u32[]{:S(2)}, u32[]{:S(2)}) async-start(bf16[4,320,256]{2,1,0:T(8,128)(2,1)} %shard_map.116), calls=%async_computation.2 | async-start | bytes 1310720 | tf_op jit(solution)/shard_map/all_to_all | solution.py:279
  86.7 0.0 copy-start.7
  86.7 4.5 %shard_map.115 = (f32[2,320,192]{2,1,0:T(8,128)}, bf16[2,320,192]{2,1,0:T(8,128)(2,1)}) custom-call(s32[2]{0:T(128)S(1)} %pad_add_fusion.me_ref, bf16[4,320,512]{2,1,0:T(8,128)(2,1)} %all-to-all-done.1.x_ref, bf16[192,4096]{1,0:T(8,128)(2,1)S(1)} %bitcast.16, bf16[192,4096]{1,0:T(8,128)(2,1)S(1)} %bitcast.19, ...), custom_call_target="tpu_custom_call" | custom-call | tf_op jit(solution)/shard_map/pallas_call | solution.py:249
  91.2 1.9 %collective-permute-start.5 = (bf16[2,320,192]{2,1,0:T(8,128)(2,1)}, bf16[2,320,192]{2,1,0:T(8,128)(2,1)S(1)}, u32[]{:S(2)}, u32[]{:S(2)}) collective-permute-start(bf16[2,320,192]{2,1,0:T(8,128)(2,1)} %get-tuple-element.34), channel_id=1, source_target_pairs={{0,64},{64,0},{1,65},{65,1},{2,66},{66,2},{3,67},{67,3},{4,68},{68... | collective-permute-start | bytes 737288 | tf_op jit(solution)/shard_map/ppermute | solution.py:273
  93.1 2.4 %all-to-all-done.2.in_ref = bf16[4,320,256]{2,1,0:T(8,128)(2,1)} async-done(((bf16[4,320,256]{2,1,0:T(8,128)(2,1)}), bf16[4,320,256]{2,1,0:T(8,128)(2,1)}, u32[]{:S(2)}, u32[]{:S(2)}) %all-to-all-start.2) | async-done | bytes 655392 | tf_op jit(solution)/shard_map/all_to_all | solution.py:279
  95.5 0.0 collective-permute-done.5.got_ref
  95.5 0.0 copy-done.7
  95.5 3.1 %shard_map.117 = (bf16[320,448]{1,0:T(8,128)(2,1)S(1)}, f32[64,192]{1,0:T(8,128)}) custom-call(f32[2,320,192]{2,1,0:T(8,128)} %get-tuple-element.33.keep_hbm, bf16[2,320,192]{2,1,0:T(8,128)(2,1)S(1)} %collective-permute-done.5.got_ref, bf16[4,320,256]{2,1,0:T(8,128)(2,1)} %all-to-all-done.2.in_ref, bf16[64,192]{1,0:T(8,128)(2,1)S(1)} %bitcast.24), custom_call_target="tpu_custom_call" | custom-call | tf_op jit(solution)/shard_map/pallas_call | solution.py:249
  98.6 1.9 %collective-permute-start.7 = (bf16[320,448]{1,0:T(8,128)(2,1)S(1)}, bf16[320,448]{1,0:T(8,128)(2,1)S(1)}, u32[]{:S(2)}, u32[]{:S(2)}) collective-permute-start(bf16[320,448]{1,0:T(8,128)(2,1)S(1)} %get-tuple-element.41.g_ref), channel_id=1, source_target_pairs={{0,64},{64,0},{1,65},{65,1},{2,66},{66,2},{3,67},{67,3},{4,68},{68... | collective-permute-start | bytes 860168 | tf_op jit(solution)/shard_map/ppermute | solution.py:273
  100.5 1.6 collective-permute-done.7.h_ref
  102.1 3.9 %shard_map.118 = (bf16[4,320,512]{2,1,0:T(8,128)(2,1)}, bf16[320,64]{1,0:T(8,128)(2,1)S(1)}) custom-call(s32[2]{0:T(128)S(1)} %pad_add_fusion.me_ref, bf16[320,448]{1,0:T(8,128)(2,1)S(1)} %get-tuple-element.41.g_ref, bf16[320,448]{1,0:T(8,128)(2,1)S(1)} %collective-permute-done.7.h_ref, bf16[192,4096]{1,0:T(8,128)(2,1)S(1)} %bitcast.17, ...), custom_call_target="tpu_custom_call" | custom-call | tf_op jit(solution)/shard_map/pallas_call | solution.py:249
  106.0 0.0 copy-start.8
  106.0 4.2 %all-to-all-start.3 = ((bf16[4,320,512]{2,1,0:T(8,128)(2,1)}), bf16[4,320,512]{2,1,0:T(8,128)(2,1)S(1)}, u32[]{:S(2)}, u32[]{:S(2)}) async-start(bf16[4,320,512]{2,1,0:T(8,128)(2,1)} %get-tuple-element.42), calls=%async_computation.3 | async-start | bytes 2621440 | tf_op jit(solution)/shard_map/all_to_all | solution.py:279
  110.2 0.1 shard_map.119.code_ref
  110.3 18.1 %all-to-all-done.3.in_ref = bf16[4,320,512]{2,1,0:T(8,128)(2,1)S(1)} async-done(((bf16[4,320,512]{2,1,0:T(8,128)(2,1)}), bf16[4,320,512]{2,1,0:T(8,128)(2,1)S(1)}, u32[]{:S(2)}, u32[]{:S(2)}) %all-to-all-start.3) | async-done | bytes 1310752 | tf_op jit(solution)/shard_map/all_to_all | solution.py:279
  128.4 0.2 shard_map.120
  128.5 0.8 reshape.20
  129.3 12.6 %all-to-all-start.4 = ((bf16[64,2,1280]{2,1,0:T(2,128)(2,1)}), bf16[64,2,1280]{2,1,0:T(2,128)(2,1)S(1)}, u32[]{:S(2)}, u32[]{:S(2)}) async-start(bf16[64,2,1280]{2,1,0:T(2,128)(2,1)} %reshape.20), calls=%async_computation.4 | async-start | bytes 655360 | tf_op jit(solution)/shard_map/all_to_all | solution.py:282
  141.9 3.1 %collective-permute-start.10 = (bf16[320,64]{1,0:T(8,128)(2,1)S(1)}, bf16[320,64]{1,0:T(8,128)(2,1)S(1)}, u32[]{:S(2)}, u32[]{:S(2)}) collective-permute-start(bf16[320,64]{1,0:T(8,128)(2,1)S(1)} %get-tuple-element.46.v0_ref), channel_id=1, source_target_pairs={{0,384},{128,0},{256,128},{384,256},{1,385},{129,1},{257,129},{385... | collective-permute-start | bytes 122888 | tf_op jit(solution)/shard_map/ppermute | solution.py:276
  145.0 2.8 %collective-permute-start.8 = (bf16[320,64]{1,0:T(8,128)(2,1)S(1)}, bf16[320,64]{1,0:T(8,128)(2,1)S(1)}, u32[]{:S(2)}, u32[]{:S(2)}) collective-permute-start(bf16[320,64]{1,0:T(8,128)(2,1)S(1)} %get-tuple-element.46.v0_ref), channel_id=1, source_target_pairs={{0,128},{128,256},{256,384},{384,0},{1,129},{129,257},{257,385},{3... | collective-permute-start | bytes 122888 | tf_op jit(solution)/shard_map/ppermute | solution.py:276
  147.8 2.5 %collective-permute-start.9 = (bf16[320,64]{1,0:T(8,128)(2,1)S(1)}, bf16[320,64]{1,0:T(8,128)(2,1)S(1)}, u32[]{:S(2)}, u32[]{:S(2)}) collective-permute-start(bf16[320,64]{1,0:T(8,128)(2,1)S(1)} %get-tuple-element.46.v0_ref), channel_id=1, source_target_pairs={{0,256},{128,384},{256,0},{384,128},{1,257},{129,385},{257,1},{385... | collective-permute-start | bytes 122888 | tf_op jit(solution)/shard_map/ppermute | solution.py:276
  150.3 0.0 collective-permute-done.10.v3_ref
  150.3 3.1 %collective-permute-done.8.v1_ref = bf16[320,64]{1,0:T(8,128)(2,1)S(1)} collective-permute-done((bf16[320,64]{1,0:T(8,128)(2,1)S(1)}, bf16[320,64]{1,0:T(8,128)(2,1)S(1)}, u32[]{:S(2)}, u32[]{:S(2)}) %collective-permute-start.8) | collective-permute-done | bytes 40992 | tf_op jit(solution)/shard_map/ppermute | solution.py:276
  153.4 2.2 %collective-permute-done.9.v2_ref = bf16[320,64]{1,0:T(8,128)(2,1)S(1)} collective-permute-done((bf16[320,64]{1,0:T(8,128)(2,1)S(1)}, bf16[320,64]{1,0:T(8,128)(2,1)S(1)}, u32[]{:S(2)}, u32[]{:S(2)}) %collective-permute-start.9) | collective-permute-done | bytes 40992 | tf_op jit(solution)/shard_map/ppermute | solution.py:276
  155.6 0.0 copy-done.5
  155.6 0.9 shard_map.122
  156.5 9.2 %all-to-all-done.4 = bf16[64,2,1280]{2,1,0:T(2,128)(2,1)S(1)} async-done(((bf16[64,2,1280]{2,1,0:T(2,128)(2,1)}), bf16[64,2,1280]{2,1,0:T(2,128)(2,1)S(1)}, u32[]{:S(2)}, u32[]{:S(2)}) %all-to-all-start.4) | async-done | bytes 327712 | tf_op jit(solution)/shard_map/all_to_all | solution.py:282
  165.8 0.8 shard_map.121
  (12 shorter events, 0.1 us)
Async XLA Ops:
  0.6 21.6 %copy-start = (bf16[1,192,4096]{2,1,0:T(8,128)(2,1)S(1)}, bf16[1,192,4096]{2,1,0:T(8,128)(2,1)}, u32[]{:S(2)}) copy-start(bf16[1,192,4096]{2,1,0:T(8,128)(2,1)} %param.13) | copy-start | bytes 4718596
  3.4 57.1 %all-to-all-start = ((bf16[64,8,640]{2,1,0:T(8,128)(2,1)}), bf16[64,8,640]{2,1,0:T(8,128)(2,1)S(1)}, u32[]{:S(2)}, u32[]{:S(2)}) async-start(bf16[64,8,640]{2,1,0:T(8,128)(2,1)} %bitcast.4), calls=%async_computation | async-start | bytes 1310720 | tf_op jit(solution)/shard_map/all_to_all | solution.py:282
  22.2 1.4 copy-start.1
  23.6 1.4 copy-start.3
  25.1 14.9 %copy-start.13 = (bf16[1,64,512]{2,1,0:T(8,128)(2,1)S(1)}, bf16[1,64,512]{2,1,0:T(8,128)(2,1)}, u32[]{:S(2)}) copy-start(bf16[1,64,512]{2,1,0:T(8,128)(2,1)} %param.17) | copy-start | bytes 196612
  25.8 0.8 copy-start.6
  26.6 28.3 %collective-permute-start = (bf16[2,4,192,512]{3,2,1,0:T(8,128)(2,1)S(1)}, bf16[2,4,192,512]{3,2,1,0:T(8,128)(2,1)}, u32[]{:S(2)}, u32[]{:S(2)}) collective-permute-start(bf16[2,4,192,512]{3,2,1,0:T(8,128)(2,1)S(1)} %get-tuple-element.25), channel_id=1, source_target_pairs={{0,64},{64,0},{1,65},{65,1},{2,66},{66,2},{3,67},{67,3},{4,68},{68... | collective-permute-start | bytes 4718600 | tf_op jit(solution)/shard_map/ppermute | solution.py:273
  28.5 14.6 %collective-permute-start.2 = (bf16[192,1024]{1,0:T(8,128)(2,1)S(1)}, bf16[192,1024]{1,0:T(8,128)(2,1)S(1)}, u32[]{:S(2)}, u32[]{:S(2)}) collective-permute-start(bf16[192,1024]{1,0:T(8,128)(2,1)S(1)} %get-tuple-element.27), channel_id=1, source_target_pairs={{0,128},{128,256},{256,384},{384,0},{1,129},{129,257},{257,385},{3... | collective-permute-start | bytes 1179656 | tf_op jit(solution)/shard_map/ppermute | solution.py:276
  31.9 20.6 %collective-permute-start.3 = (bf16[192,1024]{1,0:T(8,128)(2,1)S(1)}, bf16[192,1024]{1,0:T(8,128)(2,1)S(1)}, u32[]{:S(2)}, u32[]{:S(2)}) collective-permute-start(bf16[192,1024]{1,0:T(8,128)(2,1)S(1)} %get-tuple-element.28), channel_id=1, source_target_pairs={{0,256},{128,384},{256,0},{384,128},{1,257},{129,385},{257,1},{385... | collective-permute-start | bytes 1179656 | tf_op jit(solution)/shard_map/ppermute | solution.py:276
  36.6 17.5 %collective-permute-start.4 = (bf16[192,1024]{1,0:T(8,128)(2,1)S(1)}, bf16[192,1024]{1,0:T(8,128)(2,1)S(1)}, u32[]{:S(2)}, u32[]{:S(2)}) collective-permute-start(bf16[192,1024]{1,0:T(8,128)(2,1)S(1)} %get-tuple-element.29), channel_id=1, source_target_pairs={{0,384},{128,0},{256,128},{384,256},{1,385},{129,1},{257,129},{385... | collective-permute-start | bytes 1179656 | tf_op jit(solution)/shard_map/ppermute | solution.py:276
  40.0 3.1 %collective-permute-start.1 = (bf16[64,512]{1,0:T(8,128)(2,1)S(1)}, bf16[64,512]{1,0:T(8,128)(2,1)S(1)}, u32[]{:S(2)}, u32[]{:S(2)}) collective-permute-start(bf16[64,512]{1,0:T(8,128)(2,1)S(1)} %bitcast.30), channel_id=1, source_target_pairs={{0,64},{64,0},{1,65},{65,1},{2,66},{66,2},{3,67},{67,3},{4,68},{68... | collective-permute-start | bytes 196616 | tf_op jit(solution)/shard_map/ppermute | solution.py:273
  43.1 11.0 %copy-start.14 = (bf16[64,512]{1,0:T(8,128)(2,1)}, bf16[64,512]{1,0:T(8,128)(2,1)S(1)}, u32[]{:S(2)}) copy-start(bf16[64,512]{1,0:T(8,128)(2,1)S(1)} %collective-permute-done.1.refs_3_) | copy-start | bytes 196612
  43.2 11.0 %copy-start.9 = (bf16[192,1024]{1,0:T(8,128)(2,1)}, bf16[192,1024]{1,0:T(8,128)(2,1)S(1)}, u32[]{:S(2)}) copy-start(bf16[192,1024]{1,0:T(8,128)(2,1)S(1)} %collective-permute-done.2.refs_5_) | copy-start | bytes 1179652
  52.6 1.6 copy-start.10
  54.1 0.8 copy-start.11
  62.2 4.4 %copy-start.4 = (bf16[320,512]{1,0:T(8,128)(2,1)S(1)}, bf16[320,512]{1,0:T(8,128)(2,1)}, u32[]{:S(2)}) copy-start(bf16[320,512]{1,0:T(8,128)(2,1)} %get-tuple-element.35.refs_0_.s_ref) | copy-start | bytes 983044
  62.3 20.2 %all-to-all-start.1 = ((bf16[4,320,512]{2,1,0:T(8,128)(2,1)}), bf16[4,320,512]{2,1,0:T(8,128)(2,1)}, u32[]{:S(2)}, u32[]{:S(2)}) async-start(bf16[4,320,512]{2,1,0:T(8,128)(2,1)} %get-tuple-element.31), calls=%async_computation.1 | async-start | bytes 2621440 | tf_op jit(solution)/shard_map/all_to_all | solution.py:279
  66.7 19.9 %copy-start.2 = (bf16[1,192,4096]{2,1,0:T(8,128)(2,1)S(1)}, bf16[1,192,4096]{2,1,0:T(8,128)(2,1)}, u32[]{:S(2)}) copy-start(bf16[1,192,4096]{2,1,0:T(8,128)(2,1)} %param.14) | copy-start | bytes 4718596
  66.7 3.7 %collective-permute-start.6 = (bf16[320,512]{1,0:T(8,128)(2,1)S(1)}, bf16[320,512]{1,0:T(8,128)(2,1)S(1)}, u32[]{:S(2)}, u32[]{:S(2)}) collective-permute-start(bf16[320,512]{1,0:T(8,128)(2,1)S(1)} %copy-done.4), channel_id=1, source_target_pairs={{0,64},{64,0},{1,65},{65,1},{2,66},{66,2},{3,67},{67,3},{4,68},{68... | collective-permute-start | bytes 983048 | tf_op jit(solution)/shard_map/ppermute | solution.py:273
  70.4 0.7 copy-start.12
  82.5 13.0 %all-to-all-start.2 = ((bf16[4,320,256]{2,1,0:T(8,128)(2,1)}), bf16[4,320,256]{2,1,0:T(8,128)(2,1)}, u32[]{:S(2)}, u32[]{:S(2)}) async-start(bf16[4,320,256]{2,1,0:T(8,128)(2,1)} %shard_map.116), calls=%async_computation.2 | async-start | bytes 1310720 | tf_op jit(solution)/shard_map/all_to_all | solution.py:279
  86.7 8.8 %copy-start.7 = (bf16[1,64,192]{2,1,0:T(8,128)(2,1)S(1)}, bf16[1,64,192]{2,1,0:T(8,128)(2,1)}, u32[]{:S(2)}) copy-start(bf16[1,64,192]{2,1,0:T(8,128)(2,1)} %param.16) | copy-start | bytes 73732
  91.2 4.3 %collective-permute-start.5 = (bf16[2,320,192]{2,1,0:T(8,128)(2,1)}, bf16[2,320,192]{2,1,0:T(8,128)(2,1)S(1)}, u32[]{:S(2)}, u32[]{:S(2)}) collective-permute-start(bf16[2,320,192]{2,1,0:T(8,128)(2,1)} %get-tuple-element.34), channel_id=1, source_target_pairs={{0,64},{64,0},{1,65},{65,1},{2,66},{66,2},{3,67},{67,3},{4,68},{68... | collective-permute-start | bytes 737288 | tf_op jit(solution)/shard_map/ppermute | solution.py:273
  98.6 3.5 %collective-permute-start.7 = (bf16[320,448]{1,0:T(8,128)(2,1)S(1)}, bf16[320,448]{1,0:T(8,128)(2,1)S(1)}, u32[]{:S(2)}, u32[]{:S(2)}) collective-permute-start(bf16[320,448]{1,0:T(8,128)(2,1)S(1)} %get-tuple-element.41.g_ref), channel_id=1, source_target_pairs={{0,64},{64,0},{1,65},{65,1},{2,66},{66,2},{3,67},{67,3},{4,68},{68... | collective-permute-start | bytes 860168 | tf_op jit(solution)/shard_map/ppermute | solution.py:273
  106.0 4.2 %copy-start.8 = (s32[32,8]{0,1:T(8,128)S(1)}, s32[32,8]{0,1:T(8,128)}, u32[]{:S(2)}) copy-start(s32[32,8]{0,1:T(8,128)} %param.12) | copy-start | bytes 3076
  106.0 22.4 %all-to-all-start.3 = ((bf16[4,320,512]{2,1,0:T(8,128)(2,1)}), bf16[4,320,512]{2,1,0:T(8,128)(2,1)S(1)}, u32[]{:S(2)}, u32[]{:S(2)}) async-start(bf16[4,320,512]{2,1,0:T(8,128)(2,1)} %get-tuple-element.42), calls=%async_computation.3 | async-start | bytes 2621440 | tf_op jit(solution)/shard_map/all_to_all | solution.py:279
  110.2 45.4 %copy-start.5 = (bf16[320,512]{1,0:T(8,128)(2,1)S(1)}, bf16[320,512]{1,0:T(8,128)(2,1)}, u32[]{:S(2)}) copy-start(bf16[320,512]{1,0:T(8,128)(2,1)} %get-tuple-element.35.refs_0_.s_ref) | copy-start | bytes 983044
  129.3 36.4 %all-to-all-start.4 = ((bf16[64,2,1280]{2,1,0:T(2,128)(2,1)}), bf16[64,2,1280]{2,1,0:T(2,128)(2,1)S(1)}, u32[]{:S(2)}, u32[]{:S(2)}) async-start(bf16[64,2,1280]{2,1,0:T(2,128)(2,1)} %reshape.20), calls=%async_computation.4 | async-start | bytes 655360 | tf_op jit(solution)/shard_map/all_to_all | solution.py:282
  141.9 8.4 %collective-permute-start.10 = (bf16[320,64]{1,0:T(8,128)(2,1)S(1)}, bf16[320,64]{1,0:T(8,128)(2,1)S(1)}, u32[]{:S(2)}, u32[]{:S(2)}) collective-permute-start(bf16[320,64]{1,0:T(8,128)(2,1)S(1)} %get-tuple-element.46.v0_ref), channel_id=1, source_target_pairs={{0,384},{128,0},{256,128},{384,256},{1,385},{129,1},{257,129},{385... | collective-permute-start | bytes 122888 | tf_op jit(solution)/shard_map/ppermute | solution.py:276
  145.0 8.4 %collective-permute-start.8 = (bf16[320,64]{1,0:T(8,128)(2,1)S(1)}, bf16[320,64]{1,0:T(8,128)(2,1)S(1)}, u32[]{:S(2)}, u32[]{:S(2)}) collective-permute-start(bf16[320,64]{1,0:T(8,128)(2,1)S(1)} %get-tuple-element.46.v0_ref), channel_id=1, source_target_pairs={{0,128},{128,256},{256,384},{384,0},{1,129},{129,257},{257,385},{3... | collective-permute-start | bytes 122888 | tf_op jit(solution)/shard_map/ppermute | solution.py:276
  147.8 7.8 %collective-permute-start.9 = (bf16[320,64]{1,0:T(8,128)(2,1)S(1)}, bf16[320,64]{1,0:T(8,128)(2,1)S(1)}, u32[]{:S(2)}, u32[]{:S(2)}) collective-permute-start(bf16[320,64]{1,0:T(8,128)(2,1)S(1)} %get-tuple-element.46.v0_ref), channel_id=1, source_target_pairs={{0,256},{128,384},{256,0},{384,128},{1,257},{129,385},{257,1},{385... | collective-permute-start | bytes 122888 | tf_op jit(solution)/shard_map/ppermute | solution.py:276

commit v6 on v5

--- a/solution.py
+++ b/solution.py
@@ -9,6 +9,7 @@
 BF = jnp.bfloat16
 F32 = jnp.float32
 LANE = 128
+FLAT = 4
 PARAMS = pltpu.CompilerParams(vmem_limit_bytes=16 * 1024 * 1024)
 
 
@@ -36,6 +37,11 @@
         copy.wait()
 
 
+def expert_of(place, experts):
+    deep = experts // FLAT
+    return lax.rem(place, deep) * FLAT + lax.div(place, deep)
+
+
 def pack_kernel(ids_hbm, prob_hbm, tok_hbm, dy_hbm, out_ref, ids_ref, prob_ref, tok_ref, dy_ref, sems):
     fetch(
         [(ids_hbm, ids_ref), (prob_hbm, prob_ref), (tok_hbm, tok_ref), (dy_hbm, dy_ref)], sems
@@ -45,7 +51,7 @@
     parts = 2 * width // LANE
     span = parts * count
     row = lax.broadcasted_iota(jnp.int32, (rows, count), 0)
-    own = lax.div(row, parts)
+    own = expert_of(lax.div(row, parts), rows // parts)
     hit = jnp.zeros((rows, count), F32)
     weight = jnp.zeros((rows, count), F32)
     for k in range(ids_ref.shape[0]):
@@ -72,7 +78,7 @@
 
 def code_of(ids, experts):
     count = ids.shape[1]
-    own = lax.broadcasted_iota(jnp.int32, (experts, count), 0)
+    own = expert_of(lax.broadcasted_iota(jnp.int32, (experts, count), 0), experts)
     hit = jnp.zeros((experts, count), F32)
     for k in range(ids.shape[0]):
         hit = jnp.where(ids[k : k + 1, :] == own, 1.0, hit)
@@ -103,15 +109,16 @@
     fetch([(x_ref, x_hbm.at[x]) for x in range(chips)] + [(s_ref, s_hbm)], sems)
 
 
-def prep_kernel(me_ref, wg_ref, wu_ref, wd_ref, swap_ref, d0_ref, d1_ref, d2_ref, d3_ref):
+def prep_kernel(me_ref, wg_ref, wu_ref, wd_ref, own_ref, swap_ref, d0_ref, d1_ref, d2_ref, d3_ref):
     chip, core = me_ref[0], me_ref[1]
     chips, units, width = swap_ref.shape[1:]
-    for x in range(chips):
-        cols = lanes(2 * x + 1 - core, width)
-        swap_ref[0, x] = wg_ref[:, cols]
-        swap_ref[1, x] = wu_ref[:, cols]
     for d, ref in enumerate((d0_ref, d1_ref, d2_ref, d3_ref)):
         ref[...] = wd_ref[:, lanes(lax.rem(chip + d, chips), 2 * width)]
+    for x in range(chips):
+        for ref, which in ((own_ref, core), (swap_ref, 1 - core)):
+            cols = lanes(2 * x + which, width)
+            ref[0, x] = wg_ref[:, cols]
+            ref[1, x] = wu_ref[:, cols]
 
 
 def part_kernel(me_ref, *refs):
@@ -131,35 +138,19 @@
     fetch([(out_ref, out_hbm)], sems)
 
 
-def stream(half_hbm, half_ref, sems):
-    copies = [
-        pltpu.make_async_copy(half_hbm.at[:, x], half_ref.at[:, x], sems.at[x])
-        for x in range(half_ref.shape[1])
-    ]
-    for copy in copies:
-        copy.start()
-    return copies
-
-
-def gate_kernel(
-    me_ref, x_ref, wg_ref, wu_ref, half_hbm, keep_hbm, send_ref, half_ref, keep_ref, sems, sem
-):
-    core = me_ref[1]
+def gate_kernel(x_ref, own_ref, half_ref, keep_hbm, send_ref, keep_ref, sem):
     chips, routes, width = x_ref.shape
-    units = wg_ref.shape[0]
-    copies = stream(half_hbm, half_ref, sems)
+    units = own_ref.shape[2]
     keep = [jnp.zeros((routes, units), F32)] * 2
     send = [jnp.zeros((routes, units), F32)] * 2
     for x in range(chips):
-        cols = lanes(2 * x + core, width)
-        keep[0] = keep[0] + nt(x_ref[x], wg_ref[:, cols])
-        keep[1] = keep[1] + nt(x_ref[x], wu_ref[:, cols])
+        for i in range(2):
+            keep[i] = keep[i] + nt(x_ref[x], own_ref[i, x])
     for i in range(2):
         keep_ref[i] = keep[i]
     store = pltpu.make_async_copy(keep_ref, keep_hbm, sem.at[0])
     store.start()
     for x in range(chips):
-        copies[x].wait()
         for i in range(2):
             send[i] = send[i] + nt(x_ref[x], half_ref[i, x])
     for i in range(2):
@@ -167,47 +158,38 @@
     store.wait()
 
 
-def grad_kernel(keep_hbm, got_ref, in_ref, a_ref, out_ref, ga_ref, keep_ref, sem):
-    fetch_keep = pltpu.make_async_copy(keep_hbm, keep_ref, sem.at[0])
-    fetch_keep.start()
+def grad_kernel(keep_hbm, got_hbm, in_hbm, a_hbm, out_ref, ga_ref, keep_ref, got_ref, in_ref, a_ref, sems):
+    fetch([(keep_hbm, keep_ref), (got_hbm, got_ref), (in_hbm, in_ref), (a_hbm, a_ref)], sems)
     units = keep_ref.shape[2]
     total = in_ref[0].astype(F32)
     for x in range(1, in_ref.shape[0]):
         total += in_ref[x].astype(F32)
     low_u = total[:, units:].astype(BF)
     grad = total[:, :units] + nn(low_u, a_ref[...])
-    fetch_keep.wait()
     gate = keep_ref[0] + got_ref[0].astype(F32)
     up = keep_ref[1] + got_ref[1].astype(F32)
     sigma = jax.nn.sigmoid(gate)
     active = gate * sigma
     hidden = (active * up).astype(BF)
     ga_ref[...] = tn(low_u, hidden)
-    grad_gate = (grad * up * sigma * (1.0 + gate * (1.0 - sigma))).astype(BF)
-    grad_up = (grad * active).astype(BF)
+    out_ref[:, :units] = (grad * up * sigma * (1.0 + gate * (1.0 - sigma))).astype(BF)
     low_v = nt(hidden, a_ref[...]).astype(BF)
-    out_ref[...] = jnp.concatenate([grad_gate, grad_up, low_v], axis=1)
-
-
-def back_kernel(
-    me_ref, g_ref, h_ref, wg_ref, wu_ref, half_hbm, out_hbm, v_ref, half_ref, out_ref, sems, out_sems
-):
-    core = me_ref[1]
-    chips, _, width = out_ref.shape
-    units = wg_ref.shape[0]
-    copies = stream(half_hbm, half_ref, sems)
+    out_ref[:, units:] = jnp.concatenate([(grad * active).astype(BF), low_v], axis=1)
+
+
+def back_kernel(g_ref, h_ref, own_ref, half_ref, out_hbm, v_ref, out_ref, out_sems):
+    chips = out_ref.shape[0]
+    units = own_ref.shape[2]
     mine = [g_ref[:, i * units : (i + 1) * units] for i in range(2)]
     other = [h_ref[:, i * units : (i + 1) * units] for i in range(2)]
     stores = []
-    v_ref[...] = (g_ref[:, 2 * units :].astype(F32) + h_ref[:, 2 * units :].astype(F32)).astype(BF)
     for x in range(chips):
-        cols = lanes(2 * x + core, width)
-        term = nn(mine[0], wg_ref[:, cols]) + nn(mine[1], wu_ref[:, cols])
-        copies[x].wait()
+        term = nn(mine[0], own_ref[0, x]) + nn(mine[1], own_ref[1, x])
         term += nn(other[0], half_ref[0, x]) + nn(other[1], half_ref[1, x])
         out_ref[x] = term.astype(BF)
         stores.append(pltpu.make_async_copy(out_ref.at[x], out_hbm.at[x], out_sems.at[x]))
         stores[x].start()
+    v_ref[...] = (g_ref[:, 2 * units :].astype(F32) + h_ref[:, 2 * units :].astype(F32)).astype(BF)
     for store in stores:
         store.wait()
 
@@ -279,7 +261,7 @@
         return lax.all_to_all(block, "x", 0, 0, tiled=True)
 
     def route(block):
-        return lax.all_to_all(block, ("z", "y"), 0, 0, tiled=True)
+        return lax.all_to_all(block, ("y", "z"), 0, 0, tiled=True)
 
     parts = 2 * width // LANE
     slow = pl.BlockSpec(memory_space=pltpu.HBM)
@@ -302,9 +284,9 @@
     )
     arrived = route(packed.reshape(experts, parts, CAP * LANE))
 
-    half, *down = call(
+    own_cols, half, *down = call(
         prep_kernel,
-        (sds((2, chips, units, width), BF),) + (sds((units, 2 * width), BF),) * 4,
+        (sds((2, chips, units, width), BF),) * 2 + (sds((units, 2 * width), BF),) * 4,
         me, w_gate, w_up, w_down, scalars=1,
     )
     half = swap(half)
@@ -331,25 +313,23 @@
     keep, send = call(
         gate_kernel,
         (pltpu.HBM((2, routes, units), F32), sds((2, routes, units), BF)),
-        me, x_all, w_gate, w_up, *pin(half), scalars=1, places=[near] * 3 + [slow], ends=(far, near),
-        scratch=[
-            pltpu.VMEM(half.shape, BF), pltpu.VMEM((2, routes, units), F32), dma((chips,)), dma((1,)),
-        ],
+        x_all, own_cols, half, ends=(far, near),
+        scratch=[pltpu.VMEM((2, routes, units), F32), dma((1,))],
     )
     got = swap(send)
+    sources = (keep, got, sums, adapter_a)
     grads, grad_a = call(
         grad_kernel,
         (sds((routes, 2 * units + rank), BF), sds((rank, units), F32)),
-        *pin(keep), got, sums, adapter_a, places=[slow] + [near] * 3,
-        scratch=[pltpu.VMEM(keep.shape, F32), dma((1,))],
+        *pin(*sources), places=[slow] * 4,
+        scratch=[pltpu.VMEM(x.shape, x.dtype) for x in sources] + [dma((4,))],
     )
     grads_other = swap(grads)
     back_shape = (chips, routes, width)
     back, v_pair = call(
-        back_kernel, (pltpu.HBM((chips, routes, width), BF), sds((routes, rank), BF)),
-        me, grads, grads_other, w_gate, w_up, *pin(half), scalars=1, places=[near] * 4 + [slow],
-        ends=(far, near),
-        scratch=[pltpu.VMEM(half.shape, BF), pltpu.VMEM(back_shape, BF), dma((chips,)), dma((chips,))],
+        back_kernel, (pltpu.HBM(back_shape, BF), sds((routes, rank), BF)),
+        grads, grads_other, own_cols, half, ends=(far, near),
+        scratch=[pltpu.VMEM(back_shape, BF), dma((chips,))],
     )
     code = call(code_kernel, sds((experts, count), F32), ids.T)
     backs, code = lax.optimization_barrier((over_x(back), code))

time: 168 us -> 166 us (0.988)
  Pallas kernels: 22.8 us -> 20.7 us
  starting transfers between devices: 73.5 us -> 75.3 us
    all_to_all x2, starting transfers between devices: 31.3 us -> 33.8 us  [route(): return lax.all_to_all(block, ('y', 'z'), 0, 0, tiled=True)]
    pallas_call x11, Pallas kernels: 22.8 us -> 20.7 us  [call(): pl.pallas_call(body, out_shape=outs, in_specs=[smem] * scalars + list(pla...]
    all_to_all x2, waiting for transfers between devices: 14.8 us -> 12.8 us  [route(): return lax.all_to_all(block, ('y', 'z'), 0, 0, tiled=True)]
    unnamed x31 -> x27, local copies, waits for them, and re-layouts: 5.16 us -> 5.11 us
where the time goes in v6:
time: 166 us; the launch traced here: 165 us
  starting transfers between devices  75.3 us (45%)
  waiting for transfers between devices  62 us (37%)
  Pallas kernels  20.7 us (12%)
  local copies, waits for them, and re-layouts  5.9 us (4%)
    all_to_all x2, starting transfers between devices, route(): return lax.all_to_all(block, ('y', 'z'), 0, 0, tiled=True)  33.8 us
    all_to_all x3, waiting for transfers between devices, over_x(): return lax.all_to_all(block, 'x', 0, 0, tiled=True)  28.5 us
    pallas_call x11, Pallas kernels, call(): pl.pallas_call(body, out_shape=outs, in_specs=[smem] * scalars + list(pla...  20.7 us
    ppermute x6, starting transfers between devices, shift(): lax.ppermute(block, 'x', [(i, (i + by) % chips) for i in range(chips)])  19.8 us
    ppermute x6, waiting for transfers between devices, shift(): lax.ppermute(block, 'x', [(i, (i + by) % chips) for i in range(chips)])  16.3 us
    all_to_all x2, waiting for transfers between devices, route(): return lax.all_to_all(block, ('y', 'z'), 0, 0, tiled=True)  12.8 us
    all_to_all x3, starting transfers between devices, over_x(): return lax.all_to_all(block, 'x', 0, 0, tiled=True)  12.2 us
    ppermute x5, starting transfers between devices, swap(): return lax.ppermute(block, 'c', [(0, 1), (1, 0)])  9.59 us
  transfers between devices with their start and end apart: 16, of which 13 were waited for; matrix products, arithmetic and copies ran while one was open for 0% of the time, Pallas kernels for 6%

profile of v6, /device:TPU:8, one launch (start us, length us, event | category | flops | bytes accessed | tf_op | source)
XLA Modules:
  0.0 164.9 jit_solution(17283332470505894398)
XLA Ops:
  0.6 0.0 copy-start
  0.6 2.8 %shard_map.112 = bf16[512,640]{1,0:T(8,128)(2,1)} custom-call(s32[8,32]{1,0:T(8,128)} %bitcast.19, f32[8,32]{1,0:T(8,128)} %bitcast.26, bf16[32,512]{1,0:T(8,128)(2,1)} %tok_hbm.1, bf16[32,512]{1,0:T(8,128)(2,1)} %dy_hbm.1), custom_call_target="tpu_custom_call" | custom-call | tf_op jit(solution)/shard_map/pallas_call | solution.py:231
  3.4 18.9 %all-to-all-start = ((bf16[64,8,640]{2,1,0:T(8,128)(2,1)}), bf16[64,8,640]{2,1,0:T(8,128)(2,1)}, u32[]{:S(2)}, u32[]{:S(2)}) async-start(bf16[64,8,640]{2,1,0:T(8,128)(2,1)} %bitcast.2), calls=%async_computation | async-start | bytes 1310720 | tf_op jit(solution)/shard_map/all_to_all | solution.py:264
  22.4 0.1 pad_add_fusion.me_ref
  22.4 0.0 copy-done
  22.4 0.0 copy-start.1
  22.4 1.4 copy-done.1
  23.9 1.4 copy-done.2
  25.3 0.9 shard_map.113
  26.2 0.0 copy-start.5
  26.2 0.7 copy-done.5
  26.9 1.9 %collective-permute-start = (bf16[2,4,192,512]{3,2,1,0:T(8,128)(2,1)S(1)}, bf16[2,4,192,512]{3,2,1,0:T(8,128)(2,1)S(1)}, u32[]{:S(2)}, u32[]{:S(2)}) collective-permute-start(bf16[2,4,192,512]{3,2,1,0:T(8,128)(2,1)S(1)} %get-tuple-element.26), channel_id=1, source_target_pairs={{0,64},{64,0},{1,65},{65,1},{2,66},{66,2},{3,67},{67,3},{4,68},{68... | collective-permute-start | bytes 4718600 | tf_op jit(solution)/shard_map/ppermute | solution.py:255
  28.8 3.4 %collective-permute-start.2 = (bf16[192,1024]{1,0:T(8,128)(2,1)S(1)}, bf16[192,1024]{1,0:T(8,128)(2,1)S(1)}, u32[]{:S(2)}, u32[]{:S(2)}) collective-permute-start(bf16[192,1024]{1,0:T(8,128)(2,1)S(1)} %get-tuple-element.28), channel_id=1, source_target_pairs={{0,128},{128,256},{256,384},{384,0},{1,129},{129,257},{257,385},{3... | collective-permute-start | bytes 1179656 | tf_op jit(solution)/shard_map/ppermute | solution.py:258
  32.2 4.6 %collective-permute-start.3 = (bf16[192,1024]{1,0:T(8,128)(2,1)S(1)}, bf16[192,1024]{1,0:T(8,128)(2,1)S(1)}, u32[]{:S(2)}, u32[]{:S(2)}) collective-permute-start(bf16[192,1024]{1,0:T(8,128)(2,1)S(1)} %get-tuple-element.29), channel_id=1, source_target_pairs={{0,256},{128,384},{256,0},{384,128},{1,257},{129,385},{257,1},{385... | collective-permute-start | bytes 1179656 | tf_op jit(solution)/shard_map/ppermute | solution.py:258
  36.9 3.3 %collective-permute-start.4 = (bf16[192,1024]{1,0:T(8,128)(2,1)S(1)}, bf16[192,1024]{1,0:T(8,128)(2,1)S(1)}, u32[]{:S(2)}, u32[]{:S(2)}) collective-permute-start(bf16[192,1024]{1,0:T(8,128)(2,1)S(1)} %get-tuple-element.30), channel_id=1, source_target_pairs={{0,384},{128,0},{256,128},{384,256},{1,385},{129,1},{257,129},{385... | collective-permute-start | bytes 1179656 | tf_op jit(solution)/shard_map/ppermute | solution.py:258
  40.2 0.0 copy-done.11
  40.2 1.9 %collective-permute-start.1 = (bf16[64,512]{1,0:T(8,128)(2,1)S(1)}, bf16[64,512]{1,0:T(8,128)(2,1)S(1)}, u32[]{:S(2)}, u32[]{:S(2)}) collective-permute-start(bf16[64,512]{1,0:T(8,128)(2,1)S(1)} %bitcast.24), channel_id=1, source_target_pairs={{0,64},{64,0},{1,65},{65,1},{2,66},{66,2},{3,67},{67,3},{4,68},{68... | collective-permute-start | bytes 196616 | tf_op jit(solution)/shard_map/ppermute | solution.py:255
  42.2 1.2 collective-permute-done.1.refs_3_
  43.4 0.1 collective-permute-done.2.refs_5_
  43.4 9.4 %collective-permute-done.3.refs_6_ = bf16[192,1024]{1,0:T(8,128)(2,1)S(1)} collective-permute-done((bf16[192,1024]{1,0:T(8,128)(2,1)S(1)}, bf16[192,1024]{1,0:T(8,128)(2,1)S(1)}, u32[]{:S(2)}, u32[]{:S(2)}) %collective-permute-start.3) | collective-permute-done | bytes 393248 | tf_op jit(solution)/shard_map/ppermute | solution.py:258
  52.9 1.5 collective-permute-done.4.refs_7_
  54.4 0.0 copy-done.7
  54.4 0.0 copy-done.8
  54.4 0.8 copy-done.9
  55.2 0.0 collective-permute-done.half_ref
  55.2 4.3 %all-to-all-done = bf16[64,8,640]{2,1,0:T(8,128)(2,1)} async-done(((bf16[64,8,640]{2,1,0:T(8,128)(2,1)}), bf16[64,8,640]{2,1,0:T(8,128)(2,1)}, u32[]{:S(2)}, u32[]{:S(2)}) %all-to-all-start) | async-done | bytes 655392 | tf_op jit(solution)/shard_map/all_to_all | solution.py:264
  59.5 0.0 copy-done.12
  59.5 2.9 %shard_map.114 = (bf16[4,320,512]{2,1,0:T(8,128)(2,1)}, bf16[320,512]{1,0:T(8,128)(2,1)}) custom-call(bf16[512,640]{1,0:T(8,128)(2,1)} %bitcast.9.in_ref), custom_call_target="tpu_custom_call" | custom-call | tf_op jit(solution)/shard_map/pallas_call | solution.py:231
  62.4 0.0 copy-start.3
  62.4 4.4 %all-to-all-start.1 = ((bf16[4,320,512]{2,1,0:T(8,128)(2,1)}), bf16[4,320,512]{2,1,0:T(8,128)(2,1)}, u32[]{:S(2)}, u32[]{:S(2)}) async-start(bf16[4,320,512]{2,1,0:T(8,128)(2,1)} %get-tuple-element.32), calls=%async_computation.1 | async-start | bytes 2621440 | tf_op jit(solution)/shard_map/all_to_all | solution.py:261
  66.8 0.0 copy-done.3
  66.8 1.9 %collective-permute-start.6 = (bf16[320,512]{1,0:T(8,128)(2,1)S(1)}, bf16[320,512]{1,0:T(8,128)(2,1)S(1)}, u32[]{:S(2)}, u32[]{:S(2)}) collective-permute-start(bf16[320,512]{1,0:T(8,128)(2,1)S(1)} %copy-done.3), channel_id=1, source_target_pairs={{0,64},{64,0},{1,65},{65,1},{2,66},{66,2},{3,67},{67,3},{4,68},{68... | collective-permute-start | bytes 983048 | tf_op jit(solution)/shard_map/ppermute | solution.py:255
  68.8 1.6 collective-permute-done.6.refs_1_
  70.4 0.7 copy-done.10
  71.1 4.0 %shard_map.116 = bf16[4,320,256]{2,1,0:T(8,128)(2,1)} custom-call(s32[2]{0:T(128)S(1)} %pad_add_fusion.me_ref, bf16[320,512]{1,0:T(8,128)(2,1)} %get-tuple-element.37.refs_0_.s_ref, bf16[320,512]{1,0:T(8,128)(2,1)} %copy-done.10, bf16[64,512]{1,0:T(8,128)(2,1)} %bitcast.23, bf16[64,512]{1,0:T(8,128)(2,1)} %copy-done.12, bf16[192,1024]{1,0:T(8,128)(2,1)} %copy-done.5, ...), custom_call_target="tpu_custom_call" | custom-call | tf_op jit(solution)/shard_map/pallas_call | solution.py:231
  75.1 6.8 %all-to-all-done.1.x_ref = bf16[4,320,512]{2,1,0:T(8,128)(2,1)} async-done(((bf16[4,320,512]{2,1,0:T(8,128)(2,1)}), bf16[4,320,512]{2,1,0:T(8,128)(2,1)}, u32[]{:S(2)}, u32[]{:S(2)}) %all-to-all-start.1) | async-done | bytes 1310752 | tf_op jit(solution)/shard_map/all_to_all | solution.py:261
  81.9 4.2 %all-to-all-start.2 = ((bf16[4,320,256]{2,1,0:T(8,128)(2,1)}), bf16[4,320,256]{2,1,0:T(8,128)(2,1)}, u32[]{:S(2)}, u32[]{:S(2)}) async-start(bf16[4,320,256]{2,1,0:T(8,128)(2,1)} %shard_map.116), calls=%async_computation.2 | async-start | bytes 1310720 | tf_op jit(solution)/shard_map/all_to_all | solution.py:261
  86.1 3.4 %shard_map.115 = (f32[2,320,192]{2,1,0:T(8,128)}, bf16[2,320,192]{2,1,0:T(8,128)(2,1)S(1)}) custom-call(bf16[4,320,512]{2,1,0:T(8,128)(2,1)} %all-to-all-done.1.x_ref, bf16[2,4,192,512]{3,2,1,0:T(8,128)(2,1)S(1)} %get-tuple-element.33.own_ref, bf16[2,4,192,512]{3,2,1,0:T(8,128)(2,1)S(1)} %collective-permute-done.half_ref), custom_call_target="tpu_custom_call" | custom-call | tf_op jit(solution)/shard_map/pallas_call | solution.py:231
  89.5 1.9 %collective-permute-start.5 = (bf16[2,320,192]{2,1,0:T(8,128)(2,1)S(1)}, bf16[2,320,192]{2,1,0:T(8,128)(2,1)}, u32[]{:S(2)}, u32[]{:S(2)}) collective-permute-start(bf16[2,320,192]{2,1,0:T(8,128)(2,1)S(1)} %get-tuple-element.36), channel_id=1, source_target_pairs={{0,64},{64,0},{1,65},{65,1},{2,66},{66,2},{3,67},{67,3},{4,68},{68... | collective-permute-start | bytes 737288 | tf_op jit(solution)/shard_map/ppermute | solution.py:255
  91.4 3.5 %all-to-all-done.2.in_hbm = bf16[4,320,256]{2,1,0:T(8,128)(2,1)} async-done(((bf16[4,320,256]{2,1,0:T(8,128)(2,1)}), bf16[4,320,256]{2,1,0:T(8,128)(2,1)}, u32[]{:S(2)}, u32[]{:S(2)}) %all-to-all-start.2) | async-done | bytes 655392 | tf_op jit(solution)/shard_map/all_to_all | solution.py:261
  94.9 0.0 collective-permute-done.5.got_hbm
  94.9 2.4 %shard_map.117 = (bf16[320,448]{1,0:T(8,128)(2,1)S(1)}, f32[64,192]{1,0:T(8,128)}) custom-call(f32[2,320,192]{2,1,0:T(8,128)} %get-tuple-element.35.keep_hbm, bf16[2,320,192]{2,1,0:T(8,128)(2,1)} %collective-permute-done.5.got_hbm, bf16[4,320,256]{2,1,0:T(8,128)(2,1)} %all-to-all-done.2.in_hbm, bf16[64,192]{1,0:T(8,128)(2,1)} %bitcast.25), custom_call_target="tpu_custom_call" | custom-call | tf_op jit(solution)/shard_map/pallas_call | solution.py:231
  97.3 1.9 %collective-permute-start.7 = (bf16[320,448]{1,0:T(8,128)(2,1)S(1)}, bf16[320,448]{1,0:T(8,128)(2,1)S(1)}, u32[]{:S(2)}, u32[]{:S(2)}) collective-permute-start(bf16[320,448]{1,0:T(8,128)(2,1)S(1)} %get-tuple-element.43.g_ref), channel_id=1, source_target_pairs={{0,64},{64,0},{1,65},{65,1},{2,66},{66,2},{3,67},{67,3},{4,68},{68... | collective-permute-start | bytes 860168 | tf_op jit(solution)/shard_map/ppermute | solution.py:255
  99.3 1.6 collective-permute-done.7.h_ref
  100.8 2.3 %shard_map.118 = (bf16[4,320,512]{2,1,0:T(8,128)(2,1)}, bf16[320,64]{1,0:T(8,128)(2,1)S(1)}) custom-call(bf16[320,448]{1,0:T(8,128)(2,1)S(1)} %get-tuple-element.43.g_ref, bf16[320,448]{1,0:T(8,128)(2,1)S(1)} %collective-permute-done.7.h_ref, bf16[2,4,192,512]{3,2,1,0:T(8,128)(2,1)S(1)} %get-tuple-element.33.own_ref, ...), custom_call_target="tpu_custom_call" | custom-call | tf_op jit(solution)/shard_map/pallas_call | solution.py:231
  103.2 0.0 copy-start.6
  103.2 3.6 %all-to-all-start.3 = ((bf16[4,320,512]{2,1,0:T(8,128)(2,1)}), bf16[4,320,512]{2,1,0:T(8,128)(2,1)S(1)}, u32[]{:S(2)}, u32[]{:S(2)}) async-start(bf16[4,320,512]{2,1,0:T(8,128)(2,1)} %get-tuple-element.44), calls=%async_computation.3 | async-start | bytes 2621440 | tf_op jit(solution)/shard_map/all_to_all | solution.py:261
  106.7 0.0 copy-done.6
  106.7 0.0 copy-start.4
  106.7 0.1 shard_map.119.code_ref
  106.9 18.3 %all-to-all-done.3.in_ref = bf16[4,320,512]{2,1,0:T(8,128)(2,1)S(1)} async-done(((bf16[4,320,512]{2,1,0:T(8,128)(2,1)}), bf16[4,320,512]{2,1,0:T(8,128)(2,1)S(1)}, u32[]{:S(2)}, u32[]{:S(2)}) %all-to-all-start.3) | async-done | bytes 1310752 | tf_op jit(solution)/shard_map/all_to_all | solution.py:261
  125.2 0.2 shard_map.120
  125.3 0.8 reshape.20
  126.1 14.9 %all-to-all-start.4 = ((bf16[64,2,1280]{2,1,0:T(2,128)(2,1)}), bf16[64,2,1280]{2,1,0:T(2,128)(2,1)S(1)}, u32[]{:S(2)}, u32[]{:S(2)}) async-start(bf16[64,2,1280]{2,1,0:T(2,128)(2,1)} %reshape.20), calls=%async_computation.4 | async-start | bytes 655360 | tf_op jit(solution)/shard_map/all_to_all | solution.py:264
  141.0 3.1 %collective-permute-start.10 = (bf16[320,64]{1,0:T(8,128)(2,1)S(1)}, bf16[320,64]{1,0:T(8,128)(2,1)S(1)}, u32[]{:S(2)}, u32[]{:S(2)}) collective-permute-start(bf16[320,64]{1,0:T(8,128)(2,1)S(1)} %get-tuple-element.48.v0_ref), channel_id=1, source_target_pairs={{0,384},{128,0},{256,128},{384,256},{1,385},{129,1},{257,129},{385... | collective-permute-start | bytes 122888 | tf_op jit(solution)/shard_map/ppermute | solution.py:258
  144.1 2.8 %collective-permute-start.8 = (bf16[320,64]{1,0:T(8,128)(2,1)S(1)}, bf16[320,64]{1,0:T(8,128)(2,1)S(1)}, u32[]{:S(2)}, u32[]{:S(2)}) collective-permute-start(bf16[320,64]{1,0:T(8,128)(2,1)S(1)} %get-tuple-element.48.v0_ref), channel_id=1, source_target_pairs={{0,128},{128,256},{256,384},{384,0},{1,129},{129,257},{257,385},{3... | collective-permute-start | bytes 122888 | tf_op jit(solution)/shard_map/ppermute | solution.py:258
  146.9 2.5 %collective-permute-start.9 = (bf16[320,64]{1,0:T(8,128)(2,1)S(1)}, bf16[320,64]{1,0:T(8,128)(2,1)S(1)}, u32[]{:S(2)}, u32[]{:S(2)}) collective-permute-start(bf16[320,64]{1,0:T(8,128)(2,1)S(1)} %get-tuple-element.48.v0_ref), channel_id=1, source_target_pairs={{0,256},{128,384},{256,0},{384,128},{1,257},{129,385},{257,1},{385... | collective-permute-start | bytes 122888 | tf_op jit(solution)/shard_map/ppermute | solution.py:258
  149.4 0.0 collective-permute-done.10.v3_ref
  149.4 3.1 %collective-permute-done.8.v1_ref = bf16[320,64]{1,0:T(8,128)(2,1)S(1)} collective-permute-done((bf16[320,64]{1,0:T(8,128)(2,1)S(1)}, bf16[320,64]{1,0:T(8,128)(2,1)S(1)}, u32[]{:S(2)}, u32[]{:S(2)}) %collective-permute-start.8) | collective-permute-done | bytes 40992 | tf_op jit(solution)/shard_map/ppermute | solution.py:258
  152.5 2.2 %collective-permute-done.9.v2_ref = bf16[320,64]{1,0:T(8,128)(2,1)S(1)} collective-permute-done((bf16[320,64]{1,0:T(8,128)(2,1)S(1)}, bf16[320,64]{1,0:T(8,128)(2,1)S(1)}, u32[]{:S(2)}, u32[]{:S(2)}) %collective-permute-start.9) | collective-permute-done | bytes 40992 | tf_op jit(solution)/shard_map/ppermute | solution.py:258
  154.7 0.0 copy-done.4
  154.7 0.9 shard_map.122
  155.6 8.4 %all-to-all-done.4 = bf16[64,2,1280]{2,1,0:T(2,128)(2,1)S(1)} async-done(((bf16[64,2,1280]{2,1,0:T(2,128)(2,1)}), bf16[64,2,1280]{2,1,0:T(2,128)(2,1)S(1)}, u32[]{:S(2)}, u32[]{:S(2)}) %all-to-all-start.4) | async-done | bytes 327712 | tf_op jit(solution)/shard_map/all_to_all | solution.py:264
  164.1 0.8 shard_map.121
  (8 shorter events, 0.0 us)
Async XLA Ops:
  0.6 21.8 %copy-start = (bf16[1,192,4096]{2,1,0:T(8,128)(2,1)S(1)}, bf16[1,192,4096]{2,1,0:T(8,128)(2,1)}, u32[]{:S(2)}) copy-start(bf16[1,192,4096]{2,1,0:T(8,128)(2,1)} %param.13) | copy-start | bytes 4718596
  3.4 56.1 %all-to-all-start = ((bf16[64,8,640]{2,1,0:T(8,128)(2,1)}), bf16[64,8,640]{2,1,0:T(8,128)(2,1)}, u32[]{:S(2)}, u32[]{:S(2)}) async-start(bf16[64,8,640]{2,1,0:T(8,128)(2,1)} %bitcast.2), calls=%async_computation | async-start | bytes 1310720 | tf_op jit(solution)/shard_map/all_to_all | solution.py:264
  22.4 1.4 copy-start.1
  23.9 1.4 copy-start.2
  25.3 15.0 %copy-start.11 = (bf16[1,64,512]{2,1,0:T(8,128)(2,1)S(1)}, bf16[1,64,512]{2,1,0:T(8,128)(2,1)}, u32[]{:S(2)}) copy-start(bf16[1,64,512]{2,1,0:T(8,128)(2,1)} %param.17) | copy-start | bytes 196612
  26.2 0.8 copy-start.5
  26.9 28.3 %collective-permute-start = (bf16[2,4,192,512]{3,2,1,0:T(8,128)(2,1)S(1)}, bf16[2,4,192,512]{3,2,1,0:T(8,128)(2,1)S(1)}, u32[]{:S(2)}, u32[]{:S(2)}) collective-permute-start(bf16[2,4,192,512]{3,2,1,0:T(8,128)(2,1)S(1)} %get-tuple-element.26), channel_id=1, source_target_pairs={{0,64},{64,0},{1,65},{65,1},{2,66},{66,2},{3,67},{67,3},{4,68},{68... | collective-permute-start | bytes 4718600 | tf_op jit(solution)/shard_map/ppermute | solution.py:255
  28.8 14.6 %collective-permute-start.2 = (bf16[192,1024]{1,0:T(8,128)(2,1)S(1)}, bf16[192,1024]{1,0:T(8,128)(2,1)S(1)}, u32[]{:S(2)}, u32[]{:S(2)}) collective-permute-start(bf16[192,1024]{1,0:T(8,128)(2,1)S(1)} %get-tuple-element.28), channel_id=1, source_target_pairs={{0,128},{128,256},{256,384},{384,0},{1,129},{129,257},{257,385},{3... | collective-permute-start | bytes 1179656 | tf_op jit(solution)/shard_map/ppermute | solution.py:258
  32.2 20.6 %collective-permute-start.3 = (bf16[192,1024]{1,0:T(8,128)(2,1)S(1)}, bf16[192,1024]{1,0:T(8,128)(2,1)S(1)}, u32[]{:S(2)}, u32[]{:S(2)}) collective-permute-start(bf16[192,1024]{1,0:T(8,128)(2,1)S(1)} %get-tuple-element.29), channel_id=1, source_target_pairs={{0,256},{128,384},{256,0},{384,128},{1,257},{129,385},{257,1},{385... | collective-permute-start | bytes 1179656 | tf_op jit(solution)/shard_map/ppermute | solution.py:258
  36.9 17.5 %collective-permute-start.4 = (bf16[192,1024]{1,0:T(8,128)(2,1)S(1)}, bf16[192,1024]{1,0:T(8,128)(2,1)S(1)}, u32[]{:S(2)}, u32[]{:S(2)}) collective-permute-start(bf16[192,1024]{1,0:T(8,128)(2,1)S(1)} %get-tuple-element.30), channel_id=1, source_target_pairs={{0,384},{128,0},{256,128},{384,256},{1,385},{129,1},{257,129},{385... | collective-permute-start | bytes 1179656 | tf_op jit(solution)/shard_map/ppermute | solution.py:258
  40.2 3.1 %collective-permute-start.1 = (bf16[64,512]{1,0:T(8,128)(2,1)S(1)}, bf16[64,512]{1,0:T(8,128)(2,1)S(1)}, u32[]{:S(2)}, u32[]{:S(2)}) collective-permute-start(bf16[64,512]{1,0:T(8,128)(2,1)S(1)} %bitcast.24), channel_id=1, source_target_pairs={{0,64},{64,0},{1,65},{65,1},{2,66},{66,2},{3,67},{67,3},{4,68},{68... | collective-permute-start | bytes 196616 | tf_op jit(solution)/shard_map/ppermute | solution.py:255
  43.4 16.1 %copy-start.12 = (bf16[64,512]{1,0:T(8,128)(2,1)}, bf16[64,512]{1,0:T(8,128)(2,1)S(1)}, u32[]{:S(2)}) copy-start(bf16[64,512]{1,0:T(8,128)(2,1)S(1)} %collective-permute-done.1.refs_3_) | copy-start | bytes 196612
  43.4 11.0 %copy-start.7 = (bf16[192,1024]{1,0:T(8,128)(2,1)}, bf16[192,1024]{1,0:T(8,128)(2,1)S(1)}, u32[]{:S(2)}) copy-start(bf16[192,1024]{1,0:T(8,128)(2,1)S(1)} %collective-permute-done.2.refs_5_) | copy-start | bytes 1179652
  52.9 1.6 copy-start.8
  54.4 0.8 copy-start.9
  62.4 4.5 %copy-start.3 = (bf16[320,512]{1,0:T(8,128)(2,1)S(1)}, bf16[320,512]{1,0:T(8,128)(2,1)}, u32[]{:S(2)}) copy-start(bf16[320,512]{1,0:T(8,128)(2,1)} %get-tuple-element.37.refs_0_.s_ref) | copy-start | bytes 983044
  62.4 19.5 %all-to-all-start.1 = ((bf16[4,320,512]{2,1,0:T(8,128)(2,1)}), bf16[4,320,512]{2,1,0:T(8,128)(2,1)}, u32[]{:S(2)}, u32[]{:S(2)}) async-start(bf16[4,320,512]{2,1,0:T(8,128)(2,1)} %get-tuple-element.32), calls=%async_computation.1 | async-start | bytes 2621440 | tf_op jit(solution)/shard_map/all_to_all | solution.py:261
  66.8 3.5 %collective-permute-start.6 = (bf16[320,512]{1,0:T(8,128)(2,1)S(1)}, bf16[320,512]{1,0:T(8,128)(2,1)S(1)}, u32[]{:S(2)}, u32[]{:S(2)}) collective-permute-start(bf16[320,512]{1,0:T(8,128)(2,1)S(1)} %copy-done.3), channel_id=1, source_target_pairs={{0,64},{64,0},{1,65},{65,1},{2,66},{66,2},{3,67},{67,3},{4,68},{68... | collective-permute-start | bytes 983048 | tf_op jit(solution)/shard_map/ppermute | solution.py:255
  70.3 0.7 copy-start.10
  81.9 13.0 %all-to-all-start.2 = ((bf16[4,320,256]{2,1,0:T(8,128)(2,1)}), bf16[4,320,256]{2,1,0:T(8,128)(2,1)}, u32[]{:S(2)}, u32[]{:S(2)}) async-start(bf16[4,320,256]{2,1,0:T(8,128)(2,1)} %shard_map.116), calls=%async_computation.2 | async-start | bytes 1310720 | tf_op jit(solution)/shard_map/all_to_all | solution.py:261
  89.5 5.4 %collective-permute-start.5 = (bf16[2,320,192]{2,1,0:T(8,128)(2,1)S(1)}, bf16[2,320,192]{2,1,0:T(8,128)(2,1)}, u32[]{:S(2)}, u32[]{:S(2)}) collective-permute-start(bf16[2,320,192]{2,1,0:T(8,128)(2,1)S(1)} %get-tuple-element.36), channel_id=1, source_target_pairs={{0,64},{64,0},{1,65},{65,1},{2,66},{66,2},{3,67},{67,3},{4,68},{68... | collective-permute-start | bytes 737288 | tf_op jit(solution)/shard_map/ppermute | solution.py:255
  97.3 3.5 %collective-permute-start.7 = (bf16[320,448]{1,0:T(8,128)(2,1)S(1)}, bf16[320,448]{1,0:T(8,128)(2,1)S(1)}, u32[]{:S(2)}, u32[]{:S(2)}) collective-permute-start(bf16[320,448]{1,0:T(8,128)(2,1)S(1)} %get-tuple-element.43.g_ref), channel_id=1, source_target_pairs={{0,64},{64,0},{1,65},{65,1},{2,66},{66,2},{3,67},{67,3},{4,68},{68... | collective-permute-start | bytes 860168 | tf_op jit(solution)/shard_map/ppermute | solution.py:255
  103.2 3.6 %copy-start.6 = (s32[32,8]{0,1:T(8,128)S(1)}, s32[32,8]{0,1:T(8,128)}, u32[]{:S(2)}) copy-start(s32[32,8]{0,1:T(8,128)} %param.12) | copy-start | bytes 3076
  103.2 22.0 %all-to-all-start.3 = ((bf16[4,320,512]{2,1,0:T(8,128)(2,1)}), bf16[4,320,512]{2,1,0:T(8,128)(2,1)S(1)}, u32[]{:S(2)}, u32[]{:S(2)}) async-start(bf16[4,320,512]{2,1,0:T(8,128)(2,1)} %get-tuple-element.44), calls=%async_computation.3 | async-start | bytes 2621440 | tf_op jit(solution)/shard_map/all_to_all | solution.py:261
  106.7 48.0 %copy-start.4 = (bf16[320,512]{1,0:T(8,128)(2,1)S(1)}, bf16[320,512]{1,0:T(8,128)(2,1)}, u32[]{:S(2)}) copy-start(bf16[320,512]{1,0:T(8,128)(2,1)} %get-tuple-element.37.refs_0_.s_ref) | copy-start | bytes 983044
  126.1 37.9 %all-to-all-start.4 = ((bf16[64,2,1280]{2,1,0:T(2,128)(2,1)}), bf16[64,2,1280]{2,1,0:T(2,128)(2,1)S(1)}, u32[]{:S(2)}, u32[]{:S(2)}) async-start(bf16[64,2,1280]{2,1,0:T(2,128)(2,1)} %reshape.20), calls=%async_computation.4 | async-start | bytes 655360 | tf_op jit(solution)/shard_map/all_to_all | solution.py:264
  141.0 8.4 %collective-permute-start.10 = (bf16[320,64]{1,0:T(8,128)(2,1)S(1)}, bf16[320,64]{1,0:T(8,128)(2,1)S(1)}, u32[]{:S(2)}, u32[]{:S(2)}) collective-permute-start(bf16[320,64]{1,0:T(8,128)(2,1)S(1)} %get-tuple-element.48.v0_ref), channel_id=1, source_target_pairs={{0,384},{128,0},{256,128},{384,256},{1,385},{129,1},{257,129},{385... | collective-permute-start | bytes 122888 | tf_op jit(solution)/shard_map/ppermute | solution.py:258
  144.1 8.4 %collective-permute-start.8 = (bf16[320,64]{1,0:T(8,128)(2,1)S(1)}, bf16[320,64]{1,0:T(8,128)(2,1)S(1)}, u32[]{:S(2)}, u32[]{:S(2)}) collective-permute-start(bf16[320,64]{1,0:T(8,128)(2,1)S(1)} %get-tuple-element.48.v0_ref), channel_id=1, source_target_pairs={{0,128},{128,256},{256,384},{384,0},{1,129},{129,257},{257,385},{3... | collective-permute-start | bytes 122888 | tf_op jit(solution)/shard_map/ppermute | solution.py:258
  146.9 7.8 %collective-permute-start.9 = (bf16[320,64]{1,0:T(8,128)(2,1)S(1)}, bf16[320,64]{1,0:T(8,128)(2,1)S(1)}, u32[]{:S(2)}, u32[]{:S(2)}) collective-permute-start(bf16[320,64]{1,0:T(8,128)(2,1)S(1)} %get-tuple-element.48.v0_ref), channel_id=1, source_target_pairs={{0,256},{128,384},{256,0},{384,128},{1,257},{129,385},{257,1},{385... | collective-permute-start | bytes 122888 | tf_op jit(solution)/shard_map/ppermute | solution.py:258

commit v7 on v6

--- a/solution.py
+++ b/solution.py
@@ -76,18 +76,6 @@
         out_ref[:, s * LANE : (s + 1) * LANE] = (nn(pick, table) * scale).astype(BF)
 
 
-def code_of(ids, experts):
-    count = ids.shape[1]
-    own = expert_of(lax.broadcasted_iota(jnp.int32, (experts, count), 0), experts)
-    hit = jnp.zeros((experts, count), F32)
-    for k in range(ids.shape[0]):
-        hit = jnp.where(ids[k : k + 1, :] == own, 1.0, hit)
-    first = lax.broadcasted_iota(jnp.int32, (count, count), 0)
-    second = lax.broadcasted_iota(jnp.int32, (count, count), 1)
-    before = jnp.where(first < second, 1.0, 0.0).astype(BF)
-    return jnp.where(hit > 0.5, nn(hit.astype(BF), before), -1.0)
-
-
 def split_kernel(in_ref, x_hbm, s_hbm, x_ref, s_ref, sems):
     total = in_ref.shape[0]
     width = s_ref.shape[1]
@@ -194,19 +182,52 @@
         store.wait()
 
 
-def code_kernel(ids_ref, code_ref):
-    code_ref[...] = code_of(ids_ref[...], code_ref.shape[0])
-
-
-def total_kernel(in_ref, out_ref):
-    experts = out_ref.shape[0]
-    width = in_ref.shape[2]
+def pick_kernel(ids_ref, *pick_refs):
+    rows, count = pick_refs[0].shape
+    halves = len(pick_refs)
+    each = FLAT * CAP * halves
+    row = lax.broadcasted_iota(jnp.int32, (rows, count), 0)
+    inner = lax.rem(row, each)
+    own = lax.div(row, each) * FLAT + lax.div(inner, CAP * halves)
+    hit = jnp.zeros((rows, count), F32)
+    for k in range(ids_ref.shape[0]):
+        hit = jnp.where(ids_ref[k : k + 1, :] == own, 1.0, hit)
+    first = lax.broadcasted_iota(jnp.int32, (count, count), 0)
+    second = lax.broadcasted_iota(jnp.int32, (count, count), 1)
+    before = jnp.where(first < second, 1.0, 0.0).astype(BF)
+    code = jnp.where(hit > 0.5, nn(hit.astype(BF), before), -1.0)
+    slot = lax.div(lax.rem(inner, CAP * halves), halves).astype(F32)
+    for h, ref in enumerate(pick_refs):
+        ref[...] = jnp.where((code == slot) & (lax.rem(row, halves) == h), 1.0, 0.0).astype(BF)
+
+
+def total_kernel(in_ref, out_hbm, out_ref, sem):
+    deep = out_ref.shape[1] // CAP
     for s in range(CAP):
-        rows = slice(s * experts, (s + 1) * experts)
-        total = in_ref[0, rows].astype(F32)
-        for x in range(1, in_ref.shape[0]):
-            total += in_ref[x, rows].astype(F32)
-        out_ref[:, s * width : (s + 1) * width] = total.astype(BF)
+        for y in range(FLAT):
+            rows = slice((s * FLAT + y) * deep, (s * FLAT + y + 1) * deep)
+            total = in_ref[0, rows].astype(F32)
+            for x in range(1, in_ref.shape[0]):
+                total += in_ref[x, rows].astype(F32)
+            out_ref[y, s * deep : (s + 1) * deep] = total.astype(BF)
+    fetch([(out_ref, out_hbm)], sem)
+
+
+def repack_kernel(in_ref, out_hbm, out_ref, sem):
+    rows, width = in_ref.shape
+    part = out_ref.shape[1]
+    halves = width // part
+    each = FLAT * CAP * halves
+    deep = out_ref.shape[0] // each
+    row = lax.broadcasted_iota(jnp.int32, (out_ref.shape[0], rows), 0)
+    there = lax.broadcasted_iota(jnp.int32, (out_ref.shape[0], rows), 1)
+    came = lax.div(lax.rem(row, each), halves) * deep + lax.div(row, each)
+    total = jnp.zeros(out_ref.shape, F32)
+    for h in range(halves):
+        move = (there == came) & (lax.rem(row, halves) == h)
+        total += nn(jnp.where(move, 1.0, 0.0).astype(BF), in_ref[:, h * part : (h + 1) * part])
+    out_ref[...] = total.astype(BF)
+    fetch([(out_ref, out_hbm)], sem)
 
 
 def adapter_kernel(v0_ref, v1_ref, v2_ref, v3_ref, s_ref, o_ref):
@@ -215,13 +236,11 @@
     o_ref[...] = tn(low.astype(BF), s_ref[...])
 
 
-def combine_kernel(code_ref, r_ref, o_ref):
-    width = o_ref.shape[1]
-    total = jnp.zeros(o_ref.shape, F32)
-    for s in range(CAP):
-        pick = jnp.where(code_ref[...] == float(s), 1.0, 0.0).astype(BF)
-        total += tn(pick, r_ref[:, s * width : (s + 1) * width])
-    o_ref[...] = total.astype(BF)
+def combine_kernel(*refs):
+    *pick_refs, r_ref, o_ref = refs
+    part = r_ref.shape[1]
+    for h, ref in enumerate(pick_refs):
+        o_ref[:, h * part : (h + 1) * part] = tn(ref[...], r_ref[...]).astype(BF)
 
 
 def call(body, outs, *args, scalars=0, places=(), ends=(), scratch=()):
@@ -331,14 +350,26 @@
         grads, grads_other, own_cols, half, ends=(far, near),
         scratch=[pltpu.VMEM(back_shape, BF), dma((chips,))],
     )
-    code = call(code_kernel, sds((experts, count), F32), ids.T)
-    backs, code = lax.optimization_barrier((over_x(back), code))
-    total = call(total_kernel, sds((experts, CAP * width), BF), backs)
-    home = route(total.reshape(experts, 2, CAP * width // 2)).reshape(experts, CAP * width)
+    halves, deep = 2, experts // FLAT
+    each = FLAT * CAP * halves
+    picks = call(pick_kernel, (sds((deep * each, count), BF),) * halves, ids.T)
+    backs, *picks = lax.optimization_barrier((over_x(back), *picks))
+    shape = (FLAT, CAP * deep, width)
+    total = call(
+        total_kernel, pltpu.HBM(shape, BF), backs, ends=far, scratch=[pltpu.VMEM(shape, BF), dma((1,))]
+    )
+    near_home = lax.all_to_all(total, "y", 0, 0, tiled=True)
+    shape = (deep * each, width // halves)
+    ready = call(
+        repack_kernel, pltpu.HBM(shape, BF), near_home.reshape(routes, width), ends=far,
+        scratch=[pltpu.VMEM(shape, BF), dma((1,))],
+    )
+    ready, v_pair = lax.optimization_barrier((ready, v_pair))
+    home = lax.all_to_all(ready.reshape(deep, each, width // halves), "z", 0, 0, tiled=True)
 
     v_all = [v_pair] + [shift(v_pair, d) for d in (1, 2, 3)]
     grad_b = call(adapter_kernel, sds((rank, width), F32), *v_all, s_own)
-    out = call(combine_kernel, sds(tokens.shape, BF), code, home)
+    out = call(combine_kernel, sds(tokens.shape, BF), *picks, home.reshape(shape))
     return out, grad_a[None], grad_b[None]
 
 

time: 166 us -> 171 us (1.030)
  the two profiles are of different devices: /device:TPU:8 before, /device:TPU:64 now
where the time goes in v7:
time: 171 us; the launch traced here: 170 us
  starting transfers between devices  71.5 us (42%)
  waiting for transfers between devices  58.4 us (34%)
  Pallas kernels  23.3 us (14%)
  blocking collectives  10.8 us (6%)
  local copies, waits for them, and re-layouts  5.06 us (3%)
    all_to_all x3, waiting for transfers between devices, over_x(): return lax.all_to_all(block, 'x', 0, 0, tiled=True)  29.5 us
    pallas_call x12, Pallas kernels, call(): pl.pallas_call(body, out_shape=outs, in_specs=[smem] * scalars + list(pla...  23.3 us
    ppermute x6, starting transfers between devices, shift(): lax.ppermute(block, 'x', [(i, (i + by) % chips) for i in range(chips)])  19.7 us
    all_to_all x1, starting transfers between devices, route(): return lax.all_to_all(block, ('y', 'z'), 0, 0, tiled=True)  18.1 us
    ppermute x6, waiting for transfers between devices, shift(): lax.ppermute(block, 'x', [(i, (i + by) % chips) for i in range(chips)])  16.3 us
    all_to_all x3, starting transfers between devices, over_x(): return lax.all_to_all(block, 'x', 0, 0, tiled=True)  12.1 us
    all_to_all x1, starting transfers between devices, per_device(): lax.all_to_all(ready.reshape(deep, each, width // halves), 'z', 0, 0, til...  11.9 us
    all_to_all x1, blocking collectives, per_device(): near_home = lax.all_to_all(total, 'y', 0, 0, tiled=True)  10.8 us
  transfers between devices with their start and end apart: 16, of which 13 were waited for; matrix products, arithmetic and copies ran while one was open for 0% of the time, Pallas kernels for 6%

profile of v7, /device:TPU:64, one launch (start us, length us, event | category | flops | bytes accessed | tf_op | source)
XLA Modules:
  0.0 170.0 jit_solution(10643735107498314207)
XLA Ops:
  0.6 0.0 copy-start
  0.6 2.8 %shard_map.112 = bf16[512,640]{1,0:T(8,128)(2,1)} custom-call(s32[8,32]{1,0:T(8,128)} %bitcast.21, f32[8,32]{1,0:T(8,128)} %bitcast.28, bf16[32,512]{1,0:T(8,128)(2,1)} %tok_hbm.1, bf16[32,512]{1,0:T(8,128)(2,1)} %dy_hbm.1), custom_call_target="tpu_custom_call" | custom-call | tf_op jit(solution)/shard_map/pallas_call | solution.py:250
  3.4 18.1 %all-to-all-start = ((bf16[64,8,640]{2,1,0:T(8,128)(2,1)}), bf16[64,8,640]{2,1,0:T(8,128)(2,1)}, u32[]{:S(2)}, u32[]{:S(2)}) async-start(bf16[64,8,640]{2,1,0:T(8,128)(2,1)} %bitcast.2), calls=%async_computation | async-start | bytes 1310720 | tf_op jit(solution)/shard_map/all_to_all | solution.py:283
  21.6 0.1 pad_add_fusion.me_ref
  21.6 0.0 copy-done
  21.6 0.0 copy-start.1
  21.7 1.4 copy-done.1
  23.1 1.4 copy-done.2
  24.5 0.9 shard_map.113
  25.4 0.0 copy-start.5
  25.4 0.7 copy-done.5
  26.1 1.9 %collective-permute-start = (bf16[2,4,192,512]{3,2,1,0:T(8,128)(2,1)S(1)}, bf16[2,4,192,512]{3,2,1,0:T(8,128)(2,1)S(1)}, u32[]{:S(2)}, u32[]{:S(2)}) collective-permute-start(bf16[2,4,192,512]{3,2,1,0:T(8,128)(2,1)S(1)} %get-tuple-element.31), channel_id=1, source_target_pairs={{0,64},{64,0},{1,65},{65,1},{2,66},{66,2},{3,67},{67,3},{4,68},{68... | collective-permute-start | bytes 4718600 | tf_op jit(solution)/shard_map/ppermute | solution.py:274
  28.0 3.4 %collective-permute-start.2 = (bf16[192,1024]{1,0:T(8,128)(2,1)S(1)}, bf16[192,1024]{1,0:T(8,128)(2,1)S(1)}, u32[]{:S(2)}, u32[]{:S(2)}) collective-permute-start(bf16[192,1024]{1,0:T(8,128)(2,1)S(1)} %get-tuple-element.33), channel_id=1, source_target_pairs={{0,128},{128,256},{256,384},{384,0},{1,129},{129,257},{257,385},{3... | collective-permute-start | bytes 1179656 | tf_op jit(solution)/shard_map/ppermute | solution.py:277
  31.4 4.6 %collective-permute-start.3 = (bf16[192,1024]{1,0:T(8,128)(2,1)S(1)}, bf16[192,1024]{1,0:T(8,128)(2,1)S(1)}, u32[]{:S(2)}, u32[]{:S(2)}) collective-permute-start(bf16[192,1024]{1,0:T(8,128)(2,1)S(1)} %get-tuple-element.34), channel_id=1, source_target_pairs={{0,256},{128,384},{256,0},{384,128},{1,257},{129,385},{257,1},{385... | collective-permute-start | bytes 1179656 | tf_op jit(solution)/shard_map/ppermute | solution.py:277
  36.1 3.3 %collective-permute-start.4 = (bf16[192,1024]{1,0:T(8,128)(2,1)S(1)}, bf16[192,1024]{1,0:T(8,128)(2,1)S(1)}, u32[]{:S(2)}, u32[]{:S(2)}) collective-permute-start(bf16[192,1024]{1,0:T(8,128)(2,1)S(1)} %get-tuple-element.35), channel_id=1, source_target_pairs={{0,384},{128,0},{256,128},{384,256},{1,385},{129,1},{257,129},{385... | collective-permute-start | bytes 1179656 | tf_op jit(solution)/shard_map/ppermute | solution.py:277
  39.4 0.0 copy-done.11
  39.4 1.9 %collective-permute-start.1 = (bf16[64,512]{1,0:T(8,128)(2,1)S(1)}, bf16[64,512]{1,0:T(8,128)(2,1)S(1)}, u32[]{:S(2)}, u32[]{:S(2)}) collective-permute-start(bf16[64,512]{1,0:T(8,128)(2,1)S(1)} %bitcast.26), channel_id=1, source_target_pairs={{0,64},{64,0},{1,65},{65,1},{2,66},{66,2},{3,67},{67,3},{4,68},{68... | collective-permute-start | bytes 196616 | tf_op jit(solution)/shard_map/ppermute | solution.py:274
  41.4 1.2 collective-permute-done.1.refs_3_
  42.6 0.1 collective-permute-done.2.refs_5_
  42.6 9.4 %collective-permute-done.3.refs_6_ = bf16[192,1024]{1,0:T(8,128)(2,1)S(1)} collective-permute-done((bf16[192,1024]{1,0:T(8,128)(2,1)S(1)}, bf16[192,1024]{1,0:T(8,128)(2,1)S(1)}, u32[]{:S(2)}, u32[]{:S(2)}) %collective-permute-start.3) | collective-permute-done | bytes 393248 | tf_op jit(solution)/shard_map/ppermute | solution.py:277
  52.1 1.5 collective-permute-done.4.refs_7_
  53.6 0.0 copy-done.7
  53.6 0.0 copy-done.8
  53.6 0.8 copy-done.9
  54.4 0.0 collective-permute-done.half_ref
  54.4 3.5 %all-to-all-done = bf16[64,8,640]{2,1,0:T(8,128)(2,1)} async-done(((bf16[64,8,640]{2,1,0:T(8,128)(2,1)}), bf16[64,8,640]{2,1,0:T(8,128)(2,1)}, u32[]{:S(2)}, u32[]{:S(2)}) %all-to-all-start) | async-done | bytes 655392 | tf_op jit(solution)/shard_map/all_to_all | solution.py:283
  57.8 0.0 copy-done.12
  57.8 2.8 %shard_map.114 = (bf16[4,320,512]{2,1,0:T(8,128)(2,1)}, bf16[320,512]{1,0:T(8,128)(2,1)}) custom-call(bf16[512,640]{1,0:T(8,128)(2,1)} %bitcast.9.in_ref), custom_call_target="tpu_custom_call" | custom-call | tf_op jit(solution)/shard_map/pallas_call | solution.py:250
  60.7 0.0 copy-start.3
  60.7 4.4 %all-to-all-start.1 = ((bf16[4,320,512]{2,1,0:T(8,128)(2,1)}), bf16[4,320,512]{2,1,0:T(8,128)(2,1)}, u32[]{:S(2)}, u32[]{:S(2)}) async-start(bf16[4,320,512]{2,1,0:T(8,128)(2,1)} %get-tuple-element.37), calls=%async_computation.1 | async-start | bytes 2621440 | tf_op jit(solution)/shard_map/all_to_all | solution.py:280
  65.1 0.0 copy-done.3
  65.2 1.9 %collective-permute-start.6 = (bf16[320,512]{1,0:T(8,128)(2,1)S(1)}, bf16[320,512]{1,0:T(8,128)(2,1)S(1)}, u32[]{:S(2)}, u32[]{:S(2)}) collective-permute-start(bf16[320,512]{1,0:T(8,128)(2,1)S(1)} %copy-done.3), channel_id=1, source_target_pairs={{0,64},{64,0},{1,65},{65,1},{2,66},{66,2},{3,67},{67,3},{4,68},{68... | collective-permute-start | bytes 983048 | tf_op jit(solution)/shard_map/ppermute | solution.py:274
  67.1 1.6 collective-permute-done.6.refs_1_
  68.7 0.7 copy-done.10
  69.4 4.0 %shard_map.116 = bf16[4,320,256]{2,1,0:T(8,128)(2,1)} custom-call(s32[2]{0:T(128)S(1)} %pad_add_fusion.me_ref, bf16[320,512]{1,0:T(8,128)(2,1)} %get-tuple-element.42.refs_0_.s_ref, bf16[320,512]{1,0:T(8,128)(2,1)} %copy-done.10, bf16[64,512]{1,0:T(8,128)(2,1)} %bitcast.25, bf16[64,512]{1,0:T(8,128)(2,1)} %copy-done.12, bf16[192,1024]{1,0:T(8,128)(2,1)} %copy-done.5, ...), custom_call_target="tpu_custom_call" | custom-call | tf_op jit(solution)/shard_map/pallas_call | solution.py:250
  73.4 8.2 %all-to-all-done.1.x_ref = bf16[4,320,512]{2,1,0:T(8,128)(2,1)} async-done(((bf16[4,320,512]{2,1,0:T(8,128)(2,1)}), bf16[4,320,512]{2,1,0:T(8,128)(2,1)}, u32[]{:S(2)}, u32[]{:S(2)}) %all-to-all-start.1) | async-done | bytes 1310752 | tf_op jit(solution)/shard_map/all_to_all | solution.py:280
  81.6 4.2 %all-to-all-start.2 = ((bf16[4,320,256]{2,1,0:T(8,128)(2,1)}), bf16[4,320,256]{2,1,0:T(8,128)(2,1)}, u32[]{:S(2)}, u32[]{:S(2)}) async-start(bf16[4,320,256]{2,1,0:T(8,128)(2,1)} %shard_map.116), calls=%async_computation.2 | async-start | bytes 1310720 | tf_op jit(solution)/shard_map/all_to_all | solution.py:280
  85.8 3.4 %shard_map.115 = (f32[2,320,192]{2,1,0:T(8,128)}, bf16[2,320,192]{2,1,0:T(8,128)(2,1)S(1)}) custom-call(bf16[4,320,512]{2,1,0:T(8,128)(2,1)} %all-to-all-done.1.x_ref, bf16[2,4,192,512]{3,2,1,0:T(8,128)(2,1)S(1)} %get-tuple-element.38.own_ref, bf16[2,4,192,512]{3,2,1,0:T(8,128)(2,1)S(1)} %collective-permute-done.half_ref), custom_call_target="tpu_custom_call" | custom-call | tf_op jit(solution)/shard_map/pallas_call | solution.py:250
  89.2 1.9 %collective-permute-start.5 = (bf16[2,320,192]{2,1,0:T(8,128)(2,1)S(1)}, bf16[2,320,192]{2,1,0:T(8,128)(2,1)}, u32[]{:S(2)}, u32[]{:S(2)}) collective-permute-start(bf16[2,320,192]{2,1,0:T(8,128)(2,1)S(1)} %get-tuple-element.41), channel_id=1, source_target_pairs={{0,64},{64,0},{1,65},{65,1},{2,66},{66,2},{3,67},{67,3},{4,68},{68... | collective-permute-start | bytes 737288 | tf_op jit(solution)/shard_map/ppermute | solution.py:274
  91.2 3.5 %all-to-all-done.2.in_hbm = bf16[4,320,256]{2,1,0:T(8,128)(2,1)} async-done(((bf16[4,320,256]{2,1,0:T(8,128)(2,1)}), bf16[4,320,256]{2,1,0:T(8,128)(2,1)}, u32[]{:S(2)}, u32[]{:S(2)}) %all-to-all-start.2) | async-done | bytes 655392 | tf_op jit(solution)/shard_map/all_to_all | solution.py:280
  94.7 0.0 collective-permute-done.5.got_hbm
  94.7 2.4 %shard_map.117 = (bf16[320,448]{1,0:T(8,128)(2,1)S(1)}, f32[64,192]{1,0:T(8,128)}) custom-call(f32[2,320,192]{2,1,0:T(8,128)} %get-tuple-element.40.keep_hbm, bf16[2,320,192]{2,1,0:T(8,128)(2,1)} %collective-permute-done.5.got_hbm, bf16[4,320,256]{2,1,0:T(8,128)(2,1)} %all-to-all-done.2.in_hbm, bf16[64,192]{1,0:T(8,128)(2,1)} %bitcast.27), custom_call_target="tpu_custom_call" | custom-call | tf_op jit(solution)/shard_map/pallas_call | solution.py:250
  97.1 1.9 %collective-permute-start.7 = (bf16[320,448]{1,0:T(8,128)(2,1)S(1)}, bf16[320,448]{1,0:T(8,128)(2,1)S(1)}, u32[]{:S(2)}, u32[]{:S(2)}) collective-permute-start(bf16[320,448]{1,0:T(8,128)(2,1)S(1)} %get-tuple-element.48.g_ref), channel_id=1, source_target_pairs={{0,64},{64,0},{1,65},{65,1},{2,66},{66,2},{3,67},{67,3},{4,68},{68... | collective-permute-start | bytes 860168 | tf_op jit(solution)/shard_map/ppermute | solution.py:274
  99.0 1.6 collective-permute-done.7.h_ref
  100.6 2.3 %shard_map.118 = (bf16[4,320,512]{2,1,0:T(8,128)(2,1)}, bf16[320,64]{1,0:T(8,128)(2,1)S(1)}) custom-call(bf16[320,448]{1,0:T(8,128)(2,1)S(1)} %get-tuple-element.48.g_ref, bf16[320,448]{1,0:T(8,128)(2,1)S(1)} %collective-permute-done.7.h_ref, bf16[2,4,192,512]{3,2,1,0:T(8,128)(2,1)S(1)} %get-tuple-element.38.own_ref, ...), custom_call_target="tpu_custom_call" | custom-call | tf_op jit(solution)/shard_map/pallas_call | solution.py:250
  102.9 0.0 copy-start.6
  102.9 3.6 %all-to-all-start.3 = ((bf16[4,320,512]{2,1,0:T(8,128)(2,1)}), bf16[4,320,512]{2,1,0:T(8,128)(2,1)S(1)}, u32[]{:S(2)}, u32[]{:S(2)}) async-start(bf16[4,320,512]{2,1,0:T(8,128)(2,1)} %get-tuple-element.49), calls=%async_computation.3 | async-start | bytes 2621440 | tf_op jit(solution)/shard_map/all_to_all | solution.py:280
  106.5 0.0 copy-done.6
  106.5 0.6 shard_map.119
  107.1 17.8 %all-to-all-done.3.in_ref = bf16[4,320,512]{2,1,0:T(8,128)(2,1)S(1)} async-done(((bf16[4,320,512]{2,1,0:T(8,128)(2,1)}), bf16[4,320,512]{2,1,0:T(8,128)(2,1)S(1)}, u32[]{:S(2)}, u32[]{:S(2)}) %all-to-all-start.3) | async-done | bytes 1310752 | tf_op jit(solution)/shard_map/all_to_all | solution.py:280
  124.9 0.9 shard_map.120
  125.8 10.8 %all_to_all.30 = bf16[4,80,512]{2,1,0:T(8,128)(2,1)S(1)} all-to-all(bf16[4,80,512]{2,1,0:T(8,128)(2,1)} %shard_map.120), channel_id=1, replica_groups=mesh['x'=4,'c'=2,'z'=16,'y'=4] {'y'}, dimensions={0} | all-to-all | bytes 655360 | tf_op jit(solution)/shard_map/all_to_all | solution.py:361
  136.6 1.4 shard_map.121
  138.0 11.9 %all-to-all-start.5 = ((bf16[16,40,256]{2,1,0:T(8,128)(2,1)}), bf16[16,40,256]{2,1,0:T(8,128)(2,1)S(1)}, u32[]{:S(2)}, u32[]{:S(2)}) async-start(bf16[16,40,256]{2,1,0:T(8,128)(2,1)} %bitcast.23), calls=%async_computation.5 | async-start | bytes 655360 | tf_op jit(solution)/shard_map/all_to_all | solution.py:368
  149.9 3.1 %collective-permute-start.10 = (bf16[320,64]{1,0:T(8,128)(2,1)S(1)}, bf16[320,64]{1,0:T(8,128)(2,1)S(1)}, u32[]{:S(2)}, u32[]{:S(2)}) collective-permute-start(bf16[320,64]{1,0:T(8,128)(2,1)S(1)} %get-tuple-element.58.v0_ref), channel_id=1, source_target_pairs={{0,384},{128,0},{256,128},{384,256},{1,385},{129,1},{257,129},{385... | collective-permute-start | bytes 122888 | tf_op jit(solution)/shard_map/ppermute | solution.py:277
  152.9 2.8 %collective-permute-start.8 = (bf16[320,64]{1,0:T(8,128)(2,1)S(1)}, bf16[320,64]{1,0:T(8,128)(2,1)S(1)}, u32[]{:S(2)}, u32[]{:S(2)}) collective-permute-start(bf16[320,64]{1,0:T(8,128)(2,1)S(1)} %get-tuple-element.58.v0_ref), channel_id=1, source_target_pairs={{0,128},{128,256},{256,384},{384,0},{1,129},{129,257},{257,385},{3... | collective-permute-start | bytes 122888 | tf_op jit(solution)/shard_map/ppermute | solution.py:277
  155.7 2.5 %collective-permute-start.9 = (bf16[320,64]{1,0:T(8,128)(2,1)S(1)}, bf16[320,64]{1,0:T(8,128)(2,1)S(1)}, u32[]{:S(2)}, u32[]{:S(2)}) collective-permute-start(bf16[320,64]{1,0:T(8,128)(2,1)S(1)} %get-tuple-element.58.v0_ref), channel_id=1, source_target_pairs={{0,256},{128,384},{256,0},{384,128},{1,257},{129,385},{257,1},{385... | collective-permute-start | bytes 122888 | tf_op jit(solution)/shard_map/ppermute | solution.py:277
  158.3 0.0 collective-permute-done.10.v3_ref
  158.3 2.2 %collective-permute-done.8.v1_ref = bf16[320,64]{1,0:T(8,128)(2,1)S(1)} collective-permute-done((bf16[320,64]{1,0:T(8,128)(2,1)S(1)}, bf16[320,64]{1,0:T(8,128)(2,1)S(1)}, u32[]{:S(2)}, u32[]{:S(2)}) %collective-permute-start.8) | collective-permute-done | bytes 40992 | tf_op jit(solution)/shard_map/ppermute | solution.py:277
  160.5 3.1 %collective-permute-done.9.v2_ref = bf16[320,64]{1,0:T(8,128)(2,1)S(1)} collective-permute-done((bf16[320,64]{1,0:T(8,128)(2,1)S(1)}, bf16[320,64]{1,0:T(8,128)(2,1)S(1)}, u32[]{:S(2)}, u32[]{:S(2)}) %collective-permute-start.9) | collective-permute-done | bytes 40992 | tf_op jit(solution)/shard_map/ppermute | solution.py:277
  163.6 0.0 copy-done.4
  163.6 0.9 shard_map.123
  164.4 4.7 %all-to-all-done.5 = bf16[16,40,256]{2,1,0:T(8,128)(2,1)S(1)} async-done(((bf16[16,40,256]{2,1,0:T(8,128)(2,1)}), bf16[16,40,256]{2,1,0:T(8,128)(2,1)S(1)}, u32[]{:S(2)}, u32[]{:S(2)}) %all-to-all-start.5) | async-done | bytes 327712 | tf_op jit(solution)/shard_map/all_to_all | solution.py:368
  169.1 0.9 shard_map.122
  (8 shorter events, 0.0 us)
Async XLA Ops:
  0.6 21.0 %copy-start = (bf16[1,192,4096]{2,1,0:T(8,128)(2,1)S(1)}, bf16[1,192,4096]{2,1,0:T(8,128)(2,1)}, u32[]{:S(2)}) copy-start(bf16[1,192,4096]{2,1,0:T(8,128)(2,1)} %param.13) | copy-start | bytes 4718596
  3.4 54.4 %all-to-all-start = ((bf16[64,8,640]{2,1,0:T(8,128)(2,1)}), bf16[64,8,640]{2,1,0:T(8,128)(2,1)}, u32[]{:S(2)}, u32[]{:S(2)}) async-start(bf16[64,8,640]{2,1,0:T(8,128)(2,1)} %bitcast.2), calls=%async_computation | async-start | bytes 1310720 | tf_op jit(solution)/shard_map/all_to_all | solution.py:283
  21.6 1.4 copy-start.1
  23.1 1.4 copy-start.2
  24.5 15.0 %copy-start.11 = (bf16[1,64,512]{2,1,0:T(8,128)(2,1)S(1)}, bf16[1,64,512]{2,1,0:T(8,128)(2,1)}, u32[]{:S(2)}) copy-start(bf16[1,64,512]{2,1,0:T(8,128)(2,1)} %param.17) | copy-start | bytes 196612
  25.4 0.7 copy-start.5
  26.1 28.3 %collective-permute-start = (bf16[2,4,192,512]{3,2,1,0:T(8,128)(2,1)S(1)}, bf16[2,4,192,512]{3,2,1,0:T(8,128)(2,1)S(1)}, u32[]{:S(2)}, u32[]{:S(2)}) collective-permute-start(bf16[2,4,192,512]{3,2,1,0:T(8,128)(2,1)S(1)} %get-tuple-element.31), channel_id=1, source_target_pairs={{0,64},{64,0},{1,65},{65,1},{2,66},{66,2},{3,67},{67,3},{4,68},{68... | collective-permute-start | bytes 4718600 | tf_op jit(solution)/shard_map/ppermute | solution.py:274
  28.0 14.6 %collective-permute-start.2 = (bf16[192,1024]{1,0:T(8,128)(2,1)S(1)}, bf16[192,1024]{1,0:T(8,128)(2,1)S(1)}, u32[]{:S(2)}, u32[]{:S(2)}) collective-permute-start(bf16[192,1024]{1,0:T(8,128)(2,1)S(1)} %get-tuple-element.33), channel_id=1, source_target_pairs={{0,128},{128,256},{256,384},{384,0},{1,129},{129,257},{257,385},{3... | collective-permute-start | bytes 1179656 | tf_op jit(solution)/shard_map/ppermute | solution.py:277
  31.4 20.6 %collective-permute-start.3 = (bf16[192,1024]{1,0:T(8,128)(2,1)S(1)}, bf16[192,1024]{1,0:T(8,128)(2,1)S(1)}, u32[]{:S(2)}, u32[]{:S(2)}) collective-permute-start(bf16[192,1024]{1,0:T(8,128)(2,1)S(1)} %get-tuple-element.34), channel_id=1, source_target_pairs={{0,256},{128,384},{256,0},{384,128},{1,257},{129,385},{257,1},{385... | collective-permute-start | bytes 1179656 | tf_op jit(solution)/shard_map/ppermute | solution.py:277
  36.1 17.5 %collective-permute-start.4 = (bf16[192,1024]{1,0:T(8,128)(2,1)S(1)}, bf16[192,1024]{1,0:T(8,128)(2,1)S(1)}, u32[]{:S(2)}, u32[]{:S(2)}) collective-permute-start(bf16[192,1024]{1,0:T(8,128)(2,1)S(1)} %get-tuple-element.35), channel_id=1, source_target_pairs={{0,384},{128,0},{256,128},{384,256},{1,385},{129,1},{257,129},{385... | collective-permute-start | bytes 1179656 | tf_op jit(solution)/shard_map/ppermute | solution.py:277
  39.4 3.1 %collective-permute-start.1 = (bf16[64,512]{1,0:T(8,128)(2,1)S(1)}, bf16[64,512]{1,0:T(8,128)(2,1)S(1)}, u32[]{:S(2)}, u32[]{:S(2)}) collective-permute-start(bf16[64,512]{1,0:T(8,128)(2,1)S(1)} %bitcast.26), channel_id=1, source_target_pairs={{0,64},{64,0},{1,65},{65,1},{2,66},{66,2},{3,67},{67,3},{4,68},{68... | collective-permute-start | bytes 196616 | tf_op jit(solution)/shard_map/ppermute | solution.py:274
  42.6 15.3 %copy-start.12 = (bf16[64,512]{1,0:T(8,128)(2,1)}, bf16[64,512]{1,0:T(8,128)(2,1)S(1)}, u32[]{:S(2)}) copy-start(bf16[64,512]{1,0:T(8,128)(2,1)S(1)} %collective-permute-done.1.refs_3_) | copy-start | bytes 196612
  42.6 11.0 %copy-start.7 = (bf16[192,1024]{1,0:T(8,128)(2,1)}, bf16[192,1024]{1,0:T(8,128)(2,1)S(1)}, u32[]{:S(2)}) copy-start(bf16[192,1024]{1,0:T(8,128)(2,1)S(1)} %collective-permute-done.2.refs_5_) | copy-start | bytes 1179652
  52.0 1.6 copy-start.8
  53.6 0.8 copy-start.9
  60.7 4.5 %copy-start.3 = (bf16[320,512]{1,0:T(8,128)(2,1)S(1)}, bf16[320,512]{1,0:T(8,128)(2,1)}, u32[]{:S(2)}) copy-start(bf16[320,512]{1,0:T(8,128)(2,1)} %get-tuple-element.42.refs_0_.s_ref) | copy-start | bytes 983044
  60.7 20.9 %all-to-all-start.1 = ((bf16[4,320,512]{2,1,0:T(8,128)(2,1)}), bf16[4,320,512]{2,1,0:T(8,128)(2,1)}, u32[]{:S(2)}, u32[]{:S(2)}) async-start(bf16[4,320,512]{2,1,0:T(8,128)(2,1)} %get-tuple-element.37), calls=%async_computation.1 | async-start | bytes 2621440 | tf_op jit(solution)/shard_map/all_to_all | solution.py:280
  65.2 3.5 %collective-permute-start.6 = (bf16[320,512]{1,0:T(8,128)(2,1)S(1)}, bf16[320,512]{1,0:T(8,128)(2,1)S(1)}, u32[]{:S(2)}, u32[]{:S(2)}) collective-permute-start(bf16[320,512]{1,0:T(8,128)(2,1)S(1)} %copy-done.3), channel_id=1, source_target_pairs={{0,64},{64,0},{1,65},{65,1},{2,66},{66,2},{3,67},{67,3},{4,68},{68... | collective-permute-start | bytes 983048 | tf_op jit(solution)/shard_map/ppermute | solution.py:274
  68.7 0.7 copy-start.10
  81.6 13.0 %all-to-all-start.2 = ((bf16[4,320,256]{2,1,0:T(8,128)(2,1)}), bf16[4,320,256]{2,1,0:T(8,128)(2,1)}, u32[]{:S(2)}, u32[]{:S(2)}) async-start(bf16[4,320,256]{2,1,0:T(8,128)(2,1)} %shard_map.116), calls=%async_computation.2 | async-start | bytes 1310720 | tf_op jit(solution)/shard_map/all_to_all | solution.py:280
  89.2 5.4 %collective-permute-start.5 = (bf16[2,320,192]{2,1,0:T(8,128)(2,1)S(1)}, bf16[2,320,192]{2,1,0:T(8,128)(2,1)}, u32[]{:S(2)}, u32[]{:S(2)}) collective-permute-start(bf16[2,320,192]{2,1,0:T(8,128)(2,1)S(1)} %get-tuple-element.41), channel_id=1, source_target_pairs={{0,64},{64,0},{1,65},{65,1},{2,66},{66,2},{3,67},{67,3},{4,68},{68... | collective-permute-start | bytes 737288 | tf_op jit(solution)/shard_map/ppermute | solution.py:274
  97.1 3.5 %collective-permute-start.7 = (bf16[320,448]{1,0:T(8,128)(2,1)S(1)}, bf16[320,448]{1,0:T(8,128)(2,1)S(1)}, u32[]{:S(2)}, u32[]{:S(2)}) collective-permute-start(bf16[320,448]{1,0:T(8,128)(2,1)S(1)} %get-tuple-element.48.g_ref), channel_id=1, source_target_pairs={{0,64},{64,0},{1,65},{65,1},{2,66},{66,2},{3,67},{67,3},{4,68},{68... | collective-permute-start | bytes 860168 | tf_op jit(solution)/shard_map/ppermute | solution.py:274
  102.9 3.6 %copy-start.6 = (s32[32,8]{0,1:T(8,128)S(1)}, s32[32,8]{0,1:T(8,128)}, u32[]{:S(2)}) copy-start(s32[32,8]{0,1:T(8,128)} %param.12) | copy-start | bytes 3076
  102.9 22.0 %all-to-all-start.3 = ((bf16[4,320,512]{2,1,0:T(8,128)(2,1)}), bf16[4,320,512]{2,1,0:T(8,128)(2,1)S(1)}, u32[]{:S(2)}, u32[]{:S(2)}) async-start(bf16[4,320,512]{2,1,0:T(8,128)(2,1)} %get-tuple-element.49), calls=%async_computation.3 | async-start | bytes 2621440 | tf_op jit(solution)/shard_map/all_to_all | solution.py:280
  124.9 38.6 %copy-start.4 = (bf16[320,512]{1,0:T(8,128)(2,1)S(1)}, bf16[320,512]{1,0:T(8,128)(2,1)}, u32[]{:S(2)}) copy-start(bf16[320,512]{1,0:T(8,128)(2,1)} %get-tuple-element.42.refs_0_.s_ref) | copy-start | bytes 983044
  138.0 31.2 %all-to-all-start.5 = ((bf16[16,40,256]{2,1,0:T(8,128)(2,1)}), bf16[16,40,256]{2,1,0:T(8,128)(2,1)S(1)}, u32[]{:S(2)}, u32[]{:S(2)}) async-start(bf16[16,40,256]{2,1,0:T(8,128)(2,1)} %bitcast.23), calls=%async_computation.5 | async-start | bytes 655360 | tf_op jit(solution)/shard_map/all_to_all | solution.py:368
  149.9 8.4 %collective-permute-start.10 = (bf16[320,64]{1,0:T(8,128)(2,1)S(1)}, bf16[320,64]{1,0:T(8,128)(2,1)S(1)}, u32[]{:S(2)}, u32[]{:S(2)}) collective-permute-start(bf16[320,64]{1,0:T(8,128)(2,1)S(1)} %get-tuple-element.58.v0_ref), channel_id=1, source_target_pairs={{0,384},{128,0},{256,128},{384,256},{1,385},{129,1},{257,129},{385... | collective-permute-start | bytes 122888 | tf_op jit(solution)/shard_map/ppermute | solution.py:277
  152.9 7.5 %collective-permute-start.8 = (bf16[320,64]{1,0:T(8,128)(2,1)S(1)}, bf16[320,64]{1,0:T(8,128)(2,1)S(1)}, u32[]{:S(2)}, u32[]{:S(2)}) collective-permute-start(bf16[320,64]{1,0:T(8,128)(2,1)S(1)} %get-tuple-element.58.v0_ref), channel_id=1, source_target_pairs={{0,128},{128,256},{256,384},{384,0},{1,129},{129,257},{257,385},{3... | collective-permute-start | bytes 122888 | tf_op jit(solution)/shard_map/ppermute | solution.py:277
  155.7 7.8 %collective-permute-start.9 = (bf16[320,64]{1,0:T(8,128)(2,1)S(1)}, bf16[320,64]{1,0:T(8,128)(2,1)S(1)}, u32[]{:S(2)}, u32[]{:S(2)}) collective-permute-start(bf16[320,64]{1,0:T(8,128)(2,1)S(1)} %get-tuple-element.58.v0_ref), channel_id=1, source_target_pairs={{0,256},{128,384},{256,0},{384,128},{1,257},{129,385},{257,1},{385... | collective-permute-start | bytes 122888 | tf_op jit(solution)/shard_map/ppermute | solution.py:277

commit v8 on v6

--- a/solution.py
+++ b/solution.py
@@ -37,9 +37,17 @@
         copy.wait()
 
 
-def expert_of(place, experts):
-    deep = experts // FLAT
-    return lax.rem(place, deep) * FLAT + lax.div(place, deep)
+def low(value, size):
+    return value & (size - 1)
+
+
+def high(value, size):
+    return value >> (size.bit_length() - 1)
+
+
+def expert_of(place):
+    outer, inner = high(place, FLAT * FLAT), low(place, FLAT * FLAT)
+    return low(inner, FLAT) * (FLAT * FLAT) + outer * FLAT + high(inner, FLAT)
 
 
 def pack_kernel(ids_hbm, prob_hbm, tok_hbm, dy_hbm, out_ref, ids_ref, prob_ref, tok_ref, dy_ref, sems):
@@ -51,21 +59,21 @@
     parts = 2 * width // LANE
     span = parts * count
     row = lax.broadcasted_iota(jnp.int32, (rows, count), 0)
-    own = expert_of(lax.div(row, parts), rows // parts)
+    own = expert_of(high(row, parts))
     hit = jnp.zeros((rows, count), F32)
     weight = jnp.zeros((rows, count), F32)
     for k in range(ids_ref.shape[0]):
         same = ids_ref[k : k + 1, :] == own
         hit = jnp.where(same, 1.0, hit)
         weight = jnp.where(same, prob_ref[k : k + 1, :], weight)
-    weight = jnp.where(lax.rem(row, parts) < parts // 2, hit, weight)
+    weight = jnp.where(low(row, parts) < parts // 2, hit, weight)
     first = lax.broadcasted_iota(jnp.int32, (count, count), 0)
     second = lax.broadcasted_iota(jnp.int32, (count, count), 1)
     before = jnp.where(first < second, 1.0, 0.0).astype(BF)
     code = jnp.where(hit > 0.5, nn(hit.astype(BF), before), -1.0)
     wide_row = lax.broadcasted_iota(jnp.int32, (rows, span), 0)
     lane = lax.broadcasted_iota(jnp.int32, (rows, span), 1)
-    here = lax.rem(wide_row, parts) == lax.div(lane, count)
+    here = low(wide_row, parts) == high(lane, count)
     spread = jnp.where(here, jnp.concatenate([code] * parts, axis=1), -1.0)
     table = jnp.concatenate(
         [ref[:, c : c + LANE] for ref in (tok_ref, dy_ref) for c in range(0, width, LANE)], axis=0
@@ -78,7 +86,7 @@
 
 def code_of(ids, experts):
     count = ids.shape[1]
-    own = expert_of(lax.broadcasted_iota(jnp.int32, (experts, count), 0), experts)
+    own = expert_of(lax.broadcasted_iota(jnp.int32, (experts, count), 0))
     hit = jnp.zeros((experts, count), F32)
     for k in range(ids.shape[0]):
         hit = jnp.where(ids[k : k + 1, :] == own, 1.0, hit)
@@ -95,7 +103,7 @@
     experts = total // parts
     first = lax.broadcasted_iota(jnp.int32, (total, total), 0)
     second = lax.broadcasted_iota(jnp.int32, (total, total), 1)
-    there = lax.rem(first, experts) * parts + lax.div(first, experts)
+    there = low(first, experts) * parts + high(first, experts)
     perm = jnp.where(second == there, 1.0, 0.0).astype(BF)
     rows = nn(perm, in_ref[...]).astype(BF)
     for r in range(parts):
@@ -239,7 +247,7 @@
 
 
 def per_device(tokens, grad_out, prob, ids, w_gate, w_up, w_down, adapter_a, adapter_b):
-    experts = lax.axis_size(("z", "y"))
+    experts = lax.axis_size(("zh", "zl", "y"))
     chips = lax.axis_size("x")
     count, width = tokens.shape
     rank = adapter_b.shape[1]
@@ -261,7 +269,7 @@
         return lax.all_to_all(block, "x", 0, 0, tiled=True)
 
     def route(block):
-        return lax.all_to_all(block, ("y", "z"), 0, 0, tiled=True)
+        return lax.all_to_all(block, ("zl", "y", "zh"), 0, 0, tiled=True)
 
     parts = 2 * width // LANE
     slow = pl.BlockSpec(memory_space=pltpu.HBM)
@@ -343,8 +351,8 @@
 
 
 def solution(mesh):
-    fine = Mesh(mesh.devices.reshape(4, 2, 16, 4), ("x", "c", "z", "y"))
-    dp, ex = ("x", "c"), ("z", "y")
+    fine = Mesh(mesh.devices.reshape(4, 2, 4, 4, 4), ("x", "c", "zh", "zl", "y"))
+    dp, ex = ("x", "c"), ("zh", "zl", "y")
     specs = (
         P(ex, dp), P(ex, dp), P(ex, None), P(ex, None),
         P(ex, dp, None), P(ex, dp, None), P(ex, dp, None), P(ex, None, dp), P(ex, None, dp),

time: 166 us -> 167 us (level)
  the two profiles are of different devices: /device:TPU:8 before, /device:TPU:32 now
where the time goes in v8:
time: 167 us; the launch traced here: 166 us
  starting transfers between devices  70.5 us (42%)
  waiting for transfers between devices  68 us (41%)
  Pallas kernels  20.8 us (12%)
  local copies, waits for them, and re-layouts  5.9 us (4%)
    all_to_all x3, waiting for transfers between devices, over_x(): return lax.all_to_all(block, 'x', 0, 0, tiled=True)  30.6 us
    all_to_all x2, starting transfers between devices, route(): return lax.all_to_all(block, ('zl', 'y', 'zh'), 0, 0, tiled=True)  29 us
    pallas_call x11, Pallas kernels, call(): pl.pallas_call(body, out_shape=outs, in_specs=[smem] * scalars + list(pla...  20.8 us
    ppermute x6, starting transfers between devices, shift(): lax.ppermute(block, 'x', [(i, (i + by) % chips) for i in range(chips)])  19.8 us
    all_to_all x2, waiting for transfers between devices, route(): return lax.all_to_all(block, ('zl', 'y', 'zh'), 0, 0, tiled=True)  16.7 us
    ppermute x6, waiting for transfers between devices, shift(): lax.ppermute(block, 'x', [(i, (i + by) % chips) for i in range(chips)])  16.3 us
    all_to_all x3, starting transfers between devices, over_x(): return lax.all_to_all(block, 'x', 0, 0, tiled=True)  12.2 us
    ppermute x5, starting transfers between devices, swap(): return lax.ppermute(block, 'c', [(0, 1), (1, 0)])  9.59 us
  transfers between devices with their start and end apart: 16, of which 13 were waited for; matrix products, arithmetic and copies ran while one was open for 0% of the time, Pallas kernels for 6%

profile of v8, /device:TPU:32, one launch (start us, length us, event | category | flops | bytes accessed | tf_op | source)
XLA Modules:
  0.0 166.2 jit_solution(11311511712621539111)
XLA Ops:
  0.6 0.0 copy-start
  0.6 2.8 %shard_map.112 = bf16[512,640]{1,0:T(8,128)(2,1)} custom-call(s32[8,32]{1,0:T(8,128)} %bitcast.19, f32[8,32]{1,0:T(8,128)} %bitcast.26, bf16[32,512]{1,0:T(8,128)(2,1)} %tok_hbm.1, bf16[32,512]{1,0:T(8,128)(2,1)} %dy_hbm.1), custom_call_target="tpu_custom_call" | custom-call | tf_op jit(solution)/shard_map/pallas_call | solution.py:239
  3.5 18.6 %all-to-all-start = ((bf16[64,8,640]{2,1,0:T(8,128)(2,1)}), bf16[64,8,640]{2,1,0:T(8,128)(2,1)}, u32[]{:S(2)}, u32[]{:S(2)}) async-start(bf16[64,8,640]{2,1,0:T(8,128)(2,1)} %bitcast.2), calls=%async_computation | async-start | bytes 1310720 | tf_op jit(solution)/shard_map/all_to_all | solution.py:272
  22.1 0.1 pad_add_fusion.me_ref
  22.1 0.0 copy-done
  22.1 0.0 copy-start.1
  22.1 1.4 copy-done.1
  23.6 1.4 copy-done.2
  25.0 0.9 shard_map.113
  25.9 0.0 copy-start.5
  25.9 0.7 copy-done.5
  26.6 1.9 %collective-permute-start = (bf16[2,4,192,512]{3,2,1,0:T(8,128)(2,1)S(1)}, bf16[2,4,192,512]{3,2,1,0:T(8,128)(2,1)S(1)}, u32[]{:S(2)}, u32[]{:S(2)}) collective-permute-start(bf16[2,4,192,512]{3,2,1,0:T(8,128)(2,1)S(1)} %get-tuple-element.26), channel_id=1, source_target_pairs={{0,64},{64,0},{1,65},{65,1},{2,66},{66,2},{3,67},{67,3},{4,68},{68... | collective-permute-start | bytes 4718600 | tf_op jit(solution)/shard_map/ppermute | solution.py:263
  28.5 3.4 %collective-permute-start.2 = (bf16[192,1024]{1,0:T(8,128)(2,1)S(1)}, bf16[192,1024]{1,0:T(8,128)(2,1)S(1)}, u32[]{:S(2)}, u32[]{:S(2)}) collective-permute-start(bf16[192,1024]{1,0:T(8,128)(2,1)S(1)} %get-tuple-element.28), channel_id=1, source_target_pairs={{0,128},{128,256},{256,384},{384,0},{1,129},{129,257},{257,385},{3... | collective-permute-start | bytes 1179656 | tf_op jit(solution)/shard_map/ppermute | solution.py:266
  31.9 4.6 %collective-permute-start.3 = (bf16[192,1024]{1,0:T(8,128)(2,1)S(1)}, bf16[192,1024]{1,0:T(8,128)(2,1)S(1)}, u32[]{:S(2)}, u32[]{:S(2)}) collective-permute-start(bf16[192,1024]{1,0:T(8,128)(2,1)S(1)} %get-tuple-element.29), channel_id=1, source_target_pairs={{0,256},{128,384},{256,0},{384,128},{1,257},{129,385},{257,1},{385... | collective-permute-start | bytes 1179656 | tf_op jit(solution)/shard_map/ppermute | solution.py:266
  36.6 3.3 %collective-permute-start.4 = (bf16[192,1024]{1,0:T(8,128)(2,1)S(1)}, bf16[192,1024]{1,0:T(8,128)(2,1)S(1)}, u32[]{:S(2)}, u32[]{:S(2)}) collective-permute-start(bf16[192,1024]{1,0:T(8,128)(2,1)S(1)} %get-tuple-element.30), channel_id=1, source_target_pairs={{0,384},{128,0},{256,128},{384,256},{1,385},{129,1},{257,129},{385... | collective-permute-start | bytes 1179656 | tf_op jit(solution)/shard_map/ppermute | solution.py:266
  39.9 0.0 copy-done.11
  39.9 1.9 %collective-permute-start.1 = (bf16[64,512]{1,0:T(8,128)(2,1)S(1)}, bf16[64,512]{1,0:T(8,128)(2,1)S(1)}, u32[]{:S(2)}, u32[]{:S(2)}) collective-permute-start(bf16[64,512]{1,0:T(8,128)(2,1)S(1)} %bitcast.24), channel_id=1, source_target_pairs={{0,64},{64,0},{1,65},{65,1},{2,66},{66,2},{3,67},{67,3},{4,68},{68... | collective-permute-start | bytes 196616 | tf_op jit(solution)/shard_map/ppermute | solution.py:263
  41.9 1.2 collective-permute-done.1.refs_3_
  43.1 0.1 collective-permute-done.2.refs_5_
  43.1 9.4 %collective-permute-done.3.refs_6_ = bf16[192,1024]{1,0:T(8,128)(2,1)S(1)} collective-permute-done((bf16[192,1024]{1,0:T(8,128)(2,1)S(1)}, bf16[192,1024]{1,0:T(8,128)(2,1)S(1)}, u32[]{:S(2)}, u32[]{:S(2)}) %collective-permute-start.3) | collective-permute-done | bytes 393248 | tf_op jit(solution)/shard_map/ppermute | solution.py:266
  52.6 1.5 collective-permute-done.4.refs_7_
  54.1 0.0 copy-done.7
  54.1 0.0 copy-done.8
  54.1 0.8 copy-done.9
  54.9 0.0 collective-permute-done.half_ref
  54.9 6.5 %all-to-all-done = bf16[64,8,640]{2,1,0:T(8,128)(2,1)} async-done(((bf16[64,8,640]{2,1,0:T(8,128)(2,1)}), bf16[64,8,640]{2,1,0:T(8,128)(2,1)}, u32[]{:S(2)}, u32[]{:S(2)}) %all-to-all-start) | async-done | bytes 655392 | tf_op jit(solution)/shard_map/all_to_all | solution.py:272
  61.4 0.0 copy-done.12
  61.4 2.8 %shard_map.114 = (bf16[4,320,512]{2,1,0:T(8,128)(2,1)}, bf16[320,512]{1,0:T(8,128)(2,1)}) custom-call(bf16[512,640]{1,0:T(8,128)(2,1)} %bitcast.9.in_ref), custom_call_target="tpu_custom_call" | custom-call | tf_op jit(solution)/shard_map/pallas_call | solution.py:239
  64.3 0.0 copy-start.3
  64.3 4.4 %all-to-all-start.1 = ((bf16[4,320,512]{2,1,0:T(8,128)(2,1)}), bf16[4,320,512]{2,1,0:T(8,128)(2,1)}, u32[]{:S(2)}, u32[]{:S(2)}) async-start(bf16[4,320,512]{2,1,0:T(8,128)(2,1)} %get-tuple-element.32), calls=%async_computation.1 | async-start | bytes 2621440 | tf_op jit(solution)/shard_map/all_to_all | solution.py:269
  68.7 0.0 copy-done.3
  68.7 1.9 %collective-permute-start.6 = (bf16[320,512]{1,0:T(8,128)(2,1)S(1)}, bf16[320,512]{1,0:T(8,128)(2,1)S(1)}, u32[]{:S(2)}, u32[]{:S(2)}) collective-permute-start(bf16[320,512]{1,0:T(8,128)(2,1)S(1)} %copy-done.3), channel_id=1, source_target_pairs={{0,64},{64,0},{1,65},{65,1},{2,66},{66,2},{3,67},{67,3},{4,68},{68... | collective-permute-start | bytes 983048 | tf_op jit(solution)/shard_map/ppermute | solution.py:263
  70.6 1.6 collective-permute-done.6.refs_1_
  72.2 0.7 copy-done.10
  73.0 4.0 %shard_map.116 = bf16[4,320,256]{2,1,0:T(8,128)(2,1)} custom-call(s32[2]{0:T(128)S(1)} %pad_add_fusion.me_ref, bf16[320,512]{1,0:T(8,128)(2,1)} %get-tuple-element.37.refs_0_.s_ref, bf16[320,512]{1,0:T(8,128)(2,1)} %copy-done.10, bf16[64,512]{1,0:T(8,128)(2,1)} %bitcast.23, bf16[64,512]{1,0:T(8,128)(2,1)} %copy-done.12, bf16[192,1024]{1,0:T(8,128)(2,1)} %copy-done.5, ...), custom_call_target="tpu_custom_call" | custom-call | tf_op jit(solution)/shard_map/pallas_call | solution.py:239
  77.0 8.7 %all-to-all-done.1.x_ref = bf16[4,320,512]{2,1,0:T(8,128)(2,1)} async-done(((bf16[4,320,512]{2,1,0:T(8,128)(2,1)}), bf16[4,320,512]{2,1,0:T(8,128)(2,1)}, u32[]{:S(2)}, u32[]{:S(2)}) %all-to-all-start.1) | async-done | bytes 1310752 | tf_op jit(solution)/shard_map/all_to_all | solution.py:269
  85.7 4.2 %all-to-all-start.2 = ((bf16[4,320,256]{2,1,0:T(8,128)(2,1)}), bf16[4,320,256]{2,1,0:T(8,128)(2,1)}, u32[]{:S(2)}, u32[]{:S(2)}) async-start(bf16[4,320,256]{2,1,0:T(8,128)(2,1)} %shard_map.116), calls=%async_computation.2 | async-start | bytes 1310720 | tf_op jit(solution)/shard_map/all_to_all | solution.py:269
  89.9 3.4 %shard_map.115 = (f32[2,320,192]{2,1,0:T(8,128)}, bf16[2,320,192]{2,1,0:T(8,128)(2,1)S(1)}) custom-call(bf16[4,320,512]{2,1,0:T(8,128)(2,1)} %all-to-all-done.1.x_ref, bf16[2,4,192,512]{3,2,1,0:T(8,128)(2,1)S(1)} %get-tuple-element.33.own_ref, bf16[2,4,192,512]{3,2,1,0:T(8,128)(2,1)S(1)} %collective-permute-done.half_ref), custom_call_target="tpu_custom_call" | custom-call | tf_op jit(solution)/shard_map/pallas_call | solution.py:239
  93.3 1.9 %collective-permute-start.5 = (bf16[2,320,192]{2,1,0:T(8,128)(2,1)S(1)}, bf16[2,320,192]{2,1,0:T(8,128)(2,1)}, u32[]{:S(2)}, u32[]{:S(2)}) collective-permute-start(bf16[2,320,192]{2,1,0:T(8,128)(2,1)S(1)} %get-tuple-element.36), channel_id=1, source_target_pairs={{0,64},{64,0},{1,65},{65,1},{2,66},{66,2},{3,67},{67,3},{4,68},{68... | collective-permute-start | bytes 737288 | tf_op jit(solution)/shard_map/ppermute | solution.py:263
  95.2 3.6 %all-to-all-done.2.in_hbm = bf16[4,320,256]{2,1,0:T(8,128)(2,1)} async-done(((bf16[4,320,256]{2,1,0:T(8,128)(2,1)}), bf16[4,320,256]{2,1,0:T(8,128)(2,1)}, u32[]{:S(2)}, u32[]{:S(2)}) %all-to-all-start.2) | async-done | bytes 655392 | tf_op jit(solution)/shard_map/all_to_all | solution.py:269
  98.9 0.0 collective-permute-done.5.got_hbm
  98.9 2.4 %shard_map.117 = (bf16[320,448]{1,0:T(8,128)(2,1)S(1)}, f32[64,192]{1,0:T(8,128)}) custom-call(f32[2,320,192]{2,1,0:T(8,128)} %get-tuple-element.35.keep_hbm, bf16[2,320,192]{2,1,0:T(8,128)(2,1)} %collective-permute-done.5.got_hbm, bf16[4,320,256]{2,1,0:T(8,128)(2,1)} %all-to-all-done.2.in_hbm, bf16[64,192]{1,0:T(8,128)(2,1)} %bitcast.25), custom_call_target="tpu_custom_call" | custom-call | tf_op jit(solution)/shard_map/pallas_call | solution.py:239
  101.3 1.9 %collective-permute-start.7 = (bf16[320,448]{1,0:T(8,128)(2,1)S(1)}, bf16[320,448]{1,0:T(8,128)(2,1)S(1)}, u32[]{:S(2)}, u32[]{:S(2)}) collective-permute-start(bf16[320,448]{1,0:T(8,128)(2,1)S(1)} %get-tuple-element.43.g_ref), channel_id=1, source_target_pairs={{0,64},{64,0},{1,65},{65,1},{2,66},{66,2},{3,67},{67,3},{4,68},{68... | collective-permute-start | bytes 860168 | tf_op jit(solution)/shard_map/ppermute | solution.py:263
  103.2 1.6 collective-permute-done.7.h_ref
  104.8 2.3 %shard_map.118 = (bf16[4,320,512]{2,1,0:T(8,128)(2,1)}, bf16[320,64]{1,0:T(8,128)(2,1)S(1)}) custom-call(bf16[320,448]{1,0:T(8,128)(2,1)S(1)} %get-tuple-element.43.g_ref, bf16[320,448]{1,0:T(8,128)(2,1)S(1)} %collective-permute-done.7.h_ref, bf16[2,4,192,512]{3,2,1,0:T(8,128)(2,1)S(1)} %get-tuple-element.33.own_ref, ...), custom_call_target="tpu_custom_call" | custom-call | tf_op jit(solution)/shard_map/pallas_call | solution.py:239
  107.1 0.0 copy-start.6
  107.1 3.6 %all-to-all-start.3 = ((bf16[4,320,512]{2,1,0:T(8,128)(2,1)}), bf16[4,320,512]{2,1,0:T(8,128)(2,1)S(1)}, u32[]{:S(2)}, u32[]{:S(2)}) async-start(bf16[4,320,512]{2,1,0:T(8,128)(2,1)} %get-tuple-element.44), calls=%async_computation.3 | async-start | bytes 2621440 | tf_op jit(solution)/shard_map/all_to_all | solution.py:269
  110.7 0.0 copy-done.6
  110.7 0.0 copy-start.4
  110.7 0.2 shard_map.119.code_ref
  110.9 18.3 %all-to-all-done.3.in_ref = bf16[4,320,512]{2,1,0:T(8,128)(2,1)S(1)} async-done(((bf16[4,320,512]{2,1,0:T(8,128)(2,1)}), bf16[4,320,512]{2,1,0:T(8,128)(2,1)S(1)}, u32[]{:S(2)}, u32[]{:S(2)}) %all-to-all-start.3) | async-done | bytes 1310752 | tf_op jit(solution)/shard_map/all_to_all | solution.py:269
  129.1 0.2 shard_map.120
  129.3 0.8 reshape.20
  130.1 10.5 %all-to-all-start.4 = ((bf16[64,2,1280]{2,1,0:T(2,128)(2,1)}), bf16[64,2,1280]{2,1,0:T(2,128)(2,1)S(1)}, u32[]{:S(2)}, u32[]{:S(2)}) async-start(bf16[64,2,1280]{2,1,0:T(2,128)(2,1)} %reshape.20), calls=%async_computation.4 | async-start | bytes 655360 | tf_op jit(solution)/shard_map/all_to_all | solution.py:272
  140.6 3.1 %collective-permute-start.10 = (bf16[320,64]{1,0:T(8,128)(2,1)S(1)}, bf16[320,64]{1,0:T(8,128)(2,1)S(1)}, u32[]{:S(2)}, u32[]{:S(2)}) collective-permute-start(bf16[320,64]{1,0:T(8,128)(2,1)S(1)} %get-tuple-element.48.v0_ref), channel_id=1, source_target_pairs={{0,384},{128,0},{256,128},{384,256},{1,385},{129,1},{257,129},{385... | collective-permute-start | bytes 122888 | tf_op jit(solution)/shard_map/ppermute | solution.py:266
  143.7 2.8 %collective-permute-start.8 = (bf16[320,64]{1,0:T(8,128)(2,1)S(1)}, bf16[320,64]{1,0:T(8,128)(2,1)S(1)}, u32[]{:S(2)}, u32[]{:S(2)}) collective-permute-start(bf16[320,64]{1,0:T(8,128)(2,1)S(1)} %get-tuple-element.48.v0_ref), channel_id=1, source_target_pairs={{0,128},{128,256},{256,384},{384,0},{1,129},{129,257},{257,385},{3... | collective-permute-start | bytes 122888 | tf_op jit(solution)/shard_map/ppermute | solution.py:266
  146.4 2.5 %collective-permute-start.9 = (bf16[320,64]{1,0:T(8,128)(2,1)S(1)}, bf16[320,64]{1,0:T(8,128)(2,1)S(1)}, u32[]{:S(2)}, u32[]{:S(2)}) collective-permute-start(bf16[320,64]{1,0:T(8,128)(2,1)S(1)} %get-tuple-element.48.v0_ref), channel_id=1, source_target_pairs={{0,256},{128,384},{256,0},{384,128},{1,257},{129,385},{257,1},{385... | collective-permute-start | bytes 122888 | tf_op jit(solution)/shard_map/ppermute | solution.py:266
  149.0 0.0 collective-permute-done.10.v3_ref
  149.0 3.1 %collective-permute-done.8.v1_ref = bf16[320,64]{1,0:T(8,128)(2,1)S(1)} collective-permute-done((bf16[320,64]{1,0:T(8,128)(2,1)S(1)}, bf16[320,64]{1,0:T(8,128)(2,1)S(1)}, u32[]{:S(2)}, u32[]{:S(2)}) %collective-permute-start.8) | collective-permute-done | bytes 40992 | tf_op jit(solution)/shard_map/ppermute | solution.py:266
  152.1 2.2 %collective-permute-done.9.v2_ref = bf16[320,64]{1,0:T(8,128)(2,1)S(1)} collective-permute-done((bf16[320,64]{1,0:T(8,128)(2,1)S(1)}, bf16[320,64]{1,0:T(8,128)(2,1)S(1)}, u32[]{:S(2)}, u32[]{:S(2)}) %collective-permute-start.9) | collective-permute-done | bytes 40992 | tf_op jit(solution)/shard_map/ppermute | solution.py:266
  154.3 0.0 copy-done.4
  154.3 0.9 shard_map.122
  155.2 10.2 %all-to-all-done.4 = bf16[64,2,1280]{2,1,0:T(2,128)(2,1)S(1)} async-done(((bf16[64,2,1280]{2,1,0:T(2,128)(2,1)}), bf16[64,2,1280]{2,1,0:T(2,128)(2,1)S(1)}, u32[]{:S(2)}, u32[]{:S(2)}) %all-to-all-start.4) | async-done | bytes 327712 | tf_op jit(solution)/shard_map/all_to_all | solution.py:272
  165.4 0.8 shard_map.121
  (8 shorter events, 0.0 us)
Async XLA Ops:
  0.6 21.5 %copy-start = (bf16[1,192,4096]{2,1,0:T(8,128)(2,1)S(1)}, bf16[1,192,4096]{2,1,0:T(8,128)(2,1)}, u32[]{:S(2)}) copy-start(bf16[1,192,4096]{2,1,0:T(8,128)(2,1)} %param.13) | copy-start | bytes 4718596
  3.5 57.9 %all-to-all-start = ((bf16[64,8,640]{2,1,0:T(8,128)(2,1)}), bf16[64,8,640]{2,1,0:T(8,128)(2,1)}, u32[]{:S(2)}, u32[]{:S(2)}) async-start(bf16[64,8,640]{2,1,0:T(8,128)(2,1)} %bitcast.2), calls=%async_computation | async-start | bytes 1310720 | tf_op jit(solution)/shard_map/all_to_all | solution.py:272
  22.1 1.4 copy-start.1
  23.6 1.4 copy-start.2
  25.0 15.0 %copy-start.11 = (bf16[1,64,512]{2,1,0:T(8,128)(2,1)S(1)}, bf16[1,64,512]{2,1,0:T(8,128)(2,1)}, u32[]{:S(2)}) copy-start(bf16[1,64,512]{2,1,0:T(8,128)(2,1)} %param.17) | copy-start | bytes 196612
  25.9 0.8 copy-start.5
  26.6 28.3 %collective-permute-start = (bf16[2,4,192,512]{3,2,1,0:T(8,128)(2,1)S(1)}, bf16[2,4,192,512]{3,2,1,0:T(8,128)(2,1)S(1)}, u32[]{:S(2)}, u32[]{:S(2)}) collective-permute-start(bf16[2,4,192,512]{3,2,1,0:T(8,128)(2,1)S(1)} %get-tuple-element.26), channel_id=1, source_target_pairs={{0,64},{64,0},{1,65},{65,1},{2,66},{66,2},{3,67},{67,3},{4,68},{68... | collective-permute-start | bytes 4718600 | tf_op jit(solution)/shard_map/ppermute | solution.py:263
  28.5 14.6 %collective-permute-start.2 = (bf16[192,1024]{1,0:T(8,128)(2,1)S(1)}, bf16[192,1024]{1,0:T(8,128)(2,1)S(1)}, u32[]{:S(2)}, u32[]{:S(2)}) collective-permute-start(bf16[192,1024]{1,0:T(8,128)(2,1)S(1)} %get-tuple-element.28), channel_id=1, source_target_pairs={{0,128},{128,256},{256,384},{384,0},{1,129},{129,257},{257,385},{3... | collective-permute-start | bytes 1179656 | tf_op jit(solution)/shard_map/ppermute | solution.py:266
  31.9 20.6 %collective-permute-start.3 = (bf16[192,1024]{1,0:T(8,128)(2,1)S(1)}, bf16[192,1024]{1,0:T(8,128)(2,1)S(1)}, u32[]{:S(2)}, u32[]{:S(2)}) collective-permute-start(bf16[192,1024]{1,0:T(8,128)(2,1)S(1)} %get-tuple-element.29), channel_id=1, source_target_pairs={{0,256},{128,384},{256,0},{384,128},{1,257},{129,385},{257,1},{385... | collective-permute-start | bytes 1179656 | tf_op jit(solution)/shard_map/ppermute | solution.py:266
  36.6 17.5 %collective-permute-start.4 = (bf16[192,1024]{1,0:T(8,128)(2,1)S(1)}, bf16[192,1024]{1,0:T(8,128)(2,1)S(1)}, u32[]{:S(2)}, u32[]{:S(2)}) collective-permute-start(bf16[192,1024]{1,0:T(8,128)(2,1)S(1)} %get-tuple-element.30), channel_id=1, source_target_pairs={{0,384},{128,0},{256,128},{384,256},{1,385},{129,1},{257,129},{385... | collective-permute-start | bytes 1179656 | tf_op jit(solution)/shard_map/ppermute | solution.py:266
  39.9 3.1 %collective-permute-start.1 = (bf16[64,512]{1,0:T(8,128)(2,1)S(1)}, bf16[64,512]{1,0:T(8,128)(2,1)S(1)}, u32[]{:S(2)}, u32[]{:S(2)}) collective-permute-start(bf16[64,512]{1,0:T(8,128)(2,1)S(1)} %bitcast.24), channel_id=1, source_target_pairs={{0,64},{64,0},{1,65},{65,1},{2,66},{66,2},{3,67},{67,3},{4,68},{68... | collective-permute-start | bytes 196616 | tf_op jit(solution)/shard_map/ppermute | solution.py:263
  43.1 18.3 %copy-start.12 = (bf16[64,512]{1,0:T(8,128)(2,1)}, bf16[64,512]{1,0:T(8,128)(2,1)S(1)}, u32[]{:S(2)}) copy-start(bf16[64,512]{1,0:T(8,128)(2,1)S(1)} %collective-permute-done.1.refs_3_) | copy-start | bytes 196612
  43.1 11.0 %copy-start.7 = (bf16[192,1024]{1,0:T(8,128)(2,1)}, bf16[192,1024]{1,0:T(8,128)(2,1)S(1)}, u32[]{:S(2)}) copy-start(bf16[192,1024]{1,0:T(8,128)(2,1)S(1)} %collective-permute-done.2.refs_5_) | copy-start | bytes 1179652
  52.6 1.6 copy-start.8
  54.1 0.8 copy-start.9
  64.3 4.5 %copy-start.3 = (bf16[320,512]{1,0:T(8,128)(2,1)S(1)}, bf16[320,512]{1,0:T(8,128)(2,1)}, u32[]{:S(2)}) copy-start(bf16[320,512]{1,0:T(8,128)(2,1)} %get-tuple-element.37.refs_0_.s_ref) | copy-start | bytes 983044
  64.3 21.4 %all-to-all-start.1 = ((bf16[4,320,512]{2,1,0:T(8,128)(2,1)}), bf16[4,320,512]{2,1,0:T(8,128)(2,1)}, u32[]{:S(2)}, u32[]{:S(2)}) async-start(bf16[4,320,512]{2,1,0:T(8,128)(2,1)} %get-tuple-element.32), calls=%async_computation.1 | async-start | bytes 2621440 | tf_op jit(solution)/shard_map/all_to_all | solution.py:269
  68.7 3.5 %collective-permute-start.6 = (bf16[320,512]{1,0:T(8,128)(2,1)S(1)}, bf16[320,512]{1,0:T(8,128)(2,1)S(1)}, u32[]{:S(2)}, u32[]{:S(2)}) collective-permute-start(bf16[320,512]{1,0:T(8,128)(2,1)S(1)} %copy-done.3), channel_id=1, source_target_pairs={{0,64},{64,0},{1,65},{65,1},{2,66},{66,2},{3,67},{67,3},{4,68},{68... | collective-permute-start | bytes 983048 | tf_op jit(solution)/shard_map/ppermute | solution.py:263
  72.2 0.7 copy-start.10
  85.7 13.2 %all-to-all-start.2 = ((bf16[4,320,256]{2,1,0:T(8,128)(2,1)}), bf16[4,320,256]{2,1,0:T(8,128)(2,1)}, u32[]{:S(2)}, u32[]{:S(2)}) async-start(bf16[4,320,256]{2,1,0:T(8,128)(2,1)} %shard_map.116), calls=%async_computation.2 | async-start | bytes 1310720 | tf_op jit(solution)/shard_map/all_to_all | solution.py:269
  93.3 5.6 %collective-permute-start.5 = (bf16[2,320,192]{2,1,0:T(8,128)(2,1)S(1)}, bf16[2,320,192]{2,1,0:T(8,128)(2,1)}, u32[]{:S(2)}, u32[]{:S(2)}) collective-permute-start(bf16[2,320,192]{2,1,0:T(8,128)(2,1)S(1)} %get-tuple-element.36), channel_id=1, source_target_pairs={{0,64},{64,0},{1,65},{65,1},{2,66},{66,2},{3,67},{67,3},{4,68},{68... | collective-permute-start | bytes 737288 | tf_op jit(solution)/shard_map/ppermute | solution.py:263
  101.3 3.5 %collective-permute-start.7 = (bf16[320,448]{1,0:T(8,128)(2,1)S(1)}, bf16[320,448]{1,0:T(8,128)(2,1)S(1)}, u32[]{:S(2)}, u32[]{:S(2)}) collective-permute-start(bf16[320,448]{1,0:T(8,128)(2,1)S(1)} %get-tuple-element.43.g_ref), channel_id=1, source_target_pairs={{0,64},{64,0},{1,65},{65,1},{2,66},{66,2},{3,67},{67,3},{4,68},{68... | collective-permute-start | bytes 860168 | tf_op jit(solution)/shard_map/ppermute | solution.py:263
  107.1 3.6 %copy-start.6 = (s32[32,8]{0,1:T(8,128)S(1)}, s32[32,8]{0,1:T(8,128)}, u32[]{:S(2)}) copy-start(s32[32,8]{0,1:T(8,128)} %param.12) | copy-start | bytes 3076
  107.1 22.0 %all-to-all-start.3 = ((bf16[4,320,512]{2,1,0:T(8,128)(2,1)}), bf16[4,320,512]{2,1,0:T(8,128)(2,1)S(1)}, u32[]{:S(2)}, u32[]{:S(2)}) async-start(bf16[4,320,512]{2,1,0:T(8,128)(2,1)} %get-tuple-element.44), calls=%async_computation.3 | async-start | bytes 2621440 | tf_op jit(solution)/shard_map/all_to_all | solution.py:269
  110.7 43.6 %copy-start.4 = (bf16[320,512]{1,0:T(8,128)(2,1)S(1)}, bf16[320,512]{1,0:T(8,128)(2,1)}, u32[]{:S(2)}) copy-start(bf16[320,512]{1,0:T(8,128)(2,1)} %get-tuple-element.37.refs_0_.s_ref) | copy-start | bytes 983044
  130.1 35.3 %all-to-all-start.4 = ((bf16[64,2,1280]{2,1,0:T(2,128)(2,1)}), bf16[64,2,1280]{2,1,0:T(2,128)(2,1)S(1)}, u32[]{:S(2)}, u32[]{:S(2)}) async-start(bf16[64,2,1280]{2,1,0:T(2,128)(2,1)} %reshape.20), calls=%async_computation.4 | async-start | bytes 655360 | tf_op jit(solution)/shard_map/all_to_all | solution.py:272
  140.6 8.4 %collective-permute-start.10 = (bf16[320,64]{1,0:T(8,128)(2,1)S(1)}, bf16[320,64]{1,0:T(8,128)(2,1)S(1)}, u32[]{:S(2)}, u32[]{:S(2)}) collective-permute-start(bf16[320,64]{1,0:T(8,128)(2,1)S(1)} %get-tuple-element.48.v0_ref), channel_id=1, source_target_pairs={{0,384},{128,0},{256,128},{384,256},{1,385},{129,1},{257,129},{385... | collective-permute-start | bytes 122888 | tf_op jit(solution)/shard_map/ppermute | solution.py:266
  143.7 8.4 %collective-permute-start.8 = (bf16[320,64]{1,0:T(8,128)(2,1)S(1)}, bf16[320,64]{1,0:T(8,128)(2,1)S(1)}, u32[]{:S(2)}, u32[]{:S(2)}) collective-permute-start(bf16[320,64]{1,0:T(8,128)(2,1)S(1)} %get-tuple-element.48.v0_ref), channel_id=1, source_target_pairs={{0,128},{128,256},{256,384},{384,0},{1,129},{129,257},{257,385},{3... | collective-permute-start | bytes 122888 | tf_op jit(solution)/shard_map/ppermute | solution.py:266
  146.4 7.8 %collective-permute-start.9 = (bf16[320,64]{1,0:T(8,128)(2,1)S(1)}, bf16[320,64]{1,0:T(8,128)(2,1)S(1)}, u32[]{:S(2)}, u32[]{:S(2)}) collective-permute-start(bf16[320,64]{1,0:T(8,128)(2,1)S(1)} %get-tuple-element.48.v0_ref), channel_id=1, source_target_pairs={{0,256},{128,384},{256,0},{384,128},{1,257},{129,385},{257,1},{385... | collective-permute-start | bytes 122888 | tf_op jit(solution)/shard_map/ppermute | solution.py:266

commit v9 on v8

--- a/solution.py
+++ b/solution.py
@@ -10,7 +10,6 @@
 F32 = jnp.float32
 LANE = 128
 FLAT = 4
-PARAMS = pltpu.CompilerParams(vmem_limit_bytes=16 * 1024 * 1024)
 
 
 def nt(left, right):
@@ -96,7 +95,9 @@
     return jnp.where(hit > 0.5, nn(hit.astype(BF), before), -1.0)
 
 
-def split_kernel(in_ref, x_hbm, s_hbm, x_ref, s_ref, sems):
+def split_kernel(in_hbm, x_hbm, s_hbm, in_ref, x_ref, s_ref, sems):
+    load = pltpu.make_async_copy(in_hbm, in_ref, sems.at[0])
+    load.start()
     total = in_ref.shape[0]
     width = s_ref.shape[1]
     parts = 2 * width // LANE
@@ -105,6 +106,7 @@
     second = lax.broadcasted_iota(jnp.int32, (total, total), 1)
     there = low(first, experts) * parts + high(first, experts)
     perm = jnp.where(second == there, 1.0, 0.0).astype(BF)
+    load.wait()
     rows = nn(perm, in_ref[...]).astype(BF)
     for r in range(parts):
         ref = x_ref if r < parts // 2 else s_ref
@@ -232,7 +234,7 @@
     o_ref[...] = total.astype(BF)
 
 
-def call(body, outs, *args, scalars=0, places=(), ends=(), scratch=()):
+def call(body, outs, *args, scalars=0, places=(), ends=(), scratch=(), vmem_mib=16):
     vmem = pl.BlockSpec(memory_space=pltpu.VMEM)
     smem = pl.BlockSpec(memory_space=pltpu.SMEM)
     places = places or [vmem] * (len(args) - scalars)
@@ -242,7 +244,7 @@
         in_specs=[smem] * scalars + list(places),
         out_specs=ends or jax.tree.map(lambda _: vmem, outs),
         scratch_shapes=list(scratch),
-        compiler_params=PARAMS,
+        compiler_params=pltpu.CompilerParams(vmem_limit_bytes=vmem_mib * 1024 * 1024),
     )(*args)
 
 
@@ -304,9 +306,11 @@
 
     x_four, s_own = call(
         split_kernel, (pltpu.HBM((chips, routes, width), BF), pltpu.HBM((routes, width), BF)),
-        arrived.reshape(experts * parts, CAP * LANE),
-        ends=(far, far),
-        scratch=[pltpu.VMEM((routes, width), BF)] * 2 + [dma((chips + 1,))],
+        *pin(arrived.reshape(experts * parts, CAP * LANE)), places=[slow], ends=(far, far),
+        scratch=[
+            pltpu.VMEM((experts * parts, CAP * LANE), BF), pltpu.VMEM((routes, width), BF),
+            pltpu.VMEM((routes, width), BF), dma((chips + 1,)),
+        ],
     )
     x_all = over_x(x_four)
     s_other = swap(s_own)
@@ -341,7 +345,7 @@
     )
     code = call(code_kernel, sds((experts, count), F32), ids.T)
     backs, code = lax.optimization_barrier((over_x(back), code))
-    total = call(total_kernel, sds((experts, CAP * width), BF), backs)
+    total = call(total_kernel, sds((experts, CAP * width), BF), backs, vmem_mib=63)
     home = route(total.reshape(experts, 2, CAP * width // 2)).reshape(experts, CAP * width)
 
     v_all = [v_pair] + [shift(v_pair, d) for d in (1, 2, 3)]

time: 167 us -> 171 us (1.024)
  Pallas kernels: 20.8 us -> 22.9 us
    pallas_call x11, Pallas kernels: 20.8 us -> 22.9 us  [call(): pl.pallas_call(body, out_shape=outs, in_specs=[smem] * scalars + list(pla...]
where the time goes in v9:
time: 171 us; the launch traced here: 170 us
  starting transfers between devices  71.3 us (42%)
  waiting for transfers between devices  68.1 us (40%)
  Pallas kernels  22.9 us (13%)
  local copies, waits for them, and re-layouts  6.87 us (4%)
    all_to_all x3, waiting for transfers between devices, over_x(): return lax.all_to_all(block, 'x', 0, 0, tiled=True)  30.7 us
    all_to_all x2, starting transfers between devices, route(): return lax.all_to_all(block, ('zl', 'y', 'zh'), 0, 0, tiled=True)  29 us
    pallas_call x11, Pallas kernels, call(): pl.pallas_call(body, out_shape=outs, in_specs=[smem] * scalars + list(pla...  22.9 us
    ppermute x6, starting transfers between devices, shift(): lax.ppermute(block, 'x', [(i, (i + by) % chips) for i in range(chips)])  19.8 us
    all_to_all x2, waiting for transfers between devices, route(): return lax.all_to_all(block, ('zl', 'y', 'zh'), 0, 0, tiled=True)  16.7 us
    ppermute x6, waiting for transfers between devices, shift(): lax.ppermute(block, 'x', [(i, (i + by) % chips) for i in range(chips)])  16.3 us
    all_to_all x3, starting transfers between devices, over_x(): return lax.all_to_all(block, 'x', 0, 0, tiled=True)  12.9 us
    ppermute x5, starting transfers between devices, swap(): return lax.ppermute(block, 'c', [(0, 1), (1, 0)])  9.59 us
  transfers between devices with their start and end apart: 16, of which 13 were waited for; matrix products, arithmetic and copies ran while one was open for 0% of the time, Pallas kernels for 6%

profile of v9, /device:TPU:32, one launch (start us, length us, event | category | flops | bytes accessed | tf_op | source)
XLA Modules:
  0.0 170.1 jit_solution(6257182896252477397)
XLA Ops:
  0.6 0.0 copy-start
  0.6 2.8 %shard_map.112 = bf16[512,640]{1,0:T(8,128)(2,1)} custom-call(s32[8,32]{1,0:T(8,128)} %bitcast.19, f32[8,32]{1,0:T(8,128)} %bitcast.26, bf16[32,512]{1,0:T(8,128)(2,1)} %tok_hbm.1, bf16[32,512]{1,0:T(8,128)(2,1)} %dy_hbm.1), custom_call_target="tpu_custom_call" | custom-call | tf_op jit(solution)/shard_map/pallas_call | solution.py:241
  3.5 18.6 %all-to-all-start = ((bf16[64,8,640]{2,1,0:T(8,128)(2,1)}), bf16[64,8,640]{2,1,0:T(8,128)(2,1)}, u32[]{:S(2)}, u32[]{:S(2)}) async-start(bf16[64,8,640]{2,1,0:T(8,128)(2,1)} %bitcast.2), calls=%async_computation | async-start | bytes 1310720 | tf_op jit(solution)/shard_map/all_to_all | solution.py:274
  22.1 0.1 pad_add_fusion.me_ref
  22.1 0.0 copy-done
  22.1 0.0 copy-start.1
  22.1 1.4 copy-done.1
  23.6 1.4 copy-done.2
  25.0 0.9 shard_map.113
  25.9 0.0 copy-start.5
  25.9 0.7 copy-done.5
  26.6 1.9 %collective-permute-start = (bf16[2,4,192,512]{3,2,1,0:T(8,128)(2,1)S(1)}, bf16[2,4,192,512]{3,2,1,0:T(8,128)(2,1)S(1)}, u32[]{:S(2)}, u32[]{:S(2)}) collective-permute-start(bf16[2,4,192,512]{3,2,1,0:T(8,128)(2,1)S(1)} %get-tuple-element.26), channel_id=1, source_target_pairs={{0,64},{64,0},{1,65},{65,1},{2,66},{66,2},{3,67},{67,3},{4,68},{68... | collective-permute-start | bytes 4718600 | tf_op jit(solution)/shard_map/ppermute | solution.py:265
  28.5 3.4 %collective-permute-start.2 = (bf16[192,1024]{1,0:T(8,128)(2,1)S(1)}, bf16[192,1024]{1,0:T(8,128)(2,1)S(1)}, u32[]{:S(2)}, u32[]{:S(2)}) collective-permute-start(bf16[192,1024]{1,0:T(8,128)(2,1)S(1)} %get-tuple-element.28), channel_id=1, source_target_pairs={{0,128},{128,256},{256,384},{384,0},{1,129},{129,257},{257,385},{3... | collective-permute-start | bytes 1179656 | tf_op jit(solution)/shard_map/ppermute | solution.py:268
  31.9 4.6 %collective-permute-start.3 = (bf16[192,1024]{1,0:T(8,128)(2,1)S(1)}, bf16[192,1024]{1,0:T(8,128)(2,1)S(1)}, u32[]{:S(2)}, u32[]{:S(2)}) collective-permute-start(bf16[192,1024]{1,0:T(8,128)(2,1)S(1)} %get-tuple-element.29), channel_id=1, source_target_pairs={{0,256},{128,384},{256,0},{384,128},{1,257},{129,385},{257,1},{385... | collective-permute-start | bytes 1179656 | tf_op jit(solution)/shard_map/ppermute | solution.py:268
  36.6 3.3 %collective-permute-start.4 = (bf16[192,1024]{1,0:T(8,128)(2,1)S(1)}, bf16[192,1024]{1,0:T(8,128)(2,1)S(1)}, u32[]{:S(2)}, u32[]{:S(2)}) collective-permute-start(bf16[192,1024]{1,0:T(8,128)(2,1)S(1)} %get-tuple-element.30), channel_id=1, source_target_pairs={{0,384},{128,0},{256,128},{384,256},{1,385},{129,1},{257,129},{385... | collective-permute-start | bytes 1179656 | tf_op jit(solution)/shard_map/ppermute | solution.py:268
  39.9 0.0 copy-done.11
  39.9 1.9 %collective-permute-start.1 = (bf16[64,512]{1,0:T(8,128)(2,1)S(1)}, bf16[64,512]{1,0:T(8,128)(2,1)S(1)}, u32[]{:S(2)}, u32[]{:S(2)}) collective-permute-start(bf16[64,512]{1,0:T(8,128)(2,1)S(1)} %bitcast.24), channel_id=1, source_target_pairs={{0,64},{64,0},{1,65},{65,1},{2,66},{66,2},{3,67},{67,3},{4,68},{68... | collective-permute-start | bytes 196616 | tf_op jit(solution)/shard_map/ppermute | solution.py:265
  41.9 1.2 collective-permute-done.1.refs_3_
  43.1 0.1 collective-permute-done.2.refs_5_
  43.1 9.4 %collective-permute-done.3.refs_6_ = bf16[192,1024]{1,0:T(8,128)(2,1)S(1)} collective-permute-done((bf16[192,1024]{1,0:T(8,128)(2,1)S(1)}, bf16[192,1024]{1,0:T(8,128)(2,1)S(1)}, u32[]{:S(2)}, u32[]{:S(2)}) %collective-permute-start.3) | collective-permute-done | bytes 393248 | tf_op jit(solution)/shard_map/ppermute | solution.py:268
  52.6 1.5 collective-permute-done.4.refs_7_
  54.1 0.0 copy-done.7
  54.1 0.0 copy-done.8
  54.1 0.8 copy-done.9
  54.9 0.0 collective-permute-done.half_ref
  54.9 6.5 %all-to-all-done = bf16[64,8,640]{2,1,0:T(8,128)(2,1)} async-done(((bf16[64,8,640]{2,1,0:T(8,128)(2,1)}), bf16[64,8,640]{2,1,0:T(8,128)(2,1)}, u32[]{:S(2)}, u32[]{:S(2)}) %all-to-all-start) | async-done | bytes 655392 | tf_op jit(solution)/shard_map/all_to_all | solution.py:274
  61.4 0.0 copy-done.12
  61.4 2.9 %shard_map.114 = (bf16[4,320,512]{2,1,0:T(8,128)(2,1)}, bf16[320,512]{1,0:T(8,128)(2,1)}) custom-call(bf16[512,640]{1,0:T(8,128)(2,1)} %bitcast.9.in_hbm), custom_call_target="tpu_custom_call" | custom-call | tf_op jit(solution)/shard_map/pallas_call | solution.py:241
  64.3 0.0 copy-start.3
  64.3 4.4 %all-to-all-start.1 = ((bf16[4,320,512]{2,1,0:T(8,128)(2,1)}), bf16[4,320,512]{2,1,0:T(8,128)(2,1)}, u32[]{:S(2)}, u32[]{:S(2)}) async-start(bf16[4,320,512]{2,1,0:T(8,128)(2,1)} %get-tuple-element.32), calls=%async_computation.1 | async-start | bytes 2621440 | tf_op jit(solution)/shard_map/all_to_all | solution.py:271
  68.7 0.0 copy-done.3
  68.7 1.9 %collective-permute-start.6 = (bf16[320,512]{1,0:T(8,128)(2,1)S(1)}, bf16[320,512]{1,0:T(8,128)(2,1)S(1)}, u32[]{:S(2)}, u32[]{:S(2)}) collective-permute-start(bf16[320,512]{1,0:T(8,128)(2,1)S(1)} %copy-done.3), channel_id=1, source_target_pairs={{0,64},{64,0},{1,65},{65,1},{2,66},{66,2},{3,67},{67,3},{4,68},{68... | collective-permute-start | bytes 983048 | tf_op jit(solution)/shard_map/ppermute | solution.py:265
  70.7 1.6 collective-permute-done.6.refs_1_
  72.2 0.7 copy-done.10
  73.0 4.0 %shard_map.116 = bf16[4,320,256]{2,1,0:T(8,128)(2,1)} custom-call(s32[2]{0:T(128)S(1)} %pad_add_fusion.me_ref, bf16[320,512]{1,0:T(8,128)(2,1)} %get-tuple-element.37.refs_0_.s_ref, bf16[320,512]{1,0:T(8,128)(2,1)} %copy-done.10, bf16[64,512]{1,0:T(8,128)(2,1)} %bitcast.23, bf16[64,512]{1,0:T(8,128)(2,1)} %copy-done.12, bf16[192,1024]{1,0:T(8,128)(2,1)} %copy-done.5, ...), custom_call_target="tpu_custom_call" | custom-call | tf_op jit(solution)/shard_map/pallas_call | solution.py:241
  77.0 8.7 %all-to-all-done.1.x_ref = bf16[4,320,512]{2,1,0:T(8,128)(2,1)} async-done(((bf16[4,320,512]{2,1,0:T(8,128)(2,1)}), bf16[4,320,512]{2,1,0:T(8,128)(2,1)}, u32[]{:S(2)}, u32[]{:S(2)}) %all-to-all-start.1) | async-done | bytes 1310752 | tf_op jit(solution)/shard_map/all_to_all | solution.py:271
  85.7 4.2 %all-to-all-start.2 = ((bf16[4,320,256]{2,1,0:T(8,128)(2,1)}), bf16[4,320,256]{2,1,0:T(8,128)(2,1)}, u32[]{:S(2)}, u32[]{:S(2)}) async-start(bf16[4,320,256]{2,1,0:T(8,128)(2,1)} %shard_map.116), calls=%async_computation.2 | async-start | bytes 1310720 | tf_op jit(solution)/shard_map/all_to_all | solution.py:271
  89.9 3.4 %shard_map.115 = (f32[2,320,192]{2,1,0:T(8,128)}, bf16[2,320,192]{2,1,0:T(8,128)(2,1)S(1)}) custom-call(bf16[4,320,512]{2,1,0:T(8,128)(2,1)} %all-to-all-done.1.x_ref, bf16[2,4,192,512]{3,2,1,0:T(8,128)(2,1)S(1)} %get-tuple-element.33.own_ref, bf16[2,4,192,512]{3,2,1,0:T(8,128)(2,1)S(1)} %collective-permute-done.half_ref), custom_call_target="tpu_custom_call" | custom-call | tf_op jit(solution)/shard_map/pallas_call | solution.py:241
  93.3 1.9 %collective-permute-start.5 = (bf16[2,320,192]{2,1,0:T(8,128)(2,1)S(1)}, bf16[2,320,192]{2,1,0:T(8,128)(2,1)}, u32[]{:S(2)}, u32[]{:S(2)}) collective-permute-start(bf16[2,320,192]{2,1,0:T(8,128)(2,1)S(1)} %get-tuple-element.36), channel_id=1, source_target_pairs={{0,64},{64,0},{1,65},{65,1},{2,66},{66,2},{3,67},{67,3},{4,68},{68... | collective-permute-start | bytes 737288 | tf_op jit(solution)/shard_map/ppermute | solution.py:265
  95.2 3.6 %all-to-all-done.2.in_hbm = bf16[4,320,256]{2,1,0:T(8,128)(2,1)} async-done(((bf16[4,320,256]{2,1,0:T(8,128)(2,1)}), bf16[4,320,256]{2,1,0:T(8,128)(2,1)}, u32[]{:S(2)}, u32[]{:S(2)}) %all-to-all-start.2) | async-done | bytes 655392 | tf_op jit(solution)/shard_map/all_to_all | solution.py:271
  98.9 0.0 collective-permute-done.5.got_hbm
  98.9 2.4 %shard_map.117 = (bf16[320,448]{1,0:T(8,128)(2,1)S(1)}, f32[64,192]{1,0:T(8,128)}) custom-call(f32[2,320,192]{2,1,0:T(8,128)} %get-tuple-element.35.keep_hbm, bf16[2,320,192]{2,1,0:T(8,128)(2,1)} %collective-permute-done.5.got_hbm, bf16[4,320,256]{2,1,0:T(8,128)(2,1)} %all-to-all-done.2.in_hbm, bf16[64,192]{1,0:T(8,128)(2,1)} %bitcast.25), custom_call_target="tpu_custom_call" | custom-call | tf_op jit(solution)/shard_map/pallas_call | solution.py:241
  101.3 1.9 %collective-permute-start.7 = (bf16[320,448]{1,0:T(8,128)(2,1)S(1)}, bf16[320,448]{1,0:T(8,128)(2,1)S(1)}, u32[]{:S(2)}, u32[]{:S(2)}) collective-permute-start(bf16[320,448]{1,0:T(8,128)(2,1)S(1)} %get-tuple-element.43.g_ref), channel_id=1, source_target_pairs={{0,64},{64,0},{1,65},{65,1},{2,66},{66,2},{3,67},{67,3},{4,68},{68... | collective-permute-start | bytes 860168 | tf_op jit(solution)/shard_map/ppermute | solution.py:265
  103.2 1.6 collective-permute-done.7.h_ref
  104.8 2.3 %shard_map.118 = (bf16[4,320,512]{2,1,0:T(8,128)(2,1)}, bf16[320,64]{1,0:T(8,128)(2,1)S(1)}) custom-call(bf16[320,448]{1,0:T(8,128)(2,1)S(1)} %get-tuple-element.43.g_ref, bf16[320,448]{1,0:T(8,128)(2,1)S(1)} %collective-permute-done.7.h_ref, bf16[2,4,192,512]{3,2,1,0:T(8,128)(2,1)S(1)} %get-tuple-element.33.own_ref, ...), custom_call_target="tpu_custom_call" | custom-call | tf_op jit(solution)/shard_map/pallas_call | solution.py:241
  107.2 0.0 copy-start.6
  107.2 4.3 %all-to-all-start.3 = ((bf16[4,320,512]{2,1,0:T(8,128)(2,1)}), bf16[4,320,512]{2,1,0:T(8,128)(2,1)}, u32[]{:S(2)}, u32[]{:S(2)}) async-start(bf16[4,320,512]{2,1,0:T(8,128)(2,1)} %get-tuple-element.44), calls=%async_computation.3 | async-start | bytes 2621440 | tf_op jit(solution)/shard_map/all_to_all | solution.py:271
  111.5 0.0 copy-done.6
  111.5 0.0 copy-start.4
  111.5 0.2 shard_map.119.code_ref
  111.6 18.4 %all-to-all-done.3.in_ref = bf16[4,320,512]{2,1,0:T(8,128)(2,1)} async-done(((bf16[4,320,512]{2,1,0:T(8,128)(2,1)}), bf16[4,320,512]{2,1,0:T(8,128)(2,1)}, u32[]{:S(2)}, u32[]{:S(2)}) %all-to-all-start.3) | async-done | bytes 1310752 | tf_op jit(solution)/shard_map/all_to_all | solution.py:271
  130.0 2.2 %shard_map.120 = bf16[64,2560]{1,0:T(8,128)(2,1)} custom-call(bf16[4,320,512]{2,1,0:T(8,128)(2,1)} %all-to-all-done.3.in_ref), custom_call_target="tpu_custom_call" | custom-call | tf_op jit(solution)/shard_map/pallas_call | solution.py:241
  132.2 1.8 %reshape.20 = bf16[64,2,1280]{2,1,0:T(2,128)(2,1)} reshape(bf16[64,2560]{1,0:T(8,128)(2,1)} %shard_map.120) | data formatting | bytes 655360 | tf_op jit(solution)/shard_map/reshape | solution.py:349
  134.0 10.4 %all-to-all-start.4 = ((bf16[64,2,1280]{2,1,0:T(2,128)(2,1)}), bf16[64,2,1280]{2,1,0:T(2,128)(2,1)S(1)}, u32[]{:S(2)}, u32[]{:S(2)}) async-start(bf16[64,2,1280]{2,1,0:T(2,128)(2,1)} %reshape.20), calls=%async_computation.4 | async-start | bytes 655360 | tf_op jit(solution)/shard_map/all_to_all | solution.py:274
  144.5 3.1 %collective-permute-start.10 = (bf16[320,64]{1,0:T(8,128)(2,1)S(1)}, bf16[320,64]{1,0:T(8,128)(2,1)S(1)}, u32[]{:S(2)}, u32[]{:S(2)}) collective-permute-start(bf16[320,64]{1,0:T(8,128)(2,1)S(1)} %get-tuple-element.48.v0_ref), channel_id=1, source_target_pairs={{0,384},{128,0},{256,128},{384,256},{1,385},{129,1},{257,129},{385... | collective-permute-start | bytes 122888 | tf_op jit(solution)/shard_map/ppermute | solution.py:268
  147.5 2.8 %collective-permute-start.8 = (bf16[320,64]{1,0:T(8,128)(2,1)S(1)}, bf16[320,64]{1,0:T(8,128)(2,1)S(1)}, u32[]{:S(2)}, u32[]{:S(2)}) collective-permute-start(bf16[320,64]{1,0:T(8,128)(2,1)S(1)} %get-tuple-element.48.v0_ref), channel_id=1, source_target_pairs={{0,128},{128,256},{256,384},{384,0},{1,129},{129,257},{257,385},{3... | collective-permute-start | bytes 122888 | tf_op jit(solution)/shard_map/ppermute | solution.py:268
  150.3 2.5 %collective-permute-start.9 = (bf16[320,64]{1,0:T(8,128)(2,1)S(1)}, bf16[320,64]{1,0:T(8,128)(2,1)S(1)}, u32[]{:S(2)}, u32[]{:S(2)}) collective-permute-start(bf16[320,64]{1,0:T(8,128)(2,1)S(1)} %get-tuple-element.48.v0_ref), channel_id=1, source_target_pairs={{0,256},{128,384},{256,0},{384,128},{1,257},{129,385},{257,1},{385... | collective-permute-start | bytes 122888 | tf_op jit(solution)/shard_map/ppermute | solution.py:268
  152.8 0.0 collective-permute-done.10.v3_ref
  152.9 3.1 %collective-permute-done.8.v1_ref = bf16[320,64]{1,0:T(8,128)(2,1)S(1)} collective-permute-done((bf16[320,64]{1,0:T(8,128)(2,1)S(1)}, bf16[320,64]{1,0:T(8,128)(2,1)S(1)}, u32[]{:S(2)}, u32[]{:S(2)}) %collective-permute-start.8) | collective-permute-done | bytes 40992 | tf_op jit(solution)/shard_map/ppermute | solution.py:268
  156.0 2.2 %collective-permute-done.9.v2_ref = bf16[320,64]{1,0:T(8,128)(2,1)S(1)} collective-permute-done((bf16[320,64]{1,0:T(8,128)(2,1)S(1)}, bf16[320,64]{1,0:T(8,128)(2,1)S(1)}, u32[]{:S(2)}, u32[]{:S(2)}) %collective-permute-start.9) | collective-permute-done | bytes 40992 | tf_op jit(solution)/shard_map/ppermute | solution.py:268
  158.2 0.0 copy-done.4
  158.2 0.9 shard_map.122
  159.0 10.2 %all-to-all-done.4 = bf16[64,2,1280]{2,1,0:T(2,128)(2,1)S(1)} async-done(((bf16[64,2,1280]{2,1,0:T(2,128)(2,1)}), bf16[64,2,1280]{2,1,0:T(2,128)(2,1)S(1)}, u32[]{:S(2)}, u32[]{:S(2)}) %all-to-all-start.4) | async-done | bytes 327712 | tf_op jit(solution)/shard_map/all_to_all | solution.py:274
  169.3 0.8 shard_map.121
  (8 shorter events, 0.0 us)
Async XLA Ops:
  0.6 21.5 %copy-start = (bf16[1,192,4096]{2,1,0:T(8,128)(2,1)S(1)}, bf16[1,192,4096]{2,1,0:T(8,128)(2,1)}, u32[]{:S(2)}) copy-start(bf16[1,192,4096]{2,1,0:T(8,128)(2,1)} %param.13) | copy-start | bytes 4718596
  3.5 57.9 %all-to-all-start = ((bf16[64,8,640]{2,1,0:T(8,128)(2,1)}), bf16[64,8,640]{2,1,0:T(8,128)(2,1)}, u32[]{:S(2)}, u32[]{:S(2)}) async-start(bf16[64,8,640]{2,1,0:T(8,128)(2,1)} %bitcast.2), calls=%async_computation | async-start | bytes 1310720 | tf_op jit(solution)/shard_map/all_to_all | solution.py:274
  22.1 1.4 copy-start.1
  23.6 1.4 copy-start.2
  25.0 15.0 %copy-start.11 = (bf16[1,64,512]{2,1,0:T(8,128)(2,1)S(1)}, bf16[1,64,512]{2,1,0:T(8,128)(2,1)}, u32[]{:S(2)}) copy-start(bf16[1,64,512]{2,1,0:T(8,128)(2,1)} %param.17) | copy-start | bytes 196612
  25.9 0.8 copy-start.5
  26.6 28.3 %collective-permute-start = (bf16[2,4,192,512]{3,2,1,0:T(8,128)(2,1)S(1)}, bf16[2,4,192,512]{3,2,1,0:T(8,128)(2,1)S(1)}, u32[]{:S(2)}, u32[]{:S(2)}) collective-permute-start(bf16[2,4,192,512]{3,2,1,0:T(8,128)(2,1)S(1)} %get-tuple-element.26), channel_id=1, source_target_pairs={{0,64},{64,0},{1,65},{65,1},{2,66},{66,2},{3,67},{67,3},{4,68},{68... | collective-permute-start | bytes 4718600 | tf_op jit(solution)/shard_map/ppermute | solution.py:265
  28.5 14.6 %collective-permute-start.2 = (bf16[192,1024]{1,0:T(8,128)(2,1)S(1)}, bf16[192,1024]{1,0:T(8,128)(2,1)S(1)}, u32[]{:S(2)}, u32[]{:S(2)}) collective-permute-start(bf16[192,1024]{1,0:T(8,128)(2,1)S(1)} %get-tuple-element.28), channel_id=1, source_target_pairs={{0,128},{128,256},{256,384},{384,0},{1,129},{129,257},{257,385},{3... | collective-permute-start | bytes 1179656 | tf_op jit(solution)/shard_map/ppermute | solution.py:268
  31.9 20.6 %collective-permute-start.3 = (bf16[192,1024]{1,0:T(8,128)(2,1)S(1)}, bf16[192,1024]{1,0:T(8,128)(2,1)S(1)}, u32[]{:S(2)}, u32[]{:S(2)}) collective-permute-start(bf16[192,1024]{1,0:T(8,128)(2,1)S(1)} %get-tuple-element.29), channel_id=1, source_target_pairs={{0,256},{128,384},{256,0},{384,128},{1,257},{129,385},{257,1},{385... | collective-permute-start | bytes 1179656 | tf_op jit(solution)/shard_map/ppermute | solution.py:268
  36.6 17.5 %collective-permute-start.4 = (bf16[192,1024]{1,0:T(8,128)(2,1)S(1)}, bf16[192,1024]{1,0:T(8,128)(2,1)S(1)}, u32[]{:S(2)}, u32[]{:S(2)}) collective-permute-start(bf16[192,1024]{1,0:T(8,128)(2,1)S(1)} %get-tuple-element.30), channel_id=1, source_target_pairs={{0,384},{128,0},{256,128},{384,256},{1,385},{129,1},{257,129},{385... | collective-permute-start | bytes 1179656 | tf_op jit(solution)/shard_map/ppermute | solution.py:268
  39.9 3.1 %collective-permute-start.1 = (bf16[64,512]{1,0:T(8,128)(2,1)S(1)}, bf16[64,512]{1,0:T(8,128)(2,1)S(1)}, u32[]{:S(2)}, u32[]{:S(2)}) collective-permute-start(bf16[64,512]{1,0:T(8,128)(2,1)S(1)} %bitcast.24), channel_id=1, source_target_pairs={{0,64},{64,0},{1,65},{65,1},{2,66},{66,2},{3,67},{67,3},{4,68},{68... | collective-permute-start | bytes 196616 | tf_op jit(solution)/shard_map/ppermute | solution.py:265
  43.1 18.3 %copy-start.12 = (bf16[64,512]{1,0:T(8,128)(2,1)}, bf16[64,512]{1,0:T(8,128)(2,1)S(1)}, u32[]{:S(2)}) copy-start(bf16[64,512]{1,0:T(8,128)(2,1)S(1)} %collective-permute-done.1.refs_3_) | copy-start | bytes 196612
  43.1 11.0 %copy-start.7 = (bf16[192,1024]{1,0:T(8,128)(2,1)}, bf16[192,1024]{1,0:T(8,128)(2,1)S(1)}, u32[]{:S(2)}) copy-start(bf16[192,1024]{1,0:T(8,128)(2,1)S(1)} %collective-permute-done.2.refs_5_) | copy-start | bytes 1179652
  52.6 1.6 copy-start.8
  54.1 0.8 copy-start.9
  64.3 4.5 %copy-start.3 = (bf16[320,512]{1,0:T(8,128)(2,1)S(1)}, bf16[320,512]{1,0:T(8,128)(2,1)}, u32[]{:S(2)}) copy-start(bf16[320,512]{1,0:T(8,128)(2,1)} %get-tuple-element.37.refs_0_.s_ref) | copy-start | bytes 983044
  64.3 21.4 %all-to-all-start.1 = ((bf16[4,320,512]{2,1,0:T(8,128)(2,1)}), bf16[4,320,512]{2,1,0:T(8,128)(2,1)}, u32[]{:S(2)}, u32[]{:S(2)}) async-start(bf16[4,320,512]{2,1,0:T(8,128)(2,1)} %get-tuple-element.32), calls=%async_computation.1 | async-start | bytes 2621440 | tf_op jit(solution)/shard_map/all_to_all | solution.py:271
  68.7 3.5 %collective-permute-start.6 = (bf16[320,512]{1,0:T(8,128)(2,1)S(1)}, bf16[320,512]{1,0:T(8,128)(2,1)S(1)}, u32[]{:S(2)}, u32[]{:S(2)}) collective-permute-start(bf16[320,512]{1,0:T(8,128)(2,1)S(1)} %copy-done.3), channel_id=1, source_target_pairs={{0,64},{64,0},{1,65},{65,1},{2,66},{66,2},{3,67},{67,3},{4,68},{68... | collective-permute-start | bytes 983048 | tf_op jit(solution)/shard_map/ppermute | solution.py:265
  72.2 0.7 copy-start.10
  85.7 13.2 %all-to-all-start.2 = ((bf16[4,320,256]{2,1,0:T(8,128)(2,1)}), bf16[4,320,256]{2,1,0:T(8,128)(2,1)}, u32[]{:S(2)}, u32[]{:S(2)}) async-start(bf16[4,320,256]{2,1,0:T(8,128)(2,1)} %shard_map.116), calls=%async_computation.2 | async-start | bytes 1310720 | tf_op jit(solution)/shard_map/all_to_all | solution.py:271
  93.3 5.6 %collective-permute-start.5 = (bf16[2,320,192]{2,1,0:T(8,128)(2,1)S(1)}, bf16[2,320,192]{2,1,0:T(8,128)(2,1)}, u32[]{:S(2)}, u32[]{:S(2)}) collective-permute-start(bf16[2,320,192]{2,1,0:T(8,128)(2,1)S(1)} %get-tuple-element.36), channel_id=1, source_target_pairs={{0,64},{64,0},{1,65},{65,1},{2,66},{66,2},{3,67},{67,3},{4,68},{68... | collective-permute-start | bytes 737288 | tf_op jit(solution)/shard_map/ppermute | solution.py:265
  101.3 3.5 %collective-permute-start.7 = (bf16[320,448]{1,0:T(8,128)(2,1)S(1)}, bf16[320,448]{1,0:T(8,128)(2,1)S(1)}, u32[]{:S(2)}, u32[]{:S(2)}) collective-permute-start(bf16[320,448]{1,0:T(8,128)(2,1)S(1)} %get-tuple-element.43.g_ref), channel_id=1, source_target_pairs={{0,64},{64,0},{1,65},{65,1},{2,66},{66,2},{3,67},{67,3},{4,68},{68... | collective-permute-start | bytes 860168 | tf_op jit(solution)/shard_map/ppermute | solution.py:265
  107.2 4.3 %copy-start.6 = (s32[32,8]{0,1:T(8,128)S(1)}, s32[32,8]{0,1:T(8,128)}, u32[]{:S(2)}) copy-start(s32[32,8]{0,1:T(8,128)} %param.12) | copy-start | bytes 3076
  107.2 22.9 %all-to-all-start.3 = ((bf16[4,320,512]{2,1,0:T(8,128)(2,1)}), bf16[4,320,512]{2,1,0:T(8,128)(2,1)}, u32[]{:S(2)}, u32[]{:S(2)}) async-start(bf16[4,320,512]{2,1,0:T(8,128)(2,1)} %get-tuple-element.44), calls=%async_computation.3 | async-start | bytes 2621440 | tf_op jit(solution)/shard_map/all_to_all | solution.py:271
  111.5 46.7 %copy-start.4 = (bf16[320,512]{1,0:T(8,128)(2,1)S(1)}, bf16[320,512]{1,0:T(8,128)(2,1)}, u32[]{:S(2)}) copy-start(bf16[320,512]{1,0:T(8,128)(2,1)} %get-tuple-element.37.refs_0_.s_ref) | copy-start | bytes 983044
  134.0 35.2 %all-to-all-start.4 = ((bf16[64,2,1280]{2,1,0:T(2,128)(2,1)}), bf16[64,2,1280]{2,1,0:T(2,128)(2,1)S(1)}, u32[]{:S(2)}, u32[]{:S(2)}) async-start(bf16[64,2,1280]{2,1,0:T(2,128)(2,1)} %reshape.20), calls=%async_computation.4 | async-start | bytes 655360 | tf_op jit(solution)/shard_map/all_to_all | solution.py:274
  144.5 8.4 %collective-permute-start.10 = (bf16[320,64]{1,0:T(8,128)(2,1)S(1)}, bf16[320,64]{1,0:T(8,128)(2,1)S(1)}, u32[]{:S(2)}, u32[]{:S(2)}) collective-permute-start(bf16[320,64]{1,0:T(8,128)(2,1)S(1)} %get-tuple-element.48.v0_ref), channel_id=1, source_target_pairs={{0,384},{128,0},{256,128},{384,256},{1,385},{129,1},{257,129},{385... | collective-permute-start | bytes 122888 | tf_op jit(solution)/shard_map/ppermute | solution.py:268
  147.5 8.4 %collective-permute-start.8 = (bf16[320,64]{1,0:T(8,128)(2,1)S(1)}, bf16[320,64]{1,0:T(8,128)(2,1)S(1)}, u32[]{:S(2)}, u32[]{:S(2)}) collective-permute-start(bf16[320,64]{1,0:T(8,128)(2,1)S(1)} %get-tuple-element.48.v0_ref), channel_id=1, source_target_pairs={{0,128},{128,256},{256,384},{384,0},{1,129},{129,257},{257,385},{3... | collective-permute-start | bytes 122888 | tf_op jit(solution)/shard_map/ppermute | solution.py:268
  150.3 7.8 %collective-permute-start.9 = (bf16[320,64]{1,0:T(8,128)(2,1)S(1)}, bf16[320,64]{1,0:T(8,128)(2,1)S(1)}, u32[]{:S(2)}, u32[]{:S(2)}) collective-permute-start(bf16[320,64]{1,0:T(8,128)(2,1)S(1)} %get-tuple-element.48.v0_ref), channel_id=1, source_target_pairs={{0,256},{128,384},{256,0},{384,128},{1,257},{129,385},{257,1},{385... | collective-permute-start | bytes 122888 | tf_op jit(solution)/shard_map/ppermute | solution.py:268

commit v10 on v8

--- a/solution.py
+++ b/solution.py
@@ -96,25 +96,35 @@
     return jnp.where(hit > 0.5, nn(hit.astype(BF), before), -1.0)
 
 
-def split_kernel(in_ref, x_hbm, s_hbm, x_ref, s_ref, sems):
+def unpack(in_hbm, in_ref, rows_ref, first_part, sem):
+    load = pltpu.make_async_copy(in_hbm, in_ref, sem)
+    load.start()
     total = in_ref.shape[0]
-    width = s_ref.shape[1]
-    parts = 2 * width // LANE
+    width = rows_ref.shape[1]
+    half = width // LANE
+    parts = 2 * half
     experts = total // parts
-    first = lax.broadcasted_iota(jnp.int32, (total, total), 0)
-    second = lax.broadcasted_iota(jnp.int32, (total, total), 1)
-    there = low(first, experts) * parts + high(first, experts)
+    first = lax.broadcasted_iota(jnp.int32, (half * experts, total), 0)
+    second = lax.broadcasted_iota(jnp.int32, (half * experts, total), 1)
+    there = low(first, experts) * parts + high(first, experts) + first_part
     perm = jnp.where(second == there, 1.0, 0.0).astype(BF)
+    load.wait()
     rows = nn(perm, in_ref[...]).astype(BF)
-    for r in range(parts):
-        ref = x_ref if r < parts // 2 else s_ref
-        at = (r % (parts // 2)) * LANE
+    for r in range(half):
         for s in range(CAP):
-            ref[s * experts : (s + 1) * experts, at : at + LANE] = rows[
+            rows_ref[s * experts : (s + 1) * experts, r * LANE : (r + 1) * LANE] = rows[
                 r * experts : (r + 1) * experts, s * LANE : (s + 1) * LANE
             ]
-    chips = x_hbm.shape[0]
-    fetch([(x_ref, x_hbm.at[x]) for x in range(chips)] + [(s_ref, s_hbm)], sems)
+
+
+def split_x_kernel(in_hbm, x_hbm, in_ref, x_ref, sems):
+    unpack(in_hbm, in_ref, x_ref, 0, sems.at[0])
+    fetch([(x_ref, x_hbm.at[x]) for x in range(x_hbm.shape[0])], sems)
+
+
+def split_s_kernel(in_hbm, s_hbm, in_ref, s_ref, sems):
+    unpack(in_hbm, in_ref, s_ref, s_ref.shape[1] // LANE, sems.at[0])
+    fetch([(s_ref, s_hbm)], sems)
 
 
 def prep_kernel(me_ref, wg_ref, wu_ref, wd_ref, own_ref, swap_ref, d0_ref, d1_ref, d2_ref, d3_ref):
@@ -167,13 +177,20 @@
 
 
 def grad_kernel(keep_hbm, got_hbm, in_hbm, a_hbm, out_ref, ga_ref, keep_ref, got_ref, in_ref, a_ref, sems):
-    fetch([(keep_hbm, keep_ref), (got_hbm, got_ref), (in_hbm, in_ref), (a_hbm, a_ref)], sems)
+    pairs = [(in_hbm, in_ref), (a_hbm, a_ref), (keep_hbm, keep_ref), (got_hbm, got_ref)]
+    copies = [pltpu.make_async_copy(p, q, sems.at[i]) for i, (p, q) in enumerate(pairs)]
+    for copy in copies:
+        copy.start()
+    for copy in copies[:2]:
+        copy.wait()
     units = keep_ref.shape[2]
     total = in_ref[0].astype(F32)
     for x in range(1, in_ref.shape[0]):
         total += in_ref[x].astype(F32)
     low_u = total[:, units:].astype(BF)
     grad = total[:, :units] + nn(low_u, a_ref[...])
+    for copy in copies[2:]:
+        copy.wait()
     gate = keep_ref[0] + got_ref[0].astype(F32)
     up = keep_ref[1] + got_ref[1].astype(F32)
     sigma = jax.nn.sigmoid(gate)
@@ -302,11 +319,15 @@
     b_other = swap(adapter_b)
     arrived, half, b_other, *down = lax.optimization_barrier((arrived, half, b_other, *down))
 
-    x_four, s_own = call(
-        split_kernel, (pltpu.HBM((chips, routes, width), BF), pltpu.HBM((routes, width), BF)),
-        arrived.reshape(experts * parts, CAP * LANE),
-        ends=(far, far),
-        scratch=[pltpu.VMEM((routes, width), BF)] * 2 + [dma((chips + 1,))],
+    whole = arrived.reshape(experts * parts, CAP * LANE)
+    scratch = [pltpu.VMEM(whole.shape, BF), pltpu.VMEM((routes, width), BF), dma((chips,))]
+    x_four = call(
+        split_x_kernel, pltpu.HBM((chips, routes, width), BF), *pin(whole), places=[slow], ends=far,
+        scratch=scratch,
+    )
+    s_own = call(
+        split_s_kernel, pltpu.HBM((routes, width), BF), *pin(whole), places=[slow], ends=far,
+        scratch=scratch,
     )
     x_all = over_x(x_four)
     s_other = swap(s_own)

time: 167 us -> 167 us (level)
  waiting for transfers between devices: 68 us -> 65.8 us
  Pallas kernels: 20.8 us -> 22.7 us
    all_to_all x3, waiting for transfers between devices: 30.6 us -> 28.1 us  [over_x(): return lax.all_to_all(block, 'x', 0, 0, tiled=True)]
    pallas_call x11 -> x12, Pallas kernels: 20.8 us -> 22.7 us  [call(): pl.pallas_call(body, out_shape=outs, in_specs=[smem] * scalars + list(pla...]
    unnamed x27 -> x25, local copies, waits for them, and re-layouts: 5.11 us -> 5.09 us
  transfers between devices with their start and end apart: 16 -> 16, of which waited for: 13 -> 13; matrix products, arithmetic and copies ran while one was open for 0% -> 0% of each run, Pallas kernels for 6% -> 7%
where the time goes in v10:
time: 167 us; the launch traced here: 166 us
  starting transfers between devices  70.4 us (42%)
  waiting for transfers between devices  65.8 us (39%)
  Pallas kernels  22.7 us (14%)
  local copies, waits for them, and re-layouts  5.9 us (4%)
    all_to_all x2, starting transfers between devices, route(): return lax.all_to_all(block, ('zl', 'y', 'zh'), 0, 0, tiled=True)  29 us
    all_to_all x3, waiting for transfers between devices, over_x(): return lax.all_to_all(block, 'x', 0, 0, tiled=True)  28.1 us
    pallas_call x12, Pallas kernels, call(): pl.pallas_call(body, out_shape=outs, in_specs=[smem] * scalars + list(pla...  22.7 us
    ppermute x6, starting transfers between devices, shift(): lax.ppermute(block, 'x', [(i, (i + by) % chips) for i in range(chips)])  19.8 us
    all_to_all x2, waiting for transfers between devices, route(): return lax.all_to_all(block, ('zl', 'y', 'zh'), 0, 0, tiled=True)  16.7 us
    ppermute x6, waiting for transfers between devices, shift(): lax.ppermute(block, 'x', [(i, (i + by) % chips) for i in range(chips)])  16.3 us
    all_to_all x3, starting transfers between devices, over_x(): return lax.all_to_all(block, 'x', 0, 0, tiled=True)  12 us
    ppermute x5, starting transfers between devices, swap(): return lax.ppermute(block, 'c', [(0, 1), (1, 0)])  9.59 us
  transfers between devices with their start and end apart: 16, of which 13 were waited for; matrix products, arithmetic and copies ran while one was open for 0% of the time, Pallas kernels for 7%

profile of v10, /device:TPU:32, one launch (start us, length us, event | category | flops | bytes accessed | tf_op | source)
XLA Modules:
  0.0 165.8 jit_solution(8466196155617650)
XLA Ops:
  0.6 0.0 copy-start.1
  0.6 2.8 %shard_map.112 = bf16[512,640]{1,0:T(8,128)(2,1)} custom-call(s32[8,32]{1,0:T(8,128)} %bitcast.19, f32[8,32]{1,0:T(8,128)} %bitcast.26, bf16[32,512]{1,0:T(8,128)(2,1)} %tok_hbm.1, bf16[32,512]{1,0:T(8,128)(2,1)} %dy_hbm.1), custom_call_target="tpu_custom_call" | custom-call | tf_op jit(solution)/shard_map/pallas_call | solution.py:256
  3.5 18.6 %all-to-all-start = ((bf16[64,8,640]{2,1,0:T(8,128)(2,1)}), bf16[64,8,640]{2,1,0:T(8,128)(2,1)}, u32[]{:S(2)}, u32[]{:S(2)}) async-start(bf16[64,8,640]{2,1,0:T(8,128)(2,1)} %bitcast.2), calls=%async_computation | async-start | bytes 1310720 | tf_op jit(solution)/shard_map/all_to_all | solution.py:289
  22.1 0.1 pad_add_fusion.me_ref
  22.1 0.0 copy-done.1
  22.1 0.0 copy-start.2
  22.1 1.4 copy-done.2
  23.5 0.0 copy-start.3
  23.6 1.4 copy-done.3
  25.0 0.9 shard_map.113
  25.8 0.0 copy-start.4
  25.9 0.7 copy-done.4
  26.6 1.9 %collective-permute-start = (bf16[2,4,192,512]{3,2,1,0:T(8,128)(2,1)S(1)}, bf16[2,4,192,512]{3,2,1,0:T(8,128)(2,1)S(1)}, u32[]{:S(2)}, u32[]{:S(2)}) collective-permute-start(bf16[2,4,192,512]{3,2,1,0:T(8,128)(2,1)S(1)} %get-tuple-element.24), channel_id=1, source_target_pairs={{0,64},{64,0},{1,65},{65,1},{2,66},{66,2},{3,67},{67,3},{4,68},{68... | collective-permute-start | bytes 4718600 | tf_op jit(solution)/shard_map/ppermute | solution.py:280
  28.5 3.4 %collective-permute-start.2 = (bf16[192,1024]{1,0:T(8,128)(2,1)S(1)}, bf16[192,1024]{1,0:T(8,128)(2,1)S(1)}, u32[]{:S(2)}, u32[]{:S(2)}) collective-permute-start(bf16[192,1024]{1,0:T(8,128)(2,1)S(1)} %get-tuple-element.26), channel_id=1, source_target_pairs={{0,128},{128,256},{256,384},{384,0},{1,129},{129,257},{257,385},{3... | collective-permute-start | bytes 1179656 | tf_op jit(solution)/shard_map/ppermute | solution.py:283
  31.9 4.6 %collective-permute-start.3 = (bf16[192,1024]{1,0:T(8,128)(2,1)S(1)}, bf16[192,1024]{1,0:T(8,128)(2,1)S(1)}, u32[]{:S(2)}, u32[]{:S(2)}) collective-permute-start(bf16[192,1024]{1,0:T(8,128)(2,1)S(1)} %get-tuple-element.27), channel_id=1, source_target_pairs={{0,256},{128,384},{256,0},{384,128},{1,257},{129,385},{257,1},{385... | collective-permute-start | bytes 1179656 | tf_op jit(solution)/shard_map/ppermute | solution.py:283
  36.6 3.3 %collective-permute-start.4 = (bf16[192,1024]{1,0:T(8,128)(2,1)S(1)}, bf16[192,1024]{1,0:T(8,128)(2,1)S(1)}, u32[]{:S(2)}, u32[]{:S(2)}) collective-permute-start(bf16[192,1024]{1,0:T(8,128)(2,1)S(1)} %get-tuple-element.28), channel_id=1, source_target_pairs={{0,384},{128,0},{256,128},{384,256},{1,385},{129,1},{257,129},{385... | collective-permute-start | bytes 1179656 | tf_op jit(solution)/shard_map/ppermute | solution.py:283
  39.9 0.0 copy-done.10
  39.9 1.9 %collective-permute-start.1 = (bf16[64,512]{1,0:T(8,128)(2,1)S(1)}, bf16[64,512]{1,0:T(8,128)(2,1)S(1)}, u32[]{:S(2)}, u32[]{:S(2)}) collective-permute-start(bf16[64,512]{1,0:T(8,128)(2,1)S(1)} %bitcast.24), channel_id=1, source_target_pairs={{0,64},{64,0},{1,65},{65,1},{2,66},{66,2},{3,67},{67,3},{4,68},{68... | collective-permute-start | bytes 196616 | tf_op jit(solution)/shard_map/ppermute | solution.py:280
  41.9 1.2 collective-permute-done.1.refs_3_
  43.1 0.1 collective-permute-done.2.refs_5_
  43.1 9.4 %collective-permute-done.3.refs_6_ = bf16[192,1024]{1,0:T(8,128)(2,1)S(1)} collective-permute-done((bf16[192,1024]{1,0:T(8,128)(2,1)S(1)}, bf16[192,1024]{1,0:T(8,128)(2,1)S(1)}, u32[]{:S(2)}, u32[]{:S(2)}) %collective-permute-start.3) | collective-permute-done | bytes 393248 | tf_op jit(solution)/shard_map/ppermute | solution.py:283
  52.5 1.5 collective-permute-done.4.refs_7_
  54.1 0.0 copy-done.11
  54.1 0.0 copy-done.7
  54.1 0.7 copy-done.8
  54.8 0.0 collective-permute-done.half_ref
  54.9 6.5 %all-to-all-done = bf16[64,8,640]{2,1,0:T(8,128)(2,1)} async-done(((bf16[64,8,640]{2,1,0:T(8,128)(2,1)}), bf16[64,8,640]{2,1,0:T(8,128)(2,1)}, u32[]{:S(2)}, u32[]{:S(2)}) %all-to-all-start) | async-done | bytes 655392 | tf_op jit(solution)/shard_map/all_to_all | solution.py:289
  61.4 2.6 %shard_map.114 = bf16[4,320,512]{2,1,0:T(8,128)(2,1)} custom-call(bf16[512,640]{1,0:T(8,128)(2,1)} %bitcast.9.in_hbm), custom_call_target="tpu_custom_call" | custom-call | tf_op jit(solution)/shard_map/pallas_call | solution.py:256
  64.0 0.0 copy-done.6
  64.0 4.3 %all-to-all-start.1 = ((bf16[4,320,512]{2,1,0:T(8,128)(2,1)}), bf16[4,320,512]{2,1,0:T(8,128)(2,1)}, u32[]{:S(2)}, u32[]{:S(2)}) async-start(bf16[4,320,512]{2,1,0:T(8,128)(2,1)} %shard_map.114), calls=%async_computation.1 | async-start | bytes 2621440 | tf_op jit(solution)/shard_map/all_to_all | solution.py:286
  68.3 2.2 %shard_map.116.refs_0_.s_ref = bf16[320,512]{1,0:T(8,128)(2,1)} custom-call(bf16[512,640]{1,0:T(8,128)(2,1)} %bitcast.9.in_hbm), custom_call_target="tpu_custom_call" | custom-call | tf_op jit(solution)/shard_map/pallas_call | solution.py:256
  70.6 1.9 %collective-permute-start.6 = (bf16[320,512]{1,0:T(8,128)(2,1)}, bf16[320,512]{1,0:T(8,128)(2,1)S(1)}, u32[]{:S(2)}, u32[]{:S(2)}) collective-permute-start(bf16[320,512]{1,0:T(8,128)(2,1)} %shard_map.116.refs_0_.s_ref), channel_id=1, source_target_pairs={{0,64},{64,0},{1,65},{65,1},{2,66},{66,2},{3,67},{67,3},{4,68},{68... | collective-permute-start | bytes 983048 | tf_op jit(solution)/shard_map/ppermute | solution.py:280
  72.5 1.8 %collective-permute-done.6.refs_1_ = bf16[320,512]{1,0:T(8,128)(2,1)S(1)} collective-permute-done((bf16[320,512]{1,0:T(8,128)(2,1)}, bf16[320,512]{1,0:T(8,128)(2,1)S(1)}, u32[]{:S(2)}, u32[]{:S(2)}) %collective-permute-start.6) | collective-permute-done | bytes 327712 | tf_op jit(solution)/shard_map/ppermute | solution.py:280
  74.3 0.7 copy-done.9
  75.0 4.0 %shard_map.117 = bf16[4,320,256]{2,1,0:T(8,128)(2,1)} custom-call(s32[2]{0:T(128)S(1)} %pad_add_fusion.me_ref, bf16[320,512]{1,0:T(8,128)(2,1)} %shard_map.116.refs_0_.s_ref, bf16[320,512]{1,0:T(8,128)(2,1)} %copy-done.9, bf16[64,512]{1,0:T(8,128)(2,1)} %bitcast.23, bf16[64,512]{1,0:T(8,128)(2,1)} %copy-done.11, bf16[192,1024]{1,0:T(8,128)(2,1)} %copy-done.4, ...), custom_call_target="tpu_custom_call" | custom-call | tf_op jit(solution)/shard_map/pallas_call | solution.py:256
  79.1 6.2 %all-to-all-done.1.x_ref = bf16[4,320,512]{2,1,0:T(8,128)(2,1)} async-done(((bf16[4,320,512]{2,1,0:T(8,128)(2,1)}), bf16[4,320,512]{2,1,0:T(8,128)(2,1)}, u32[]{:S(2)}, u32[]{:S(2)}) %all-to-all-start.1) | async-done | bytes 1310752 | tf_op jit(solution)/shard_map/all_to_all | solution.py:286
  85.3 4.2 %all-to-all-start.2 = ((bf16[4,320,256]{2,1,0:T(8,128)(2,1)}), bf16[4,320,256]{2,1,0:T(8,128)(2,1)}, u32[]{:S(2)}, u32[]{:S(2)}) async-start(bf16[4,320,256]{2,1,0:T(8,128)(2,1)} %shard_map.117), calls=%async_computation.2 | async-start | bytes 1310720 | tf_op jit(solution)/shard_map/all_to_all | solution.py:286
  89.5 3.4 %shard_map.115 = (f32[2,320,192]{2,1,0:T(8,128)}, bf16[2,320,192]{2,1,0:T(8,128)(2,1)S(1)}) custom-call(bf16[4,320,512]{2,1,0:T(8,128)(2,1)} %all-to-all-done.1.x_ref, bf16[2,4,192,512]{3,2,1,0:T(8,128)(2,1)S(1)} %get-tuple-element.30.own_ref, bf16[2,4,192,512]{3,2,1,0:T(8,128)(2,1)S(1)} %collective-permute-done.half_ref), custom_call_target="tpu_custom_call" | custom-call | tf_op jit(solution)/shard_map/pallas_call | solution.py:256
  92.9 1.9 %collective-permute-start.5 = (bf16[2,320,192]{2,1,0:T(8,128)(2,1)S(1)}, bf16[2,320,192]{2,1,0:T(8,128)(2,1)}, u32[]{:S(2)}, u32[]{:S(2)}) collective-permute-start(bf16[2,320,192]{2,1,0:T(8,128)(2,1)S(1)} %get-tuple-element.33), channel_id=1, source_target_pairs={{0,64},{64,0},{1,65},{65,1},{2,66},{66,2},{3,67},{67,3},{4,68},{68... | collective-permute-start | bytes 737288 | tf_op jit(solution)/shard_map/ppermute | solution.py:280
  94.8 3.7 %all-to-all-done.2.in_hbm = bf16[4,320,256]{2,1,0:T(8,128)(2,1)} async-done(((bf16[4,320,256]{2,1,0:T(8,128)(2,1)}), bf16[4,320,256]{2,1,0:T(8,128)(2,1)}, u32[]{:S(2)}, u32[]{:S(2)}) %all-to-all-start.2) | async-done | bytes 655392 | tf_op jit(solution)/shard_map/all_to_all | solution.py:286
  98.5 0.0 collective-permute-done.5.got_hbm
  98.5 2.3 %shard_map.118 = (bf16[320,448]{1,0:T(8,128)(2,1)S(1)}, f32[64,192]{1,0:T(8,128)}) custom-call(f32[2,320,192]{2,1,0:T(8,128)} %get-tuple-element.32.keep_hbm, bf16[2,320,192]{2,1,0:T(8,128)(2,1)} %collective-permute-done.5.got_hbm, bf16[4,320,256]{2,1,0:T(8,128)(2,1)} %all-to-all-done.2.in_hbm, bf16[64,192]{1,0:T(8,128)(2,1)} %bitcast.25), custom_call_target="tpu_custom_call" | custom-call | tf_op jit(solution)/shard_map/pallas_call | solution.py:256
  100.8 1.9 %collective-permute-start.7 = (bf16[320,448]{1,0:T(8,128)(2,1)S(1)}, bf16[320,448]{1,0:T(8,128)(2,1)S(1)}, u32[]{:S(2)}, u32[]{:S(2)}) collective-permute-start(bf16[320,448]{1,0:T(8,128)(2,1)S(1)} %get-tuple-element.39.g_ref), channel_id=1, source_target_pairs={{0,64},{64,0},{1,65},{65,1},{2,66},{66,2},{3,67},{67,3},{4,68},{68... | collective-permute-start | bytes 860168 | tf_op jit(solution)/shard_map/ppermute | solution.py:280
  102.8 1.6 collective-permute-done.7.h_ref
  104.4 2.3 %shard_map.119 = (bf16[4,320,512]{2,1,0:T(8,128)(2,1)}, bf16[320,64]{1,0:T(8,128)(2,1)S(1)}) custom-call(bf16[320,448]{1,0:T(8,128)(2,1)S(1)} %get-tuple-element.39.g_ref, bf16[320,448]{1,0:T(8,128)(2,1)S(1)} %collective-permute-done.7.h_ref, bf16[2,4,192,512]{3,2,1,0:T(8,128)(2,1)S(1)} %get-tuple-element.30.own_ref, ...), custom_call_target="tpu_custom_call" | custom-call | tf_op jit(solution)/shard_map/pallas_call | solution.py:256
  106.7 0.0 copy-start.5
  106.7 3.6 %all-to-all-start.3 = ((bf16[4,320,512]{2,1,0:T(8,128)(2,1)}), bf16[4,320,512]{2,1,0:T(8,128)(2,1)S(1)}, u32[]{:S(2)}, u32[]{:S(2)}) async-start(bf16[4,320,512]{2,1,0:T(8,128)(2,1)} %get-tuple-element.40), calls=%async_computation.3 | async-start | bytes 2621440 | tf_op jit(solution)/shard_map/all_to_all | solution.py:286
  110.3 0.0 copy-done.5
  110.3 0.0 copy-start
  110.3 0.2 shard_map.120.code_ref
  110.4 18.3 %all-to-all-done.3.in_ref = bf16[4,320,512]{2,1,0:T(8,128)(2,1)S(1)} async-done(((bf16[4,320,512]{2,1,0:T(8,128)(2,1)}), bf16[4,320,512]{2,1,0:T(8,128)(2,1)S(1)}, u32[]{:S(2)}, u32[]{:S(2)}) %all-to-all-start.3) | async-done | bytes 1310752 | tf_op jit(solution)/shard_map/all_to_all | solution.py:286
  128.7 0.2 shard_map.121
  128.9 0.8 reshape.20
  129.7 10.4 %all-to-all-start.4 = ((bf16[64,2,1280]{2,1,0:T(2,128)(2,1)}), bf16[64,2,1280]{2,1,0:T(2,128)(2,1)S(1)}, u32[]{:S(2)}, u32[]{:S(2)}) async-start(bf16[64,2,1280]{2,1,0:T(2,128)(2,1)} %reshape.20), calls=%async_computation.4 | async-start | bytes 655360 | tf_op jit(solution)/shard_map/all_to_all | solution.py:289
  140.1 3.1 %collective-permute-start.10 = (bf16[320,64]{1,0:T(8,128)(2,1)S(1)}, bf16[320,64]{1,0:T(8,128)(2,1)S(1)}, u32[]{:S(2)}, u32[]{:S(2)}) collective-permute-start(bf16[320,64]{1,0:T(8,128)(2,1)S(1)} %get-tuple-element.44.v0_ref), channel_id=1, source_target_pairs={{0,384},{128,0},{256,128},{384,256},{1,385},{129,1},{257,129},{385... | collective-permute-start | bytes 122888 | tf_op jit(solution)/shard_map/ppermute | solution.py:283
  143.2 2.8 %collective-permute-start.8 = (bf16[320,64]{1,0:T(8,128)(2,1)S(1)}, bf16[320,64]{1,0:T(8,128)(2,1)S(1)}, u32[]{:S(2)}, u32[]{:S(2)}) collective-permute-start(bf16[320,64]{1,0:T(8,128)(2,1)S(1)} %get-tuple-element.44.v0_ref), channel_id=1, source_target_pairs={{0,128},{128,256},{256,384},{384,0},{1,129},{129,257},{257,385},{3... | collective-permute-start | bytes 122888 | tf_op jit(solution)/shard_map/ppermute | solution.py:283
  146.0 2.5 %collective-permute-start.9 = (bf16[320,64]{1,0:T(8,128)(2,1)S(1)}, bf16[320,64]{1,0:T(8,128)(2,1)S(1)}, u32[]{:S(2)}, u32[]{:S(2)}) collective-permute-start(bf16[320,64]{1,0:T(8,128)(2,1)S(1)} %get-tuple-element.44.v0_ref), channel_id=1, source_target_pairs={{0,256},{128,384},{256,0},{384,128},{1,257},{129,385},{257,1},{385... | collective-permute-start | bytes 122888 | tf_op jit(solution)/shard_map/ppermute | solution.py:283
  148.5 0.0 collective-permute-done.10.v3_ref
  148.5 3.1 %collective-permute-done.8.v1_ref = bf16[320,64]{1,0:T(8,128)(2,1)S(1)} collective-permute-done((bf16[320,64]{1,0:T(8,128)(2,1)S(1)}, bf16[320,64]{1,0:T(8,128)(2,1)S(1)}, u32[]{:S(2)}, u32[]{:S(2)}) %collective-permute-start.8) | collective-permute-done | bytes 40992 | tf_op jit(solution)/shard_map/ppermute | solution.py:283
  151.6 2.2 %collective-permute-done.9.v2_ref = bf16[320,64]{1,0:T(8,128)(2,1)S(1)} collective-permute-done((bf16[320,64]{1,0:T(8,128)(2,1)S(1)}, bf16[320,64]{1,0:T(8,128)(2,1)S(1)}, u32[]{:S(2)}, u32[]{:S(2)}) %collective-permute-start.9) | collective-permute-done | bytes 40992 | tf_op jit(solution)/shard_map/ppermute | solution.py:283
  153.8 0.0 copy-done
  153.8 0.9 shard_map.123
  154.7 10.2 %all-to-all-done.4 = bf16[64,2,1280]{2,1,0:T(2,128)(2,1)S(1)} async-done(((bf16[64,2,1280]{2,1,0:T(2,128)(2,1)}), bf16[64,2,1280]{2,1,0:T(2,128)(2,1)S(1)}, u32[]{:S(2)}, u32[]{:S(2)}) %all-to-all-start.4) | async-done | bytes 327712 | tf_op jit(solution)/shard_map/all_to_all | solution.py:289
  164.9 0.8 shard_map.122
  (7 shorter events, 0.0 us)
Async XLA Ops:
  0.6 21.5 %copy-start.1 = (bf16[1,192,4096]{2,1,0:T(8,128)(2,1)S(1)}, bf16[1,192,4096]{2,1,0:T(8,128)(2,1)}, u32[]{:S(2)}) copy-start(bf16[1,192,4096]{2,1,0:T(8,128)(2,1)} %param.13) | copy-start | bytes 4718596
  3.5 57.9 %all-to-all-start = ((bf16[64,8,640]{2,1,0:T(8,128)(2,1)}), bf16[64,8,640]{2,1,0:T(8,128)(2,1)}, u32[]{:S(2)}, u32[]{:S(2)}) async-start(bf16[64,8,640]{2,1,0:T(8,128)(2,1)} %bitcast.2), calls=%async_computation | async-start | bytes 1310720 | tf_op jit(solution)/shard_map/all_to_all | solution.py:289
  22.1 1.4 copy-start.2
  23.5 1.4 copy-start.3
  25.0 15.0 %copy-start.10 = (bf16[1,64,512]{2,1,0:T(8,128)(2,1)S(1)}, bf16[1,64,512]{2,1,0:T(8,128)(2,1)}, u32[]{:S(2)}) copy-start(bf16[1,64,512]{2,1,0:T(8,128)(2,1)} %param.17) | copy-start | bytes 196612
  25.8 0.7 copy-start.4
  26.6 28.3 %collective-permute-start = (bf16[2,4,192,512]{3,2,1,0:T(8,128)(2,1)S(1)}, bf16[2,4,192,512]{3,2,1,0:T(8,128)(2,1)S(1)}, u32[]{:S(2)}, u32[]{:S(2)}) collective-permute-start(bf16[2,4,192,512]{3,2,1,0:T(8,128)(2,1)S(1)} %get-tuple-element.24), channel_id=1, source_target_pairs={{0,64},{64,0},{1,65},{65,1},{2,66},{66,2},{3,67},{67,3},{4,68},{68... | collective-permute-start | bytes 4718600 | tf_op jit(solution)/shard_map/ppermute | solution.py:280
  28.5 14.6 %collective-permute-start.2 = (bf16[192,1024]{1,0:T(8,128)(2,1)S(1)}, bf16[192,1024]{1,0:T(8,128)(2,1)S(1)}, u32[]{:S(2)}, u32[]{:S(2)}) collective-permute-start(bf16[192,1024]{1,0:T(8,128)(2,1)S(1)} %get-tuple-element.26), channel_id=1, source_target_pairs={{0,128},{128,256},{256,384},{384,0},{1,129},{129,257},{257,385},{3... | collective-permute-start | bytes 1179656 | tf_op jit(solution)/shard_map/ppermute | solution.py:283
  31.9 20.6 %collective-permute-start.3 = (bf16[192,1024]{1,0:T(8,128)(2,1)S(1)}, bf16[192,1024]{1,0:T(8,128)(2,1)S(1)}, u32[]{:S(2)}, u32[]{:S(2)}) collective-permute-start(bf16[192,1024]{1,0:T(8,128)(2,1)S(1)} %get-tuple-element.27), channel_id=1, source_target_pairs={{0,256},{128,384},{256,0},{384,128},{1,257},{129,385},{257,1},{385... | collective-permute-start | bytes 1179656 | tf_op jit(solution)/shard_map/ppermute | solution.py:283
  36.6 17.5 %collective-permute-start.4 = (bf16[192,1024]{1,0:T(8,128)(2,1)S(1)}, bf16[192,1024]{1,0:T(8,128)(2,1)S(1)}, u32[]{:S(2)}, u32[]{:S(2)}) collective-permute-start(bf16[192,1024]{1,0:T(8,128)(2,1)S(1)} %get-tuple-element.28), channel_id=1, source_target_pairs={{0,384},{128,0},{256,128},{384,256},{1,385},{129,1},{257,129},{385... | collective-permute-start | bytes 1179656 | tf_op jit(solution)/shard_map/ppermute | solution.py:283
  39.9 3.1 %collective-permute-start.1 = (bf16[64,512]{1,0:T(8,128)(2,1)S(1)}, bf16[64,512]{1,0:T(8,128)(2,1)S(1)}, u32[]{:S(2)}, u32[]{:S(2)}) collective-permute-start(bf16[64,512]{1,0:T(8,128)(2,1)S(1)} %bitcast.24), channel_id=1, source_target_pairs={{0,64},{64,0},{1,65},{65,1},{2,66},{66,2},{3,67},{67,3},{4,68},{68... | collective-permute-start | bytes 196616 | tf_op jit(solution)/shard_map/ppermute | solution.py:280
  43.1 11.0 %copy-start.11 = (bf16[64,512]{1,0:T(8,128)(2,1)}, bf16[64,512]{1,0:T(8,128)(2,1)S(1)}, u32[]{:S(2)}) copy-start(bf16[64,512]{1,0:T(8,128)(2,1)S(1)} %collective-permute-done.1.refs_3_) | copy-start | bytes 196612
  43.1 20.9 %copy-start.6 = (bf16[192,1024]{1,0:T(8,128)(2,1)}, bf16[192,1024]{1,0:T(8,128)(2,1)S(1)}, u32[]{:S(2)}) copy-start(bf16[192,1024]{1,0:T(8,128)(2,1)S(1)} %collective-permute-done.2.refs_5_) | copy-start | bytes 1179652
  52.5 1.6 copy-start.7
  54.1 0.7 copy-start.8
  64.0 21.3 %all-to-all-start.1 = ((bf16[4,320,512]{2,1,0:T(8,128)(2,1)}), bf16[4,320,512]{2,1,0:T(8,128)(2,1)}, u32[]{:S(2)}, u32[]{:S(2)}) async-start(bf16[4,320,512]{2,1,0:T(8,128)(2,1)} %shard_map.114), calls=%async_computation.1 | async-start | bytes 2621440 | tf_op jit(solution)/shard_map/all_to_all | solution.py:286
  70.6 3.7 %collective-permute-start.6 = (bf16[320,512]{1,0:T(8,128)(2,1)}, bf16[320,512]{1,0:T(8,128)(2,1)S(1)}, u32[]{:S(2)}, u32[]{:S(2)}) collective-permute-start(bf16[320,512]{1,0:T(8,128)(2,1)} %shard_map.116.refs_0_.s_ref), channel_id=1, source_target_pairs={{0,64},{64,0},{1,65},{65,1},{2,66},{66,2},{3,67},{67,3},{4,68},{68... | collective-permute-start | bytes 983048 | tf_op jit(solution)/shard_map/ppermute | solution.py:280
  74.3 0.7 copy-start.9
  85.3 13.2 %all-to-all-start.2 = ((bf16[4,320,256]{2,1,0:T(8,128)(2,1)}), bf16[4,320,256]{2,1,0:T(8,128)(2,1)}, u32[]{:S(2)}, u32[]{:S(2)}) async-start(bf16[4,320,256]{2,1,0:T(8,128)(2,1)} %shard_map.117), calls=%async_computation.2 | async-start | bytes 1310720 | tf_op jit(solution)/shard_map/all_to_all | solution.py:286
  92.9 5.6 %collective-permute-start.5 = (bf16[2,320,192]{2,1,0:T(8,128)(2,1)S(1)}, bf16[2,320,192]{2,1,0:T(8,128)(2,1)}, u32[]{:S(2)}, u32[]{:S(2)}) collective-permute-start(bf16[2,320,192]{2,1,0:T(8,128)(2,1)S(1)} %get-tuple-element.33), channel_id=1, source_target_pairs={{0,64},{64,0},{1,65},{65,1},{2,66},{66,2},{3,67},{67,3},{4,68},{68... | collective-permute-start | bytes 737288 | tf_op jit(solution)/shard_map/ppermute | solution.py:280
  100.8 3.5 %collective-permute-start.7 = (bf16[320,448]{1,0:T(8,128)(2,1)S(1)}, bf16[320,448]{1,0:T(8,128)(2,1)S(1)}, u32[]{:S(2)}, u32[]{:S(2)}) collective-permute-start(bf16[320,448]{1,0:T(8,128)(2,1)S(1)} %get-tuple-element.39.g_ref), channel_id=1, source_target_pairs={{0,64},{64,0},{1,65},{65,1},{2,66},{66,2},{3,67},{67,3},{4,68},{68... | collective-permute-start | bytes 860168 | tf_op jit(solution)/shard_map/ppermute | solution.py:280
  106.7 3.6 %copy-start.5 = (s32[32,8]{0,1:T(8,128)S(1)}, s32[32,8]{0,1:T(8,128)}, u32[]{:S(2)}) copy-start(s32[32,8]{0,1:T(8,128)} %param.12) | copy-start | bytes 3076
  106.7 22.0 %all-to-all-start.3 = ((bf16[4,320,512]{2,1,0:T(8,128)(2,1)}), bf16[4,320,512]{2,1,0:T(8,128)(2,1)S(1)}, u32[]{:S(2)}, u32[]{:S(2)}) async-start(bf16[4,320,512]{2,1,0:T(8,128)(2,1)} %get-tuple-element.40), calls=%async_computation.3 | async-start | bytes 2621440 | tf_op jit(solution)/shard_map/all_to_all | solution.py:286
  110.3 43.5 %copy-start = (bf16[320,512]{1,0:T(8,128)(2,1)S(1)}, bf16[320,512]{1,0:T(8,128)(2,1)}, u32[]{:S(2)}) copy-start(bf16[320,512]{1,0:T(8,128)(2,1)} %shard_map.116.refs_0_.s_ref) | copy-start | bytes 983044
  129.7 35.2 %all-to-all-start.4 = ((bf16[64,2,1280]{2,1,0:T(2,128)(2,1)}), bf16[64,2,1280]{2,1,0:T(2,128)(2,1)S(1)}, u32[]{:S(2)}, u32[]{:S(2)}) async-start(bf16[64,2,1280]{2,1,0:T(2,128)(2,1)} %reshape.20), calls=%async_computation.4 | async-start | bytes 655360 | tf_op jit(solution)/shard_map/all_to_all | solution.py:289
  140.1 8.4 %collective-permute-start.10 = (bf16[320,64]{1,0:T(8,128)(2,1)S(1)}, bf16[320,64]{1,0:T(8,128)(2,1)S(1)}, u32[]{:S(2)}, u32[]{:S(2)}) collective-permute-start(bf16[320,64]{1,0:T(8,128)(2,1)S(1)} %get-tuple-element.44.v0_ref), channel_id=1, source_target_pairs={{0,384},{128,0},{256,128},{384,256},{1,385},{129,1},{257,129},{385... | collective-permute-start | bytes 122888 | tf_op jit(solution)/shard_map/ppermute | solution.py:283
  143.2 8.4 %collective-permute-start.8 = (bf16[320,64]{1,0:T(8,128)(2,1)S(1)}, bf16[320,64]{1,0:T(8,128)(2,1)S(1)}, u32[]{:S(2)}, u32[]{:S(2)}) collective-permute-start(bf16[320,64]{1,0:T(8,128)(2,1)S(1)} %get-tuple-element.44.v0_ref), channel_id=1, source_target_pairs={{0,128},{128,256},{256,384},{384,0},{1,129},{129,257},{257,385},{3... | collective-permute-start | bytes 122888 | tf_op jit(solution)/shard_map/ppermute | solution.py:283
  146.0 7.8 %collective-permute-start.9 = (bf16[320,64]{1,0:T(8,128)(2,1)S(1)}, bf16[320,64]{1,0:T(8,128)(2,1)S(1)}, u32[]{:S(2)}, u32[]{:S(2)}) collective-permute-start(bf16[320,64]{1,0:T(8,128)(2,1)S(1)} %get-tuple-element.44.v0_ref), channel_id=1, source_target_pairs={{0,256},{128,384},{256,0},{384,128},{1,257},{129,385},{257,1},{385... | collective-permute-start | bytes 122888 | tf_op jit(solution)/shard_map/ppermute | solution.py:283
